TPU v7x, 32 devices: a whole 2x2x4 slice. The times are simulated.
32 devices in a mesh: section: 2 (over core), dp: 4 (over z), tensor: 4 (over y, x).
Axes of the slice: x: 2, y: 2, z: 4, core: 2. Of those that a mesh axis runs over, the one named last changes fastest.
Arguments:
- boundary: bfloat16 [2, 8, 256, 1792], P('section', 'dp', 'tensor'), may hold values from -6 to 6
- lengths: int32 [8], P('dp'), may hold values from 32 to 256, as said below
- norm_gains: float32 [2, 2, 1792], P('section'), may hold values from 0.5 to 1.5
- conv_taps: float32 [2, 3, 1792], P('section'), may hold values from -3 to 3
- lin_qk: bfloat16 [1792, 2, 256], P('dp', None, 'tensor'), may hold values from -0.125 to 0.125
- win_qk: bfloat16 [1792, 2, 1792], P('dp', None, 'tensor'), may hold values from -0.125 to 0.125
- value_gate: bfloat16 [2, 1792, 2, 1792], P('section', 'dp', None, 'tensor'), may hold values from -0.125 to 0.125
- out_weight: bfloat16 [2, 1792, 1792], P('section', 'tensor', 'dp'), may hold values from -1 to 1
- gate_up: bfloat16 [2, 1792, 2, 4864], P('section', 'dp', None, 'tensor'), may hold values from -0.125 to 0.125
- down_weight: bfloat16 [2, 4864, 1792], P('section', 'tensor', 'dp'), may hold values from -0.078125 to 0.078125
Outputs:
- ends: float32 [2, 8, 256, 1792], P('section', 'dp', 'tensor')
- grad_gains: float32 [2, 2, 1792], P('section')
- grad_taps: float32 [2, 3, 1792], P('section')
- grad_lin_qk: float32 [1792, 2, 256], P('dp', None, 'tensor')
- grad_win_qk: float32 [1792, 2, 1792], P('dp', None, 'tensor')
- grad_value_gate: float32 [2, 1792, 2, 1792], P('section', 'dp', None, 'tensor')
- grad_out_weight: float32 [2, 1792, 1792], P('section', 'tensor', 'dp')
- grad_gate_up: float32 [2, 1792, 2, 4864], P('section', 'dp', None, 'tensor')
- grad_down_weight: float32 [2, 4864, 1792], P('section', 'tensor', 'dp')
Inputs may be any that keep to these rules, and one draw needn't show every extreme that they name: `lengths`: in each aligned block of 2 sequences (those of one dp index) one sequence, drawn from the seed, has length 256.
All inputs are finite; a program needn't handle non-finite values.
Results may differ from a plain program's by a relative error of at most 0.04.
Values may be sent and summed in bfloat16 or wider, within the bound.
No kernel may reach another device: no remote copies, remote signals or barrier semaphores. Data moves between devices by JAX's collectives and lax.ppermute only.
A program may use at most 320 MiB of HBM per device.

v0:
```python
import math

import jax
import jax.numpy as jnp
from jax import lax
from jax.sharding import PartitionSpec as P

WIN = 64
HD = 112


EPS = 1e-06


def from_behind(block, axis, distance):
    devices = range(lax.axis_size(axis))
    route = [(i - distance, i) for i in devices if i - distance in devices]
    return lax.ppermute(block, axis, route)


def silu_slope(value):
    sigma = jax.nn.sigmoid(value)
    return sigma * (1.0 + value * (1.0 - sigma))


def rms_rows(rows, gain):
    scale = lax.rsqrt(jnp.mean(rows * rows, axis=-1, keepdims=True) + EPS)
    return (scale, rows * scale * gain)


def rms_back(rows, scale, gain, grad):
    normal = rows * scale
    weighted = grad * gain
    inner = jnp.mean(weighted * normal, axis=-1, keepdims=True)
    return (scale * (weighted - normal * inner), jnp.sum(grad * normal, axis=0))


def causal_conv(values, taps):
    total = values * taps[0]
    for offset in range(1, taps.shape[0]):
        moved = jnp.pad(values[:-offset], ((offset, 0), (0, 0)))
        total = total + moved * taps[offset]
    return total


def conv_back(grad, values, taps):
    grad_values = grad * taps[0]
    grad_taps = [jnp.sum(grad * values, axis=0)]
    for offset in range(1, taps.shape[0]):
        grad_values = grad_values + jnp.pad(grad[offset:], ((0, offset), (0, 0))) * taps[offset]
        grad_taps.append(jnp.sum(grad[offset:] * values[:-offset], axis=0))
    return (grad_values, jnp.stack(grad_taps))


def spread_rows(rows):
    return lax.all_gather(rows, "tensor", axis=0, tiled=True)


def collect_rows(terms):
    return lax.psum_scatter(
        terms.astype(jnp.bfloat16), "tensor", scatter_dimension=0, tiled=True
    ).astype(jnp.float32)


def spread_grads(rows):
    return lax.all_gather(rows, "tensor", axis=0, tiled=True)


def collect_grads(terms):
    return lax.psum_scatter(
        terms.astype(jnp.bfloat16), "tensor", scatter_dimension=0, tiled=True
    ).astype(jnp.float32)


def fetch_weights(local):
    vgate_part, outw_part, gup_part, down_part = local
    return (
        lax.all_gather(vgate_part, "dp", axis=0, tiled=True),
        lax.all_gather(outw_part, "dp", axis=1, tiled=True),
        lax.all_gather(gup_part, "dp", axis=0, tiled=True),
        lax.all_gather(down_part, "dp", axis=1, tiled=True),
    )


def fetch_again(local):
    vgate_part, outw_part, gup_part, down_part = local
    return (
        lax.all_gather(vgate_part, "dp", axis=0, tiled=True),
        lax.all_gather(outw_part, "dp", axis=1, tiled=True),
        lax.all_gather(gup_part, "dp", axis=0, tiled=True),
        lax.all_gather(down_part, "dp", axis=1, tiled=True),
    )


def reduce_grads(grads):
    vgate_part, outw_part, gup_part, down_part = grads
    return (
        lax.psum_scatter(
            vgate_part.astype(jnp.bfloat16), "dp", scatter_dimension=0, tiled=True
        ).astype(jnp.float32),
        lax.psum_scatter(
            outw_part.astype(jnp.bfloat16), "dp", scatter_dimension=1, tiled=True
        ).astype(jnp.float32),
        lax.psum_scatter(
            gup_part.astype(jnp.bfloat16), "dp", scatter_dimension=0, tiled=True
        ).astype(jnp.float32),
        lax.psum_scatter(
            down_part.astype(jnp.bfloat16), "dp", scatter_dimension=1, tiled=True
        ).astype(jnp.float32),
    )


def project_pair(full, weight, heads):
    length = full.shape[0]
    query_key_pair = jnp.dot(
        full, weight.reshape(weight.shape[0], -1), preferred_element_type=jnp.float32
    )
    query_key_pair = query_key_pair.astype(jnp.bfloat16).reshape(length, 2, heads, -1)
    return (query_key_pair[:, 0], query_key_pair[:, 1])


def score_block(query_rows, key_rows):
    window_width = query_rows.shape[-1]
    return jnp.einsum(
        "loc,moc->olm", query_rows, key_rows, preferred_element_type=jnp.float32
    ) / math.sqrt(window_width)


def causal_mask(length):
    place = jnp.arange(length)
    return (place[None, :] <= place[:, None], place)


def taylor_probs(logit_scores):
    causal, place = causal_mask(logit_scores.shape[-1])
    kernel = jnp.where(causal[None], 1.0 + logit_scores + 0.5 * logit_scores * logit_scores, 0.0)
    total = jnp.sum(kernel, axis=-1, keepdims=True)
    return (kernel / total, total, causal)


def window_probs(logit_scores):
    causal, place = causal_mask(logit_scores.shape[-1])
    allowed = causal & (place[:, None] - place[None, :] < WIN)
    return jax.nn.softmax(jnp.where(allowed[None], logit_scores, -1e30), axis=-1)


def attend(probs, values, heads):
    length = values.shape[0]
    mixed = jnp.einsum(
        "hqk,khd->qhd",
        probs.astype(jnp.bfloat16),
        values.reshape(length, heads, -1),
        preferred_element_type=jnp.float32,
    )
    return mixed.reshape(length, -1)


def taylor_forward(full, values, lin_weight, win_weight):
    heads = values.shape[1] // HD
    query_rows, key_rows = project_pair(full, lin_weight, heads)
    probs = taylor_probs(score_block(query_rows, key_rows))[0]
    return attend(probs, values, heads)


def window_forward(full, values, lin_weight, win_weight):
    heads = values.shape[1] // HD
    query_rows, key_rows = project_pair(full, win_weight, heads)
    return attend(window_probs(score_block(query_rows, key_rows)), values, heads)


def attend_back(exact, values, grad_mixed, heads):
    length = values.shape[0]
    grad_heads = grad_mixed.reshape(length, heads, -1)
    grad_values = jnp.einsum(
        "hqk,qhd->khd", exact.astype(jnp.bfloat16), grad_heads, preferred_element_type=jnp.float32
    )
    grad_probs = jnp.einsum(
        "qhd,khd->hqk",
        grad_heads,
        values.reshape(length, heads, -1),
        preferred_element_type=jnp.float32,
    )
    centre = jnp.sum(exact * grad_probs, axis=-1, keepdims=True)
    return (grad_values.reshape(length, -1), grad_probs - centre)


def pair_back(full, weight, query_rows, key_rows, score_gradient):
    window_width = query_rows.shape[-1]
    grad_queries = (
        jnp.einsum("trs,stn->rtn", score_gradient, key_rows, preferred_element_type=jnp.float32)
        / math.sqrt(window_width)
    ).astype(jnp.bfloat16)
    grad_keys = (
        jnp.einsum("vpw,pve->wve", score_gradient, query_rows, preferred_element_type=jnp.float32)
        / math.sqrt(window_width)
    ).astype(jnp.bfloat16)
    grad_pair = jnp.stack([grad_queries, grad_keys], axis=1).reshape(full.shape[0], -1)
    grad_weight = jnp.einsum(
        "nd,nc->dc", full, grad_pair, preferred_element_type=jnp.float32
    ).reshape(weight.shape)
    grad_full = jnp.einsum(
        "nc,dc->nd",
        grad_pair,
        weight.reshape(weight.shape[0], -1),
        preferred_element_type=jnp.float32,
    )
    return (grad_full, grad_weight)


def taylor_backward(full, values, grad_mixed, lin_weight, win_weight):
    heads = values.shape[1] // HD
    query_rows, key_rows = project_pair(full, lin_weight, heads)
    logit_scores = score_block(query_rows, key_rows)
    exact, total, causal = taylor_probs(logit_scores)
    grad_values, centred = attend_back(exact, values, grad_mixed, heads)
    score_gradient = jnp.where(causal[None], centred / total * (1.0 + logit_scores), 0.0).astype(
        jnp.bfloat16
    )
    grad_full, grad_lin = pair_back(full, lin_weight, query_rows, key_rows, score_gradient)
    return (grad_values, grad_full, grad_lin, jnp.zeros(win_weight.shape, jnp.float32))


def window_backward(full, values, grad_mixed, lin_weight, win_weight):
    heads = values.shape[1] // HD
    query_rows, key_rows = project_pair(full, win_weight, heads)
    exact = window_probs(score_block(query_rows, key_rows))
    grad_values, centred = attend_back(exact, values, grad_mixed, heads)
    score_gradient = (exact * centred).astype(jnp.bfloat16)
    grad_full, grad_win = pair_back(full, win_weight, query_rows, key_rows, score_gradient)
    return (grad_values, grad_full, jnp.zeros(lin_weight.shape, jnp.float32), grad_win)


def layer_forward(rows, weights, gains, taps, first):
    lin_w, win_w, vgate_w, outw_w, gup_w, down_w = weights
    window_width = rows.shape[1]
    scale_one, normed = rms_rows(rows, gains[0])
    full_one = spread_rows(normed.astype(jnp.bfloat16))
    length = full_one.shape[0]
    both = jnp.dot(
        full_one, vgate_w.reshape(window_width, -1), preferred_element_type=jnp.float32
    ).reshape(length, 2, -1)
    pre_values = both[:, 0]
    gate_mix = both[:, 1]
    values = causal_conv(pre_values, taps).astype(jnp.bfloat16)
    mixed = lax.cond(first, taylor_forward, window_forward, full_one, values, lin_w, win_w)
    gated = (mixed * jax.nn.silu(gate_mix)).astype(jnp.bfloat16)
    hidden = rows + collect_rows(jnp.dot(gated, outw_w, preferred_element_type=jnp.float32))
    scale_two, normed_two = rms_rows(hidden, gains[1])
    full_two = spread_rows(normed_two.astype(jnp.bfloat16))
    halves = jnp.dot(
        full_two, gup_w.reshape(window_width, -1), preferred_element_type=jnp.float32
    ).reshape(length, 2, -1)
    gate = halves[:, 0]
    upper = halves[:, 1]
    inner = (jax.nn.silu(gate) * upper).astype(jnp.bfloat16)
    output = hidden + collect_rows(jnp.dot(inner, down_w, preferred_element_type=jnp.float32))
    return (
        rows,
        scale_one,
        full_one,
        pre_values,
        gate_mix,
        values,
        mixed,
        gated,
        hidden,
        scale_two,
        full_two,
        gate,
        upper,
        inner,
        output,
    )


def layer_backward(kept, grad_out, weights, gains, taps, first):
    (
        rows,
        scale_one,
        full_one,
        pre_values,
        gate_mix,
        values,
        mixed,
        gated,
        hidden,
        scale_two,
        full_two,
        gate,
        upper,
        inner,
        output,
    ) = kept
    lin_w, win_w, vgate_w, outw_w, gup_w, down_w = weights
    window_width = rows.shape[1]
    branch_two = spread_grads(grad_out.astype(jnp.bfloat16))
    grad_down = jnp.einsum("nf,nd->fd", inner, branch_two, preferred_element_type=jnp.float32)
    grad_inner = jnp.einsum("nd,fd->nf", branch_two, down_w, preferred_element_type=jnp.float32)
    grad_gate = (grad_inner * upper * silu_slope(gate)).astype(jnp.bfloat16)
    grad_upper = (grad_inner * jax.nn.silu(gate)).astype(jnp.bfloat16)
    grad_halves = jnp.concatenate([grad_gate, grad_upper], axis=1)
    grad_gate_up = jnp.einsum(
        "nd,nc->dc", full_two, grad_halves, preferred_element_type=jnp.float32
    ).reshape(gup_w.shape)
    grad_second = collect_grads(
        jnp.einsum(
            "nc,dc->nd",
            grad_halves,
            gup_w.reshape(window_width, -1),
            preferred_element_type=jnp.float32,
        )
    )
    back_two, gain_two = rms_back(hidden, scale_two, gains[1], grad_second)
    grad_hidden = grad_out + back_two
    branch_one = spread_grads(grad_hidden.astype(jnp.bfloat16))
    grad_outw = jnp.einsum("nc,nd->cd", gated, branch_one, preferred_element_type=jnp.float32)
    grad_gated = jnp.einsum("nd,cd->nc", branch_one, outw_w, preferred_element_type=jnp.float32)
    grad_mixed = (grad_gated * jax.nn.silu(gate_mix)).astype(jnp.bfloat16)
    grad_mix_gate = (grad_gated * mixed * silu_slope(gate_mix)).astype(jnp.bfloat16)
    grad_values, grad_first_part, grad_lin, grad_win = lax.cond(
        first, taylor_backward, window_backward, full_one, values, grad_mixed, lin_w, win_w
    )
    grad_pre, grad_taps = conv_back(grad_values, pre_values, taps)
    grad_pair = jnp.concatenate([grad_pre.astype(jnp.bfloat16), grad_mix_gate], axis=1)
    grad_vgate = jnp.einsum(
        "nd,nc->dc", full_one, grad_pair, preferred_element_type=jnp.float32
    ).reshape(vgate_w.shape)
    grad_first_part = grad_first_part + jnp.einsum(
        "nc,dc->nd",
        grad_pair,
        vgate_w.reshape(window_width, -1),
        preferred_element_type=jnp.float32,
    )
    grad_first = collect_grads(grad_first_part)
    back_one, gain_one = rms_back(rows, scale_one, gains[0], grad_first)
    grad_rows = grad_hidden + back_one
    return (
        grad_rows,
        (grad_lin, grad_win),
        (grad_vgate, grad_outw, grad_gate_up, grad_down),
        jnp.stack([gain_one, gain_two]),
        grad_taps,
    )


def send_forward(rows):
    return from_behind(rows, "section", 1)


def send_back(rows):
    return from_behind(rows, "section", -1)


def body(
    boundary,
    lengths,
    norm_gains,
    conv_taps,
    lin_qk,
    win_qk,
    value_gate,
    out_weight,
    gate_up,
    down_weight,
):
    first = lax.axis_index("section") == 0
    count = boundary.shape[1]
    rows_dev = boundary.shape[2]
    window_width = boundary.shape[3]
    gains = norm_gains[0]
    channels = value_gate.shape[-1]
    offset = lax.axis_index("tensor") * channels
    taps = lax.dynamic_slice_in_dim(conv_taps[0], offset, channels, 1)
    local = (value_gate[0], out_weight[0], gate_up[0], down_weight[0])
    place = lax.axis_index("tensor") * rows_dev + jnp.arange(rows_dev)
    masks = (place[None, :] < lengths[:, None]).astype(jnp.float32)[:, :, None]
    own = boundary[0].astype(jnp.float32)
    pair_held = (
        lax.all_gather(lin_qk, "dp", axis=0, tiled=True),
        lax.all_gather(win_qk, "dp", axis=0, tiled=True),
    )
    received = jnp.zeros((rows_dev, window_width), jnp.bfloat16)
    kept_list = []
    for tick in range(count + 1):
        entering = jnp.where(first, own[min(tick, count - 1)], received.astype(jnp.float32))
        kept = layer_forward(
            entering, tuple(pair_held) + tuple(fetch_weights(local)), gains, taps, first
        )
        kept_list.append(kept)
        if tick < count:
            received = send_forward(kept[-1].astype(jnp.bfloat16))
    returned = jnp.zeros((rows_dev, window_width), jnp.bfloat16)
    grad_total = None
    pair_total = None
    gain_total = jnp.zeros((2, window_width), jnp.float32)
    taps_total = jnp.zeros((taps.shape[0], channels), jnp.float32)
    grad_list = []
    for tick in range(count + 1):
        mine = kept_list[max(tick - 1, 0)]
        later = kept_list[min(tick + 1, count)]
        chosen = jax.tree.map(lambda one, two: jnp.where(first, one, two), mine, later)
        valid = jnp.where(first, tick >= 1, tick < count)
        cot_index = min(tick, count - 1)
        cotangent = jnp.where(
            first, returned.astype(jnp.float32), own[cot_index] * masks[cot_index]
        )
        grad_rows, pair_part, grads, gain_part, taps_part = layer_backward(
            chosen, cotangent, tuple(pair_held) + tuple(fetch_again(local)), gains, taps, first
        )
        grads = tuple((jnp.where(valid, grad, 0.0) for grad in grads))
        pair_part = tuple((jnp.where(valid, grad, 0.0) for grad in pair_part))
        if grad_total is None:
            grad_total = grads
            pair_total = pair_part
        else:
            grad_total = tuple((total + grad for total, grad in zip(grad_total, grads)))
            pair_total = tuple((total + grad for total, grad in zip(pair_total, pair_part)))
        gain_total = gain_total + jnp.where(valid, gain_part, 0.0)
        taps_total = taps_total + jnp.where(valid, taps_part, 0.0)
        grad_list.append(grad_rows)
        if tick < count:
            returned = send_back(grad_rows.astype(jnp.bfloat16))
    pieces = []
    for index in range(count):
        pieces.append(
            jnp.where(first, grad_list[index + 1], kept_list[index + 1][-1] * masks[index])
        )
    ends = jnp.stack(pieces)[None]
    shards = reduce_grads(grad_total)
    lin_part, win_part = (
        lax.psum_scatter(
            pair_total[0].astype(jnp.bfloat16), "dp", scatter_dimension=0, tiled=True
        ).astype(jnp.float32),
        lax.psum_scatter(
            pair_total[1].astype(jnp.bfloat16), "dp", scatter_dimension=0, tiled=True
        ).astype(jnp.float32),
    )
    lin_grad, win_grad = (
        lax.psum(lin_part.astype(jnp.bfloat16), "section").astype(jnp.float32),
        lax.psum(win_part.astype(jnp.bfloat16), "section").astype(jnp.float32),
    )
    full_taps = lax.dynamic_update_slice_in_dim(
        jnp.zeros(conv_taps.shape[1:], jnp.float32), taps_total, offset, 1
    )
    gain_sum, taps_sum = lax.psum((gain_total, full_taps), ("dp", "tensor"))
    return (
        ends,
        gain_sum[None],
        taps_sum[None],
        lin_grad,
        win_grad,
        shards[0][None],
        shards[1][None],
        shards[2][None],
        shards[3][None],
    )


def solution(mesh):
    in_specs = (
        P("section", "dp", "tensor", None),
        P("dp"),
        P("section", None, None),
        P("section", None, None),
        P("dp", None, "tensor"),
        P("dp", None, "tensor"),
        P("section", "dp", None, "tensor"),
        P("section", "tensor", "dp"),
        P("section", "dp", None, "tensor"),
        P("section", "tensor", "dp"),
    )
    out_specs = (
        P("section", "dp", "tensor", None),
        P("section", None, None),
        P("section", None, None),
        P("dp", None, "tensor"),
        P("dp", None, "tensor"),
        P("section", "dp", None, "tensor"),
        P("section", "tensor", "dp"),
        P("section", "dp", None, "tensor"),
        P("section", "tensor", "dp"),
    )
    return jax.shard_map(body, mesh=mesh, in_specs=in_specs, out_specs=out_specs, check_vma=False)
```

profile of v0, /device:TPU:0, one launch (start us, length us, event | category | flops | bytes accessed | tf_op | source)
XLA Modules:
  0.0 1965.9 jit_solution(12778588064387372448)
XLA Ops:
  13.8 15.3 all_gather.37
  29.0 34.0 %all_gather.77 = bf16[1792,2,64]{2,1,0:T(2,128)(2,1)S(1)} all-gather(bf16[448,2,64]{2,1,0:T(2,128)(2,1)S(1)} %copy.208), channel_id=1, replica_groups=mesh['section'=2,'dp'=4,'tensor'=4] {'dp'}, dimensions={0}, use_global_device_ids=true | all-gather | bytes 573440 | tf_op jit(solution)/shard_map/all_gather | solution.py:379
  63.0 37.3 %all-gather.14.cloned.1.call-done = bf16[1,448,1792]{1,0,2:T(2,128)(2,1)} async-done(((bf16[1,448,448]{1,0,2:T(2,128)(2,1)}), bf16[1,448,1792]{1,0,2:T(2,128)(2,1)}) %all-gather.14.cloned.1.call-update) | async-done | bytes 1605648 | tf_op jit(solution)/shard_map/all_gather | solution.py:79
  100.3 8.7 copy.212
  109.1 63.6 %all-gather.12.cloned.1.call-done = bf16[1,1792,2,448]{3,2,0,1:T(2,128)(2,1)} async-done(((bf16[1,448,2,448]{3,2,0,1:T(2,128)(2,1)}), bf16[1,1792,2,448]{3,2,0,1:T(2,128)(2,1)}) %all-gather.12.cloned.1.call-update) | async-done | bytes 3211280 | tf_op jit(solution)/shard_map/all_gather | solution.py:78
  172.7 9.9 copy.207
  187.9 57.1 %all-gather.10.cloned.1.call-done = bf16[1792,2,448]{2,1,0:T(2,128)(2,1)} async-done(((bf16[448,2,448]{2,1,0:T(2,128)(2,1)}), bf16[1792,2,448]{2,1,0:T(2,128)(2,1)}) %all-gather.10.cloned.1.call-update) | async-done | bytes 3211280 | tf_op jit(solution)/shard_map/all_gather | solution.py:380
  245.1 9.3 conditional.6
  259.2 37.6 %reduce-scatter.20.cloned.1.call-done = bf16[64,1792]{1,0:T(8,128)(2,1)} async-done(((bf16[256,1792]{1,0:T(8,128)(2,1)}), bf16[64,1792]{1,0:T(8,128)(2,1)}) %reduce-scatter.20.cloned.1.call-update) | async-done | bytes 229392 | tf_op jit(solution)/shard_map/reduce_scatter | solution.py:60
  298.8 13.0 all_gather.79
  311.8 148.9 %all-gather.16.cloned.1.call-done = bf16[1,1792,2,1216]{3,2,0,1:T(2,128)(2,1)} async-done(((bf16[1,448,2,1216]{3,2,0,1:T(2,128)(2,1)}), bf16[1,1792,2,1216]{3,2,0,1:T(2,128)(2,1)}) %all-gather.16.cloned.1.call-update) | async-done | bytes 8716304 | tf_op jit(solution)/shard_map/all_gather | solution.py:80
  460.7 23.1 %copy.214 = bf16[1,1792,2,1216]{1,3,2,0:T(8,128)(2,1)} copy(bf16[1,1792,2,1216]{3,2,0,1:T(2,128)(2,1)} %all-gather.16.cloned.1.call-done) | data formatting | bytes 17432576 | tf_op jit(solution)/shard_map/all_gather | solution.py:80
  483.8 6.2 fusion.176
  492.7 54.9 %all-gather.18.cloned.1.call-done = bf16[1,1216,1792]{1,2,0:T(8,128)(2,1)} async-done(((bf16[1,1216,448]{1,2,0:T(8,128)(2,1)}), bf16[1,1216,1792]{1,2,0:T(8,128)(2,1)}) %all-gather.18.cloned.1.call-update) | async-done | bytes 4358160 | tf_op jit(solution)/shard_map/all_gather | solution.py:81
  552.9 25.1 %reduce-scatter.22.cloned.1.call-done = bf16[64,1792]{1,0:T(8,128)(2,1)} async-done(((bf16[256,1792]{1,0:T(8,128)(2,1)}), bf16[64,1792]{1,0:T(8,128)(2,1)}) %reduce-scatter.22.cloned.1.call-update) | async-done | bytes 229392 | tf_op jit(solution)/shard_map/reduce_scatter | solution.py:60
  583.9 14.1 all_gather.82
  602.6 9.3 conditional.7
  615.5 12.4 all_gather.83
  627.9 27.9 %reduce-scatter.24.cloned.1.call-done = bf16[64,1792]{1,0:T(8,128)(2,1)} async-done(((bf16[256,1792]{1,0:T(8,128)(2,1)}), bf16[64,1792]{1,0:T(8,128)(2,1)}) %reduce-scatter.24.cloned.1.call-update) | async-done | bytes 229392 | tf_op jit(solution)/shard_map/reduce_scatter | solution.py:60
  657.1 12.4 all_gather.84
  691.9 22.2 %reduce-scatter.26.cloned.1.call-done = bf16[64,1792]{1,0:T(8,128)(2,1)} async-done(((bf16[256,1792]{1,0:T(8,128)(2,1)}), bf16[64,1792]{1,0:T(8,128)(2,1)}) %reduce-scatter.26.cloned.1.call-update) | async-done | bytes 229392 | tf_op jit(solution)/shard_map/reduce_scatter | solution.py:70
  714.1 30.3 %reduce-scatter.30.cloned.1.call-done = bf16[64,1792]{1,0:T(8,128)(2,1)} async-done(((bf16[256,1792]{1,0:T(8,128)(2,1)}), bf16[64,1792]{1,0:T(8,128)(2,1)}) %reduce-scatter.30.cloned.1.call-update) | async-done | bytes 229392 | tf_op jit(solution)/shard_map/reduce_scatter | solution.py:60
  752.2 13.5 all_gather.86
  769.3 8.4 conditional.9
  783.5 10.7 all_gather.85
  801.3 27.9 %conditional.8 = (f32[256,448]{0,1:T(8,128)}, f32[256,1792]{1,0:T(8,128)}, f32[1792,2,64]{0,2,1:T(8,128)}, f32[1792,2,448]{2,1,0:T(2,128)}) conditional(s32[]{:T(128)} %convert_element_type.440, (bf16[1792,2,448]{2,1,0:T(2,128)(2,1)}, bf16[256,1792]{1,0:T(8,128)(2,1)}, bf16[256,448]{0,1:T(8,128)(2,1)}, bf16[256,448]{0,1:T(8,128)(2,1)}) %tuple.54, ...), branch_computations={%region_19.23_spmd, %region_23.26_spmd} | conditional | flops 2823946752 | bytes 72491184 | solution.py:320
  840.1 12.1 all_gather.88
  852.3 38.7 %reduce-scatter.28.cloned.1.call-done = bf16[64,1792]{1,0:T(8,128)(2,1)} async-done(((bf16[256,1792]{1,0:T(8,128)(2,1)}), bf16[64,1792]{1,0:T(8,128)(2,1)}) %reduce-scatter.28.cloned.1.call-update) | async-done | bytes 229392 | tf_op jit(solution)/shard_map/reduce_scatter | solution.py:70
  903.6 14.9 all_gather.87
  927.2 25.3 %reduce-scatter.34.cloned.1.call-done = bf16[64,1792]{1,0:T(8,128)(2,1)} async-done(((bf16[256,1792]{1,0:T(8,128)(2,1)}), bf16[64,1792]{1,0:T(8,128)(2,1)}) %reduce-scatter.34.cloned.1.call-update) | async-done | bytes 229392 | tf_op jit(solution)/shard_map/reduce_scatter | solution.py:70
  956.8 11.8 all_gather.89
  970.1 27.2 %conditional.10 = (f32[256,448]{0,1:T(8,128)}, f32[256,1792]{1,0:T(8,128)}, f32[1792,2,64]{0,2,1:T(8,128)}, f32[1792,2,448]{2,1,0:T(2,128)}) conditional(s32[]{:T(128)} %convert_element_type.440, (bf16[1792,2,448]{2,1,0:T(2,128)(2,1)}, bf16[256,1792]{1,0:T(8,128)(2,1)S(1)}, bf16[256,448]{0,1:T(8,128)(2,1)}, bf16[256,448]{0,1:T(8,128)(2,1)}) %tuple.58, ...), branch_computations={%region_39.43_spmd, %region_43.46_spmd} | conditional | flops 2823946752 | bytes 68804728 | solution.py:320
  1005.5 40.8 %reduce-scatter.36.cloned.1.call-done = bf16[64,1792]{1,0:T(8,128)(2,1)} async-done(((bf16[256,1792]{1,0:T(8,128)(2,1)}), bf16[64,1792]{1,0:T(8,128)(2,1)}) %reduce-scatter.36.cloned.1.call-update) | async-done | bytes 229392 | tf_op jit(solution)/shard_map/reduce_scatter | solution.py:70
  1054.1 13.0 all_gather.90
  1077.8 27.0 %reduce-scatter.38.cloned.1.call-done = bf16[64,1792]{1,0:T(8,128)(2,1)} async-done(((bf16[256,1792]{1,0:T(8,128)(2,1)}), bf16[64,1792]{1,0:T(8,128)(2,1)}) %reduce-scatter.38.cloned.1.call-update) | async-done | bytes 229392 | tf_op jit(solution)/shard_map/reduce_scatter | solution.py:70
  1108.4 12.3 all_gather.91
  1122.3 20.0 %conditional.11 = (f32[256,448]{0,1:T(8,128)S(1)}, f32[256,1792]{1,0:T(8,128)}, f32[1792,2,64]{0,2,1:T(8,128)}, f32[1792,2,448]{2,1,0:T(2,128)}) conditional(s32[]{:T(128)} %convert_element_type.440, (bf16[1792,2,448]{2,1,0:T(2,128)(2,1)}, bf16[256,1792]{1,0:T(8,128)(2,1)S(1)}, bf16[256,448]{0,1:T(8,128)(2,1)S(1)}, ...), branch_computations={%region_50.54_spmd, %region_54.57_spmd} | conditional | flops 2823946752 | bytes 73392360 | solution.py:320
  1177.8 9.9 fusion.230
  1191.5 8.6 fusion.228
  1203.7 10.0 add_convert_fusion
  1213.8 12.6 copy.232
  1226.4 23.4 %copy.233 = bf16[1792,2,1216]{2,1,0:T(2,128)(2,1)} copy(bf16[1792,2,1216]{0,2,1:T(8,128)(2,1)} %bitcast.796) | data formatting | bytes 17432576 | tf_op jit(solution)/shard_map/convert_element_type | solution.py:105
  1255.5 9.9 copy.231
  1265.4 9.2 add_convert_fusion.1
  1280.8 79.9 %all-reduce.15 = (f32[1,2,1792]{2,1,0:T(2,128)}, f32[1,3,1792]{2,0,1:T(1,128)}) all-reduce(f32[1,2,1792]{2,1,0:T(2,128)S(1)} %fusion.309, f32[1,3,1792]{2,0,1:T(1,128)S(1)} %dynamic_update_slice.4), channel_id=1, replica_groups=mesh['section'=2,'dp'=4,'tensor'=4] {'dp','tensor'}, use_global_device_ids=true, to_apply=%region_66.67 | all-reduce | flops 8960 | bytes 71680 | tf_op jit(solution)/shard_map/psum | solution.py:445
  1365.4 8.2 reduce-scatter.44.cloned.1.call-done
  1376.3 556.3 %all-reduce.21.cloned.1.call-done = (bf16[1792,2,448]{2,1,0:T(2,128)(2,1)}, bf16[1792,2,448]{2,1,0:T(2,128)(2,1)}, bf16[1792,2,1216]{2,1,0:T(2,128)(2,1)}) async-done(((bf16[1792,2,448]{2,1,0:T(2,128)(2,1)}, bf16[1792,2,448]{2,1,0:T(2,128)(2,1)}, bf16[1792,2,1216]{2,1,0:T(2,128)(2,1)}), (bf16[1792,2,448]{2,1,0:T(2,128)(2,1)}, bf16[1792,2,448]{2,1,0:T(2,128)(2,1)}, ...) | async-done | bytes 15138832
  1943.8 10.4 all-reduce.23.cloned.1.call-done
  (538 shorter events, 335.5 us)
Async XLA Ops:
  7.2 93.1 %all-gather.14.cloned.1.call-start = ((), (), s32[]{:S(2)}) async-start(), calls=%async_computation.30 | async-start | bytes 4587520 | tf_op jit(solution)/shard_map/all_gather | solution.py:79
  10.8 161.9 %all-gather.12.cloned.1.call-start = ((), (), s32[]{:S(2)}) async-start(), calls=%async_computation.29 | async-start | bytes 4587520 | tf_op jit(solution)/shard_map/all_gather | solution.py:78
  11.6 233.5 %all-gather.10.cloned.1.call-start = ((), (), s32[]{:S(2)}) async-start(), calls=%async_computation.15 | async-start | bytes 4587520 | tf_op jit(solution)/shard_map/all_gather | solution.py:380
  12.3 284.5 %reduce-scatter.20.cloned.1.call-start = ((), (), s32[]{:S(2)}) async-start(), calls=%async_computation.16 | async-start | bytes 1146880 | tf_op jit(solution)/shard_map/reduce_scatter | solution.py:60
  13.6 95.4 %copy-start.142 = (f32[64]{0:T(128)}, f32[64]{0:T(128)S(1)}, u32[]{:S(2)}) copy-start(f32[64]{0:T(128)S(1)} %multiply_reduce_fusion.14) | copy-start | bytes 772
  109.1 504.1 %copy-start.7 = (bf16[1,448,1792]{2,1,0:T(8,128)(2,1)}, bf16[1,448,1792]{2,1,0:T(8,128)(2,1)S(1)}, u32[]{:S(2)}) copy-start(bf16[1,448,1792]{2,1,0:T(8,128)(2,1)S(1)} %copy.212) | copy-start | bytes 4816900
  258.0 202.8 %all-gather.16.cloned.1.call-start = ((), (), s32[]{:S(2)}) async-start(), calls=%async_computation.31 | async-start | bytes 11468800 | tf_op jit(solution)/shard_map/all_gather | solution.py:80
  258.5 289.1 %all-gather.18.cloned.1.call-start = ((), (), s32[]{:S(2)}) async-start(), calls=%async_computation.32 | async-start | bytes 5734400 | tf_op jit(solution)/shard_map/all_gather | solution.py:81
  259.1 318.9 %reduce-scatter.22.cloned.1.call-start = ((), (), s32[]{:S(2)}) async-start(), calls=%async_computation.17 | async-start | bytes 1146880 | tf_op jit(solution)/shard_map/reduce_scatter | solution.py:60
  492.7 88.3 %copy-start.146 = (s32[2]{0:T(128)S(1)}, s32[2]{0:T(128)}, u32[]{:S(2)}) copy-start(s32[2]{0:T(128)} %param.23) | copy-start | bytes 28
  552.5 103.2 %reduce-scatter.24.cloned.1.call-start = ((), (), s32[]{:S(2)}) async-start(), calls=%async_computation.18 | async-start | bytes 1146880 | tf_op jit(solution)/shard_map/reduce_scatter | solution.py:60
  579.3 2.8 collective-permute-start
  615.5 98.7 %reduce-scatter.26.cloned.1.call-start = ((), (), s32[]{:S(2)}) async-start(), calls=%async_computation.19 | async-start | bytes 1146880 | tf_op jit(solution)/shard_map/reduce_scatter | solution.py:70
  657.0 87.4 %copy-start.35 = (f32[64,1792]{1,0:T(8,128)}, f32[64,1792]{1,0:T(8,128)S(1)}, u32[]{:S(2)}) copy-start(f32[64,1792]{1,0:T(8,128)S(1)} %get-tuple-element.361) | copy-start | bytes 1376260
  687.1 57.3 %reduce-scatter.30.cloned.1.call-start = ((), (), s32[]{:S(2)}) async-start(), calls=%async_computation.21 | async-start | bytes 1146880 | tf_op jit(solution)/shard_map/reduce_scatter | solution.py:60
  687.1 57.2 %copy-start.34 = (f32[64,1792]{1,0:T(8,128)S(1)}, f32[64,1792]{1,0:T(8,128)}, u32[]{:S(2)}) copy-start(f32[64,1792]{1,0:T(8,128)} %copy-done.33) | copy-start | bytes 1376260
  691.9 145.5 %reduce-scatter.32.cloned.1.call-start = ((), (), s32[]{:S(2)}) async-start(), calls=%async_computation.22 | async-start | bytes 1146880 | tf_op jit(solution)/shard_map/reduce_scatter | solution.py:60
  746.3 3.1 collective-permute-start.2
  751.4 353.4 %copy-start.5 = (f32[64,1792]{1,0:T(8,128)}, f32[64,1792]{1,0:T(8,128)S(1)}, u32[]{:S(2)}) copy-start(f32[64,1792]{1,0:T(8,128)S(1)} %get-tuple-element.353) | copy-start | bytes 1376260
  783.5 107.4 %reduce-scatter.28.cloned.1.call-start = ((), (), s32[]{:S(2)}) async-start(), calls=%async_computation.20 | async-start | bytes 1146880 | tf_op jit(solution)/shard_map/reduce_scatter | solution.py:70
  798.4 34.6 %copy-start.104 = (bf16[256,448]{0,1:T(8,128)(2,1)}, bf16[256,448]{0,1:T(8,128)(2,1)S(1)}, u32[]{:S(2)}) copy-start(bf16[256,448]{0,1:T(8,128)(2,1)S(1)} %get-tuple-element.396) | copy-start | bytes 688132
  801.3 168.9 %copy-start.10 = (bf16[256,1792]{1,0:T(8,128)(2,1)}, bf16[256,1792]{1,0:T(8,128)(2,1)S(1)}, u32[]{:S(2)}) copy-start(bf16[256,1792]{1,0:T(8,128)(2,1)S(1)} %get-tuple-element.405) | copy-start | bytes 2752516
  837.3 115.2 %reduce-scatter.34.cloned.1.call-start = ((), (), s32[]{:S(2)}) async-start(), calls=%async_computation.23 | async-start | bytes 1146880 | tf_op jit(solution)/shard_map/reduce_scatter | solution.py:70
  892.7 25.8 %slice-start.9 = ((s8[4587520]{0:T(1024)(128)(4,1)}), s8[4194304]{0:T(1024)(128)(4,1)S(1)}, s32[]{:S(2)}) async-start(s8[4587520]{0:T(1024)(128)(4,1)} %bitcast.916), calls=%async_computation.46 | async-start | bytes 8388608
  894.1 24.4 %copy-start.19 = (f32[256,2,1216]{0,2,1:T(8,128)S(1)}, f32[256,2,1216]{0,2,1:T(8,128)}, u32[]{:S(2)}) copy-start(f32[256,2,1216]{0,2,1:T(8,128)} %copy-done.17) | copy-start | bytes 7471108
  894.1 24.4 %slice-start.10 = ((s8[4587520]{0:T(1024)(128)(4,1)}), s8[393216]{0:T(1024)(128)(4,1)S(1)}, s32[]{:S(2)}) async-start(s8[4587520]{0:T(1024)(128)(4,1)} %bitcast.916), calls=%async_computation.47 | async-start | bytes 786432
  894.1 7.9 collective-permute-start.1
  895.7 26.3 %slice-start.3 = ((s8[8716288]{0:T(1024)(128)(4,1)}), s8[4194304]{0:T(1024)(128)(4,1)S(1)}, s32[]{:S(2)}) async-start(s8[8716288]{0:T(1024)(128)(4,1)} %bitcast.784), calls=%async_computation.40 | async-start | bytes 8388608
  895.7 26.3 %slice-start.4 = ((s8[8716288]{0:T(1024)(128)(4,1)}), s8[4194304]{0:T(1024)(128)(4,1)S(1)}, s32[]{:S(2)}) async-start(s8[8716288]{0:T(1024)(128)(4,1)} %bitcast.784), calls=%async_computation.41 | async-start | bytes 8388608
  922.0 30.6 %copy-start.56 = (bf16[64,1792]{1,0:T(8,128)(2,1)S(1)}, bf16[64,1792]{1,0:T(8,128)(2,1)}, u32[]{:S(2)}) copy-start(bf16[64,1792]{1,0:T(8,128)(2,1)} %reduce-scatter.32.cloned.1.call-done) | copy-start | bytes 688132
  925.5 120.8 %reduce-scatter.36.cloned.1.call-start = ((), (), s32[]{:S(2)}) async-start(), calls=%async_computation.24 | async-start | bytes 1146880 | tf_op jit(solution)/shard_map/reduce_scatter | solution.py:70
  1001.9 44.5 %copy-start.140 = (f32[64]{0:T(128)S(1)}, f32[64]{0:T(128)}, u32[]{:S(2)}) copy-start(f32[64]{0:T(128)} %get-tuple-element.423) | copy-start | bytes 772
  1005.4 42.3 %copy-start.36 = (f32[64,1792]{1,0:T(8,128)S(1)}, f32[64,1792]{1,0:T(8,128)}, u32[]{:S(2)}) copy-start(f32[64,1792]{1,0:T(8,128)} %copy-done.35) | copy-start | bytes 1376260
  1005.5 42.3 %copy-start.91 = (f32[64,1792]{1,0:T(8,128)S(1)}, f32[64,1792]{1,0:T(8,128)}, u32[]{:S(2)}) copy-start(f32[64,1792]{1,0:T(8,128)} %get-tuple-element.350) | copy-start | bytes 1376260
  1005.5 99.3 %reduce-scatter.38.cloned.1.call-start = ((), (), s32[]{:S(2)}) async-start(), calls=%async_computation.25 | async-start | bytes 1146880 | tf_op jit(solution)/shard_map/reduce_scatter | solution.py:70
  1046.3 27.9 %slice-start.6 = ((s8[8716288]{0:T(1024)(128)(4,1)}), s8[4194304]{0:T(1024)(128)(4,1)S(1)}, s32[]{:S(2)}) async-start(s8[8716288]{0:T(1024)(128)(4,1)} %bitcast.787), calls=%async_computation.43 | async-start | bytes 8388608
  1050.6 3.4 collective-permute-start.3
  1074.2 30.6 %copy-start.138 = (f32[64]{0:T(128)S(1)}, f32[64]{0:T(128)}, u32[]{:S(2)}) copy-start(f32[64]{0:T(128)} %get-tuple-element.424) | copy-start | bytes 772
  1077.8 200.1 %reduce-scatter.46.cloned.1.call-start = ((), (), s32[]{:S(2)}) async-start(), calls=%async_computation.33 | async-start | bytes 573440
  1147.3 132.2 %reduce-scatter.40.cloned.1.call-start = ((), (), s32[]{:S(2)}) async-start(), calls=%async_computation.26 | async-start | bytes 1146880 | tf_op jit(solution)/shard_map/reduce_scatter | solution.py:70
  1156.0 204.8 %reduce-scatter.42.cloned.1.call-start = ((), (), s32[]{:S(2)}) async-start(), calls=%async_computation.27 | async-start | bytes 1146880 | tf_op jit(solution)/shard_map/reduce_scatter | solution.py:60
  1161.5 201.7 %reduce-scatter.48.cloned.1.call-start = ((), (), s32[]{:S(2)}) async-start(), calls=%async_computation.34 | async-start | bytes 2293760
  1167.0 206.5 %reduce-scatter.44.cloned.1.call-start = ((), (), s32[]{:S(2)}) async-start(), calls=%async_computation.28 | async-start | bytes 5734400 | tf_op jit(solution)/shard_map/reduce_scatter | solution.py:107
  1176.3 756.2 %all-reduce.21.cloned.1.call-start = ((), (), s32[]{:S(2)}) async-start(), calls=%async_computation.35 | async-start | bytes 33030144
  1226.4 23.4 %copy-start.100 = (bf16[256,448]{0,1:T(8,128)(2,1)S(1)}, bf16[256,448]{0,1:T(8,128)(2,1)}, u32[]{:S(2)}) copy-start(bf16[256,448]{0,1:T(8,128)(2,1)} %get-tuple-element.392) | copy-start | bytes 688132
  1274.7 679.5 %all-reduce.23.cloned.1.call-start = ((), (), s32[]{:S(2)}) async-start(), calls=%async_computation.36 | async-start | bytes 2097152 | tf_op jit(solution)/shard_map/psum | solution.py:439
  1276.6 84.2 %copy-start.90 = (f32[64,1792]{1,0:T(8,128)S(1)}, f32[64,1792]{1,0:T(8,128)}, u32[]{:S(2)}) copy-start(f32[64,1792]{1,0:T(8,128)} %get-tuple-element.346) | copy-start | bytes 1376260
  1277.5 84.6 %copy-start.89 = (f32[1,64,1792]{2,1,0:T(8,128)S(1)}, f32[1,64,1792]{2,1,0:T(8,128)}, u32[]{:S(2)}) copy-start(f32[1,64,1792]{2,1,0:T(8,128)} %get-tuple-element.398) | copy-start | bytes 1376260
  (126 other events, 756.9 us)
Sparse Core Ops, SparseCore 0:
  10.9 89.3 all-gather.13
  101.9 70.7 all-gather.11
  174.3 70.7 all-gather.9
  258.1 38.6 reduce-scatter.19
  298.2 162.4 all-gather.15
  462.1 85.4 all-gather.17
  552.6 25.3 reduce-scatter.21
  615.6 40.1 reduce-scatter.23
  687.2 26.8 reduce-scatter.25
  717.5 26.8 reduce-scatter.29
  783.6 35.4 reduce-scatter.31
  837.5 53.4 reduce-scatter.27
  925.6 26.8 reduce-scatter.33
  1005.6 40.6 reduce-scatter.35
  1077.9 26.8 reduce-scatter.37
  1147.4 37.9 reduce-scatter.45
  1189.0 25.2 reduce-scatter.39
  1217.9 26.8 reduce-scatter.41
  1247.8 39.4 reduce-scatter.47
  1290.1 83.3 reduce-scatter.43
  1376.6 555.9 all-reduce.20
  1935.6 18.5 all-reduce.22
where the time goes:
time: 1980 us; the launch traced here: 1970 us
  waiting for transfers between devices  1220 us (62%)
  blocking collectives  269 us (14%)
  matrix products  209 us (11%)
  local copies, waits for them, and re-layouts  153 us (8%)
  other arithmetic  89.4 us (5%)
    unnamed x25, waiting for transfers between devices  559 us
    reduce_scatter x6, waiting for transfers between devices, collect_grads(): lax.psum_scatter(terms.astype(jnp.bfloat16), 'tensor', scatter_dimension=...  154 us
    all_gather x1, waiting for transfers between devices, fetch_weights(): lax.all_gather(gup_part, 'dp', axis=0, tiled=True)  149 us
    reduce_scatter x6, waiting for transfers between devices, collect_rows(): lax.psum_scatter(terms.astype(jnp.bfloat16), 'tensor', scatter_dimension=...  121 us
    all_gather x6, blocking collectives, spread_rows(): return lax.all_gather(rows, 'tensor', axis=0, tiled=True)  80.4 us
    psum x1, blocking collectives, body(): gain_sum, taps_sum = lax.psum((gain_total, full_taps), ('dp', 'tensor'))  79.9 us
    all_gather x6, blocking collectives, spread_grads(): return lax.all_gather(rows, 'tensor', axis=0, tiled=True)  75.1 us
    all_gather x1, waiting for transfers between devices, fetch_weights(): lax.all_gather(vgate_part, 'dp', axis=0, tiled=True)  63.6 us
  transfers between devices with their start and end apart: 26, of which 20 were waited for; matrix products, arithmetic and copies ran while one was open for 13% of the time, Pallas kernels for 0%

commit v1 on v0

v1 whole, which is shorter than its diff:
```python
import math

import jax
import jax.numpy as jnp
from jax import lax
from jax.sharding import PartitionSpec as P

WIN = 64
HD = 112
LANES = 128

EPS = 1e-06


def silu_slope(value):
    sigma = jax.nn.sigmoid(value)
    return sigma * (1.0 + value * (1.0 - sigma))


def rms_rows(rows, gain):
    scale = lax.rsqrt(jnp.mean(rows * rows, axis=-1, keepdims=True) + EPS)
    return (scale, rows * scale * gain)


def rms_back(rows, scale, gain, grad):
    normal = rows * scale
    weighted = grad * gain
    inner = jnp.mean(weighted * normal, axis=-1, keepdims=True)
    return (scale * (weighted - normal * inner), jnp.sum(grad * normal, axis=0))


def causal_conv(values, taps):
    total = values * taps[0]
    for offset in range(1, taps.shape[0]):
        moved = jnp.pad(values[:, :-offset], ((0, 0), (offset, 0), (0, 0)))
        total = total + moved * taps[offset]
    return total


def conv_back(grad, values, taps):
    grad_values = grad * taps[0]
    grad_taps = [jnp.sum(grad * values, axis=(0, 1))]
    for offset in range(1, taps.shape[0]):
        moved = jnp.pad(grad[:, offset:], ((0, 0), (0, offset), (0, 0)))
        grad_values = grad_values + moved * taps[offset]
        grad_taps.append(jnp.sum(grad[:, offset:] * values[:, :-offset], axis=(0, 1)))
    return (grad_values, jnp.stack(grad_taps))


def swap(block):
    return lax.ppermute(block, "section", [(0, 1), (1, 0)])


def spread(rows):
    mine = lax.all_gather(rows.astype(jnp.bfloat16), "tensor", axis=0, tiled=True)
    return jnp.concatenate([mine, swap(mine)], axis=0)


def collect(terms):
    length = terms.shape[0] // 2
    size = lax.axis_size("tensor")
    count = length // size
    index = lax.axis_index("tensor")
    arrived = swap(terms[length:].astype(jnp.bfloat16))
    part = terms[:length] + arrived.astype(jnp.float32)
    low = part.astype(jnp.bfloat16)
    total = lax.dynamic_slice_in_dim(part, index * count, count, 0)
    for offset in range(1, size):
        block = lax.dynamic_slice_in_dim(low, (index ^ offset) * count, count, 0)
        pairs = [(i, i ^ offset) for i in range(size)]
        total = total + lax.ppermute(block, "tensor", pairs).astype(jnp.float32)
    return total


def sum_all(block):
    for axis in ("section", "tensor", "dp"):
        size = lax.axis_size(axis)
        step = 1
        while step < size:
            pairs = [(i, i ^ step) for i in range(size)]
            block = block + lax.ppermute(block, axis, pairs)
            step *= 2
    return block


def widen(columns):
    return jnp.pad(columns, ((0, 0), (0, -columns.shape[1] % LANES)))


def dot(one, two):
    return jnp.dot(one, two, preferred_element_type=jnp.float32)


def dot_nt(one, two):
    return lax.dot_general(one, two, (((1,), (1,)), ((), ())), preferred_element_type=jnp.float32)


def dot_tn(one, two):
    return lax.dot_general(one, two, (((0,), (0,)), ((), ())), preferred_element_type=jnp.float32)


def heads_of(block, width):
    return block.reshape(2, block.shape[0] // 2, -1, width)


def score_parts(queries, keys, first):
    length = queries.shape[1]
    width = queries.shape[-1]
    scores = jnp.einsum(
        "sihc,sjhc->shij", queries, keys, preferred_element_type=jnp.float32
    ) / math.sqrt(width)
    place = jnp.arange(length)
    causal = place[None, :] <= place[:, None]
    if first:
        kernel = jnp.where(causal, 1.0 + scores + 0.5 * scores * scores, 0.0)
        total = jnp.sum(kernel, axis=-1, keepdims=True)
        slope = jnp.where(causal, (1.0 + scores) / total, 0.0)
        return (kernel / total, slope)
    allowed = causal & (place[:, None] - place[None, :] < WIN)
    probs = jax.nn.softmax(jnp.where(allowed, scores, -1e30), axis=-1)
    return (probs, probs)


def layer_forward(rows, gains, taps, attn, feed, channels, first):
    width = (attn.shape[1] - (channels + LANES - 1) // LANES * LANES - 2 * channels) // 2
    hidden_units = feed.shape[1] // 3
    scale_one, normed = rms_rows(rows, gains[0])
    full_one = spread(normed)
    both = dot(full_one, attn[:, : 2 * channels + 2 * width])
    length = full_one.shape[0] // 2
    pre_values = both[:, :channels].reshape(2, length, channels)
    gate_mix = both[:, channels : 2 * channels]
    values = causal_conv(pre_values, taps).astype(jnp.bfloat16).reshape(2, length, -1, HD)
    head_width = width // (channels // HD)
    queries = heads_of(both[:, 2 * channels : 2 * channels + width].astype(jnp.bfloat16), head_width)
    keys = heads_of(both[:, 2 * channels + width :].astype(jnp.bfloat16), head_width)
    probs, slope = score_parts(queries, keys, first)
    mixed = jnp.einsum(
        "shij,sjhc->sihc", probs.astype(jnp.bfloat16), values, preferred_element_type=jnp.float32
    ).reshape(2 * length, channels)
    gated = (mixed * jax.nn.silu(gate_mix)).astype(jnp.bfloat16)
    out_t = attn[:, 2 * channels + 2 * width :][:, :channels]
    hidden = rows + collect(dot_nt(gated, out_t))
    scale_two, normed_two = rms_rows(hidden, gains[1])
    full_two = spread(normed_two)
    halves = dot(full_two, feed[:, : 2 * hidden_units])
    gate = halves[:, :hidden_units]
    upper = halves[:, hidden_units:]
    inner = (jax.nn.silu(gate) * upper).astype(jnp.bfloat16)
    output = hidden + collect(dot_nt(inner, feed[:, 2 * hidden_units :]))
    kept = (
        rows, scale_one, full_one, pre_values, gate_mix, values, queries, keys, probs, slope,
        mixed, gated, out_t, hidden, scale_two, full_two, gate, upper, inner,
    )
    return (output, kept)


def layer_backward(kept, grad_out, gains, taps, attn, feed, channels, first):
    (
        rows, scale_one, full_one, pre_values, gate_mix, values, queries, keys, probs, slope,
        mixed, gated, out_t, hidden, scale_two, full_two, gate, upper, inner,
    ) = kept
    hidden_units = feed.shape[1] // 3
    length = full_one.shape[0] // 2
    branch_two = spread(grad_out)
    grad_down = scatter(dot_tn(branch_two, inner))
    grad_inner = dot(branch_two, feed[:, 2 * hidden_units :])
    grad_gate = (grad_inner * upper * silu_slope(gate)).astype(jnp.bfloat16)
    grad_upper = (grad_inner * jax.nn.silu(gate)).astype(jnp.bfloat16)
    grad_halves = jnp.concatenate([grad_gate, grad_upper], axis=1)
    grad_gate_up = scatter(dot_tn(full_two, grad_halves))
    grad_second = collect(dot_nt(grad_halves, feed[:, : 2 * hidden_units]))
    back_two, gain_two = rms_back(hidden, scale_two, gains[1], grad_second)
    grad_hidden = grad_out + back_two
    branch_one = spread(grad_hidden)
    grad_outw = scatter(dot_tn(branch_one, gated))
    grad_gated = dot(branch_one, out_t)
    grad_mixed = (grad_gated * jax.nn.silu(gate_mix)).astype(jnp.bfloat16)
    grad_mix_gate = (grad_gated * mixed * silu_slope(gate_mix)).astype(jnp.bfloat16)
    grad_heads = heads_of(grad_mixed, HD)
    low = probs.astype(jnp.bfloat16)
    grad_values = jnp.einsum("shij,sihc->sjhc", low, grad_heads, preferred_element_type=jnp.float32)
    grad_probs = jnp.einsum("sihc,sjhc->shij", grad_heads, values, preferred_element_type=jnp.float32)
    centred = grad_probs - jnp.sum(probs * grad_probs, axis=-1, keepdims=True)
    score_grad = (centred * slope).astype(jnp.bfloat16)
    root = math.sqrt(queries.shape[-1])
    grad_queries = jnp.einsum("shij,sjhc->sihc", score_grad, keys, preferred_element_type=jnp.float32)
    grad_keys = jnp.einsum("shij,sihc->sjhc", score_grad, queries, preferred_element_type=jnp.float32)
    grad_queries = (grad_queries / root).astype(jnp.bfloat16).reshape(2 * length, -1)
    grad_keys = (grad_keys / root).astype(jnp.bfloat16).reshape(2 * length, -1)
    grad_pre, grad_taps = conv_back(grad_values.reshape(2, length, channels), pre_values, taps)
    grad_pre = grad_pre.astype(jnp.bfloat16).reshape(2 * length, channels)
    grad_both = jnp.concatenate([grad_pre, grad_mix_gate, grad_queries, grad_keys], axis=1)
    grad_attn = scatter(dot_tn(full_one, grad_both))
    grad_first = collect(dot_nt(grad_both, attn[:, : grad_both.shape[1]]))
    back_one, gain_one = rms_back(rows, scale_one, gains[0], grad_first)
    grad_rows = grad_hidden + back_one
    grads = (grad_attn, grad_outw, grad_gate_up, grad_down)
    return (grad_rows, grads, jnp.stack([gain_one, gain_two]), grad_taps)


def scatter(grad):
    return lax.psum_scatter(grad.astype(jnp.bfloat16), "dp", scatter_dimension=0, tiled=True)


def body(
    boundary, lengths, norm_gains, conv_taps, lin_qk, win_qk, value_gate, out_weight, gate_up, down_weight
):
    core = lax.axis_index("section")
    index = lax.axis_index("tensor")
    lower = core == 0
    rows_dev, model = boundary.shape[2:]
    channels = value_gate.shape[-1] // 2
    units = gate_up.shape[-1] // 2

    def half(block, axis, which):
        size = block.shape[axis] // 2
        return lax.dynamic_slice_in_dim(block, which * size, size, axis)

    def both_layers(build):
        mine = build(core)
        other = swap(build(1 - core))
        return (jnp.where(lower, mine, other), jnp.where(lower, other, mine))

    def attn_piece(which):
        values = half(value_gate[0], 2, which)
        return jnp.concatenate(
            [values[:, 0], values[:, 1], widen(half(out_weight[0], 0, which).T)], axis=1
        )

    def feed_piece(which):
        pair = half(gate_up[0], 2, which)
        down = half(down_weight[0], 0, which).T
        return jnp.concatenate([widen(pair[:, 0]), widen(pair[:, 1]), widen(down)], axis=1)

    def with_pair(piece, pair):
        pair = half(pair, 2, core)
        return jnp.concatenate(
            [piece[:, : 2 * channels], pair[:, 0], pair[:, 1], piece[:, 2 * channels :]], axis=1
        )

    def fetch(piece):
        return lax.all_gather(piece, "dp", axis=0, tiled=True)

    attn_parts = both_layers(attn_piece)
    feed_parts = both_layers(feed_piece)
    attn_zero = fetch(with_pair(attn_parts[0], lin_qk))
    feed_zero = fetch(feed_parts[0])
    attn_one = fetch(with_pair(attn_parts[1], win_qk))
    feed_one = fetch(feed_parts[1])

    small = jnp.concatenate([norm_gains[0], conv_taps[0]], axis=0)
    small_other = swap(small)
    small_zero = jnp.where(lower, small, small_other)
    small_one = jnp.where(lower, small_other, small)
    offset = (2 * index + core) * channels

    def own_taps(block):
        return lax.dynamic_slice_in_dim(block[2:], offset, channels, 1)

    held = boundary[0]
    keep = lax.dynamic_index_in_dim(held, core, 0, keepdims=False)
    other = swap(lax.dynamic_index_in_dim(held, 1 - core, 0, keepdims=False))
    entering = jnp.where(lower, keep, other).astype(jnp.float32)
    cotangent = jnp.where(lower, other, keep).astype(jnp.float32)
    length = lax.dynamic_index_in_dim(lengths, core, 0, keepdims=False)
    place = index * rows_dev + jnp.arange(rows_dev)
    mask = (place < length).astype(jnp.float32)[:, None]

    middle, kept_zero = layer_forward(
        entering, small_zero[:2], own_taps(small_zero), attn_zero, feed_zero, channels, True
    )
    middle = middle.astype(jnp.bfloat16).astype(jnp.float32)
    final, kept_one = layer_forward(
        middle, small_one[:2], own_taps(small_one), attn_one, feed_one, channels, False
    )
    grad_middle, grads_one, gains_one, taps_one = layer_backward(
        kept_one, cotangent * mask, small_one[:2], own_taps(small_one), attn_one, feed_one, channels, False
    )
    grad_middle = grad_middle.astype(jnp.bfloat16).astype(jnp.float32)
    grad_start, grads_zero, gains_zero, taps_zero = layer_backward(
        kept_zero, grad_middle, small_zero[:2], own_taps(small_zero), attn_zero, feed_zero, channels, True
    )

    def own_small(gains, taps):
        spot = jnp.zeros((taps.shape[0], model), jnp.float32)
        return jnp.concatenate([gains, lax.dynamic_update_slice_in_dim(spot, taps, offset, 1)], axis=0)

    sums = sum_all(jnp.stack([own_small(gains_zero, taps_zero), own_small(gains_one, taps_one)]))
    sums = lax.dynamic_index_in_dim(sums, core, 0, keepdims=True)

    final = final * mask
    ends_keep = jnp.where(lower, grad_start, final)
    ends_other = swap(jnp.where(lower, final, grad_start))
    ends = jnp.where(lower, jnp.stack([ends_keep, ends_other]), jnp.stack([ends_other, ends_keep]))

    def home(zero, one):
        mine = jnp.where(lower, zero, one)
        other = swap(jnp.where(lower, one, zero))
        return (jnp.where(lower, mine, other), jnp.where(lower, other, mine))

    def halves(low, high, axis):
        return jnp.concatenate([low, high], axis=axis).astype(jnp.float32)

    def pair_home(grads):
        block = grads[:, 2 * channels :]
        size = block.shape[1] // 2
        other = swap(block)
        low = jnp.where(lower, block, other)
        high = jnp.where(lower, other, block)
        return jnp.stack(
            [halves(low[:, :size], high[:, :size], 1), halves(low[:, size:], high[:, size:], 1)], axis=1
        )

    low, high = home(grads_zero[0][:, : 2 * channels], grads_one[0][:, : 2 * channels])
    vgate_grad = jnp.stack(
        [
            halves(low[:, :channels], high[:, :channels], 1),
            halves(low[:, channels:], high[:, channels:], 1),
        ],
        axis=1,
    )
    low, high = home(grads_zero[1], grads_one[1])
    out_grad = halves(low.T, high.T, 0)
    low, high = home(grads_zero[2], grads_one[2])
    wide = low.shape[1] // 2
    gate_up_grad = jnp.stack(
        [
            halves(low[:, :units], high[:, :units], 1),
            halves(low[:, wide : wide + units], high[:, wide : wide + units], 1),
        ],
        axis=1,
    )
    low, high = home(grads_zero[3], grads_one[3])
    down_grad = halves(low[:, :units].T, high[:, :units].T, 0)
    return (
        ends[None],
        sums[:, :2],
        sums[:, 2:],
        pair_home(grads_zero[0]),
        pair_home(grads_one[0]),
        vgate_grad[None],
        out_grad[None],
        gate_up_grad[None],
        down_grad[None],
    )


def solution(mesh):
    in_specs = (
        P("section", "dp", "tensor", None),
        P("dp"),
        P("section", None, None),
        P("section", None, None),
        P("dp", None, "tensor"),
        P("dp", None, "tensor"),
        P("section", "dp", None, "tensor"),
        P("section", "tensor", "dp"),
        P("section", "dp", None, "tensor"),
        P("section", "tensor", "dp"),
    )
    out_specs = (
        P("section", "dp", "tensor", None),
        P("section", None, None),
        P("section", None, None),
        P("dp", None, "tensor"),
        P("dp", None, "tensor"),
        P("section", "dp", None, "tensor"),
        P("section", "tensor", "dp"),
        P("section", "dp", None, "tensor"),
        P("section", "tensor", "dp"),
    )
    return jax.shard_map(body, mesh=mesh, in_specs=in_specs, out_specs=out_specs, check_vma=False)
```

time: 1980 us -> 977 us (0.49)
  waiting for transfers between devices: 1220 us -> 558 us
  blocking collectives: 269 us -> 113 us
  matrix products: 209 us -> 101 us
  local copies, waits for them, and re-layouts: 153 us -> 84.7 us
  other arithmetic: 89.4 us -> 47 us
  starting transfers between devices: 8.63 us -> 47.4 us
    unnamed x25 -> x12, waiting for transfers between devices: 559 us -> 0.2 us
    all_gather x5 -> x4, waiting for transfers between devices: 362 us -> 185 us  [fetch(): return lax.all_gather(piece, 'dp', axis=0, tiled=True)]
    dot_general x69 -> x35, matrix products: 209 us -> 98.3 us  [the longest x8 34.2 us: dot_tn(): lax.dot_general(one, two, (((0,), (0,)), ((), ())), preferred_element_typ...]
    ppermute x4 -> x56, waiting for transfers between devices: 4.15 us -> 110 us  [the longest x24 63 us: collect(): total = total + lax.ppermute(block, 'tensor', pairs).astype(jnp.float32)]
    psum x1 -> x0, blocking collectives: 79.9 us -> none  [body(): gain_sum, taps_sum = lax.psum((gain_total, full_taps), ('dp', 'tensor'))]
    all_gather x13 -> x8, blocking collectives: 190 us -> 113 us  [spread(): lax.all_gather(rows.astype(jnp.bfloat16), 'tensor', axis=0, tiled=True)]
    convert_element_type x3 -> x4, local copies, waits for them, and re-layouts: 45.9 us -> 0.57 us  [the longest x2 0.29 us: layer_backward(): grad_keys = (grad_keys / root).astype(jnp.bfloat16).reshape(2 * length, -1)]
    all_gather x3 -> x0, local copies, waits for them, and re-layouts: 41.6 us -> none  [the longest x1 23.1 us: fetch_weights(): lax.all_gather(gup_part, 'dp', axis=0, tiled=True)]
  transfers between devices with their start and end apart: 26 -> 68, of which waited for: 20 -> 41; matrix products, arithmetic and copies ran while one was open for 13% -> 17% of each run, Pallas kernels for 0% -> 0%
where the time goes in v1:
time: 977 us; the launch traced here: 967 us
  waiting for transfers between devices  558 us (57%)
  blocking collectives  113 us (12%)
  matrix products  101 us (10%)
  local copies, waits for them, and re-layouts  84.7 us (9%)
  starting transfers between devices  47.4 us (5%)
  other arithmetic  47 us (5%)
  between operations  16.9 us (2%)
    reduce_scatter x8, waiting for transfers between devices, scatter(): lax.psum_scatter(grad.astype(jnp.bfloat16), 'dp', scatter_dimension=0, ti...  262 us
    all_gather x4, waiting for transfers between devices, fetch(): return lax.all_gather(piece, 'dp', axis=0, tiled=True)  185 us
    all_gather x8, blocking collectives, spread(): lax.all_gather(rows.astype(jnp.bfloat16), 'tensor', axis=0, tiled=True)  113 us
    ppermute x24, waiting for transfers between devices, collect(): total = total + lax.ppermute(block, 'tensor', pairs).astype(jnp.float32)  63 us
    unnamed x242, local copies, waits for them, and re-layouts  41.7 us
    dot_general x8, matrix products, dot_tn(): lax.dot_general(one, two, (((0,), (0,)), ((), ())), preferred_element_typ...  34.2 us
    dot_general x8, matrix products, dot(): return jnp.dot(one, two, preferred_element_type=jnp.float32)  32.4 us
    ppermute x24, starting transfers between devices, collect(): total = total + lax.ppermute(block, 'tensor', pairs).astype(jnp.float32)  28.3 us
  transfers between devices with their start and end apart: 68, of which 41 were waited for; matrix products, arithmetic and copies ran while one was open for 17% of the time, Pallas kernels for 0%

profile of v1, /device:TPU:0, one launch (start us, length us, event | category | flops | bytes accessed | tf_op | source)
XLA Modules:
  0.0 967.4 jit_solution(15434023207547307242)
XLA Ops:
  15.3 6.4 constant_dynamic-slice_fusion.27
  32.0 15.0 %all_gather.36 = bf16[256,1792]{1,0:T(8,128)(2,1)S(1)} all-gather(bf16[64,1792]{1,0:T(8,128)(2,1)S(1)} %fusion.75), channel_id=1, replica_groups=mesh['section'=2,'dp'=4,'tensor'=4] {'tensor'}, dimensions={0}, use_global_device_ids=true | all-gather | bytes 1146880 | tf_op jit(solution)/shard_map/all_gather | solution.py:55
  53.2 21.2 %all-gather.5.cloned.1.call-done = bf16[1792,768]{1,0:T(8,128)(2,1)} async-done(((bf16[448,768]{1,0:T(8,128)(2,1)}), bf16[1792,768]{1,0:T(8,128)(2,1)}) %all-gather.5.cloned.1.call-update) | async-done | bytes 2752528 | tf_op jit(solution)/shard_map/all_gather | solution.py:243
  74.5 4.2 fusion.142
  97.8 5.0 collective-permute-done.5
  102.8 4.8 collective-permute-done.7
  110.3 12.7 %all_gather.38 = bf16[256,1792]{1,0:T(8,128)(2,1)S(1)} all-gather(bf16[64,1792]{1,0:T(8,128)(2,1)S(1)} %multiply_convert_fusion.14), channel_id=1, replica_groups=mesh['section'=2,'dp'=4,'tensor'=4] {'tensor'}, dimensions={0}, use_global_device_ids=true | all-gather | bytes 1146880 | tf_op jit(solution)/shard_map/all_gather | solution.py:55
  126.5 73.8 %all-gather.7.cloned.1.call-done = bf16[1792,1920]{1,0:T(8,128)(2,1)} async-done(((bf16[448,1920]{1,0:T(8,128)(2,1)}), bf16[1792,1920]{1,0:T(8,128)(2,1)}) %all-gather.7.cloned.1.call-update) | async-done | bytes 6881296 | tf_op jit(solution)/shard_map/all_gather | solution.py:243
  200.4 5.4 fusion.7
  206.2 4.4 fusion.29
  220.7 4.9 collective-permute-done.11
  225.6 5.0 collective-permute-done.13
  232.4 13.2 %all_gather.40 = bf16[256,1792]{1,0:T(8,128)(2,1)S(1)} all-gather(bf16[64,1792]{1,0:T(8,128)(2,1)S(1)} %fusion.82), channel_id=1, replica_groups=mesh['section'=2,'dp'=4,'tensor'=4] {'tensor'}, dimensions={0}, use_global_device_ids=true | all-gather | bytes 1146880 | tf_op jit(solution)/shard_map/all_gather | solution.py:55
  249.1 30.8 %all-gather.9.cloned.1.call-done = bf16[1792,1152]{1,0:T(8,128)(2,1)} async-done(((bf16[448,1152]{1,0:T(8,128)(2,1)}), bf16[1792,1152]{1,0:T(8,128)(2,1)}) %all-gather.9.cloned.1.call-update) | async-done | bytes 4128784 | tf_op jit(solution)/shard_map/all_gather | solution.py:243
  279.9 5.7 fusion.143
  308.5 19.9 %all_gather.42 = bf16[256,1792]{1,0:T(8,128)(2,1)S(1)} all-gather(bf16[64,1792]{1,0:T(8,128)(2,1)S(1)} %copy-done.26), channel_id=1, replica_groups=mesh['section'=2,'dp'=4,'tensor'=4] {'tensor'}, dimensions={0}, use_global_device_ids=true | all-gather | bytes 1146880 | tf_op jit(solution)/shard_map/all_gather | solution.py:55
  328.9 13.2 %all_gather.44 = bf16[256,1792]{1,0:T(8,128)(2,1)S(1)} all-gather(bf16[64,1792]{1,0:T(8,128)(2,1)S(1)} %multiply_convert_fusion.12), channel_id=1, replica_groups=mesh['section'=2,'dp'=4,'tensor'=4] {'tensor'}, dimensions={0}, use_global_device_ids=true | all-gather | bytes 1146880 | tf_op jit(solution)/shard_map/all_gather | solution.py:55
  345.6 59.3 %all-gather.11.cloned.1.call-done = bf16[1792,1920]{1,0:T(8,128)(2,1)} async-done(((bf16[448,1920]{1,0:T(8,128)(2,1)}), bf16[1792,1920]{1,0:T(8,128)(2,1)}) %all-gather.11.cloned.1.call-update) | async-done | bytes 6881296 | tf_op jit(solution)/shard_map/all_gather | solution.py:243
  404.9 5.5 fusion.3
  422.4 5.0 collective-permute-done.22
  427.4 5.1 collective-permute-done.24
  435.2 13.5 %all_gather.45 = bf16[256,1792]{1,0:T(8,128)(2,1)} all-gather(bf16[64,1792]{1,0:T(8,128)(2,1)S(1)} %get-tuple-element.79), channel_id=1, replica_groups=mesh['section'=2,'dp'=4,'tensor'=4] {'tensor'}, dimensions={0}, use_global_device_ids=true | all-gather | bytes 1146880 | tf_op jit(solution)/shard_map/all_gather | solution.py:55
  454.5 3.4 multiply_convert_fusion.10
  475.8 4.9 collective-permute-done.27
  480.8 4.3 collective-permute-done.29
  486.9 13.1 %all_gather.46 = bf16[256,1792]{1,0:T(8,128)(2,1)S(1)} all-gather(bf16[64,1792]{1,0:T(8,128)(2,1)S(1)} %fusion.87), channel_id=1, replica_groups=mesh['section'=2,'dp'=4,'tensor'=4] {'tensor'}, dimensions={0}, use_global_device_ids=true | all-gather | bytes 1146880 | tf_op jit(solution)/shard_map/all_gather | solution.py:55
  517.4 3.5 collective-permute-done.32
  520.9 3.9 collective-permute-done.34
  527.7 12.4 %all_gather.47 = bf16[256,1792]{1,0:T(8,128)(2,1)S(1)} all-gather(bf16[64,1792]{1,0:T(8,128)(2,1)S(1)} %get-tuple-element.71), channel_id=1, replica_groups=mesh['section'=2,'dp'=4,'tensor'=4] {'tensor'}, dimensions={0}, use_global_device_ids=true | all-gather | bytes 1146880 | tf_op jit(solution)/shard_map/all_gather | solution.py:55
  545.7 4.6 convolution_convert_fusion.3
  551.4 4.5 convolution_convert_fusion.4
  555.9 10.8 %reduce-scatter.9.cloned.1.call-start = ((), (), s32[]{:S(2)}) async-start(), calls=%async_computation.12 | async-start | bytes 2293760 | tf_op jit(solution)/shard_map/reduce_scatter | solution.py:203
  567.1 3.5 multiply_convert_fusion.8
  577.1 3.9 convolution_convert_fusion.5
  582.2 5.3 convolution_convert_fusion.2
  588.6 6.4 convolution_convert_fusion
  600.8 6.3 convolution_convert_fusion.1
  608.2 3.3 fusion.23
  622.6 4.5 collective-permute-done.37
  627.1 4.2 collective-permute-done.39
  643.0 10.5 %collective-permute-done.47 = f32[2,5,1792]{2,0,1:T(2,128)S(1)} collective-permute-done((f32[2,5,1792]{2,0,1:T(2,128)S(1)}, f32[2,5,1792]{2,0,1:T(2,128)S(1)}, u32[]{:S(2)}, u32[]{:S(2)}) %collective-permute-start.47) | collective-permute-done | bytes 71712 | tf_op jit(solution)/shard_map/ppermute | solution.py:81
  654.0 7.5 collective-permute-done.48
  662.5 6.1 collective-permute-done.49
  678.0 32.4 %reduce-scatter.9.cloned.1.call-done = bf16[448,512]{1,0:T(8,128)(2,1)} async-done(((bf16[1792,512]{1,0:T(8,128)(2,1)}), bf16[448,512]{1,0:T(8,128)(2,1)}) %reduce-scatter.9.cloned.1.call-update) | async-done | bytes 458768 | tf_op jit(solution)/shard_map/reduce_scatter | solution.py:203
  711.5 61.5 %reduce-scatter.11.cloned.1.call-done = bf16[448,896]{1,0:T(8,128)(2,1)} async-done(((bf16[1792,896]{1,0:T(8,128)(2,1)}), bf16[448,896]{1,0:T(8,128)(2,1)}) %reduce-scatter.11.cloned.1.call-update) | async-done | bytes 802832 | tf_op jit(solution)/shard_map/reduce_scatter | solution.py:203
  777.5 81.7 %reduce-scatter.19.cloned.1.call-done = bf16[448,1280]{1,0:T(8,128)(2,1)} async-done(((bf16[1792,1280]{1,0:T(8,128)(2,1)}), bf16[448,1280]{1,0:T(8,128)(2,1)}) %reduce-scatter.19.cloned.1.call-update) | async-done | bytes 1146896 | tf_op jit(solution)/shard_map/reduce_scatter | solution.py:203
  859.3 86.0 %reduce-scatter.17.cloned.1.call-done = bf16[448,1280]{1,0:T(8,128)(2,1)} async-done(((bf16[1792,1280]{1,0:T(8,128)(2,1)}), bf16[448,1280]{1,0:T(8,128)(2,1)}) %reduce-scatter.17.cloned.1.call-update) | async-done | bytes 1146896 | tf_op jit(solution)/shard_map/reduce_scatter | solution.py:203
  954.5 5.7 copy.289
  (570 shorter events, 222.1 us)
Async XLA Ops:
  7.2 67.3 %all-gather.5.cloned.1.call-start = ((), (), s32[]{:S(2)}) async-start(), calls=%async_computation.8 | async-start | bytes 3440640 | tf_op jit(solution)/shard_map/all_gather | solution.py:243
  14.7 185.7 %all-gather.7.cloned.1.call-start = ((), (), s32[]{:S(2)}) async-start(), calls=%async_computation.9 | async-start | bytes 8601600 | tf_op jit(solution)/shard_map/all_gather | solution.py:243
  28.1 251.8 %all-gather.9.cloned.1.call-start = ((), (), s32[]{:S(2)}) async-start(), calls=%async_computation.10 | async-start | bytes 5160960 | tf_op jit(solution)/shard_map/all_gather | solution.py:243
  90.9 314.0 %all-gather.11.cloned.1.call-start = ((), (), s32[]{:S(2)}) async-start(), calls=%async_computation.11 | async-start | bytes 8601600 | tf_op jit(solution)/shard_map/all_gather | solution.py:243
  94.2 8.6 collective-permute-start.5
  95.8 11.8 %collective-permute-start.7 = (bf16[64,1792]{1,0:T(8,128)(2,1)S(1)}, bf16[64,1792]{1,0:T(8,128)(2,1)S(1)}, u32[]{:S(2)}, u32[]{:S(2)}) collective-permute-start(bf16[64,1792]{1,0:T(8,128)(2,1)S(1)} %get-tuple-element.163), channel_id=1, source_target_pairs={{0,3},{1,2},{2,1},{3,0},{4,7},{5,6},{6,5},{7,4},{8,11},{9,10},{10,... | collective-permute-start | bytes 688136 | tf_op jit(solution)/shard_map/ppermute | solution.py:71
  97.3 11.7 %collective-permute-start.6 = (bf16[64,1792]{1,0:T(8,128)(2,1)S(1)}, bf16[64,1792]{1,0:T(8,128)(2,1)S(1)}, u32[]{:S(2)}, u32[]{:S(2)}) collective-permute-start(bf16[64,1792]{1,0:T(8,128)(2,1)S(1)} %get-tuple-element.164), channel_id=1, source_target_pairs={{0,2},{1,3},{2,0},{3,1},{4,6},{5,7},{6,4},{7,5},{8,10},{9,11},{10,... | collective-permute-start | bytes 688136 | tf_op jit(solution)/shard_map/ppermute | solution.py:71
  212.5 457.5 %reduce-scatter.15.cloned.1.call-start = ((), (), s32[]{:S(2)}) async-start(), calls=%async_computation.15 | async-start | bytes 1146880 | tf_op jit(solution)/shard_map/reduce_scatter | solution.py:203
  217.1 8.5 collective-permute-start.11
  218.5 12.1 %collective-permute-start.13 = (bf16[64,1792]{1,0:T(8,128)(2,1)S(1)}, bf16[64,1792]{1,0:T(8,128)(2,1)S(1)}, u32[]{:S(2)}, u32[]{:S(2)}) collective-permute-start(bf16[64,1792]{1,0:T(8,128)(2,1)S(1)} %get-tuple-element.160), channel_id=1, source_target_pairs={{0,3},{1,2},{2,1},{3,0},{4,7},{5,6},{6,5},{7,4},{8,11},{9,10},{10,... | collective-permute-start | bytes 688136 | tf_op jit(solution)/shard_map/ppermute | solution.py:71
  220.0 12.0 %collective-permute-start.12 = (bf16[64,1792]{1,0:T(8,128)(2,1)S(1)}, bf16[64,1792]{1,0:T(8,128)(2,1)S(1)}, u32[]{:S(2)}, u32[]{:S(2)}) collective-permute-start(bf16[64,1792]{1,0:T(8,128)(2,1)S(1)} %get-tuple-element.161), channel_id=1, source_target_pairs={{0,2},{1,3},{2,0},{3,1},{4,6},{5,7},{6,4},{7,5},{8,10},{9,11},{10,... | collective-permute-start | bytes 688136 | tf_op jit(solution)/shard_map/ppermute | solution.py:71
  305.0 23.5 %collective-permute-start.16 = (bf16[64,1792]{1,0:T(8,128)(2,1)S(1)}, bf16[64,1792]{1,0:T(8,128)(2,1)S(1)}, u32[]{:S(2)}, u32[]{:S(2)}) collective-permute-start(bf16[64,1792]{1,0:T(8,128)(2,1)S(1)} %get-tuple-element.152), channel_id=1, source_target_pairs={{0,1},{1,0},{2,3},{3,2},{4,5},{5,4},{6,7},{7,6},{8,9},{9,8},{10,11... | collective-permute-start | bytes 688136 | tf_op jit(solution)/shard_map/ppermute | solution.py:71
  306.5 21.9 %collective-permute-start.18 = (bf16[64,1792]{1,0:T(8,128)(2,1)S(1)}, bf16[64,1792]{1,0:T(8,128)(2,1)S(1)}, u32[]{:S(2)}, u32[]{:S(2)}) collective-permute-start(bf16[64,1792]{1,0:T(8,128)(2,1)S(1)} %get-tuple-element.153), channel_id=1, source_target_pairs={{0,3},{1,2},{2,1},{3,0},{4,7},{5,6},{6,5},{7,4},{8,11},{9,10},{10,... | collective-permute-start | bytes 688136 | tf_op jit(solution)/shard_map/ppermute | solution.py:71
  308.0 20.5 %collective-permute-start.17 = (bf16[64,1792]{1,0:T(8,128)(2,1)S(1)}, bf16[64,1792]{1,0:T(8,128)(2,1)S(1)}, u32[]{:S(2)}, u32[]{:S(2)}) collective-permute-start(bf16[64,1792]{1,0:T(8,128)(2,1)S(1)} %get-tuple-element.154), channel_id=1, source_target_pairs={{0,2},{1,3},{2,0},{3,1},{4,6},{5,7},{6,4},{7,5},{8,10},{9,11},{10,... | collective-permute-start | bytes 688136 | tf_op jit(solution)/shard_map/ppermute | solution.py:71
  328.5 13.7 %collective-permute-start.19 = (bf16[256,1792]{1,0:T(8,128)(2,1)S(1)}, bf16[256,1792]{1,0:T(8,128)(2,1)S(1)}, u32[]{:S(2)}, u32[]{:S(2)}) collective-permute-start(bf16[256,1792]{1,0:T(8,128)(2,1)S(1)} %all_gather.42), channel_id=1, source_target_pairs={{0,16},{16,0},{1,17},{17,1},{2,18},{18,2},{3,19},{19,3},{4,20},{20... | collective-permute-start | bytes 2752520 | tf_op jit(solution)/shard_map/ppermute | solution.py:51
  418.8 8.5 collective-permute-start.22
  420.4 12.1 %collective-permute-start.24 = (bf16[64,1792]{1,0:T(8,128)(2,1)S(1)}, bf16[64,1792]{1,0:T(8,128)(2,1)S(1)}, u32[]{:S(2)}, u32[]{:S(2)}) collective-permute-start(bf16[64,1792]{1,0:T(8,128)(2,1)S(1)} %get-tuple-element.150), channel_id=1, source_target_pairs={{0,3},{1,2},{2,1},{3,0},{4,7},{5,6},{6,5},{7,4},{8,11},{9,10},{10,... | collective-permute-start | bytes 688136 | tf_op jit(solution)/shard_map/ppermute | solution.py:71
  421.8 12.0 %collective-permute-start.23 = (bf16[64,1792]{1,0:T(8,128)(2,1)S(1)}, bf16[64,1792]{1,0:T(8,128)(2,1)S(1)}, u32[]{:S(2)}, u32[]{:S(2)}) collective-permute-start(bf16[64,1792]{1,0:T(8,128)(2,1)S(1)} %get-tuple-element.151), channel_id=1, source_target_pairs={{0,2},{1,3},{2,0},{3,1},{4,6},{5,7},{6,4},{7,5},{8,10},{9,11},{10,... | collective-permute-start | bytes 688136 | tf_op jit(solution)/shard_map/ppermute | solution.py:71
  448.7 4.5 collective-permute-start.25
  472.2 8.5 collective-permute-start.27
  472.7 12.3 %collective-permute-start.29 = (bf16[64,1792]{1,0:T(8,128)(2,1)S(1)}, bf16[64,1792]{1,0:T(8,128)(2,1)S(1)}, u32[]{:S(2)}, u32[]{:S(2)}) collective-permute-start(bf16[64,1792]{1,0:T(8,128)(2,1)S(1)} %get-tuple-element.145), channel_id=1, source_target_pairs={{0,3},{1,2},{2,1},{3,0},{4,7},{5,6},{6,5},{7,4},{8,11},{9,10},{10,... | collective-permute-start | bytes 688136 | tf_op jit(solution)/shard_map/ppermute | solution.py:71
  474.2 12.2 %collective-permute-start.28 = (bf16[64,1792]{1,0:T(8,128)(2,1)S(1)}, bf16[64,1792]{1,0:T(8,128)(2,1)S(1)}, u32[]{:S(2)}, u32[]{:S(2)}) collective-permute-start(bf16[64,1792]{1,0:T(8,128)(2,1)S(1)} %get-tuple-element.146), channel_id=1, source_target_pairs={{0,2},{1,3},{2,0},{3,1},{4,6},{5,7},{6,4},{7,5},{8,10},{9,11},{10,... | collective-permute-start | bytes 688136 | tf_op jit(solution)/shard_map/ppermute | solution.py:71
  512.2 8.7 collective-permute-start.32
  512.2 12.6 %collective-permute-start.34 = (bf16[64,1792]{1,0:T(8,128)(2,1)}, bf16[64,1792]{1,0:T(8,128)(2,1)S(1)}, u32[]{:S(2)}, u32[]{:S(2)}) collective-permute-start(bf16[64,1792]{1,0:T(8,128)(2,1)} %get-tuple-element.142), channel_id=1, source_target_pairs={{0,3},{1,2},{2,1},{3,0},{4,7},{5,6},{6,5},{7,4},{8,11},{9,10},{10,... | collective-permute-start | bytes 688136 | tf_op jit(solution)/shard_map/ppermute | solution.py:71
  513.7 12.5 %collective-permute-start.33 = (bf16[64,1792]{1,0:T(8,128)(2,1)}, bf16[64,1792]{1,0:T(8,128)(2,1)S(1)}, u32[]{:S(2)}, u32[]{:S(2)}) collective-permute-start(bf16[64,1792]{1,0:T(8,128)(2,1)} %get-tuple-element.143), channel_id=1, source_target_pairs={{0,2},{1,3},{2,0},{3,1},{4,6},{5,7},{6,4},{7,5},{8,10},{9,11},{10,... | collective-permute-start | bytes 688136 | tf_op jit(solution)/shard_map/ppermute | solution.py:71
  517.3 152.7 %reduce-scatter.13.cloned.1.call-start = ((), (), s32[]{:S(2)}) async-start(), calls=%async_computation.14 | async-start | bytes 1146880 | tf_op jit(solution)/shard_map/reduce_scatter | solution.py:203
  545.7 125.4 %reduce-scatter.23.cloned.1.call-start = ((), (), s32[]{:S(2)}) async-start(), calls=%async_computation.19 | async-start | bytes 2867200 | tf_op jit(solution)/shard_map/reduce_scatter | solution.py:203
  550.3 120.8 %reduce-scatter.21.cloned.1.call-start = ((), (), s32[]{:S(2)}) async-start(), calls=%async_computation.18 | async-start | bytes 2867200 | tf_op jit(solution)/shard_map/reduce_scatter | solution.py:203
  555.9 154.5 %reduce-scatter.9.cloned.1.call-start = ((), (), s32[]{:S(2)}) async-start(), calls=%async_computation.12 | async-start | bytes 2293760 | tf_op jit(solution)/shard_map/reduce_scatter | solution.py:203
  581.1 192.0 %reduce-scatter.11.cloned.1.call-start = ((), (), s32[]{:S(2)}) async-start(), calls=%async_computation.13 | async-start | bytes 4014080 | tf_op jit(solution)/shard_map/reduce_scatter | solution.py:203
  587.5 271.8 %reduce-scatter.19.cloned.1.call-start = ((), (), s32[]{:S(2)}) async-start(), calls=%async_computation.17 | async-start | bytes 5734400 | tf_op jit(solution)/shard_map/reduce_scatter | solution.py:203
  595.0 350.3 %reduce-scatter.17.cloned.1.call-start = ((), (), s32[]{:S(2)}) async-start(), calls=%async_computation.16 | async-start | bytes 5734400 | tf_op jit(solution)/shard_map/reduce_scatter | solution.py:203
  599.6 14.9 %collective-permute-start.36 = (bf16[256,1792]{1,0:T(8,128)(2,1)S(1)}, bf16[256,1792]{1,0:T(8,128)(2,1)}, u32[]{:S(2)}, u32[]{:S(2)}) collective-permute-start(bf16[256,1792]{1,0:T(8,128)(2,1)S(1)} %slice.649), channel_id=1, source_target_pairs={{0,16},{16,0},{1,17},{17,1},{2,18},{18,2},{3,19},{19,3},{4,20},{20... | collective-permute-start | bytes 2752520 | tf_op jit(solution)/shard_map/ppermute | solution.py:51
  613.4 20.6 %collective-permute-start.40 = (bf16[256,1792]{1,0:T(8,128)(2,1)S(1)}, bf16[256,1792]{1,0:T(8,128)(2,1)}, u32[]{:S(2)}, u32[]{:S(2)}) collective-permute-start(bf16[256,1792]{1,0:T(8,128)(2,1)S(1)} %slice.648), channel_id=1, source_target_pairs={{0,16},{16,0},{1,17},{17,1},{2,18},{18,2},{3,19},{19,3},{4,20},{20... | collective-permute-start | bytes 2752520 | tf_op jit(solution)/shard_map/ppermute | solution.py:51
  618.5 8.7 collective-permute-start.37
  618.9 12.4 %collective-permute-start.39 = (bf16[64,1792]{1,0:T(8,128)(2,1)}, bf16[64,1792]{1,0:T(8,128)(2,1)S(1)}, u32[]{:S(2)}, u32[]{:S(2)}) collective-permute-start(bf16[64,1792]{1,0:T(8,128)(2,1)} %get-tuple-element.139), channel_id=1, source_target_pairs={{0,3},{1,2},{2,1},{3,0},{4,7},{5,6},{6,5},{7,4},{8,11},{9,10},{10,... | collective-permute-start | bytes 688136 | tf_op jit(solution)/shard_map/ppermute | solution.py:71
  620.3 12.2 %collective-permute-start.38 = (bf16[64,1792]{1,0:T(8,128)(2,1)S(1)}, bf16[64,1792]{1,0:T(8,128)(2,1)S(1)}, u32[]{:S(2)}, u32[]{:S(2)}) collective-permute-start(bf16[64,1792]{1,0:T(8,128)(2,1)S(1)} %get-tuple-element.140), channel_id=1, source_target_pairs={{0,2},{1,3},{2,0},{3,1},{4,6},{5,7},{6,4},{7,5},{8,10},{9,11},{10,... | collective-permute-start | bytes 688136 | tf_op jit(solution)/shard_map/ppermute | solution.py:71
  636.2 5.3 collective-permute-start.46
  637.9 15.7 %collective-permute-start.41 = (bf16[64,1792]{1,0:T(8,128)(2,1)S(1)}, bf16[64,1792]{1,0:T(8,128)(2,1)S(1)}, u32[]{:S(2)}, u32[]{:S(2)}) collective-permute-start(bf16[64,1792]{1,0:T(8,128)(2,1)S(1)} %get-tuple-element.135), channel_id=1, source_target_pairs={{0,1},{1,0},{2,3},{3,2},{4,5},{5,4},{6,7},{7,6},{8,9},{9,8},{10,11... | collective-permute-start | bytes 688136 | tf_op jit(solution)/shard_map/ppermute | solution.py:71
  638.4 15.2 %collective-permute-start.43 = (bf16[64,1792]{1,0:T(8,128)(2,1)S(1)}, bf16[64,1792]{1,0:T(8,128)(2,1)S(1)}, u32[]{:S(2)}, u32[]{:S(2)}) collective-permute-start(bf16[64,1792]{1,0:T(8,128)(2,1)S(1)} %get-tuple-element.136), channel_id=1, source_target_pairs={{0,3},{1,2},{2,1},{3,0},{4,7},{5,6},{6,5},{7,4},{8,11},{9,10},{10,... | collective-permute-start | bytes 688136 | tf_op jit(solution)/shard_map/ppermute | solution.py:71
  639.8 13.8 %collective-permute-start.42 = (bf16[64,1792]{1,0:T(8,128)(2,1)S(1)}, bf16[64,1792]{1,0:T(8,128)(2,1)S(1)}, u32[]{:S(2)}, u32[]{:S(2)}) collective-permute-start(bf16[64,1792]{1,0:T(8,128)(2,1)S(1)} %get-tuple-element.137), channel_id=1, source_target_pairs={{0,2},{1,3},{2,0},{3,1},{4,6},{5,7},{6,4},{7,5},{8,10},{9,11},{10,... | collective-permute-start | bytes 688136 | tf_op jit(solution)/shard_map/ppermute | solution.py:71
  641.6 11.9 %collective-permute-start.47 = (f32[2,5,1792]{2,0,1:T(2,128)S(1)}, f32[2,5,1792]{2,0,1:T(2,128)S(1)}, u32[]{:S(2)}, u32[]{:S(2)}) collective-permute-start(f32[2,5,1792]{2,0,1:T(2,128)S(1)} %fusion.185), channel_id=1, source_target_pairs={{0,2},{1,3},{2,0},{3,1},{4,6},{5,7},{6,4},{7,5},{8,10},{9,11},{10,... | collective-permute-start | bytes 215048 | tf_op jit(solution)/shard_map/ppermute | solution.py:81
  653.5 7.9 collective-permute-start.48
  661.5 7.2 collective-permute-start.49
  662.5 11.2 %collective-permute-start.44 = (f32[64,1792]{1,0:T(8,128)}, f32[64,1792]{1,0:T(8,128)S(1)}, u32[]{:S(2)}, u32[]{:S(2)}) collective-permute-start(f32[64,1792]{1,0:T(8,128)} %broadcast_select_fusion.18), channel_id=1, source_target_pairs={{0,16},{16,0},{1,17},{17,1},{2,18},{18,2},{3,19},{19,3},{4,20},{20... | collective-permute-start | bytes 1376264 | tf_op jit(solution)/shard_map/ppermute | solution.py:51
  711.5 62.9 %collective-permute-start.50 = (bf16[448,64]{1,0:T(8,128)(2,1)S(1)}, bf16[448,64]{1,0:T(8,128)(2,1)S(1)}, u32[]{:S(2)}, u32[]{:S(2)}) collective-permute-start(bf16[448,64]{1,0:T(8,128)(2,1)S(1)} %slice.498), channel_id=1, source_target_pairs={{0,16},{16,0},{1,17},{17,1},{2,18},{18,2},{3,19},{19,3},{4,20},{20... | collective-permute-start | bytes 172040 | tf_op jit(solution)/shard_map/ppermute | solution.py:51
  776.9 173.0 %collective-permute-start.51 = (bf16[448,448]{1,0:T(8,128)(2,1)S(1)}, bf16[448,448]{1,0:T(8,128)(2,1)S(1)}, u32[]{:S(2)}, u32[]{:S(2)}) collective-permute-start(bf16[448,448]{1,0:T(8,128)(2,1)S(1)} %get-tuple-element.167), channel_id=1, source_target_pairs={{0,16},{16,0},{1,17},{17,1},{2,18},{18,2},{3,19},{19,3},{4,20},{20... | collective-permute-start | bytes 1204232 | tf_op jit(solution)/shard_map/ppermute | solution.py:51
  946.7 6.8 collective-permute-start.54
  (129 other events, 732.0 us)
Sparse Core Ops, SparseCore 0:
  14.8 59.5 all-gather.4
  76.6 123.7 all-gather.6
  202.0 77.9 all-gather.8
  281.3 123.5 all-gather.10
  517.4 22.4 reduce-scatter.14
  545.8 22.6 reduce-scatter.12
  570.8 45.9 reduce-scatter.22
  619.7 49.4 reduce-scatter.20
  671.6 38.8 reduce-scatter.8
  712.6 60.3 reduce-scatter.10
  776.0 83.1 reduce-scatter.18
  861.6 83.6 reduce-scatter.16

commit v2 on v1

--- a/solution.py
+++ b/solution.py
@@ -155,7 +155,7 @@
     return (output, kept)
 
 
-def layer_backward(kept, grad_out, gains, taps, attn, feed, channels, first):
+def layer_backward(kept, grad_out, gains, taps, attn, feed, channels, first, queue):
     (
         rows, scale_one, full_one, pre_values, gate_mix, values, queries, keys, probs, slope,
         mixed, gated, out_t, hidden, scale_two, full_two, gate, upper, inner,
@@ -163,17 +163,18 @@
     hidden_units = feed.shape[1] // 3
     length = full_one.shape[0] // 2
     branch_two = spread(grad_out)
-    grad_down = scatter(dot_tn(branch_two, inner))
+    branch_two, grad_down = product_first(branch_two, inner, branch_two)
     grad_inner = dot(branch_two, feed[:, 2 * hidden_units :])
     grad_gate = (grad_inner * upper * silu_slope(gate)).astype(jnp.bfloat16)
     grad_upper = (grad_inner * jax.nn.silu(gate)).astype(jnp.bfloat16)
     grad_halves = jnp.concatenate([grad_gate, grad_upper], axis=1)
-    grad_gate_up = scatter(dot_tn(full_two, grad_halves))
+    grad_halves, grad_gate_up = product_first(full_two, grad_halves, grad_halves)
+    feed_grads = queue.scatter(grad_gate_up, grad_down)
     grad_second = collect(dot_nt(grad_halves, feed[:, : 2 * hidden_units]))
     back_two, gain_two = rms_back(hidden, scale_two, gains[1], grad_second)
     grad_hidden = grad_out + back_two
     branch_one = spread(grad_hidden)
-    grad_outw = scatter(dot_tn(branch_one, gated))
+    branch_one, grad_outw = product_first(branch_one, gated, branch_one)
     grad_gated = dot(branch_one, out_t)
     grad_mixed = (grad_gated * jax.nn.silu(gate_mix)).astype(jnp.bfloat16)
     grad_mix_gate = (grad_gated * mixed * silu_slope(gate_mix)).astype(jnp.bfloat16)
@@ -191,16 +192,29 @@
     grad_pre, grad_taps = conv_back(grad_values.reshape(2, length, channels), pre_values, taps)
     grad_pre = grad_pre.astype(jnp.bfloat16).reshape(2 * length, channels)
     grad_both = jnp.concatenate([grad_pre, grad_mix_gate, grad_queries, grad_keys], axis=1)
-    grad_attn = scatter(dot_tn(full_one, grad_both))
+    grad_both, grad_attn = product_first(full_one, grad_both, grad_both)
+    attn_grads = queue.scatter(grad_attn, grad_outw)
     grad_first = collect(dot_nt(grad_both, attn[:, : grad_both.shape[1]]))
     back_one, gain_one = rms_back(rows, scale_one, gains[0], grad_first)
     grad_rows = grad_hidden + back_one
-    grads = (grad_attn, grad_outw, grad_gate_up, grad_down)
-    return (grad_rows, grads, jnp.stack([gain_one, gain_two]), grad_taps)
-
-
-def scatter(grad):
-    return lax.psum_scatter(grad.astype(jnp.bfloat16), "dp", scatter_dimension=0, tiled=True)
+    return (grad_rows, (feed_grads, attn_grads), jnp.stack([gain_one, gain_two]), grad_taps)
+
+
+class Queue:
+    def __init__(self):
+        self.last = None
+
+    def scatter(self, *grads):
+        block = jnp.concatenate(grads, axis=1) if len(grads) > 1 else grads[0]
+        if self.last is not None:
+            block, self.last = lax.optimization_barrier((block, self.last))
+        self.last = lax.psum_scatter(block, "dp", scatter_dimension=0, tiled=True)
+        return self.last
+
+
+def product_first(one, two, chain):
+    grad = widen(dot_tn(one, two).astype(jnp.bfloat16))
+    return lax.optimization_barrier((chain, grad))
 
 
 def body(
@@ -274,12 +288,15 @@
     final, kept_one = layer_forward(
         middle, small_one[:2], own_taps(small_one), attn_one, feed_one, channels, False
     )
+    queue = Queue()
     grad_middle, grads_one, gains_one, taps_one = layer_backward(
-        kept_one, cotangent * mask, small_one[:2], own_taps(small_one), attn_one, feed_one, channels, False
+        kept_one, cotangent * mask, small_one[:2], own_taps(small_one), attn_one, feed_one, channels, False,
+        queue,
     )
     grad_middle = grad_middle.astype(jnp.bfloat16).astype(jnp.float32)
     grad_start, grads_zero, gains_zero, taps_zero = layer_backward(
-        kept_zero, grad_middle, small_zero[:2], own_taps(small_zero), attn_zero, feed_zero, channels, True
+        kept_zero, grad_middle, small_zero[:2], own_taps(small_zero), attn_zero, feed_zero, channels, True,
+        queue,
     )
 
     def own_small(gains, taps):
@@ -302,8 +319,7 @@
     def halves(low, high, axis):
         return jnp.concatenate([low, high], axis=axis).astype(jnp.float32)
 
-    def pair_home(grads):
-        block = grads[:, 2 * channels :]
+    def pair_home(block):
         size = block.shape[1] // 2
         other = swap(block)
         low = jnp.where(lower, block, other)
@@ -312,18 +328,25 @@
             [halves(low[:, :size], high[:, :size], 1), halves(low[:, size:], high[:, size:], 1)], axis=1
         )
 
-    low, high = home(grads_zero[0][:, : 2 * channels], grads_one[0][:, : 2 * channels])
+    def split_pair(grads):
+        out = (channels + LANES - 1) // LANES * LANES
+        both = 2 * channels
+        width = grads.shape[1] - out
+        return (jnp.concatenate([grads[:, :both], grads[:, width:]], axis=1), grads[:, both:width])
+
+    attn_zero, pair_zero = split_pair(grads_zero[1])
+    attn_one, pair_one = split_pair(grads_one[1])
+    low, high = home(attn_zero, attn_one)
     vgate_grad = jnp.stack(
         [
             halves(low[:, :channels], high[:, :channels], 1),
-            halves(low[:, channels:], high[:, channels:], 1),
+            halves(low[:, channels : 2 * channels], high[:, channels : 2 * channels], 1),
         ],
         axis=1,
     )
-    low, high = home(grads_zero[1], grads_one[1])
-    out_grad = halves(low.T, high.T, 0)
-    low, high = home(grads_zero[2], grads_one[2])
-    wide = low.shape[1] // 2
+    out_grad = halves(low[:, 2 * channels : 3 * channels].T, high[:, 2 * channels : 3 * channels].T, 0)
+    low, high = home(grads_zero[0], grads_one[0])
+    wide = low.shape[1] // 3
     gate_up_grad = jnp.stack(
         [
             halves(low[:, :units], high[:, :units], 1),
@@ -331,14 +354,13 @@
         ],
         axis=1,
     )
-    low, high = home(grads_zero[3], grads_one[3])
-    down_grad = halves(low[:, :units].T, high[:, :units].T, 0)
+    down_grad = halves(low[:, 2 * wide : 2 * wide + units].T, high[:, 2 * wide : 2 * wide + units].T, 0)
     return (
         ends[None],
         sums[:, :2],
         sums[:, 2:],
-        pair_home(grads_zero[0]),
-        pair_home(grads_one[0]),
+        pair_home(pair_zero),
+        pair_home(pair_one),
         vgate_grad[None],
         out_grad[None],
         gate_up_grad[None],

time: 977 us -> 841 us (0.86)
  waiting for transfers between devices: 558 us -> 397 us
  other arithmetic: 47 us -> 64 us
  blocking collectives: 113 us -> 125 us
    reduce_scatter x8 -> x4, waiting for transfers between devices: 262 us -> 117 us  [scatter(): self.last = lax.psum_scatter(block, 'dp', scatter_dimension=0, tiled=True)]
    concatenate x2 -> x8, other arithmetic: 0.15 us -> 21 us  [the longest x4 17.6 us: scatter(): block = jnp.concatenate(grads, axis=1) if len(grads) > 1 else grads[0]]
    all_gather x4, waiting for transfers between devices: 185 us -> 171 us  [fetch(): return lax.all_gather(piece, 'dp', axis=0, tiled=True)]
    all_gather x8, blocking collectives: 113 us -> 125 us  [spread(): lax.all_gather(rows.astype(jnp.bfloat16), 'tensor', axis=0, tiled=True)]
    reduce_scatter x8 -> x4, starting transfers between devices: 11.1 us -> 0.16 us  [scatter(): self.last = lax.psum_scatter(block, 'dp', scatter_dimension=0, tiled=True)]
    unnamed x242 -> x196, local copies, waits for them, and re-layouts: 41.7 us -> 34.7 us
    ppermute x27 -> x25, waiting for transfers between devices: 23.3 us -> 21.9 us  [swap(): return lax.ppermute(block, 'section', [(0, 1), (1, 0)])]
  transfers between devices with their start and end apart: 68 -> 62, of which waited for: 41 -> 42; matrix products, arithmetic and copies ran while one was open for 17% -> 25% of each run, Pallas kernels for 0% -> 0%
where the time goes in v2:
time: 841 us; the launch traced here: 831 us
  waiting for transfers between devices  397 us (47%)
  blocking collectives  125 us (15%)
  matrix products  97.4 us (12%)
  local copies, waits for them, and re-layouts  91.4 us (11%)
  other arithmetic  64 us (8%)
  starting transfers between devices  39 us (5%)
  between operations  16.7 us (2%)
    all_gather x4, waiting for transfers between devices, fetch(): return lax.all_gather(piece, 'dp', axis=0, tiled=True)  171 us
    all_gather x8, blocking collectives, spread(): lax.all_gather(rows.astype(jnp.bfloat16), 'tensor', axis=0, tiled=True)  125 us
    reduce_scatter x4, waiting for transfers between devices, scatter(): self.last = lax.psum_scatter(block, 'dp', scatter_dimension=0, tiled=True)  117 us
    ppermute x24, waiting for transfers between devices, collect(): total = total + lax.ppermute(block, 'tensor', pairs).astype(jnp.float32)  67.8 us
    unnamed x196, local copies, waits for them, and re-layouts  34.7 us
    dot_general x8, matrix products, dot(): return jnp.dot(one, two, preferred_element_type=jnp.float32)  32.7 us
    ppermute x24, starting transfers between devices, collect(): total = total + lax.ppermute(block, 'tensor', pairs).astype(jnp.float32)  27.9 us
    dot_general x8, matrix products, dot_nt(): lax.dot_general(one, two, (((1,), (1,)), ((), ())), preferred_element_typ...  26.6 us
  transfers between devices with their start and end apart: 62, of which 42 were waited for; matrix products, arithmetic and copies ran while one was open for 25% of the time, Pallas kernels for 0%

profile of v2, /device:TPU:0, one launch (start us, length us, event | category | flops | bytes accessed | tf_op | source)
XLA Modules:
  0.0 830.9 jit_solution(1681834580289750433)
XLA Ops:
  15.3 6.4 constant_dynamic-slice_fusion.27
  32.6 15.1 %all_gather.36 = bf16[256,1792]{1,0:T(8,128)(2,1)S(1)} all-gather(bf16[64,1792]{1,0:T(8,128)(2,1)S(1)} %fusion.75), channel_id=1, replica_groups=mesh['section'=2,'dp'=4,'tensor'=4] {'tensor'}, dimensions={0}, use_global_device_ids=true | all-gather | bytes 1146880 | tf_op jit(solution)/shard_map/all_gather | solution.py:55
  54.0 20.5 %all-gather.5.cloned.1.call-done = bf16[1792,768]{1,0:T(8,128)(2,1)} async-done(((bf16[448,768]{1,0:T(8,128)(2,1)}), bf16[1792,768]{1,0:T(8,128)(2,1)}) %all-gather.5.cloned.1.call-update) | async-done | bytes 2752528 | tf_op jit(solution)/shard_map/all_gather | solution.py:257
  74.5 4.2 fusion.134
  98.5 4.9 collective-permute-done.5
  103.4 5.3 collective-permute-done.7
  111.5 12.1 %all_gather.38 = bf16[256,1792]{1,0:T(8,128)(2,1)S(1)} all-gather(bf16[64,1792]{1,0:T(8,128)(2,1)S(1)} %multiply_convert_fusion.14), channel_id=1, replica_groups=mesh['section'=2,'dp'=4,'tensor'=4] {'tensor'}, dimensions={0}, use_global_device_ids=true | all-gather | bytes 1146880 | tf_op jit(solution)/shard_map/all_gather | solution.py:55
  127.0 73.4 %all-gather.7.cloned.1.call-done = bf16[1792,1920]{1,0:T(8,128)(2,1)} async-done(((bf16[448,1920]{1,0:T(8,128)(2,1)}), bf16[1792,1920]{1,0:T(8,128)(2,1)}) %all-gather.7.cloned.1.call-update) | async-done | bytes 6881296 | tf_op jit(solution)/shard_map/all_gather | solution.py:257
  200.4 5.4 fusion.7
  207.3 3.5 fusion.29
  221.0 4.9 collective-permute-done.11
  225.9 5.1 collective-permute-done.13
  232.8 25.4 %all_gather.40 = bf16[256,1792]{1,0:T(8,128)(2,1)S(1)} all-gather(bf16[64,1792]{1,0:T(8,128)(2,1)S(1)} %fusion.82), channel_id=1, replica_groups=mesh['section'=2,'dp'=4,'tensor'=4] {'tensor'}, dimensions={0}, use_global_device_ids=true | all-gather | bytes 1146880 | tf_op jit(solution)/shard_map/all_gather | solution.py:55
  261.7 18.2 %all-gather.9.cloned.1.call-done = bf16[1792,1152]{1,0:T(8,128)(2,1)} async-done(((bf16[448,1152]{1,0:T(8,128)(2,1)}), bf16[1792,1152]{1,0:T(8,128)(2,1)}) %all-gather.9.cloned.1.call-update) | async-done | bytes 4128784 | tf_op jit(solution)/shard_map/all_gather | solution.py:257
  279.9 5.7 fusion.135
  309.6 19.9 %all_gather.42 = bf16[256,1792]{1,0:T(8,128)(2,1)S(1)} all-gather(bf16[64,1792]{1,0:T(8,128)(2,1)S(1)} %copy-done.34), channel_id=1, replica_groups=mesh['section'=2,'dp'=4,'tensor'=4] {'tensor'}, dimensions={0}, use_global_device_ids=true | all-gather | bytes 1146880 | tf_op jit(solution)/shard_map/all_gather | solution.py:55
  330.0 13.0 %all_gather.43 = bf16[256,1792]{1,0:T(8,128)(2,1)S(1)} all-gather(bf16[64,1792]{1,0:T(8,128)(2,1)S(1)} %multiply_convert_fusion.12), channel_id=1, replica_groups=mesh['section'=2,'dp'=4,'tensor'=4] {'tensor'}, dimensions={0}, use_global_device_ids=true | all-gather | bytes 1146880 | tf_op jit(solution)/shard_map/all_gather | solution.py:55
  346.4 58.5 %all-gather.11.cloned.1.call-done = bf16[1792,1920]{1,0:T(8,128)(2,1)} async-done(((bf16[448,1920]{1,0:T(8,128)(2,1)}), bf16[1792,1920]{1,0:T(8,128)(2,1)}) %all-gather.11.cloned.1.call-update) | async-done | bytes 6881296 | tf_op jit(solution)/shard_map/all_gather | solution.py:257
  404.9 5.4 fusion.3
  413.7 3.5 multiply_convert_fusion.3
  418.4 6.2 convolution_convert_fusion.1
  424.7 5.6 pad_maximum_fusion.1
  430.4 5.3 fusion.1
  442.2 5.0 collective-permute-done.22
  447.1 5.1 collective-permute-done.24
  455.0 13.4 %all_gather.45 = bf16[256,1792]{1,0:T(8,128)(2,1)} all-gather(bf16[64,1792]{1,0:T(8,128)(2,1)S(1)} %get-tuple-element.108), channel_id=1, replica_groups=mesh['section'=2,'dp'=4,'tensor'=4] {'tensor'}, dimensions={0}, use_global_device_ids=true | all-gather | bytes 1146880 | tf_op jit(solution)/shard_map/all_gather | solution.py:55
  486.5 5.4 convolution_convert_fusion.2
  493.2 4.6 pad_maximum_fusion.2
  497.8 51.2 %reduce-scatter.5.cloned.1.call-done = bf16[448,1920]{1,0:T(8,128)(2,1)} async-done(((bf16[1792,1920]{1,0:T(8,128)(2,1)}), bf16[448,1920]{1,0:T(8,128)(2,1)}) %reduce-scatter.5.cloned.1.call-update) | async-done | bytes 1720336 | tf_op jit(solution)/shard_map/reduce_scatter | solution.py:211
  549.1 4.0 fusion.14
  559.6 5.0 collective-permute-done.27
  564.6 5.1 collective-permute-done.29
  571.6 13.0 %all_gather.46 = bf16[256,1792]{1,0:T(8,128)(2,1)S(1)} all-gather(bf16[64,1792]{1,0:T(8,128)(2,1)S(1)} %fusion.87), channel_id=1, replica_groups=mesh['section'=2,'dp'=4,'tensor'=4] {'tensor'}, dimensions={0}, use_global_device_ids=true | all-gather | bytes 1146880 | tf_op jit(solution)/shard_map/all_gather | solution.py:55
  588.9 3.5 multiply_convert_fusion.1
  593.6 6.2 convolution_convert_fusion
  599.8 5.6 pad_maximum_fusion
  605.4 22.2 %reduce-scatter.7.cloned.1.call-done = bf16[448,1152]{1,0:T(8,128)(2,1)} async-done(((bf16[1792,1152]{1,0:T(8,128)(2,1)}), bf16[448,1152]{1,0:T(8,128)(2,1)}) %reduce-scatter.7.cloned.1.call-update) | async-done | bytes 1032208 | tf_op jit(solution)/shard_map/reduce_scatter | solution.py:211
  627.7 5.3 fusion.5
  639.4 5.0 collective-permute-done.32
  644.4 5.1 collective-permute-done.34
  651.4 13.4 %all_gather.47 = bf16[256,1792]{1,0:T(8,128)(2,1)} all-gather(bf16[64,1792]{1,0:T(8,128)(2,1)S(1)} %get-tuple-element.100), channel_id=1, replica_groups=mesh['section'=2,'dp'=4,'tensor'=4] {'tensor'}, dimensions={0}, use_global_device_ids=true | all-gather | bytes 1146880 | tf_op jit(solution)/shard_map/all_gather | solution.py:55
  683.3 4.1 convolution_convert_fusion.5
  707.1 3.9 collective-permute-done.37
  723.9 26.8 %reduce-scatter.9.cloned.1.call-done = bf16[448,1920]{1,0:T(8,128)(2,1)} async-done(((bf16[1792,1920]{1,0:T(8,128)(2,1)}), bf16[448,1920]{1,0:T(8,128)(2,1)}) %reduce-scatter.9.cloned.1.call-update) | async-done | bytes 1720336 | tf_op jit(solution)/shard_map/reduce_scatter | solution.py:211
  762.7 5.3 collective-permute-done.48
  770.4 9.2 %collective-permute-done.49 = f32[2,5,1792]{2,0,1:T(2,128)S(1)} collective-permute-done((f32[2,5,1792]{2,0,1:T(2,128)S(1)}, f32[2,5,1792]{2,0,1:T(2,128)S(1)}, u32[]{:S(2)}, u32[]{:S(2)}) %collective-permute-start.49) | collective-permute-done | bytes 71712 | tf_op jit(solution)/shard_map/ppermute | solution.py:81
  786.8 5.7 copy.242
  794.2 16.6 %reduce-scatter.11.cloned.1.call-done = bf16[448,768]{1,0:T(8,128)(2,1)} async-done(((bf16[1792,768]{1,0:T(8,128)(2,1)}), bf16[448,768]{1,0:T(8,128)(2,1)}) %reduce-scatter.11.cloned.1.call-update) | async-done | bytes 688144 | tf_op jit(solution)/shard_map/reduce_scatter | solution.py:211
  (520 shorter events, 237.0 us)
Async XLA Ops:
  7.2 67.3 %all-gather.5.cloned.1.call-start = ((), (), s32[]{:S(2)}) async-start(), calls=%async_computation.4 | async-start | bytes 3440640 | tf_op jit(solution)/shard_map/all_gather | solution.py:257
  14.7 185.7 %all-gather.7.cloned.1.call-start = ((), (), s32[]{:S(2)}) async-start(), calls=%async_computation.5 | async-start | bytes 8601600 | tf_op jit(solution)/shard_map/all_gather | solution.py:257
  28.1 251.8 %all-gather.9.cloned.1.call-start = ((), (), s32[]{:S(2)}) async-start(), calls=%async_computation.6 | async-start | bytes 5160960 | tf_op jit(solution)/shard_map/all_gather | solution.py:257
  47.7 4.1 collective-permute-start.2
  87.1 4.5 collective-permute-start.4
  91.6 313.3 %all-gather.11.cloned.1.call-start = ((), (), s32[]{:S(2)}) async-start(), calls=%async_computation.7 | async-start | bytes 8601600 | tf_op jit(solution)/shard_map/all_gather | solution.py:257
  94.9 8.5 %collective-permute-start.5 = (bf16[64,1792]{1,0:T(8,128)(2,1)S(1)}, bf16[64,1792]{1,0:T(8,128)(2,1)S(1)}, u32[]{:S(2)}, u32[]{:S(2)}) collective-permute-start(bf16[64,1792]{1,0:T(8,128)(2,1)S(1)} %get-tuple-element.189), channel_id=1, source_target_pairs={{0,1},{1,0},{2,3},{3,2},{4,5},{5,4},{6,7},{7,6},{8,9},{9,8},{10,11... | collective-permute-start | bytes 688136 | tf_op jit(solution)/shard_map/ppermute | solution.py:71
  96.5 12.2 %collective-permute-start.7 = (bf16[64,1792]{1,0:T(8,128)(2,1)S(1)}, bf16[64,1792]{1,0:T(8,128)(2,1)S(1)}, u32[]{:S(2)}, u32[]{:S(2)}) collective-permute-start(bf16[64,1792]{1,0:T(8,128)(2,1)S(1)} %get-tuple-element.190), channel_id=1, source_target_pairs={{0,3},{1,2},{2,1},{3,0},{4,7},{5,6},{6,5},{7,4},{8,11},{9,10},{10,... | collective-permute-start | bytes 688136 | tf_op jit(solution)/shard_map/ppermute | solution.py:71
  98.0 12.1 %collective-permute-start.6 = (bf16[64,1792]{1,0:T(8,128)(2,1)S(1)}, bf16[64,1792]{1,0:T(8,128)(2,1)S(1)}, u32[]{:S(2)}, u32[]{:S(2)}) collective-permute-start(bf16[64,1792]{1,0:T(8,128)(2,1)S(1)} %get-tuple-element.191), channel_id=1, source_target_pairs={{0,2},{1,3},{2,0},{3,1},{4,6},{5,7},{6,4},{7,5},{8,10},{9,11},{10,... | collective-permute-start | bytes 688136 | tf_op jit(solution)/shard_map/ppermute | solution.py:71
  212.8 336.2 %reduce-scatter.5.cloned.1.call-start = ((), (), s32[]{:S(2)}) async-start(), calls=%async_computation.8 | async-start | bytes 8601600 | tf_op jit(solution)/shard_map/reduce_scatter | solution.py:211
  217.4 8.5 %collective-permute-start.11 = (bf16[64,1792]{1,0:T(8,128)(2,1)S(1)}, bf16[64,1792]{1,0:T(8,128)(2,1)S(1)}, u32[]{:S(2)}, u32[]{:S(2)}) collective-permute-start(bf16[64,1792]{1,0:T(8,128)(2,1)S(1)} %get-tuple-element.186), channel_id=1, source_target_pairs={{0,1},{1,0},{2,3},{3,2},{4,5},{5,4},{6,7},{7,6},{8,9},{9,8},{10,11... | collective-permute-start | bytes 688136 | tf_op jit(solution)/shard_map/ppermute | solution.py:71
  218.9 12.1 %collective-permute-start.13 = (bf16[64,1792]{1,0:T(8,128)(2,1)S(1)}, bf16[64,1792]{1,0:T(8,128)(2,1)S(1)}, u32[]{:S(2)}, u32[]{:S(2)}) collective-permute-start(bf16[64,1792]{1,0:T(8,128)(2,1)S(1)} %get-tuple-element.187), channel_id=1, source_target_pairs={{0,3},{1,2},{2,1},{3,0},{4,7},{5,6},{6,5},{7,4},{8,11},{9,10},{10,... | collective-permute-start | bytes 688136 | tf_op jit(solution)/shard_map/ppermute | solution.py:71
  220.4 12.0 %collective-permute-start.12 = (bf16[64,1792]{1,0:T(8,128)(2,1)S(1)}, bf16[64,1792]{1,0:T(8,128)(2,1)S(1)}, u32[]{:S(2)}, u32[]{:S(2)}) collective-permute-start(bf16[64,1792]{1,0:T(8,128)(2,1)S(1)} %get-tuple-element.188), channel_id=1, source_target_pairs={{0,2},{1,3},{2,0},{3,1},{4,6},{5,7},{6,4},{7,5},{8,10},{9,11},{10,... | collective-permute-start | bytes 688136 | tf_op jit(solution)/shard_map/ppermute | solution.py:71
  306.0 23.5 %collective-permute-start.16 = (bf16[64,1792]{1,0:T(8,128)(2,1)S(1)}, bf16[64,1792]{1,0:T(8,128)(2,1)S(1)}, u32[]{:S(2)}, u32[]{:S(2)}) collective-permute-start(bf16[64,1792]{1,0:T(8,128)(2,1)S(1)} %get-tuple-element.179), channel_id=1, source_target_pairs={{0,1},{1,0},{2,3},{3,2},{4,5},{5,4},{6,7},{7,6},{8,9},{9,8},{10,11... | collective-permute-start | bytes 688136 | tf_op jit(solution)/shard_map/ppermute | solution.py:71
  307.6 21.9 %collective-permute-start.18 = (bf16[64,1792]{1,0:T(8,128)(2,1)S(1)}, bf16[64,1792]{1,0:T(8,128)(2,1)S(1)}, u32[]{:S(2)}, u32[]{:S(2)}) collective-permute-start(bf16[64,1792]{1,0:T(8,128)(2,1)S(1)} %get-tuple-element.180), channel_id=1, source_target_pairs={{0,3},{1,2},{2,1},{3,0},{4,7},{5,6},{6,5},{7,4},{8,11},{9,10},{10,... | collective-permute-start | bytes 688136 | tf_op jit(solution)/shard_map/ppermute | solution.py:71
  309.1 20.5 %collective-permute-start.17 = (bf16[64,1792]{1,0:T(8,128)(2,1)S(1)}, bf16[64,1792]{1,0:T(8,128)(2,1)S(1)}, u32[]{:S(2)}, u32[]{:S(2)}) collective-permute-start(bf16[64,1792]{1,0:T(8,128)(2,1)S(1)} %get-tuple-element.181), channel_id=1, source_target_pairs={{0,2},{1,3},{2,0},{3,1},{4,6},{5,7},{6,4},{7,5},{8,10},{9,11},{10,... | collective-permute-start | bytes 688136 | tf_op jit(solution)/shard_map/ppermute | solution.py:71
  329.5 13.5 %collective-permute-start.19 = (bf16[256,1792]{1,0:T(8,128)(2,1)S(1)}, bf16[256,1792]{1,0:T(8,128)(2,1)S(1)}, u32[]{:S(2)}, u32[]{:S(2)}) collective-permute-start(bf16[256,1792]{1,0:T(8,128)(2,1)S(1)} %all_gather.42), channel_id=1, source_target_pairs={{0,16},{16,0},{1,17},{17,1},{2,18},{18,2},{3,19},{19,3},{4,20},{20... | collective-permute-start | bytes 2752520 | tf_op jit(solution)/shard_map/ppermute | solution.py:51
  430.3 197.3 %reduce-scatter.7.cloned.1.call-start = ((), (), s32[]{:S(2)}) async-start(), calls=%async_computation.9 | async-start | bytes 5160960 | tf_op jit(solution)/shard_map/reduce_scatter | solution.py:211
  438.6 8.5 %collective-permute-start.22 = (bf16[64,1792]{1,0:T(8,128)(2,1)S(1)}, bf16[64,1792]{1,0:T(8,128)(2,1)S(1)}, u32[]{:S(2)}, u32[]{:S(2)}) collective-permute-start(bf16[64,1792]{1,0:T(8,128)(2,1)S(1)} %get-tuple-element.176), channel_id=1, source_target_pairs={{0,1},{1,0},{2,3},{3,2},{4,5},{5,4},{6,7},{7,6},{8,9},{9,8},{10,11... | collective-permute-start | bytes 688136 | tf_op jit(solution)/shard_map/ppermute | solution.py:71
  440.1 12.1 %collective-permute-start.24 = (bf16[64,1792]{1,0:T(8,128)(2,1)S(1)}, bf16[64,1792]{1,0:T(8,128)(2,1)S(1)}, u32[]{:S(2)}, u32[]{:S(2)}) collective-permute-start(bf16[64,1792]{1,0:T(8,128)(2,1)S(1)} %get-tuple-element.177), channel_id=1, source_target_pairs={{0,3},{1,2},{2,1},{3,0},{4,7},{5,6},{6,5},{7,4},{8,11},{9,10},{10,... | collective-permute-start | bytes 688136 | tf_op jit(solution)/shard_map/ppermute | solution.py:71
  441.6 12.0 %collective-permute-start.23 = (bf16[64,1792]{1,0:T(8,128)(2,1)S(1)}, bf16[64,1792]{1,0:T(8,128)(2,1)S(1)}, u32[]{:S(2)}, u32[]{:S(2)}) collective-permute-start(bf16[64,1792]{1,0:T(8,128)(2,1)S(1)} %get-tuple-element.178), channel_id=1, source_target_pairs={{0,2},{1,3},{2,0},{3,1},{4,6},{5,7},{6,4},{7,5},{8,10},{9,11},{10,... | collective-permute-start | bytes 688136 | tf_op jit(solution)/shard_map/ppermute | solution.py:71
  468.4 4.5 collective-permute-start.25
  549.0 201.7 %reduce-scatter.9.cloned.1.call-start = ((), (), s32[]{:S(2)}) async-start(), calls=%async_computation.10 | async-start | bytes 8601600 | tf_op jit(solution)/shard_map/reduce_scatter | solution.py:211
  556.1 8.5 %collective-permute-start.27 = (bf16[64,1792]{1,0:T(8,128)(2,1)S(1)}, bf16[64,1792]{1,0:T(8,128)(2,1)S(1)}, u32[]{:S(2)}, u32[]{:S(2)}) collective-permute-start(bf16[64,1792]{1,0:T(8,128)(2,1)S(1)} %get-tuple-element.171), channel_id=1, source_target_pairs={{0,1},{1,0},{2,3},{3,2},{4,5},{5,4},{6,7},{7,6},{8,9},{9,8},{10,11... | collective-permute-start | bytes 688136 | tf_op jit(solution)/shard_map/ppermute | solution.py:71
  557.6 12.1 %collective-permute-start.29 = (bf16[64,1792]{1,0:T(8,128)(2,1)S(1)}, bf16[64,1792]{1,0:T(8,128)(2,1)S(1)}, u32[]{:S(2)}, u32[]{:S(2)}) collective-permute-start(bf16[64,1792]{1,0:T(8,128)(2,1)S(1)} %get-tuple-element.172), channel_id=1, source_target_pairs={{0,3},{1,2},{2,1},{3,0},{4,7},{5,6},{6,5},{7,4},{8,11},{9,10},{10,... | collective-permute-start | bytes 688136 | tf_op jit(solution)/shard_map/ppermute | solution.py:71
  559.1 12.0 %collective-permute-start.28 = (bf16[64,1792]{1,0:T(8,128)(2,1)S(1)}, bf16[64,1792]{1,0:T(8,128)(2,1)S(1)}, u32[]{:S(2)}, u32[]{:S(2)}) collective-permute-start(bf16[64,1792]{1,0:T(8,128)(2,1)S(1)} %get-tuple-element.173), channel_id=1, source_target_pairs={{0,2},{1,3},{2,0},{3,1},{4,6},{5,7},{6,4},{7,5},{8,10},{9,11},{10,... | collective-permute-start | bytes 688136 | tf_op jit(solution)/shard_map/ppermute | solution.py:71
  627.6 183.2 %reduce-scatter.11.cloned.1.call-start = ((), (), s32[]{:S(2)}) async-start(), calls=%async_computation.11 | async-start | bytes 3440640 | tf_op jit(solution)/shard_map/reduce_scatter | solution.py:211
  635.9 8.5 %collective-permute-start.32 = (bf16[64,1792]{1,0:T(8,128)(2,1)S(1)}, bf16[64,1792]{1,0:T(8,128)(2,1)S(1)}, u32[]{:S(2)}, u32[]{:S(2)}) collective-permute-start(bf16[64,1792]{1,0:T(8,128)(2,1)S(1)} %get-tuple-element.168), channel_id=1, source_target_pairs={{0,1},{1,0},{2,3},{3,2},{4,5},{5,4},{6,7},{7,6},{8,9},{9,8},{10,11... | collective-permute-start | bytes 688136 | tf_op jit(solution)/shard_map/ppermute | solution.py:71
  637.4 12.1 %collective-permute-start.34 = (bf16[64,1792]{1,0:T(8,128)(2,1)S(1)}, bf16[64,1792]{1,0:T(8,128)(2,1)S(1)}, u32[]{:S(2)}, u32[]{:S(2)}) collective-permute-start(bf16[64,1792]{1,0:T(8,128)(2,1)S(1)} %get-tuple-element.169), channel_id=1, source_target_pairs={{0,3},{1,2},{2,1},{3,0},{4,7},{5,6},{6,5},{7,4},{8,11},{9,10},{10,... | collective-permute-start | bytes 688136 | tf_op jit(solution)/shard_map/ppermute | solution.py:71
  638.9 12.0 %collective-permute-start.33 = (bf16[64,1792]{1,0:T(8,128)(2,1)S(1)}, bf16[64,1792]{1,0:T(8,128)(2,1)S(1)}, u32[]{:S(2)}, u32[]{:S(2)}) collective-permute-start(bf16[64,1792]{1,0:T(8,128)(2,1)S(1)} %get-tuple-element.170), channel_id=1, source_target_pairs={{0,2},{1,3},{2,0},{3,1},{4,6},{5,7},{6,4},{7,5},{8,10},{9,11},{10,... | collective-permute-start | bytes 688136 | tf_op jit(solution)/shard_map/ppermute | solution.py:71
  664.7 8.5 %collective-permute-start.35 = (bf16[256,1792]{1,0:T(8,128)(2,1)}, bf16[256,1792]{1,0:T(8,128)(2,1)}, u32[]{:S(2)}, u32[]{:S(2)}) collective-permute-start(bf16[256,1792]{1,0:T(8,128)(2,1)} %all_gather.47), channel_id=1, source_target_pairs={{0,16},{16,0},{1,17},{17,1},{2,18},{18,2},{3,19},{19,3},{4,20},{20... | collective-permute-start | bytes 2752520 | tf_op jit(solution)/shard_map/ppermute | solution.py:51
  671.4 18.3 %collective-permute-start.40 = (bf16[256,1792]{1,0:T(8,128)(2,1)}, bf16[256,1792]{1,0:T(8,128)(2,1)}, u32[]{:S(2)}, u32[]{:S(2)}) collective-permute-start(bf16[256,1792]{1,0:T(8,128)(2,1)} %slice.654), channel_id=1, source_target_pairs={{0,16},{16,0},{1,17},{17,1},{2,18},{18,2},{3,19},{19,3},{4,20},{20... | collective-permute-start | bytes 2752520 | tf_op jit(solution)/shard_map/ppermute | solution.py:51
  689.7 8.0 collective-permute-start.36
  692.8 27.2 %collective-permute-start.41 = (bf16[64,1792]{1,0:T(8,128)(2,1)S(1)}, bf16[64,1792]{1,0:T(8,128)(2,1)S(1)}, u32[]{:S(2)}, u32[]{:S(2)}) collective-permute-start(bf16[64,1792]{1,0:T(8,128)(2,1)S(1)} %get-tuple-element.162), channel_id=1, source_target_pairs={{0,1},{1,0},{2,3},{3,2},{4,5},{5,4},{6,7},{7,6},{8,9},{9,8},{10,11... | collective-permute-start | bytes 688136 | tf_op jit(solution)/shard_map/ppermute | solution.py:71
  692.9 27.1 %collective-permute-start.43 = (bf16[64,1792]{1,0:T(8,128)(2,1)S(1)}, bf16[64,1792]{1,0:T(8,128)(2,1)S(1)}, u32[]{:S(2)}, u32[]{:S(2)}) collective-permute-start(bf16[64,1792]{1,0:T(8,128)(2,1)S(1)} %get-tuple-element.163), channel_id=1, source_target_pairs={{0,3},{1,2},{2,1},{3,0},{4,7},{5,6},{6,5},{7,4},{8,11},{9,10},{10,... | collective-permute-start | bytes 688136 | tf_op jit(solution)/shard_map/ppermute | solution.py:71
  701.9 9.2 %collective-permute-start.37 = (bf16[64,1792]{1,0:T(8,128)(2,1)}, bf16[64,1792]{1,0:T(8,128)(2,1)S(1)}, u32[]{:S(2)}, u32[]{:S(2)}) collective-permute-start(bf16[64,1792]{1,0:T(8,128)(2,1)} %get-tuple-element.165), channel_id=1, source_target_pairs={{0,1},{1,0},{2,3},{3,2},{4,5},{5,4},{6,7},{7,6},{8,9},{9,8},{10,11... | collective-permute-start | bytes 688136 | tf_op jit(solution)/shard_map/ppermute | solution.py:71
  703.9 11.8 %collective-permute-start.39 = (bf16[64,1792]{1,0:T(8,128)(2,1)}, bf16[64,1792]{1,0:T(8,128)(2,1)S(1)}, u32[]{:S(2)}, u32[]{:S(2)}) collective-permute-start(bf16[64,1792]{1,0:T(8,128)(2,1)} %get-tuple-element.166), channel_id=1, source_target_pairs={{0,3},{1,2},{2,1},{3,0},{4,7},{5,6},{6,5},{7,4},{8,11},{9,10},{10,... | collective-permute-start | bytes 688136 | tf_op jit(solution)/shard_map/ppermute | solution.py:71
  705.3 12.7 %collective-permute-start.38 = (bf16[64,1792]{1,0:T(8,128)(2,1)S(1)}, bf16[64,1792]{1,0:T(8,128)(2,1)}, u32[]{:S(2)}, u32[]{:S(2)}) collective-permute-start(bf16[64,1792]{1,0:T(8,128)(2,1)S(1)} %get-tuple-element.167), channel_id=1, source_target_pairs={{0,2},{1,3},{2,0},{3,1},{4,6},{5,7},{6,4},{7,5},{8,10},{9,11},{10,... | collective-permute-start | bytes 688136 | tf_op jit(solution)/shard_map/ppermute | solution.py:71
  711.7 10.0 %collective-permute-start.42 = (bf16[64,1792]{1,0:T(8,128)(2,1)S(1)}, bf16[64,1792]{1,0:T(8,128)(2,1)S(1)}, u32[]{:S(2)}, u32[]{:S(2)}) collective-permute-start(bf16[64,1792]{1,0:T(8,128)(2,1)S(1)} %get-tuple-element.164), channel_id=1, source_target_pairs={{0,2},{1,3},{2,0},{3,1},{4,6},{5,7},{6,4},{7,5},{8,10},{9,11},{10,... | collective-permute-start | bytes 688136 | tf_op jit(solution)/shard_map/ppermute | solution.py:71
  719.9 31.9 %collective-permute-start.45 = (f32[2,5,1792]{2,0,1:T(2,128)S(1)}, f32[2,5,1792]{2,0,1:T(2,128)S(1)}, u32[]{:S(2)}, u32[]{:S(2)}) collective-permute-start(f32[2,5,1792]{2,0,1:T(2,128)S(1)} %pad_maximum_fusion.13), channel_id=1, source_target_pairs={{0,16},{16,0},{1,17},{17,1},{2,18},{18,2},{3,19},{19,3},{4,20},{20... | collective-permute-start | bytes 215048 | tf_op jit(solution)/shard_map/ppermute | solution.py:81
  751.7 29.1 %collective-permute-start.44 = (f32[64,1792]{1,0:T(8,128)S(1)}, f32[64,1792]{1,0:T(8,128)S(1)}, u32[]{:S(2)}, u32[]{:S(2)}) collective-permute-start(f32[64,1792]{1,0:T(8,128)S(1)} %broadcast_select_fusion.14), channel_id=1, source_target_pairs={{0,16},{16,0},{1,17},{17,1},{2,18},{18,2},{3,19},{19,3},{4,20},{20... | collective-permute-start | bytes 1376264 | tf_op jit(solution)/shard_map/ppermute | solution.py:51
  751.9 4.7 collective-permute-start.46
  753.7 31.8 %collective-permute-start.53 = (bf16[448,1920]{1,0:T(8,128)(2,1)S(1)}, bf16[448,1920]{1,0:T(8,128)(2,1)S(1)}, u32[]{:S(2)}, u32[]{:S(2)}) collective-permute-start(bf16[448,1920]{1,0:T(8,128)(2,1)S(1)} %broadcast_select_fusion.2), channel_id=1, source_target_pairs={{0,16},{16,0},{1,17},{17,1},{2,18},{18,2},{3,19},{19,3},{4,20},{20... | collective-permute-start | bytes 5160968 | tf_op jit(solution)/shard_map/ppermute | solution.py:51
  756.7 4.4 collective-permute-start.47
  761.2 6.8 collective-permute-start.48
  768.0 11.6 %collective-permute-start.49 = (f32[2,5,1792]{2,0,1:T(2,128)S(1)}, f32[2,5,1792]{2,0,1:T(2,128)S(1)}, u32[]{:S(2)}, u32[]{:S(2)}) collective-permute-start(f32[2,5,1792]{2,0,1:T(2,128)S(1)} %add.449), channel_id=1, source_target_pairs={{0,8},{4,12},{8,0},{12,4},{1,9},{5,13},{9,1},{13,5},{2,10},{6,14},... | collective-permute-start | bytes 215048 | tf_op jit(solution)/shard_map/ppermute | solution.py:81
  770.3 11.6 %collective-permute-start.51 = (bf16[448,448]{1,0:T(8,128)(2,1)S(1)}, bf16[448,448]{1,0:T(8,128)(2,1)S(1)}, u32[]{:S(2)}, u32[]{:S(2)}) collective-permute-start(bf16[448,448]{1,0:T(8,128)(2,1)S(1)} %slice.519), channel_id=1, source_target_pairs={{0,16},{16,0},{1,17},{17,1},{2,18},{18,2},{3,19},{19,3},{4,20},{20... | collective-permute-start | bytes 1204232 | tf_op jit(solution)/shard_map/ppermute | solution.py:51
  811.8 3.8 collective-permute-start.50
  (100 other events, 634.0 us)
Sparse Core Ops, SparseCore 0:
  14.8 59.5 all-gather.4
  76.6 123.7 all-gather.6
  202.0 77.8 all-gather.8
  281.3 123.5 all-gather.10
  430.4 118.5 reduce-scatter.4
  551.3 76.2 reduce-scatter.6
  629.9 120.7 reduce-scatter.8
  753.1 57.6 reduce-scatter.10

commit v3 on v2

--- a/solution.py
+++ b/solution.py
@@ -3,6 +3,7 @@
 import jax
 import jax.numpy as jnp
 from jax import lax
+from jax.experimental.layout import Layout, with_layout_constraint
 from jax.sharding import PartitionSpec as P
 
 WIN = 64
@@ -121,12 +122,23 @@
     return (probs, probs)
 
 
-def layer_forward(rows, gains, taps, attn, feed, channels, first):
-    width = (attn.shape[1] - (channels + LANES - 1) // LANES * LANES - 2 * channels) // 2
-    hidden_units = feed.shape[1] // 3
+def gates(halves, units):
+    main = units // LANES * LANES
+    stop = main + units
+    return (
+        (halves[:, :main], halves[:, main : 2 * main]),
+        (halves[:, 2 * main : stop], halves[:, stop : 2 * units]),
+    )
+
+
+def layer_forward(rows, gains, taps, weights, first):
+    mix, out_t, pair, down = weights
+    channels = out_t.shape[1]
+    width = mix.shape[1] // 2 - channels
+    units = down.shape[1]
     scale_one, normed = rms_rows(rows, gains[0])
     full_one = spread(normed)
-    both = dot(full_one, attn[:, : 2 * channels + 2 * width])
+    both = dot(full_one, mix)
     length = full_one.shape[0] // 2
     pre_values = both[:, :channels].reshape(2, length, channels)
     gate_mix = both[:, channels : 2 * channels]
@@ -139,38 +151,44 @@
         "shij,sjhc->sihc", probs.astype(jnp.bfloat16), values, preferred_element_type=jnp.float32
     ).reshape(2 * length, channels)
     gated = (mixed * jax.nn.silu(gate_mix)).astype(jnp.bfloat16)
-    out_t = attn[:, 2 * channels + 2 * width :][:, :channels]
     hidden = rows + collect(dot_nt(gated, out_t))
     scale_two, normed_two = rms_rows(hidden, gains[1])
     full_two = spread(normed_two)
-    halves = dot(full_two, feed[:, : 2 * hidden_units])
-    gate = halves[:, :hidden_units]
-    upper = halves[:, hidden_units:]
-    inner = (jax.nn.silu(gate) * upper).astype(jnp.bfloat16)
-    output = hidden + collect(dot_nt(inner, feed[:, 2 * hidden_units :]))
+    halves = dot(full_two, pair)
+    inner = jnp.concatenate(
+        [(jax.nn.silu(gate) * upper).astype(jnp.bfloat16) for gate, upper in gates(halves, units)], axis=1
+    )
+    output = hidden + collect(dot_nt(inner, down))
     kept = (
         rows, scale_one, full_one, pre_values, gate_mix, values, queries, keys, probs, slope,
-        mixed, gated, out_t, hidden, scale_two, full_two, gate, upper, inner,
+        mixed, gated, hidden, scale_two, full_two, halves, inner,
     )
     return (output, kept)
 
 
-def layer_backward(kept, grad_out, gains, taps, attn, feed, channels, first, queue):
+def layer_backward(kept, grad_out, gains, taps, weights, first, queue, tail):
     (
         rows, scale_one, full_one, pre_values, gate_mix, values, queries, keys, probs, slope,
-        mixed, gated, out_t, hidden, scale_two, full_two, gate, upper, inner,
+        mixed, gated, hidden, scale_two, full_two, halves, inner,
     ) = kept
-    hidden_units = feed.shape[1] // 3
+    mix, out_t, pair, down = weights
+    channels = out_t.shape[1]
+    units = down.shape[1]
+    main = units // LANES * LANES
     length = full_one.shape[0] // 2
     branch_two = spread(grad_out)
     branch_two, grad_down = product_first(branch_two, inner, branch_two)
-    grad_inner = dot(branch_two, feed[:, 2 * hidden_units :])
-    grad_gate = (grad_inner * upper * silu_slope(gate)).astype(jnp.bfloat16)
-    grad_upper = (grad_inner * jax.nn.silu(gate)).astype(jnp.bfloat16)
-    grad_halves = jnp.concatenate([grad_gate, grad_upper], axis=1)
+    grad_inner = dot(branch_two, down)
+    parts = []
+    for (gate, upper), grad in zip(gates(halves, units), (grad_inner[:, :main], grad_inner[:, main:])):
+        parts.append((grad * upper * silu_slope(gate)).astype(jnp.bfloat16))
+        parts.append((grad * jax.nn.silu(gate)).astype(jnp.bfloat16))
+    filler = jnp.zeros((2 * length, pair.shape[1] - 2 * units), jnp.bfloat16)
+    grad_halves = jnp.concatenate([*parts, filler], axis=1)
     grad_halves, grad_gate_up = product_first(full_two, grad_halves, grad_halves)
-    feed_grads = queue.scatter(grad_gate_up, grad_down)
-    grad_second = collect(dot_nt(grad_halves, feed[:, : 2 * hidden_units]))
+    rest = jnp.pad(grad_down[:, main : units - tail], ((0, 0), (2 * units, 0)))
+    queue.scatter(grad_down[:, :main], grad_gate_up + rest)
+    grad_second = collect(dot_nt(grad_halves, pair))
     back_two, gain_two = rms_back(hidden, scale_two, gains[1], grad_second)
     grad_hidden = grad_out + back_two
     branch_one = spread(grad_hidden)
@@ -193,27 +211,30 @@
     grad_pre = grad_pre.astype(jnp.bfloat16).reshape(2 * length, channels)
     grad_both = jnp.concatenate([grad_pre, grad_mix_gate, grad_queries, grad_keys], axis=1)
     grad_both, grad_attn = product_first(full_one, grad_both, grad_both)
-    attn_grads = queue.scatter(grad_attn, grad_outw)
-    grad_first = collect(dot_nt(grad_both, attn[:, : grad_both.shape[1]]))
+    queue.scatter(grad_attn, grad_outw, grad_down[:, units - tail :])
+    grad_first = collect(dot_nt(grad_both, mix))
     back_one, gain_one = rms_back(rows, scale_one, gains[0], grad_first)
     grad_rows = grad_hidden + back_one
-    return (grad_rows, (feed_grads, attn_grads), jnp.stack([gain_one, gain_two]), grad_taps)
+    return (grad_rows, jnp.stack([gain_one, gain_two]), grad_taps)
+
+
+def by_rows(block):
+    return with_layout_constraint(block, Layout(major_to_minor=(0, 1)))
 
 
 class Queue:
     def __init__(self):
-        self.last = None
+        self.done = []
 
     def scatter(self, *grads):
-        block = jnp.concatenate(grads, axis=1) if len(grads) > 1 else grads[0]
-        if self.last is not None:
-            block, self.last = lax.optimization_barrier((block, self.last))
-        self.last = lax.psum_scatter(block, "dp", scatter_dimension=0, tiled=True)
-        return self.last
+        block = by_rows(jnp.concatenate(grads, axis=1))
+        if self.done:
+            block, self.done[-1] = lax.optimization_barrier((block, self.done[-1]))
+        self.done.append(by_rows(lax.psum_scatter(block, "dp", scatter_dimension=0, tiled=True)))
 
 
 def product_first(one, two, chain):
-    grad = widen(dot_tn(one, two).astype(jnp.bfloat16))
+    grad = dot_tn(one, two).astype(jnp.bfloat16)
     return lax.optimization_barrier((chain, grad))
 
 
@@ -226,6 +247,8 @@
     rows_dev, model = boundary.shape[2:]
     channels = value_gate.shape[-1] // 2
     units = gate_up.shape[-1] // 2
+    main = units // LANES * LANES
+    tail = -(3 * channels + lin_qk.shape[-1]) % LANES
 
     def half(block, axis, which):
         size = block.shape[axis] // 2
@@ -238,30 +261,38 @@
 
     def attn_piece(which):
         values = half(value_gate[0], 2, which)
+        last = half(down_weight[0], 0, which)[units - tail :]
         return jnp.concatenate(
-            [values[:, 0], values[:, 1], widen(half(out_weight[0], 0, which).T)], axis=1
+            [values[:, 0], values[:, 1], half(out_weight[0], 0, which).T, last.T], axis=1
         )
 
     def feed_piece(which):
         pair = half(gate_up[0], 2, which)
         down = half(down_weight[0], 0, which).T
-        return jnp.concatenate([widen(pair[:, 0]), widen(pair[:, 1]), widen(down)], axis=1)
-
-    def with_pair(piece, pair):
-        pair = half(pair, 2, core)
         return jnp.concatenate(
-            [piece[:, : 2 * channels], pair[:, 0], pair[:, 1], piece[:, 2 * channels :]], axis=1
+            [down[:, :main], pair[:, 0, :main], pair[:, 1, :main], pair[:, 0, main:], pair[:, 1, main:], down[:, main : units - tail]],
+            axis=1,
         )
 
     def fetch(piece):
         return lax.all_gather(piece, "dp", axis=0, tiled=True)
+
+    def with_pair(attn, pair):
+        pair = half(pair, 2, core)
+        both = 2 * channels
+        return jnp.concatenate([attn[:, :both], pair[:, 0], pair[:, 1], attn[:, both:]], axis=1)
+
+    def parts_of(feed, attn):
+        stop = attn.shape[1] - tail
+        down = jnp.concatenate([feed[:, :main], feed[:, main + 2 * units :], attn[:, stop:]], axis=1)
+        return (attn[:, : stop - channels], attn[:, stop - channels : stop], feed[:, main:], down)
 
     attn_parts = both_layers(attn_piece)
     feed_parts = both_layers(feed_piece)
     attn_zero = fetch(with_pair(attn_parts[0], lin_qk))
-    feed_zero = fetch(feed_parts[0])
+    weights_zero = parts_of(fetch(feed_parts[0]), attn_zero)
     attn_one = fetch(with_pair(attn_parts[1], win_qk))
-    feed_one = fetch(feed_parts[1])
+    weights_one = parts_of(fetch(feed_parts[1]), attn_one)
 
     small = jnp.concatenate([norm_gains[0], conv_taps[0]], axis=0)
     small_other = swap(small)
@@ -282,22 +313,22 @@
     mask = (place < length).astype(jnp.float32)[:, None]
 
     middle, kept_zero = layer_forward(
-        entering, small_zero[:2], own_taps(small_zero), attn_zero, feed_zero, channels, True
+        entering, small_zero[:2], own_taps(small_zero), weights_zero, True
     )
     middle = middle.astype(jnp.bfloat16).astype(jnp.float32)
     final, kept_one = layer_forward(
-        middle, small_one[:2], own_taps(small_one), attn_one, feed_one, channels, False
+        middle, small_one[:2], own_taps(small_one), weights_one, False
     )
     queue = Queue()
-    grad_middle, grads_one, gains_one, taps_one = layer_backward(
-        kept_one, cotangent * mask, small_one[:2], own_taps(small_one), attn_one, feed_one, channels, False,
-        queue,
+    grad_middle, gains_one, taps_one = layer_backward(
+        kept_one, cotangent * mask, small_one[:2], own_taps(small_one), weights_one, False, queue, tail
     )
     grad_middle = grad_middle.astype(jnp.bfloat16).astype(jnp.float32)
-    grad_start, grads_zero, gains_zero, taps_zero = layer_backward(
-        kept_zero, grad_middle, small_zero[:2], own_taps(small_zero), attn_zero, feed_zero, channels, True,
-        queue,
-    )
+    grad_start, gains_zero, taps_zero = layer_backward(
+        kept_zero, grad_middle, small_zero[:2], own_taps(small_zero), weights_zero, True, queue, tail
+    )
+
+    grads_one, grads_zero = queue.done[:2], queue.done[2:]
 
     def own_small(gains, taps):
         spot = jnp.zeros((taps.shape[0], model), jnp.float32)
@@ -328,14 +359,14 @@
             [halves(low[:, :size], high[:, :size], 1), halves(low[:, size:], high[:, size:], 1)], axis=1
         )
 
-    def split_pair(grads):
-        out = (channels + LANES - 1) // LANES * LANES
+    def split_pair(grads, tail):
         both = 2 * channels
-        width = grads.shape[1] - out
-        return (jnp.concatenate([grads[:, :both], grads[:, width:]], axis=1), grads[:, both:width])
-
-    attn_zero, pair_zero = split_pair(grads_zero[1])
-    attn_one, pair_one = split_pair(grads_one[1])
+        stop = grads.shape[1] - tail
+        rest = jnp.concatenate([grads[:, :both], grads[:, stop - channels : stop]], axis=1)
+        return (rest, grads[:, both : stop - channels], grads[:, stop:])
+
+    attn_zero, pair_zero, down_zero = split_pair(grads_zero[1], tail)
+    attn_one, pair_one, down_one = split_pair(grads_one[1], tail)
     low, high = home(attn_zero, attn_one)
     vgate_grad = jnp.stack(
         [
@@ -344,17 +375,23 @@
         ],
         axis=1,
     )
-    out_grad = halves(low[:, 2 * channels : 3 * channels].T, high[:, 2 * channels : 3 * channels].T, 0)
+    out_grad = halves(low[:, 2 * channels :].T, high[:, 2 * channels :].T, 0)
+    low_tail, high_tail = home(down_zero, down_one)
+
+    def unpack(block, last):
+        wide = block[:, main:]
+        (gate, upper), (gate_rest, upper_rest) = gates(wide, units)
+        down = jnp.concatenate([block[:, :main], wide[:, 2 * units :], last], axis=1)
+        return (
+            jnp.concatenate([gate, gate_rest], axis=1),
+            jnp.concatenate([upper, upper_rest], axis=1),
+            down.T,
+        )
+
     low, high = home(grads_zero[0], grads_one[0])
-    wide = low.shape[1] // 3
-    gate_up_grad = jnp.stack(
-        [
-            halves(low[:, :units], high[:, :units], 1),
-            halves(low[:, wide : wide + units], high[:, wide : wide + units], 1),
-        ],
-        axis=1,
-    )
-    down_grad = halves(low[:, 2 * wide : 2 * wide + units].T, high[:, 2 * wide : 2 * wide + units].T, 0)
+    low, high = unpack(low, low_tail), unpack(high, high_tail)
+    gate_up_grad = jnp.stack([halves(low[0], high[0], 1), halves(low[1], high[1], 1)], axis=1)
+    down_grad = halves(low[2], high[2], 0)
     return (
         ends[None],
         sums[:, :2],

time: 841 us -> 822 us (0.977)
  local copies, waits for them, and re-layouts: 91.4 us -> 122 us
  waiting for transfers between devices: 397 us -> 379 us
  matrix products: 97.4 us -> 85.8 us
  blocking collectives: 125 us -> 114 us
    reduce_scatter x4, waiting for transfers between devices: 117 us -> 94.9 us  [scatter(): lax.psum_scatter(block, 'dp', scatter_dimension=0, tiled=True)]
    concatenate x1 -> x6, local copies, waits for them, and re-layouts: 3.08 us -> 21.3 us  [the longest x1 7.07 us: scatter(): block = by_rows(jnp.concatenate(grads, axis=1))]
    slice x8 -> x30, local copies, waits for them, and re-layouts: 2.49 us -> 18.3 us  [the longest x2 3.61 us: parts_of(): feed[:, :main]]
    all_gather x8, blocking collectives: 125 us -> 114 us  [spread(): lax.all_gather(rows.astype(jnp.bfloat16), 'tensor', axis=0, tiled=True)]
    concatenate x9 -> x7, other arithmetic: 21.4 us -> 10.6 us  [the longest x3 8.18 us: scatter(): block = by_rows(jnp.concatenate(grads, axis=1))]
    ppermute x25 -> x26, waiting for transfers between devices: 21.9 us -> 19.6 us  [swap(): return lax.ppermute(block, 'section', [(0, 1), (1, 0)])]
    unnamed x196 -> x258, local copies, waits for them, and re-layouts: 34.7 us -> 36.9 us
  transfers between devices with their start and end apart: 62 -> 63, of which waited for: 42 -> 41; matrix products, arithmetic and copies ran while one was open for 25% -> 26% of each run, Pallas kernels for 0% -> 0%
where the time goes in v3:
time: 822 us; the launch traced here: 812 us
  waiting for transfers between devices  379 us (46%)
  local copies, waits for them, and re-layouts  122 us (15%)
  blocking collectives  114 us (14%)
  matrix products  85.8 us (10%)
  other arithmetic  56.8 us (7%)
  starting transfers between devices  37.1 us (5%)
  between operations  17.3 us (2%)
    all_gather x4, waiting for transfers between devices, fetch(): return lax.all_gather(piece, 'dp', axis=0, tiled=True)  172 us
    all_gather x8, blocking collectives, spread(): lax.all_gather(rows.astype(jnp.bfloat16), 'tensor', axis=0, tiled=True)  114 us
    reduce_scatter x4, waiting for transfers between devices, scatter(): lax.psum_scatter(block, 'dp', scatter_dimension=0, tiled=True)  94.9 us
    ppermute x24, waiting for transfers between devices, collect(): total = total + lax.ppermute(block, 'tensor', pairs).astype(jnp.float32)  70.4 us
    unnamed x258, local copies, waits for them, and re-layouts  36.9 us
    ppermute x24, starting transfers between devices, collect(): total = total + lax.ppermute(block, 'tensor', pairs).astype(jnp.float32)  26.5 us
    dot_general x8, matrix products, dot(): return jnp.dot(one, two, preferred_element_type=jnp.float32)  25.9 us
    dot_general x8, matrix products, dot_tn(): lax.dot_general(one, two, (((0,), (0,)), ((), ())), preferred_element_typ...  25 us
  transfers between devices with their start and end apart: 63, of which 41 were waited for; matrix products, arithmetic and copies ran while one was open for 26% of the time, Pallas kernels for 0%

profile of v3, /device:TPU:0, one launch (start us, length us, event | category | flops | bytes accessed | tf_op | source)
XLA Modules:
  0.0 811.8 jit_solution(14838328273923052456)
XLA Ops:
  18.4 6.0 constant_dynamic-slice_fusion.26
  26.2 3.6 concatenate.268
  33.6 3.3 broadcast_select_fusion.4
  40.9 14.7 %all_gather.36 = bf16[256,1792]{1,0:T(8,128)(2,1)S(1)} all-gather(bf16[64,1792]{1,0:T(8,128)(2,1)S(1)} %fusion.54), channel_id=1, replica_groups=mesh['section'=2,'dp'=4,'tensor'=4] {'tensor'}, dimensions={0}, use_global_device_ids=true | all-gather | bytes 1146880 | tf_op jit(solution)/shard_map/all_gather | solution.py:56
  59.1 17.4 %all-gather.5.cloned.1.call-done = bf16[1792,768]{1,0:T(8,128)(2,1)} async-done(((bf16[448,768]{1,0:T(8,128)(2,1)}), bf16[1792,768]{1,0:T(8,128)(2,1)}) %all-gather.5.cloned.1.call-update) | async-done | bytes 2752528 | tf_op jit(solution)/shard_map/all_gather | solution.py:278
  76.5 3.2 fusion.123
  98.7 5.2 collective-permute-done.5
  103.9 4.9 collective-permute-done.7
  112.0 13.2 %all_gather.38 = bf16[256,1792]{1,0:T(8,128)(2,1)S(1)} all-gather(bf16[64,1792]{1,0:T(8,128)(2,1)S(1)} %multiply_convert_fusion.14), channel_id=1, replica_groups=mesh['section'=2,'dp'=4,'tensor'=4] {'tensor'}, dimensions={0}, use_global_device_ids=true | all-gather | bytes 1146880 | tf_op jit(solution)/shard_map/all_gather | solution.py:56
  127.7 67.1 %all-gather.7.cloned.1.call-done = bf16[1792,1792]{1,0:T(8,128)(2,1)} async-done(((bf16[448,1792]{1,0:T(8,128)(2,1)}), bf16[1792,1792]{1,0:T(8,128)(2,1)}) %all-gather.7.cloned.1.call-update) | async-done | bytes 6422544 | tf_op jit(solution)/shard_map/all_gather | solution.py:278
  197.9 5.5 fusion.7
  215.3 5.0 collective-permute-done.11
  220.2 5.1 collective-permute-done.13
  227.1 12.8 %all_gather.40 = bf16[256,1792]{1,0:T(8,128)(2,1)S(1)} all-gather(bf16[64,1792]{1,0:T(8,128)(2,1)S(1)} %fusion.61), channel_id=1, replica_groups=mesh['section'=2,'dp'=4,'tensor'=4] {'tensor'}, dimensions={0}, use_global_device_ids=true | all-gather | bytes 1146880 | tf_op jit(solution)/shard_map/all_gather | solution.py:56
  243.4 31.6 %all-gather.9.cloned.1.call-done = bf16[1792,1152]{1,0:T(8,128)(2,1)} async-done(((bf16[448,1152]{1,0:T(8,128)(2,1)}), bf16[1792,1152]{1,0:T(8,128)(2,1)}) %all-gather.9.cloned.1.call-update) | async-done | bytes 4128784 | tf_op jit(solution)/shard_map/all_gather | solution.py:278
  275.0 5.7 fusion.124
  299.0 20.0 %all_gather.42 = bf16[256,1792]{1,0:T(8,128)(2,1)S(1)} all-gather(bf16[64,1792]{1,0:T(8,128)(2,1)S(1)} %copy-done.44), channel_id=1, replica_groups=mesh['section'=2,'dp'=4,'tensor'=4] {'tensor'}, dimensions={0}, use_global_device_ids=true | all-gather | bytes 1146880 | tf_op jit(solution)/shard_map/all_gather | solution.py:56
  319.4 14.1 %all_gather.43 = bf16[256,1792]{1,0:T(8,128)(2,1)} all-gather(bf16[64,1792]{1,0:T(8,128)(2,1)S(1)} %multiply_convert_fusion.12), channel_id=1, replica_groups=mesh['section'=2,'dp'=4,'tensor'=4] {'tensor'}, dimensions={0}, use_global_device_ids=true | all-gather | bytes 1146880 | tf_op jit(solution)/shard_map/all_gather | solution.py:56
  336.1 56.3 %all-gather.11.cloned.1.call-done = bf16[1792,1792]{1,0:T(8,128)(2,1)} async-done(((bf16[448,1792]{1,0:T(8,128)(2,1)}), bf16[1792,1792]{1,0:T(8,128)(2,1)}) %all-gather.11.cloned.1.call-update) | async-done | bytes 6422544 | tf_op jit(solution)/shard_map/all_gather | solution.py:278
  408.9 3.2 concatenate.277
  412.1 4.5 convolution_convert_fusion.1
  421.5 5.3 fusion.1
  433.3 5.0 collective-permute-done.22
  438.3 5.1 collective-permute-done.24
  446.1 13.0 %all_gather.45 = bf16[256,1792]{1,0:T(8,128)(2,1)} all-gather(bf16[64,1792]{1,0:T(8,128)(2,1)S(1)} %get-tuple-element.114), channel_id=1, replica_groups=mesh['section'=2,'dp'=4,'tensor'=4] {'tensor'}, dimensions={0}, use_global_device_ids=true | all-gather | bytes 1146880 | tf_op jit(solution)/shard_map/all_gather | solution.py:56
  478.6 5.4 convolution_convert_fusion.2
  484.0 7.1 concatenate.288
  491.1 41.4 %reduce-scatter.5.cloned.1.call-done = bf16[448,1792]{1,0:T(8,128)(2,1)} async-done(((bf16[1792,1792]{1,0:T(8,128)(2,1)}), bf16[448,1792]{1,0:T(8,128)(2,1)}) %reduce-scatter.5.cloned.1.call-update) | async-done | bytes 1605648 | tf_op jit(solution)/shard_map/reduce_scatter | solution.py:233
  533.0 4.0 fusion.9
  543.5 5.0 collective-permute-done.27
  548.5 5.1 collective-permute-done.29
  555.5 12.8 %all_gather.46 = bf16[256,1792]{1,0:T(8,128)(2,1)S(1)} all-gather(bf16[64,1792]{1,0:T(8,128)(2,1)S(1)} %fusion.66), channel_id=1, replica_groups=mesh['section'=2,'dp'=4,'tensor'=4] {'tensor'}, dimensions={0}, use_global_device_ids=true | all-gather | bytes 1146880 | tf_op jit(solution)/shard_map/all_gather | solution.py:56
  580.0 3.3 concatenate.281
  583.2 4.5 convolution_convert_fusion
  591.4 20.2 %reduce-scatter.7.cloned.1.call-done = bf16[448,1152]{1,0:T(8,128)(2,1)} async-done(((bf16[1792,1152]{1,0:T(8,128)(2,1)}), bf16[448,1152]{1,0:T(8,128)(2,1)}) %reduce-scatter.7.cloned.1.call-update) | async-done | bytes 1032208 | tf_op jit(solution)/shard_map/reduce_scatter | solution.py:233
  611.8 4.9 fusion.5
  623.2 5.0 collective-permute-done.32
  628.1 5.1 collective-permute-done.34
  635.1 12.9 %all_gather.47 = bf16[256,1792]{1,0:T(8,128)(2,1)S(1)} all-gather(bf16[64,1792]{1,0:T(8,128)(2,1)S(1)} %get-tuple-element.106), channel_id=1, replica_groups=mesh['section'=2,'dp'=4,'tensor'=4] {'tensor'}, dimensions={0}, use_global_device_ids=true | all-gather | bytes 1146880 | tf_op jit(solution)/shard_map/all_gather | solution.py:56
  649.1 3.6 fusion.40
  664.1 4.1 convolution_convert_fusion.5
  686.8 5.9 collective-permute-done.37
  692.7 4.3 collective-permute-done.39
  704.1 23.2 %reduce-scatter.9.cloned.1.call-done = bf16[448,1792]{1,0:T(8,128)(2,1)} async-done(((bf16[1792,1792]{1,0:T(8,128)(2,1)}), bf16[448,1792]{1,0:T(8,128)(2,1)}) %reduce-scatter.9.cloned.1.call-update) | async-done | bytes 1605648 | tf_op jit(solution)/shard_map/reduce_scatter | solution.py:233
  738.0 7.0 collective-permute-done.48
  745.9 9.9 %collective-permute-done.49 = f32[2,5,1792]{2,0,1:T(2,128)S(1)} collective-permute-done((f32[2,5,1792]{2,0,1:T(2,128)S(1)}, f32[2,5,1792]{2,0,1:T(2,128)S(1)}, u32[]{:S(2)}, u32[]{:S(2)}) %collective-permute-start.49) | collective-permute-done | bytes 71712 | tf_op jit(solution)/shard_map/ppermute | solution.py:82
  770.8 5.7 copy.266
  776.5 10.1 %reduce-scatter.11.cloned.1.call-done = bf16[448,768]{1,0:T(8,128)(2,1)} async-done(((bf16[1792,768]{1,0:T(8,128)(2,1)}), bf16[448,768]{1,0:T(8,128)(2,1)}) %reduce-scatter.11.cloned.1.call-update) | async-done | bytes 688144 | tf_op jit(solution)/shard_map/reduce_scatter | solution.py:233
  (620 shorter events, 253.2 us)
Async XLA Ops:
  7.2 69.3 %all-gather.5.cloned.1.call-start = ((), (), s32[]{:S(2)}) async-start(), calls=%async_computation.4 | async-start | bytes 3440640 | tf_op jit(solution)/shard_map/all_gather | solution.py:278
  16.7 178.2 %all-gather.7.cloned.1.call-start = ((), (), s32[]{:S(2)}) async-start(), calls=%async_computation.5 | async-start | bytes 8028160 | tf_op jit(solution)/shard_map/all_gather | solution.py:278
  36.9 238.0 %all-gather.9.cloned.1.call-start = ((), (), s32[]{:S(2)}) async-start(), calls=%async_computation.6 | async-start | bytes 5160960 | tf_op jit(solution)/shard_map/all_gather | solution.py:278
  87.9 4.5 collective-permute-start.4
  92.3 300.1 %all-gather.11.cloned.1.call-start = ((), (), s32[]{:S(2)}) async-start(), calls=%async_computation.7 | async-start | bytes 8028160 | tf_op jit(solution)/shard_map/all_gather | solution.py:278
  95.2 8.7 %collective-permute-start.5 = (bf16[64,1792]{1,0:T(8,128)(2,1)}, bf16[64,1792]{1,0:T(8,128)(2,1)S(1)}, u32[]{:S(2)}, u32[]{:S(2)}) collective-permute-start(bf16[64,1792]{1,0:T(8,128)(2,1)} %get-tuple-element.211), channel_id=1, source_target_pairs={{0,1},{1,0},{2,3},{3,2},{4,5},{5,4},{6,7},{7,6},{8,9},{9,8},{10,11... | collective-permute-start | bytes 688136 | tf_op jit(solution)/shard_map/ppermute | solution.py:72
  96.6 12.2 %collective-permute-start.7 = (bf16[64,1792]{1,0:T(8,128)(2,1)}, bf16[64,1792]{1,0:T(8,128)(2,1)S(1)}, u32[]{:S(2)}, u32[]{:S(2)}) collective-permute-start(bf16[64,1792]{1,0:T(8,128)(2,1)} %get-tuple-element.212), channel_id=1, source_target_pairs={{0,3},{1,2},{2,1},{3,0},{4,7},{5,6},{6,5},{7,4},{8,11},{9,10},{10,... | collective-permute-start | bytes 688136 | tf_op jit(solution)/shard_map/ppermute | solution.py:72
  98.1 11.8 %collective-permute-start.6 = (bf16[64,1792]{1,0:T(8,128)(2,1)S(1)}, bf16[64,1792]{1,0:T(8,128)(2,1)S(1)}, u32[]{:S(2)}, u32[]{:S(2)}) collective-permute-start(bf16[64,1792]{1,0:T(8,128)(2,1)S(1)} %get-tuple-element.213), channel_id=1, source_target_pairs={{0,2},{1,3},{2,0},{3,1},{4,6},{5,7},{6,4},{7,5},{8,10},{9,11},{10,... | collective-permute-start | bytes 688136 | tf_op jit(solution)/shard_map/ppermute | solution.py:72
  207.5 324.9 %reduce-scatter.5.cloned.1.call-start = ((), (), s32[]{:S(2)}) async-start(), calls=%async_computation.8 | async-start | bytes 8028160 | tf_op jit(solution)/shard_map/reduce_scatter | solution.py:233
  211.7 8.5 %collective-permute-start.11 = (bf16[64,1792]{1,0:T(8,128)(2,1)S(1)}, bf16[64,1792]{1,0:T(8,128)(2,1)S(1)}, u32[]{:S(2)}, u32[]{:S(2)}) collective-permute-start(bf16[64,1792]{1,0:T(8,128)(2,1)S(1)} %get-tuple-element.208), channel_id=1, source_target_pairs={{0,1},{1,0},{2,3},{3,2},{4,5},{5,4},{6,7},{7,6},{8,9},{9,8},{10,11... | collective-permute-start | bytes 688136 | tf_op jit(solution)/shard_map/ppermute | solution.py:72
  213.2 12.1 %collective-permute-start.13 = (bf16[64,1792]{1,0:T(8,128)(2,1)S(1)}, bf16[64,1792]{1,0:T(8,128)(2,1)S(1)}, u32[]{:S(2)}, u32[]{:S(2)}) collective-permute-start(bf16[64,1792]{1,0:T(8,128)(2,1)S(1)} %get-tuple-element.209), channel_id=1, source_target_pairs={{0,3},{1,2},{2,1},{3,0},{4,7},{5,6},{6,5},{7,4},{8,11},{9,10},{10,... | collective-permute-start | bytes 688136 | tf_op jit(solution)/shard_map/ppermute | solution.py:72
  214.7 12.0 %collective-permute-start.12 = (bf16[64,1792]{1,0:T(8,128)(2,1)S(1)}, bf16[64,1792]{1,0:T(8,128)(2,1)S(1)}, u32[]{:S(2)}, u32[]{:S(2)}) collective-permute-start(bf16[64,1792]{1,0:T(8,128)(2,1)S(1)} %get-tuple-element.210), channel_id=1, source_target_pairs={{0,2},{1,3},{2,0},{3,1},{4,6},{5,7},{6,4},{7,5},{8,10},{9,11},{10,... | collective-permute-start | bytes 688136 | tf_op jit(solution)/shard_map/ppermute | solution.py:72
  295.4 23.5 %collective-permute-start.16 = (bf16[64,1792]{1,0:T(8,128)(2,1)S(1)}, bf16[64,1792]{1,0:T(8,128)(2,1)S(1)}, u32[]{:S(2)}, u32[]{:S(2)}) collective-permute-start(bf16[64,1792]{1,0:T(8,128)(2,1)S(1)} %get-tuple-element.201), channel_id=1, source_target_pairs={{0,1},{1,0},{2,3},{3,2},{4,5},{5,4},{6,7},{7,6},{8,9},{9,8},{10,11... | collective-permute-start | bytes 688136 | tf_op jit(solution)/shard_map/ppermute | solution.py:72
  297.0 22.0 %collective-permute-start.18 = (bf16[64,1792]{1,0:T(8,128)(2,1)S(1)}, bf16[64,1792]{1,0:T(8,128)(2,1)S(1)}, u32[]{:S(2)}, u32[]{:S(2)}) collective-permute-start(bf16[64,1792]{1,0:T(8,128)(2,1)S(1)} %get-tuple-element.202), channel_id=1, source_target_pairs={{0,3},{1,2},{2,1},{3,0},{4,7},{5,6},{6,5},{7,4},{8,11},{9,10},{10,... | collective-permute-start | bytes 688136 | tf_op jit(solution)/shard_map/ppermute | solution.py:72
  298.5 20.5 %collective-permute-start.17 = (bf16[64,1792]{1,0:T(8,128)(2,1)S(1)}, bf16[64,1792]{1,0:T(8,128)(2,1)S(1)}, u32[]{:S(2)}, u32[]{:S(2)}) collective-permute-start(bf16[64,1792]{1,0:T(8,128)(2,1)S(1)} %get-tuple-element.203), channel_id=1, source_target_pairs={{0,2},{1,3},{2,0},{3,1},{4,6},{5,7},{6,4},{7,5},{8,10},{9,11},{10,... | collective-permute-start | bytes 688136 | tf_op jit(solution)/shard_map/ppermute | solution.py:72
  318.9 14.6 %collective-permute-start.19 = (bf16[256,1792]{1,0:T(8,128)(2,1)S(1)}, bf16[256,1792]{1,0:T(8,128)(2,1)S(1)}, u32[]{:S(2)}, u32[]{:S(2)}) collective-permute-start(bf16[256,1792]{1,0:T(8,128)(2,1)S(1)} %all_gather.42), channel_id=1, source_target_pairs={{0,16},{16,0},{1,17},{17,1},{2,18},{18,2},{3,19},{19,3},{4,20},{20... | collective-permute-start | bytes 2752520 | tf_op jit(solution)/shard_map/ppermute | solution.py:52
  333.5 64.4 %collective-permute-start.20 = (bf16[256,1792]{1,0:T(8,128)(2,1)}, bf16[256,1792]{1,0:T(8,128)(2,1)}, u32[]{:S(2)}, u32[]{:S(2)}) collective-permute-start(bf16[256,1792]{1,0:T(8,128)(2,1)} %all_gather.43), channel_id=1, source_target_pairs={{0,16},{16,0},{1,17},{17,1},{2,18},{18,2},{3,19},{19,3},{4,20},{20... | collective-permute-start | bytes 2752520 | tf_op jit(solution)/shard_map/ppermute | solution.py:52
  421.2 190.3 %reduce-scatter.7.cloned.1.call-start = ((), (), s32[]{:S(2)}) async-start(), calls=%async_computation.9 | async-start | bytes 5160960 | tf_op jit(solution)/shard_map/reduce_scatter | solution.py:233
  429.7 8.5 %collective-permute-start.22 = (bf16[64,1792]{1,0:T(8,128)(2,1)S(1)}, bf16[64,1792]{1,0:T(8,128)(2,1)S(1)}, u32[]{:S(2)}, u32[]{:S(2)}) collective-permute-start(bf16[64,1792]{1,0:T(8,128)(2,1)S(1)} %get-tuple-element.198), channel_id=1, source_target_pairs={{0,1},{1,0},{2,3},{3,2},{4,5},{5,4},{6,7},{7,6},{8,9},{9,8},{10,11... | collective-permute-start | bytes 688136 | tf_op jit(solution)/shard_map/ppermute | solution.py:72
  431.3 12.1 %collective-permute-start.24 = (bf16[64,1792]{1,0:T(8,128)(2,1)S(1)}, bf16[64,1792]{1,0:T(8,128)(2,1)S(1)}, u32[]{:S(2)}, u32[]{:S(2)}) collective-permute-start(bf16[64,1792]{1,0:T(8,128)(2,1)S(1)} %get-tuple-element.199), channel_id=1, source_target_pairs={{0,3},{1,2},{2,1},{3,0},{4,7},{5,6},{6,5},{7,4},{8,11},{9,10},{10,... | collective-permute-start | bytes 688136 | tf_op jit(solution)/shard_map/ppermute | solution.py:72
  432.7 12.0 %collective-permute-start.23 = (bf16[64,1792]{1,0:T(8,128)(2,1)S(1)}, bf16[64,1792]{1,0:T(8,128)(2,1)S(1)}, u32[]{:S(2)}, u32[]{:S(2)}) collective-permute-start(bf16[64,1792]{1,0:T(8,128)(2,1)S(1)} %get-tuple-element.200), channel_id=1, source_target_pairs={{0,2},{1,3},{2,0},{3,1},{4,6},{5,7},{6,4},{7,5},{8,10},{9,11},{10,... | collective-permute-start | bytes 688136 | tf_op jit(solution)/shard_map/ppermute | solution.py:72
  459.1 5.7 collective-permute-start.25
  532.5 194.8 %reduce-scatter.9.cloned.1.call-start = ((), (), s32[]{:S(2)}) async-start(), calls=%async_computation.10 | async-start | bytes 8028160 | tf_op jit(solution)/shard_map/reduce_scatter | solution.py:233
  540.0 8.5 %collective-permute-start.27 = (bf16[64,1792]{1,0:T(8,128)(2,1)S(1)}, bf16[64,1792]{1,0:T(8,128)(2,1)S(1)}, u32[]{:S(2)}, u32[]{:S(2)}) collective-permute-start(bf16[64,1792]{1,0:T(8,128)(2,1)S(1)} %get-tuple-element.193), channel_id=1, source_target_pairs={{0,1},{1,0},{2,3},{3,2},{4,5},{5,4},{6,7},{7,6},{8,9},{9,8},{10,11... | collective-permute-start | bytes 688136 | tf_op jit(solution)/shard_map/ppermute | solution.py:72
  541.5 12.1 %collective-permute-start.29 = (bf16[64,1792]{1,0:T(8,128)(2,1)S(1)}, bf16[64,1792]{1,0:T(8,128)(2,1)S(1)}, u32[]{:S(2)}, u32[]{:S(2)}) collective-permute-start(bf16[64,1792]{1,0:T(8,128)(2,1)S(1)} %get-tuple-element.194), channel_id=1, source_target_pairs={{0,3},{1,2},{2,1},{3,0},{4,7},{5,6},{6,5},{7,4},{8,11},{9,10},{10,... | collective-permute-start | bytes 688136 | tf_op jit(solution)/shard_map/ppermute | solution.py:72
  543.0 12.0 %collective-permute-start.28 = (bf16[64,1792]{1,0:T(8,128)(2,1)S(1)}, bf16[64,1792]{1,0:T(8,128)(2,1)S(1)}, u32[]{:S(2)}, u32[]{:S(2)}) collective-permute-start(bf16[64,1792]{1,0:T(8,128)(2,1)S(1)} %get-tuple-element.195), channel_id=1, source_target_pairs={{0,2},{1,3},{2,0},{3,1},{4,6},{5,7},{6,4},{7,5},{8,10},{9,11},{10,... | collective-permute-start | bytes 688136 | tf_op jit(solution)/shard_map/ppermute | solution.py:72
  611.6 175.1 %reduce-scatter.11.cloned.1.call-start = ((), (), s32[]{:S(2)}) async-start(), calls=%async_computation.11 | async-start | bytes 3440640 | tf_op jit(solution)/shard_map/reduce_scatter | solution.py:233
  619.6 8.5 %collective-permute-start.32 = (bf16[64,1792]{1,0:T(8,128)(2,1)S(1)}, bf16[64,1792]{1,0:T(8,128)(2,1)S(1)}, u32[]{:S(2)}, u32[]{:S(2)}) collective-permute-start(bf16[64,1792]{1,0:T(8,128)(2,1)S(1)} %get-tuple-element.190), channel_id=1, source_target_pairs={{0,1},{1,0},{2,3},{3,2},{4,5},{5,4},{6,7},{7,6},{8,9},{9,8},{10,11... | collective-permute-start | bytes 688136 | tf_op jit(solution)/shard_map/ppermute | solution.py:72
  621.1 12.1 %collective-permute-start.34 = (bf16[64,1792]{1,0:T(8,128)(2,1)S(1)}, bf16[64,1792]{1,0:T(8,128)(2,1)S(1)}, u32[]{:S(2)}, u32[]{:S(2)}) collective-permute-start(bf16[64,1792]{1,0:T(8,128)(2,1)S(1)} %get-tuple-element.191), channel_id=1, source_target_pairs={{0,3},{1,2},{2,1},{3,0},{4,7},{5,6},{6,5},{7,4},{8,11},{9,10},{10,... | collective-permute-start | bytes 688136 | tf_op jit(solution)/shard_map/ppermute | solution.py:72
  622.6 12.0 %collective-permute-start.33 = (bf16[64,1792]{1,0:T(8,128)(2,1)S(1)}, bf16[64,1792]{1,0:T(8,128)(2,1)S(1)}, u32[]{:S(2)}, u32[]{:S(2)}) collective-permute-start(bf16[64,1792]{1,0:T(8,128)(2,1)S(1)} %get-tuple-element.192), channel_id=1, source_target_pairs={{0,2},{1,3},{2,0},{3,1},{4,6},{5,7},{6,4},{7,5},{8,10},{9,11},{10,... | collective-permute-start | bytes 688136 | tf_op jit(solution)/shard_map/ppermute | solution.py:72
  648.1 6.2 collective-permute-start.35
  653.9 16.1 %collective-permute-start.40 = (bf16[256,1792]{1,0:T(8,128)(2,1)}, bf16[256,1792]{1,0:T(8,128)(2,1)}, u32[]{:S(2)}, u32[]{:S(2)}) collective-permute-start(bf16[256,1792]{1,0:T(8,128)(2,1)} %slice.874), channel_id=1, source_target_pairs={{0,16},{16,0},{1,17},{17,1},{2,18},{18,2},{3,19},{19,3},{4,20},{20... | collective-permute-start | bytes 2752520 | tf_op jit(solution)/shard_map/ppermute | solution.py:52
  669.5 8.3 %collective-permute-start.36 = (bf16[256,1792]{1,0:T(8,128)(2,1)S(1)}, bf16[256,1792]{1,0:T(8,128)(2,1)S(1)}, u32[]{:S(2)}, u32[]{:S(2)}) collective-permute-start(bf16[256,1792]{1,0:T(8,128)(2,1)S(1)} %slice.875), channel_id=1, source_target_pairs={{0,16},{16,0},{1,17},{17,1},{2,18},{18,2},{3,19},{19,3},{4,20},{20... | collective-permute-start | bytes 2752520 | tf_op jit(solution)/shard_map/ppermute | solution.py:52
  674.2 24.5 %collective-permute-start.41 = (bf16[64,1792]{1,0:T(8,128)(2,1)}, bf16[64,1792]{1,0:T(8,128)(2,1)}, u32[]{:S(2)}, u32[]{:S(2)}) collective-permute-start(bf16[64,1792]{1,0:T(8,128)(2,1)} %get-tuple-element.184), channel_id=1, source_target_pairs={{0,1},{1,0},{2,3},{3,2},{4,5},{5,4},{6,7},{7,6},{8,9},{9,8},{10,11... | collective-permute-start | bytes 688136 | tf_op jit(solution)/shard_map/ppermute | solution.py:72
  674.2 24.5 %collective-permute-start.43 = (bf16[64,1792]{1,0:T(8,128)(2,1)}, bf16[64,1792]{1,0:T(8,128)(2,1)}, u32[]{:S(2)}, u32[]{:S(2)}) collective-permute-start(bf16[64,1792]{1,0:T(8,128)(2,1)} %get-tuple-element.185), channel_id=1, source_target_pairs={{0,3},{1,2},{2,1},{3,0},{4,7},{5,6},{6,5},{7,4},{8,11},{9,10},{10,... | collective-permute-start | bytes 688136 | tf_op jit(solution)/shard_map/ppermute | solution.py:72
  681.0 11.6 %collective-permute-start.37 = (bf16[64,1792]{1,0:T(8,128)(2,1)S(1)}, bf16[64,1792]{1,0:T(8,128)(2,1)S(1)}, u32[]{:S(2)}, u32[]{:S(2)}) collective-permute-start(bf16[64,1792]{1,0:T(8,128)(2,1)S(1)} %get-tuple-element.187), channel_id=1, source_target_pairs={{0,1},{1,0},{2,3},{3,2},{4,5},{5,4},{6,7},{7,6},{8,9},{9,8},{10,11... | collective-permute-start | bytes 688136 | tf_op jit(solution)/shard_map/ppermute | solution.py:72
  683.2 13.7 %collective-permute-start.39 = (bf16[64,1792]{1,0:T(8,128)(2,1)S(1)}, bf16[64,1792]{1,0:T(8,128)(2,1)S(1)}, u32[]{:S(2)}, u32[]{:S(2)}) collective-permute-start(bf16[64,1792]{1,0:T(8,128)(2,1)S(1)} %get-tuple-element.188), channel_id=1, source_target_pairs={{0,3},{1,2},{2,1},{3,0},{4,7},{5,6},{6,5},{7,4},{8,11},{9,10},{10,... | collective-permute-start | bytes 688136 | tf_op jit(solution)/shard_map/ppermute | solution.py:72
  684.6 12.4 %collective-permute-start.38 = (bf16[64,1792]{1,0:T(8,128)(2,1)S(1)}, bf16[64,1792]{1,0:T(8,128)(2,1)S(1)}, u32[]{:S(2)}, u32[]{:S(2)}) collective-permute-start(bf16[64,1792]{1,0:T(8,128)(2,1)S(1)} %get-tuple-element.189), channel_id=1, source_target_pairs={{0,2},{1,3},{2,0},{3,1},{4,6},{5,7},{6,4},{7,5},{8,10},{9,11},{10,... | collective-permute-start | bytes 688136 | tf_op jit(solution)/shard_map/ppermute | solution.py:72
  692.6 9.2 %collective-permute-start.42 = (bf16[64,1792]{1,0:T(8,128)(2,1)}, bf16[64,1792]{1,0:T(8,128)(2,1)S(1)}, u32[]{:S(2)}, u32[]{:S(2)}) collective-permute-start(bf16[64,1792]{1,0:T(8,128)(2,1)} %get-tuple-element.186), channel_id=1, source_target_pairs={{0,2},{1,3},{2,0},{3,1},{4,6},{5,7},{6,4},{7,5},{8,10},{9,11},{10,... | collective-permute-start | bytes 688136 | tf_op jit(solution)/shard_map/ppermute | solution.py:72
  698.5 28.8 %collective-permute-start.45 = (f32[2,5,1792]{2,0,1:T(2,128)S(1)}, f32[2,5,1792]{2,0,1:T(2,128)S(1)}, u32[]{:S(2)}, u32[]{:S(2)}) collective-permute-start(f32[2,5,1792]{2,0,1:T(2,128)S(1)} %pad_maximum_fusion.22), channel_id=1, source_target_pairs={{0,16},{16,0},{1,17},{17,1},{2,18},{18,2},{3,19},{19,3},{4,20},{20... | collective-permute-start | bytes 215048 | tf_op jit(solution)/shard_map/ppermute | solution.py:82
  727.5 4.4 collective-permute-start.46
  729.2 27.9 %collective-permute-start.44 = (f32[64,1792]{1,0:T(8,128)S(1)}, f32[64,1792]{1,0:T(8,128)S(1)}, u32[]{:S(2)}, u32[]{:S(2)}) collective-permute-start(f32[64,1792]{1,0:T(8,128)S(1)} %broadcast_select_fusion.14), channel_id=1, source_target_pairs={{0,16},{16,0},{1,17},{17,1},{2,18},{18,2},{3,19},{19,3},{4,20},{20... | collective-permute-start | bytes 1376264 | tf_op jit(solution)/shard_map/ppermute | solution.py:52
  733.8 27.9 %collective-permute-start.53 = (bf16[448,1792]{1,0:T(8,128)(2,1)S(1)}, bf16[448,1792]{1,0:T(8,128)(2,1)S(1)}, u32[]{:S(2)}, u32[]{:S(2)}) collective-permute-start(bf16[448,1792]{1,0:T(8,128)(2,1)S(1)} %broadcast_select_fusion.2), channel_id=1, source_target_pairs={{0,16},{16,0},{1,17},{17,1},{2,18},{18,2},{3,19},{19,3},{4,20},{20... | collective-permute-start | bytes 4816904 | tf_op jit(solution)/shard_map/ppermute | solution.py:52
  736.4 8.5 %collective-permute-start.48 = (f32[2,5,1792]{2,0,1:T(2,128)S(1)}, f32[2,5,1792]{2,0,1:T(2,128)S(1)}, u32[]{:S(2)}, u32[]{:S(2)}) collective-permute-start(f32[2,5,1792]{2,0,1:T(2,128)S(1)} %add.461), channel_id=1, source_target_pairs={{0,4},{4,0},{8,12},{12,8},{1,5},{5,1},{9,13},{13,9},{2,6},{6,2},{1... | collective-permute-start | bytes 215048 | tf_op jit(solution)/shard_map/ppermute | solution.py:82
  745.0 10.8 %collective-permute-start.49 = (f32[2,5,1792]{2,0,1:T(2,128)S(1)}, f32[2,5,1792]{2,0,1:T(2,128)S(1)}, u32[]{:S(2)}, u32[]{:S(2)}) collective-permute-start(f32[2,5,1792]{2,0,1:T(2,128)S(1)} %add.462), channel_id=1, source_target_pairs={{0,8},{4,12},{8,0},{12,4},{1,9},{5,13},{9,1},{13,5},{2,10},{6,14},... | collective-permute-start | bytes 215048 | tf_op jit(solution)/shard_map/ppermute | solution.py:82
  745.9 12.3 %collective-permute-start.51 = (bf16[448,448]{1,0:T(8,128)(2,1)S(1)}, bf16[448,448]{1,0:T(8,128)(2,1)S(1)}, u32[]{:S(2)}, u32[]{:S(2)}) collective-permute-start(bf16[448,448]{1,0:T(8,128)(2,1)S(1)} %slice.583), channel_id=1, source_target_pairs={{0,16},{16,0},{1,17},{17,1},{2,18},{18,2},{3,19},{19,3},{4,20},{20... | collective-permute-start | bytes 1204232 | tf_op jit(solution)/shard_map/ppermute | solution.py:52
  787.7 8.1 collective-permute-start.50
  792.7 5.3 collective-permute-start.52
  (134 other events, 1055.7 us)
Sparse Core Ops, SparseCore 0:
  16.8 59.5 all-gather.4
  78.6 116.2 all-gather.6
  197.0 77.8 all-gather.8
  276.4 116.0 all-gather.10
  421.4 111.0 reduce-scatter.4
  535.2 76.2 reduce-scatter.6
  614.0 113.3 reduce-scatter.8
  729.8 56.8 reduce-scatter.10

commit v4 on v3

--- a/solution.py
+++ b/solution.py
@@ -1,14 +1,18 @@
+import functools
 import math
 
 import jax
 import jax.numpy as jnp
 from jax import lax
+from jax.experimental import pallas as pl
 from jax.experimental.layout import Layout, with_layout_constraint
+from jax.experimental.pallas import tpu as pltpu
 from jax.sharding import PartitionSpec as P
 
 WIN = 64
 HD = 112
 LANES = 128
+WIDE = 256
 
 EPS = 1e-06
 
@@ -52,9 +56,13 @@
     return lax.ppermute(block, "section", [(0, 1), (1, 0)])
 
 
+def spread_pair(rows):
+    mine = lax.all_gather(rows.astype(jnp.bfloat16), "tensor", axis=0, tiled=True)
+    return (mine, swap(mine))
+
+
 def spread(rows):
-    mine = lax.all_gather(rows.astype(jnp.bfloat16), "tensor", axis=0, tiled=True)
-    return jnp.concatenate([mine, swap(mine)], axis=0)
+    return jnp.concatenate(spread_pair(rows), axis=0)
 
 
 def collect(terms):
@@ -131,15 +139,14 @@
     )
 
 
-def layer_forward(rows, gains, taps, weights, first):
+def attn_forward(rows, gain, taps, weights, first):
     mix, out_t, pair, down = weights
     channels = out_t.shape[1]
     width = mix.shape[1] // 2 - channels
-    units = down.shape[1]
-    scale_one, normed = rms_rows(rows, gains[0])
-    full_one = spread(normed)
-    both = dot(full_one, mix)
-    length = full_one.shape[0] // 2
+    scale, normed = rms_rows(rows, gain)
+    full = spread(normed)
+    both = dot(full, mix)
+    length = full.shape[0] // 2
     pre_values = both[:, :channels].reshape(2, length, channels)
     gate_mix = both[:, channels : 2 * channels]
     values = causal_conv(pre_values, taps).astype(jnp.bfloat16).reshape(2, length, -1, HD)
@@ -152,48 +159,148 @@
     ).reshape(2 * length, channels)
     gated = (mixed * jax.nn.silu(gate_mix)).astype(jnp.bfloat16)
     hidden = rows + collect(dot_nt(gated, out_t))
-    scale_two, normed_two = rms_rows(hidden, gains[1])
-    full_two = spread(normed_two)
-    halves = dot(full_two, pair)
+    kept = (
+        rows, scale, full, pre_values, gate_mix, values, queries, keys, probs, slope, mixed, gated,
+    )
+    return (hidden, kept)
+
+
+def feed_forward(hidden, gain, weights):
+    mix, out_t, pair, down = weights
+    scale, normed = rms_rows(hidden, gain)
+    full = spread(normed)
+    halves = dot(full, pair)
     inner = jnp.concatenate(
-        [(jax.nn.silu(gate) * upper).astype(jnp.bfloat16) for gate, upper in gates(halves, units)], axis=1
+        [(jax.nn.silu(gate) * upper).astype(jnp.bfloat16) for gate, upper in gates(halves, down.shape[1])],
+        axis=1,
     )
     output = hidden + collect(dot_nt(inner, down))
-    kept = (
-        rows, scale_one, full_one, pre_values, gate_mix, values, queries, keys, probs, slope,
-        mixed, gated, hidden, scale_two, full_two, halves, inner,
-    )
-    return (output, kept)
-
-
-def layer_backward(kept, grad_out, gains, taps, weights, first, queue, tail):
-    (
-        rows, scale_one, full_one, pre_values, gate_mix, values, queries, keys, probs, slope,
-        mixed, gated, hidden, scale_two, full_two, halves, inner,
-    ) = kept
+    return (output, (hidden, scale, full, halves, inner))
+
+
+def feed_backward(kept, grad_out, gain, weights, queue, tail):
+    hidden, scale, full, halves, inner = kept
     mix, out_t, pair, down = weights
-    channels = out_t.shape[1]
     units = down.shape[1]
     main = units // LANES * LANES
-    length = full_one.shape[0] // 2
-    branch_two = spread(grad_out)
-    branch_two, grad_down = product_first(branch_two, inner, branch_two)
-    grad_inner = dot(branch_two, down)
+    branch = spread(grad_out)
+    branch, grad_down = product_first(branch, inner, branch)
+    grad_inner = dot(branch, down)
     parts = []
     for (gate, upper), grad in zip(gates(halves, units), (grad_inner[:, :main], grad_inner[:, main:])):
         parts.append((grad * upper * silu_slope(gate)).astype(jnp.bfloat16))
         parts.append((grad * jax.nn.silu(gate)).astype(jnp.bfloat16))
-    filler = jnp.zeros((2 * length, pair.shape[1] - 2 * units), jnp.bfloat16)
+    filler = jnp.zeros((full.shape[0], pair.shape[1] - 2 * units), jnp.bfloat16)
     grad_halves = jnp.concatenate([*parts, filler], axis=1)
-    grad_halves, grad_gate_up = product_first(full_two, grad_halves, grad_halves)
+    grad_halves, grad_gate_up = product_first(full, grad_halves, grad_halves)
     rest = jnp.pad(grad_down[:, main : units - tail], ((0, 0), (2 * units, 0)))
     queue.scatter(grad_down[:, :main], grad_gate_up + rest)
-    grad_second = collect(dot_nt(grad_halves, pair))
-    back_two, gain_two = rms_back(hidden, scale_two, gains[1], grad_second)
-    grad_hidden = grad_out + back_two
-    branch_one = spread(grad_hidden)
-    branch_one, grad_outw = product_first(branch_one, gated, branch_one)
-    grad_gated = dot(branch_one, out_t)
+    grad = collect(dot_nt(grad_halves, pair))
+    back, grad_gain = rms_back(hidden, scale, gain, grad)
+    return (grad_out + back, grad_gain, grad_down[:, units - tail :])
+
+
+def feed_kernel(
+    units, tail, near_ref, far_ref, near_grad_ref, far_grad_ref, feed_ref, last_ref,
+    block_ref, rest_ref, halves_ref, inner_ref, rows_ref, grads_ref,
+):
+    main = units // LANES * LANES
+    over = units - main
+    length = near_ref.shape[0]
+    rows_ref[:length] = near_ref[...]
+    rows_ref[length:] = far_ref[...]
+    grads_ref[:length] = near_grad_ref[...]
+    grads_ref[length:] = far_grad_ref[...]
+    rows = rows_ref[...]
+    branch = grads_ref[...]
+
+    def lanes(block):
+        return lax.broadcasted_iota(jnp.int32, block.shape, 1)
+
+    def parts(gate, upper, grad):
+        sigma = jax.nn.sigmoid(gate)
+        act = gate * sigma
+        slope = sigma * (1.0 + gate * (1.0 - sigma))
+        return (act * upper, grad * upper * slope, grad * act)
+
+    for start in range(0, main, WIDE):
+        first, second, third = (pl.ds(start + i * main, WIDE) for i in range(3))
+        gate = dot(rows, feed_ref[:, second])
+        upper = dot(rows, feed_ref[:, third])
+        grad = dot(branch, feed_ref[:, first])
+        inner, grad_gate, grad_upper = (part.astype(jnp.bfloat16) for part in parts(gate, upper, grad))
+        inner_ref[:, first] = inner
+        halves_ref[:, first] = grad_gate
+        halves_ref[:, second] = grad_upper
+        block_ref[:, first] = dot_tn(branch, inner).astype(jnp.bfloat16)
+        block_ref[:, second] = dot_tn(rows, grad_gate).astype(jnp.bfloat16)
+        block_ref[:, third] = dot_tn(rows, grad_upper).astype(jnp.bfloat16)
+
+    ends = feed_ref[:, pl.ds(3 * main, WIDE)]
+    both = dot(rows, ends)
+    upper = pltpu.roll(both, WIDE - over, 1)
+    grad = pltpu.roll(dot(branch, ends), WIDE - 2 * over, 1)[:, :LANES]
+    more = pltpu.roll(dot(branch, last_ref[...]), over, 1)
+    grad = jnp.where(lanes(grad) < over - tail, grad, more)
+    inner, grad_gate, grad_upper = (
+        jnp.where(lanes(part) < over, part, 0.0)
+        for part in parts(both[:, :LANES], upper[:, :LANES], grad)
+    )
+    inner = inner.astype(jnp.bfloat16)
+    inner_ref[:, pl.ds(main, over)] = inner[:, :over]
+    empty = jnp.zeros_like(grad_gate)
+    wide = jnp.concatenate([grad_gate, empty], axis=1)
+    wide = wide + pltpu.roll(jnp.concatenate([grad_upper, empty], axis=1), over, 1)
+    wide = wide.astype(jnp.bfloat16)
+    halves_ref[:, pl.ds(2 * main, WIDE)] = wide
+    down = dot_tn(branch, inner)
+    moved = pltpu.roll(jnp.concatenate([down, jnp.zeros_like(down)], axis=1), 2 * over, 1)
+    wide = dot_tn(rows, wide)
+    block_ref[:, pl.ds(3 * main, WIDE)] = jnp.where(lanes(wide) < 2 * over, wide, moved).astype(jnp.bfloat16)
+    rest_ref[...] = pltpu.roll(down, LANES - over + tail, 1)[:, :tail].astype(jnp.bfloat16)
+
+
+def feed_both(units, tail, near, far, near_grad, far_grad, feed, attn):
+    count, model = 2 * near.shape[0], near.shape[1]
+    main = units // LANES * LANES
+    shapes = (
+        (model, feed.shape[1]),
+        (model, tail),
+        (count, feed.shape[1] - main),
+        (count, units),
+    )
+
+    def whole(shape):
+        return pl.BlockSpec(shape, lambda step: (0, 0))
+
+    end = attn.shape[1] // LANES - 1
+    return pl.pallas_call(
+        functools.partial(feed_kernel, units, tail),
+        grid=(1,),
+        out_shape=[jax.ShapeDtypeStruct(shape, jnp.bfloat16) for shape in shapes],
+        in_specs=[whole(block.shape) for block in (near, far, near_grad, far_grad, feed)]
+        + [pl.BlockSpec((model, LANES), lambda step: (0, end))],
+        out_specs=[whole(shape) for shape in shapes],
+        scratch_shapes=[pltpu.VMEM((count, model), jnp.bfloat16)] * 2,
+        compiler_params=pltpu.CompilerParams(vmem_limit_bytes=56 * 2**20),
+        cost_estimate=pl.CostEstimate(
+            flops=8 * count * model * feed.shape[1] // 2,
+            bytes_accessed=20 * 2**20,
+            transcendentals=count * units,
+        ),
+    )(near, far, near_grad, far_grad, feed, attn)
+
+
+def attn_backward(kept, grad_hidden, gain, taps, weights, queue, rest):
+    (
+        rows, scale, full, pre_values, gate_mix, values, queries, keys, probs, slope, mixed, gated,
+    ) = kept
+    mix, out_t, pair, down = weights
+    channels = out_t.shape[1]
+    length = full.shape[0] // 2
+    branch = spread(grad_hidden)
+    branch, grad_outw = product_first(branch, gated, branch)
+    grad_gated = dot(branch, out_t)
     grad_mixed = (grad_gated * jax.nn.silu(gate_mix)).astype(jnp.bfloat16)
     grad_mix_gate = (grad_gated * mixed * silu_slope(gate_mix)).astype(jnp.bfloat16)
     grad_heads = heads_of(grad_mixed, HD)
@@ -210,12 +317,11 @@
     grad_pre, grad_taps = conv_back(grad_values.reshape(2, length, channels), pre_values, taps)
     grad_pre = grad_pre.astype(jnp.bfloat16).reshape(2 * length, channels)
     grad_both = jnp.concatenate([grad_pre, grad_mix_gate, grad_queries, grad_keys], axis=1)
-    grad_both, grad_attn = product_first(full_one, grad_both, grad_both)
-    queue.scatter(grad_attn, grad_outw, grad_down[:, units - tail :])
-    grad_first = collect(dot_nt(grad_both, mix))
-    back_one, gain_one = rms_back(rows, scale_one, gains[0], grad_first)
-    grad_rows = grad_hidden + back_one
-    return (grad_rows, jnp.stack([gain_one, gain_two]), grad_taps)
+    grad_both, grad_attn = product_first(full, grad_both, grad_both)
+    queue.scatter(grad_attn, grad_outw, rest)
+    grad = collect(dot_nt(grad_both, mix))
+    back, grad_gain = rms_back(rows, scale, gain, grad)
+    return (grad_hidden + back, grad_gain, grad_taps)
 
 
 def by_rows(block):
@@ -227,7 +333,7 @@
         self.done = []
 
     def scatter(self, *grads):
-        block = by_rows(jnp.concatenate(grads, axis=1))
+        block = by_rows(jnp.concatenate(grads, axis=1) if len(grads) > 1 else grads[0])
         if self.done:
             block, self.done[-1] = lax.optimization_barrier((block, self.done[-1]))
         self.done.append(by_rows(lax.psum_scatter(block, "dp", scatter_dimension=0, tiled=True)))
@@ -292,7 +398,8 @@
     attn_zero = fetch(with_pair(attn_parts[0], lin_qk))
     weights_zero = parts_of(fetch(feed_parts[0]), attn_zero)
     attn_one = fetch(with_pair(attn_parts[1], win_qk))
-    weights_one = parts_of(fetch(feed_parts[1]), attn_one)
+    feed_one = fetch(feed_parts[1])
+    weights_one = parts_of(feed_one, attn_one)
 
     small = jnp.concatenate([norm_gains[0], conv_taps[0]], axis=0)
     small_other = swap(small)
@@ -312,21 +419,34 @@
     place = index * rows_dev + jnp.arange(rows_dev)
     mask = (place < length).astype(jnp.float32)[:, None]
 
-    middle, kept_zero = layer_forward(
-        entering, small_zero[:2], own_taps(small_zero), weights_zero, True
-    )
+    queue = Queue()
+    gains_zero, gains_one = small_zero[:2], small_one[:2]
+    hidden, kept_zero = attn_forward(entering, gains_zero[0], own_taps(small_zero), weights_zero, True)
+    middle, kept_feed = feed_forward(hidden, gains_zero[1], weights_zero)
     middle = middle.astype(jnp.bfloat16).astype(jnp.float32)
-    final, kept_one = layer_forward(
-        middle, small_one[:2], own_taps(small_one), weights_one, False
-    )
-    queue = Queue()
-    grad_middle, gains_one, taps_one = layer_backward(
-        kept_one, cotangent * mask, small_one[:2], own_taps(small_one), weights_one, False, queue, tail
-    )
+
+    hidden, kept_one = attn_forward(middle, gains_one[0], own_taps(small_one), weights_one, False)
+    scale, normed = rms_rows(hidden, gains_one[1])
+    grad_out = cotangent * mask
+    block, rest, grad_halves, inner = feed_both(
+        units, tail, *spread_pair(normed), *spread_pair(grad_out), feed_one, attn_one
+    )
+    queue.scatter(block)
+    final = hidden + collect(dot_nt(inner, weights_one[3]))
+    back, gain_two = rms_back(hidden, scale, gains_one[1], collect(dot_nt(grad_halves, weights_one[2])))
+    grad_middle, gain_one, taps_one = attn_backward(
+        kept_one, grad_out + back, gains_one[0], own_taps(small_one), weights_one, queue, rest
+    )
+    gains_one = jnp.stack([gain_one, gain_two])
+
     grad_middle = grad_middle.astype(jnp.bfloat16).astype(jnp.float32)
-    grad_start, gains_zero, taps_zero = layer_backward(
-        kept_zero, grad_middle, small_zero[:2], own_taps(small_zero), weights_zero, True, queue, tail
-    )
+    grad_hidden, gain_two, rest = feed_backward(
+        kept_feed, grad_middle, gains_zero[1], weights_zero, queue, tail
+    )
+    grad_start, gain_one, taps_zero = attn_backward(
+        kept_zero, grad_hidden, gains_zero[0], own_taps(small_zero), weights_zero, queue, rest
+    )
+    gains_zero = jnp.stack([gain_one, gain_two])
 
     grads_one, grads_zero = queue.done[:2], queue.done[2:]
 

time: 822 us -> 807 us (0.982)
  Pallas kernels: 0 us -> 16.1 us
  waiting for transfers between devices: 379 us -> 365 us
    pallas_call x0 -> x1, Pallas kernels: none -> 16.1 us  [feed_both(): pl.pallas_call(functools.partial(feed_kernel, units, tail), grid=(1,), ou...]
    ppermute x24, waiting for transfers between devices: 70.4 us -> 60.1 us  [collect(): total = total + lax.ppermute(block, 'tensor', pairs).astype(jnp.float32)]
    unnamed x258 -> x230, local copies, waits for them, and re-layouts: 36.9 us -> 32 us
    dot_general x8 -> x6, matrix products: 25 us -> 20.1 us  [dot_tn(): lax.dot_general(one, two, (((0,), (0,)), ((), ())), preferred_element_typ...]
    dot_general x8 -> x6, matrix products: 25.9 us -> 21.7 us  [dot(): return jnp.dot(one, two, preferred_element_type=jnp.float32)]
    concatenate x11 -> x8, local copies, waits for them, and re-layouts: 19.5 us -> 15.8 us  [the longest x1 7.27 us: scatter(): jnp.concatenate(grads, axis=1)]
  transfers between devices with their start and end apart: 63 -> 63, of which waited for: 41 -> 35; matrix products, arithmetic and copies ran while one was open for 26% -> 28% of each run, Pallas kernels for 0% -> 0%
where the time goes in v4:
time: 807 us; the launch traced here: 797 us
  waiting for transfers between devices  365 us (45%)
  local copies, waits for them, and re-layouts  118 us (15%)
  blocking collectives  109 us (14%)
  matrix products  77.9 us (10%)
  other arithmetic  55.8 us (7%)
  starting transfers between devices  38.5 us (5%)
  between operations  16.9 us (2%)
  Pallas kernels  16.1 us (2%)
    all_gather x4, waiting for transfers between devices, fetch(): return lax.all_gather(piece, 'dp', axis=0, tiled=True)  168 us
    all_gather x8, blocking collectives, spread_pair(): lax.all_gather(rows.astype(jnp.bfloat16), 'tensor', axis=0, tiled=True)  109 us
    reduce_scatter x4, waiting for transfers between devices, scatter(): lax.psum_scatter(block, 'dp', scatter_dimension=0, tiled=True)  96.6 us
    ppermute x24, waiting for transfers between devices, collect(): total = total + lax.ppermute(block, 'tensor', pairs).astype(jnp.float32)  60.1 us
    unnamed x230, local copies, waits for them, and re-layouts  32 us
    ppermute x24, starting transfers between devices, collect(): total = total + lax.ppermute(block, 'tensor', pairs).astype(jnp.float32)  28.5 us
    dot_general x8, matrix products, dot_nt(): lax.dot_general(one, two, (((1,), (1,)), ((), ())), preferred_element_typ...  23.3 us
    ppermute x5, waiting for transfers between devices, sum_all(): block = block + lax.ppermute(block, axis, pairs)  22 us
  transfers between devices with their start and end apart: 63, of which 35 were waited for; matrix products, arithmetic and copies ran while one was open for 28% of the time, Pallas kernels for 0%

profile of v4, /device:TPU:0, one launch (start us, length us, event | category | flops | bytes accessed | tf_op | source)
XLA Modules:
  0.0 796.7 jit_solution(15248828237643701941)
XLA Ops:
  20.3 5.9 constant_dynamic-slice_fusion.26
  27.7 3.7 concatenate.253
  35.2 3.4 broadcast_select_fusion.4
  42.2 14.7 %all_gather.36 = bf16[256,1792]{1,0:T(8,128)(2,1)S(1)} all-gather(bf16[64,1792]{1,0:T(8,128)(2,1)S(1)} %fusion.55), channel_id=1, replica_groups=mesh['section'=2,'dp'=4,'tensor'=4] {'tensor'}, dimensions={0}, use_global_device_ids=true | all-gather | bytes 1146880 | tf_op jit(solution)/shard_map/all_gather | solution.py:60
  60.4 16.0 %all-gather.5.cloned.1.call-done = bf16[1792,768]{1,0:T(8,128)(2,1)} async-done(((bf16[448,768]{1,0:T(8,128)(2,1)}), bf16[1792,768]{1,0:T(8,128)(2,1)}) %all-gather.5.cloned.1.call-update) | async-done | bytes 2752528 | tf_op jit(solution)/shard_map/all_gather | solution.py:384
  76.4 3.2 fusion.121
  94.4 3.2 fusion.115
  101.2 5.0 collective-permute-done.5
  106.2 5.1 collective-permute-done.6
  112.7 12.4 %all_gather.38 = bf16[256,1792]{1,0:T(8,128)(2,1)S(1)} all-gather(bf16[64,1792]{1,0:T(8,128)(2,1)S(1)} %multiply_convert_fusion.11), channel_id=1, replica_groups=mesh['section'=2,'dp'=4,'tensor'=4] {'tensor'}, dimensions={0}, use_global_device_ids=true | all-gather | bytes 1146880 | tf_op jit(solution)/shard_map/all_gather | solution.py:60
  128.6 66.2 %all-gather.7.cloned.1.call-done = bf16[1792,1792]{1,0:T(8,128)(2,1)} async-done(((bf16[448,1792]{1,0:T(8,128)(2,1)}), bf16[1792,1792]{1,0:T(8,128)(2,1)}) %all-gather.7.cloned.1.call-update) | async-done | bytes 6422544 | tf_op jit(solution)/shard_map/all_gather | solution.py:384
  198.0 5.6 fusion.5
  216.3 5.0 collective-permute-done.11
  221.3 5.3 collective-permute-done.12
  227.0 11.8 %all_gather.40 = bf16[256,1792]{1,0:T(8,128)(2,1)S(1)} all-gather(bf16[64,1792]{1,0:T(8,128)(2,1)S(1)} %fusion.62), channel_id=1, replica_groups=mesh['section'=2,'dp'=4,'tensor'=4] {'tensor'}, dimensions={0}, use_global_device_ids=true | all-gather | bytes 1146880 | tf_op jit(solution)/shard_map/all_gather | solution.py:60
  242.2 32.2 %all-gather.9.cloned.1.call-done.last_ref = bf16[1792,1152]{1,0:T(8,128)(2,1)} async-done(((bf16[448,1152]{1,0:T(8,128)(2,1)}), bf16[1792,1152]{1,0:T(8,128)(2,1)}) %all-gather.9.cloned.1.call-update) | async-done | bytes 4128784 | tf_op jit(solution)/shard_map/all_gather | solution.py:384
  274.3 5.7 fusion.122
  304.1 19.1 %all_gather.43.near_grad_ref = bf16[256,1792]{1,0:T(8,128)(2,1)S(1)} all-gather(bf16[64,1792]{1,0:T(8,128)(2,1)S(1)} %copy-done.36), channel_id=1, replica_groups=mesh['section'=2,'dp'=4,'tensor'=4] {'tensor'}, dimensions={0}, use_global_device_ids=true | all-gather | bytes 1146880 | tf_op jit(solution)/shard_map/all_gather | solution.py:60
  323.7 14.1 %all_gather.42.near_ref = bf16[256,1792]{1,0:T(8,128)(2,1)} all-gather(bf16[64,1792]{1,0:T(8,128)(2,1)S(1)} %multiply_convert_fusion.9), channel_id=1, replica_groups=mesh['section'=2,'dp'=4,'tensor'=4] {'tensor'}, dimensions={0}, use_global_device_ids=true | all-gather | bytes 1146880 | tf_op jit(solution)/shard_map/all_gather | solution.py:60
  337.9 54.0 %all-gather.11.cloned.1.call-done.feed_ref = bf16[1792,1792]{1,0:T(8,128)(2,1)} async-done(((bf16[448,1792]{1,0:T(8,128)(2,1)}), bf16[1792,1792]{1,0:T(8,128)(2,1)}) %all-gather.11.cloned.1.call-update) | async-done | bytes 6422544 | tf_op jit(solution)/shard_map/all_gather | solution.py:384
  391.9 16.1 %shard_map.169 = (bf16[1792,1792]{1,0:T(8,128)(2,1)}, bf16[1792,32]{1,0:T(8,128)(2,1)}, bf16[512,1280]{1,0:T(8,128)(2,1)}, bf16[512,608]{1,0:T(8,128)(2,1)}) custom-call(bf16[256,1792]{1,0:T(8,128)(2,1)} %all_gather.42.near_ref, bf16[256,1792]{1,0:T(8,128)(2,1)} %collective-permute-done.19.far_ref, bf16[256,1792]{1,0:T(8,128)(2,1)} %copy-done.33, ...), custom_call_target="tpu_custom_call" | custom-call | flops 6576668672 | bytes 20971520 | tf_op jit(solution)/shard_map/pallas_call | solution.py:277
  408.0 5.3 fusion.1
  419.8 5.0 collective-permute-done.22
  424.7 5.3 collective-permute-done.23
  431.4 12.5 %all_gather.45 = bf16[256,1792]{1,0:T(8,128)(2,1)} all-gather(bf16[64,1792]{1,0:T(8,128)(2,1)S(1)} %get-tuple-element.114), channel_id=1, replica_groups=mesh['section'=2,'dp'=4,'tensor'=4] {'tensor'}, dimensions={0}, use_global_device_ids=true | all-gather | bytes 1146880 | tf_op jit(solution)/shard_map/all_gather | solution.py:60
  463.0 5.3 convolution_convert_fusion.1
  468.3 7.3 concatenate.269
  475.6 43.6 %reduce-scatter.5.cloned.1.call-done = bf16[448,1792]{1,0:T(8,128)(2,1)} async-done(((bf16[1792,1792]{1,0:T(8,128)(2,1)}), bf16[448,1792]{1,0:T(8,128)(2,1)}) %reduce-scatter.5.cloned.1.call-update) | async-done | bytes 1605648 | tf_op jit(solution)/shard_map/reduce_scatter | solution.py:339
  519.3 4.3 fusion.7
  530.1 5.0 collective-permute-done.27
  535.0 5.3 collective-permute-done.28
  540.9 12.2 %all_gather.46 = bf16[256,1792]{1,0:T(8,128)(2,1)S(1)} all-gather(bf16[64,1792]{1,0:T(8,128)(2,1)S(1)} %fusion.67), channel_id=1, replica_groups=mesh['section'=2,'dp'=4,'tensor'=4] {'tensor'}, dimensions={0}, use_global_device_ids=true | all-gather | bytes 1146880 | tf_op jit(solution)/shard_map/all_gather | solution.py:60
  569.7 4.5 convolution_convert_fusion
  575.7 3.1 pad_maximum_fusion
  578.8 19.5 %reduce-scatter.7.cloned.1.call-done = bf16[448,1152]{1,0:T(8,128)(2,1)} async-done(((bf16[1792,1152]{1,0:T(8,128)(2,1)}), bf16[448,1152]{1,0:T(8,128)(2,1)}) %reduce-scatter.7.cloned.1.call-update) | async-done | bytes 1032208 | tf_op jit(solution)/shard_map/reduce_scatter | solution.py:339
  598.3 5.3 fusion.3
  610.1 5.0 collective-permute-done.32
  615.0 5.3 collective-permute-done.33
  620.8 12.0 %all_gather.47 = bf16[256,1792]{1,0:T(8,128)(2,1)S(1)} all-gather(bf16[64,1792]{1,0:T(8,128)(2,1)S(1)} %get-tuple-element.106), channel_id=1, replica_groups=mesh['section'=2,'dp'=4,'tensor'=4] {'tensor'}, dimensions={0}, use_global_device_ids=true | all-gather | bytes 1146880 | tf_op jit(solution)/shard_map/all_gather | solution.py:60
  651.8 4.1 convolution_convert_fusion.3
  666.5 3.3 fusion.106
  676.0 3.3 collective-permute-done.37
  680.9 3.4 collective-permute-done.39
  690.6 23.4 %reduce-scatter.9.cloned.1.call-done = bf16[448,1792]{1,0:T(8,128)(2,1)} async-done(((bf16[1792,1792]{1,0:T(8,128)(2,1)}), bf16[448,1792]{1,0:T(8,128)(2,1)}) %reduce-scatter.9.cloned.1.call-update) | async-done | bytes 1605648 | tf_op jit(solution)/shard_map/reduce_scatter | solution.py:339
  724.7 7.0 collective-permute-done.48
  732.7 9.9 %collective-permute-done.49 = f32[2,5,1792]{2,0,1:T(2,128)S(1)} collective-permute-done((f32[2,5,1792]{2,0,1:T(2,128)S(1)}, f32[2,5,1792]{2,0,1:T(2,128)S(1)}, u32[]{:S(2)}, u32[]{:S(2)}) %collective-permute-start.49) | collective-permute-done | bytes 71712 | tf_op jit(solution)/shard_map/ppermute | solution.py:90
  757.5 5.7 copy.254
  763.2 10.1 %reduce-scatter.11.cloned.1.call-done = bf16[448,768]{1,0:T(8,128)(2,1)} async-done(((bf16[1792,768]{1,0:T(8,128)(2,1)}), bf16[448,768]{1,0:T(8,128)(2,1)}) %reduce-scatter.11.cloned.1.call-update) | async-done | bytes 688144 | tf_op jit(solution)/shard_map/reduce_scatter | solution.py:339
  (576 shorter events, 236.6 us)
Async XLA Ops:
  7.2 69.2 %all-gather.5.cloned.1.call-start = ((), (), s32[]{:S(2)}) async-start(), calls=%async_computation.4 | async-start | bytes 3440640 | tf_op jit(solution)/shard_map/all_gather | solution.py:384
  16.7 178.2 %all-gather.7.cloned.1.call-start = ((), (), s32[]{:S(2)}) async-start(), calls=%async_computation.5 | async-start | bytes 8028160 | tf_op jit(solution)/shard_map/all_gather | solution.py:384
  38.6 235.7 %all-gather.9.cloned.1.call-start = ((), (), s32[]{:S(2)}) async-start(), calls=%async_computation.6 | async-start | bytes 5160960 | tf_op jit(solution)/shard_map/all_gather | solution.py:384
  89.8 4.5 collective-permute-start.4
  94.3 297.6 %all-gather.11.cloned.1.call-start = ((), (), s32[]{:S(2)}) async-start(), calls=%async_computation.7 | async-start | bytes 8028160 | tf_op jit(solution)/shard_map/all_gather | solution.py:384
  97.7 8.5 %collective-permute-start.5 = (bf16[64,1792]{1,0:T(8,128)(2,1)S(1)}, bf16[64,1792]{1,0:T(8,128)(2,1)S(1)}, u32[]{:S(2)}, u32[]{:S(2)}) collective-permute-start(bf16[64,1792]{1,0:T(8,128)(2,1)S(1)} %get-tuple-element.207), channel_id=1, source_target_pairs={{0,1},{1,0},{2,3},{3,2},{4,5},{5,4},{6,7},{7,6},{8,9},{9,8},{10,11... | collective-permute-start | bytes 688136 | tf_op jit(solution)/shard_map/ppermute | solution.py:80
  99.2 12.1 %collective-permute-start.6 = (bf16[64,1792]{1,0:T(8,128)(2,1)S(1)}, bf16[64,1792]{1,0:T(8,128)(2,1)S(1)}, u32[]{:S(2)}, u32[]{:S(2)}) collective-permute-start(bf16[64,1792]{1,0:T(8,128)(2,1)S(1)} %get-tuple-element.209), channel_id=1, source_target_pairs={{0,2},{1,3},{2,0},{3,1},{4,6},{5,7},{6,4},{7,5},{8,10},{9,11},{10,... | collective-permute-start | bytes 688136 | tf_op jit(solution)/shard_map/ppermute | solution.py:80
  100.7 10.6 %collective-permute-start.7 = (bf16[64,1792]{1,0:T(8,128)(2,1)S(1)}, bf16[64,1792]{1,0:T(8,128)(2,1)S(1)}, u32[]{:S(2)}, u32[]{:S(2)}) collective-permute-start(bf16[64,1792]{1,0:T(8,128)(2,1)S(1)} %get-tuple-element.208), channel_id=1, source_target_pairs={{0,3},{1,2},{2,1},{3,0},{4,7},{5,6},{6,5},{7,4},{8,11},{9,10},{10,... | collective-permute-start | bytes 688136 | tf_op jit(solution)/shard_map/ppermute | solution.py:80
  208.2 311.0 %reduce-scatter.5.cloned.1.call-start = ((), (), s32[]{:S(2)}) async-start(), calls=%async_computation.8 | async-start | bytes 8028160 | tf_op jit(solution)/shard_map/reduce_scatter | solution.py:339
  212.8 8.5 %collective-permute-start.11 = (bf16[64,1792]{1,0:T(8,128)(2,1)S(1)}, bf16[64,1792]{1,0:T(8,128)(2,1)S(1)}, u32[]{:S(2)}, u32[]{:S(2)}) collective-permute-start(bf16[64,1792]{1,0:T(8,128)(2,1)S(1)} %get-tuple-element.204), channel_id=1, source_target_pairs={{0,1},{1,0},{2,3},{3,2},{4,5},{5,4},{6,7},{7,6},{8,9},{9,8},{10,11... | collective-permute-start | bytes 688136 | tf_op jit(solution)/shard_map/ppermute | solution.py:80
  214.3 12.3 %collective-permute-start.12 = (bf16[64,1792]{1,0:T(8,128)(2,1)S(1)}, bf16[64,1792]{1,0:T(8,128)(2,1)S(1)}, u32[]{:S(2)}, u32[]{:S(2)}) collective-permute-start(bf16[64,1792]{1,0:T(8,128)(2,1)S(1)} %get-tuple-element.206), channel_id=1, source_target_pairs={{0,2},{1,3},{2,0},{3,1},{4,6},{5,7},{6,4},{7,5},{8,10},{9,11},{10,... | collective-permute-start | bytes 688136 | tf_op jit(solution)/shard_map/ppermute | solution.py:80
  215.8 10.8 %collective-permute-start.13 = (bf16[64,1792]{1,0:T(8,128)(2,1)S(1)}, bf16[64,1792]{1,0:T(8,128)(2,1)S(1)}, u32[]{:S(2)}, u32[]{:S(2)}) collective-permute-start(bf16[64,1792]{1,0:T(8,128)(2,1)S(1)} %get-tuple-element.205), channel_id=1, source_target_pairs={{0,3},{1,2},{2,1},{3,0},{4,7},{5,6},{6,5},{7,4},{8,11},{9,10},{10,... | collective-permute-start | bytes 688136 | tf_op jit(solution)/shard_map/ppermute | solution.py:80
  300.5 22.7 %collective-permute-start.16 = (bf16[64,1792]{1,0:T(8,128)(2,1)S(1)}, bf16[64,1792]{1,0:T(8,128)(2,1)S(1)}, u32[]{:S(2)}, u32[]{:S(2)}) collective-permute-start(bf16[64,1792]{1,0:T(8,128)(2,1)S(1)} %get-tuple-element.197), channel_id=1, source_target_pairs={{0,1},{1,0},{2,3},{3,2},{4,5},{5,4},{6,7},{7,6},{8,9},{9,8},{10,11... | collective-permute-start | bytes 688136 | tf_op jit(solution)/shard_map/ppermute | solution.py:80
  302.1 21.2 %collective-permute-start.17 = (bf16[64,1792]{1,0:T(8,128)(2,1)S(1)}, bf16[64,1792]{1,0:T(8,128)(2,1)S(1)}, u32[]{:S(2)}, u32[]{:S(2)}) collective-permute-start(bf16[64,1792]{1,0:T(8,128)(2,1)S(1)} %get-tuple-element.199), channel_id=1, source_target_pairs={{0,2},{1,3},{2,0},{3,1},{4,6},{5,7},{6,4},{7,5},{8,10},{9,11},{10,... | collective-permute-start | bytes 688136 | tf_op jit(solution)/shard_map/ppermute | solution.py:80
  303.6 19.7 %collective-permute-start.18 = (bf16[64,1792]{1,0:T(8,128)(2,1)S(1)}, bf16[64,1792]{1,0:T(8,128)(2,1)S(1)}, u32[]{:S(2)}, u32[]{:S(2)}) collective-permute-start(bf16[64,1792]{1,0:T(8,128)(2,1)S(1)} %get-tuple-element.198), channel_id=1, source_target_pairs={{0,3},{1,2},{2,1},{3,0},{4,7},{5,6},{6,5},{7,4},{8,11},{9,10},{10,... | collective-permute-start | bytes 688136 | tf_op jit(solution)/shard_map/ppermute | solution.py:80
  323.2 14.7 %collective-permute-start.20 = (bf16[256,1792]{1,0:T(8,128)(2,1)S(1)}, bf16[256,1792]{1,0:T(8,128)(2,1)}, u32[]{:S(2)}, u32[]{:S(2)}) collective-permute-start(bf16[256,1792]{1,0:T(8,128)(2,1)S(1)} %all_gather.43.near_grad_ref), channel_id=1, source_target_pairs={{0,16},{16,0},{1,17},{17,1},{2,18},{18,2},{3,19},{19,3},{4,20},{20... | collective-permute-start | bytes 2752520 | tf_op jit(solution)/shard_map/ppermute | solution.py:56
  337.8 54.1 %collective-permute-start.19 = (bf16[256,1792]{1,0:T(8,128)(2,1)}, bf16[256,1792]{1,0:T(8,128)(2,1)}, u32[]{:S(2)}, u32[]{:S(2)}) collective-permute-start(bf16[256,1792]{1,0:T(8,128)(2,1)} %all_gather.42.near_ref), channel_id=1, source_target_pairs={{0,16},{16,0},{1,17},{17,1},{2,18},{18,2},{3,19},{19,3},{4,20},{20... | collective-permute-start | bytes 2752520 | tf_op jit(solution)/shard_map/ppermute | solution.py:56
  407.9 190.3 %reduce-scatter.7.cloned.1.call-start = ((), (), s32[]{:S(2)}) async-start(), calls=%async_computation.9 | async-start | bytes 5160960 | tf_op jit(solution)/shard_map/reduce_scatter | solution.py:339
  416.2 8.5 %collective-permute-start.22 = (bf16[64,1792]{1,0:T(8,128)(2,1)S(1)}, bf16[64,1792]{1,0:T(8,128)(2,1)S(1)}, u32[]{:S(2)}, u32[]{:S(2)}) collective-permute-start(bf16[64,1792]{1,0:T(8,128)(2,1)S(1)} %get-tuple-element.194), channel_id=1, source_target_pairs={{0,1},{1,0},{2,3},{3,2},{4,5},{5,4},{6,7},{7,6},{8,9},{9,8},{10,11... | collective-permute-start | bytes 688136 | tf_op jit(solution)/shard_map/ppermute | solution.py:80
  417.8 12.3 %collective-permute-start.23 = (bf16[64,1792]{1,0:T(8,128)(2,1)S(1)}, bf16[64,1792]{1,0:T(8,128)(2,1)S(1)}, u32[]{:S(2)}, u32[]{:S(2)}) collective-permute-start(bf16[64,1792]{1,0:T(8,128)(2,1)S(1)} %get-tuple-element.196), channel_id=1, source_target_pairs={{0,2},{1,3},{2,0},{3,1},{4,6},{5,7},{6,4},{7,5},{8,10},{9,11},{10,... | collective-permute-start | bytes 688136 | tf_op jit(solution)/shard_map/ppermute | solution.py:80
  419.2 10.8 %collective-permute-start.24 = (bf16[64,1792]{1,0:T(8,128)(2,1)S(1)}, bf16[64,1792]{1,0:T(8,128)(2,1)S(1)}, u32[]{:S(2)}, u32[]{:S(2)}) collective-permute-start(bf16[64,1792]{1,0:T(8,128)(2,1)S(1)} %get-tuple-element.195), channel_id=1, source_target_pairs={{0,3},{1,2},{2,1},{3,0},{4,7},{5,6},{6,5},{7,4},{8,11},{9,10},{10,... | collective-permute-start | bytes 688136 | tf_op jit(solution)/shard_map/ppermute | solution.py:80
  443.8 4.5 collective-permute-start.25
  519.2 194.8 %reduce-scatter.9.cloned.1.call-start = ((), (), s32[]{:S(2)}) async-start(), calls=%async_computation.10 | async-start | bytes 8028160 | tf_op jit(solution)/shard_map/reduce_scatter | solution.py:339
  526.5 8.5 %collective-permute-start.27 = (bf16[64,1792]{1,0:T(8,128)(2,1)S(1)}, bf16[64,1792]{1,0:T(8,128)(2,1)S(1)}, u32[]{:S(2)}, u32[]{:S(2)}) collective-permute-start(bf16[64,1792]{1,0:T(8,128)(2,1)S(1)} %get-tuple-element.189), channel_id=1, source_target_pairs={{0,1},{1,0},{2,3},{3,2},{4,5},{5,4},{6,7},{7,6},{8,9},{9,8},{10,11... | collective-permute-start | bytes 688136 | tf_op jit(solution)/shard_map/ppermute | solution.py:80
  528.1 12.3 %collective-permute-start.28 = (bf16[64,1792]{1,0:T(8,128)(2,1)S(1)}, bf16[64,1792]{1,0:T(8,128)(2,1)S(1)}, u32[]{:S(2)}, u32[]{:S(2)}) collective-permute-start(bf16[64,1792]{1,0:T(8,128)(2,1)S(1)} %get-tuple-element.191), channel_id=1, source_target_pairs={{0,2},{1,3},{2,0},{3,1},{4,6},{5,7},{6,4},{7,5},{8,10},{9,11},{10,... | collective-permute-start | bytes 688136 | tf_op jit(solution)/shard_map/ppermute | solution.py:80
  529.5 10.8 %collective-permute-start.29 = (bf16[64,1792]{1,0:T(8,128)(2,1)S(1)}, bf16[64,1792]{1,0:T(8,128)(2,1)S(1)}, u32[]{:S(2)}, u32[]{:S(2)}) collective-permute-start(bf16[64,1792]{1,0:T(8,128)(2,1)S(1)} %get-tuple-element.190), channel_id=1, source_target_pairs={{0,3},{1,2},{2,1},{3,0},{4,7},{5,6},{6,5},{7,4},{8,11},{9,10},{10,... | collective-permute-start | bytes 688136 | tf_op jit(solution)/shard_map/ppermute | solution.py:80
  598.3 175.1 %reduce-scatter.11.cloned.1.call-start = ((), (), s32[]{:S(2)}) async-start(), calls=%async_computation.11 | async-start | bytes 3440640 | tf_op jit(solution)/shard_map/reduce_scatter | solution.py:339
  606.5 8.5 %collective-permute-start.32 = (bf16[64,1792]{1,0:T(8,128)(2,1)S(1)}, bf16[64,1792]{1,0:T(8,128)(2,1)S(1)}, u32[]{:S(2)}, u32[]{:S(2)}) collective-permute-start(bf16[64,1792]{1,0:T(8,128)(2,1)S(1)} %get-tuple-element.186), channel_id=1, source_target_pairs={{0,1},{1,0},{2,3},{3,2},{4,5},{5,4},{6,7},{7,6},{8,9},{9,8},{10,11... | collective-permute-start | bytes 688136 | tf_op jit(solution)/shard_map/ppermute | solution.py:80
  608.1 12.3 %collective-permute-start.33 = (bf16[64,1792]{1,0:T(8,128)(2,1)S(1)}, bf16[64,1792]{1,0:T(8,128)(2,1)S(1)}, u32[]{:S(2)}, u32[]{:S(2)}) collective-permute-start(bf16[64,1792]{1,0:T(8,128)(2,1)S(1)} %get-tuple-element.188), channel_id=1, source_target_pairs={{0,2},{1,3},{2,0},{3,1},{4,6},{5,7},{6,4},{7,5},{8,10},{9,11},{10,... | collective-permute-start | bytes 688136 | tf_op jit(solution)/shard_map/ppermute | solution.py:80
  609.5 10.8 %collective-permute-start.34 = (bf16[64,1792]{1,0:T(8,128)(2,1)S(1)}, bf16[64,1792]{1,0:T(8,128)(2,1)S(1)}, u32[]{:S(2)}, u32[]{:S(2)}) collective-permute-start(bf16[64,1792]{1,0:T(8,128)(2,1)S(1)} %get-tuple-element.187), channel_id=1, source_target_pairs={{0,3},{1,2},{2,1},{3,0},{4,7},{5,6},{6,5},{7,4},{8,11},{9,10},{10,... | collective-permute-start | bytes 688136 | tf_op jit(solution)/shard_map/ppermute | solution.py:80
  632.9 6.7 collective-permute-start.35
  639.0 19.7 %collective-permute-start.40 = (bf16[256,1792]{1,0:T(8,128)(2,1)}, bf16[256,1792]{1,0:T(8,128)(2,1)}, u32[]{:S(2)}, u32[]{:S(2)}) collective-permute-start(bf16[256,1792]{1,0:T(8,128)(2,1)} %slice.804), channel_id=1, source_target_pairs={{0,16},{16,0},{1,17},{17,1},{2,18},{18,2},{3,19},{19,3},{4,20},{20... | collective-permute-start | bytes 2752520 | tf_op jit(solution)/shard_map/ppermute | solution.py:56
  658.1 8.3 %collective-permute-start.36 = (bf16[256,1792]{1,0:T(8,128)(2,1)}, bf16[256,1792]{1,0:T(8,128)(2,1)}, u32[]{:S(2)}, u32[]{:S(2)}) collective-permute-start(bf16[256,1792]{1,0:T(8,128)(2,1)} %slice.805), channel_id=1, source_target_pairs={{0,16},{16,0},{1,17},{17,1},{2,18},{18,2},{3,19},{19,3},{4,20},{20... | collective-permute-start | bytes 2752520 | tf_op jit(solution)/shard_map/ppermute | solution.py:56
  662.2 23.7 %collective-permute-start.41 = (bf16[64,1792]{1,0:T(8,128)(2,1)}, bf16[64,1792]{1,0:T(8,128)(2,1)S(1)}, u32[]{:S(2)}, u32[]{:S(2)}) collective-permute-start(bf16[64,1792]{1,0:T(8,128)(2,1)} %get-tuple-element.180), channel_id=1, source_target_pairs={{0,1},{1,0},{2,3},{3,2},{4,5},{5,4},{6,7},{7,6},{8,9},{9,8},{10,11... | collective-permute-start | bytes 688136 | tf_op jit(solution)/shard_map/ppermute | solution.py:80
  662.8 23.1 %collective-permute-start.42 = (bf16[64,1792]{1,0:T(8,128)(2,1)}, bf16[64,1792]{1,0:T(8,128)(2,1)S(1)}, u32[]{:S(2)}, u32[]{:S(2)}) collective-permute-start(bf16[64,1792]{1,0:T(8,128)(2,1)} %get-tuple-element.182), channel_id=1, source_target_pairs={{0,2},{1,3},{2,0},{3,1},{4,6},{5,7},{6,4},{7,5},{8,10},{9,11},{10,... | collective-permute-start | bytes 688136 | tf_op jit(solution)/shard_map/ppermute | solution.py:80
  670.6 8.7 %collective-permute-start.37 = (bf16[64,1792]{1,0:T(8,128)(2,1)}, bf16[64,1792]{1,0:T(8,128)(2,1)S(1)}, u32[]{:S(2)}, u32[]{:S(2)}) collective-permute-start(bf16[64,1792]{1,0:T(8,128)(2,1)} %get-tuple-element.183), channel_id=1, source_target_pairs={{0,1},{1,0},{2,3},{3,2},{4,5},{5,4},{6,7},{7,6},{8,9},{9,8},{10,11... | collective-permute-start | bytes 688136 | tf_op jit(solution)/shard_map/ppermute | solution.py:80
  671.4 9.6 %collective-permute-start.38 = (bf16[64,1792]{1,0:T(8,128)(2,1)S(1)}, bf16[64,1792]{1,0:T(8,128)(2,1)S(1)}, u32[]{:S(2)}, u32[]{:S(2)}) collective-permute-start(bf16[64,1792]{1,0:T(8,128)(2,1)S(1)} %get-tuple-element.185), channel_id=1, source_target_pairs={{0,2},{1,3},{2,0},{3,1},{4,6},{5,7},{6,4},{7,5},{8,10},{9,11},{10,... | collective-permute-start | bytes 688136 | tf_op jit(solution)/shard_map/ppermute | solution.py:80
  672.8 11.5 %collective-permute-start.39 = (bf16[64,1792]{1,0:T(8,128)(2,1)S(1)}, bf16[64,1792]{1,0:T(8,128)(2,1)S(1)}, u32[]{:S(2)}, u32[]{:S(2)}) collective-permute-start(bf16[64,1792]{1,0:T(8,128)(2,1)S(1)} %get-tuple-element.184), channel_id=1, source_target_pairs={{0,3},{1,2},{2,1},{3,0},{4,7},{5,6},{6,5},{7,4},{8,11},{9,10},{10,... | collective-permute-start | bytes 688136 | tf_op jit(solution)/shard_map/ppermute | solution.py:80
  679.3 9.0 %collective-permute-start.43 = (bf16[64,1792]{1,0:T(8,128)(2,1)}, bf16[64,1792]{1,0:T(8,128)(2,1)S(1)}, u32[]{:S(2)}, u32[]{:S(2)}) collective-permute-start(bf16[64,1792]{1,0:T(8,128)(2,1)} %get-tuple-element.181), channel_id=1, source_target_pairs={{0,3},{1,2},{2,1},{3,0},{4,7},{5,6},{6,5},{7,4},{8,11},{9,10},{10,... | collective-permute-start | bytes 688136 | tf_op jit(solution)/shard_map/ppermute | solution.py:80
  685.8 28.3 %collective-permute-start.45 = (f32[2,5,1792]{2,0,1:T(2,128)S(1)}, f32[2,5,1792]{2,0,1:T(2,128)S(1)}, u32[]{:S(2)}, u32[]{:S(2)}) collective-permute-start(f32[2,5,1792]{2,0,1:T(2,128)S(1)} %pad_maximum_fusion.15), channel_id=1, source_target_pairs={{0,16},{16,0},{1,17},{17,1},{2,18},{18,2},{3,19},{19,3},{4,20},{20... | collective-permute-start | bytes 215048 | tf_op jit(solution)/shard_map/ppermute | solution.py:90
  714.2 4.4 collective-permute-start.46
  715.9 27.9 %collective-permute-start.44 = (f32[64,1792]{1,0:T(8,128)S(1)}, f32[64,1792]{1,0:T(8,128)S(1)}, u32[]{:S(2)}, u32[]{:S(2)}) collective-permute-start(f32[64,1792]{1,0:T(8,128)S(1)} %broadcast_select_fusion.14), channel_id=1, source_target_pairs={{0,16},{16,0},{1,17},{17,1},{2,18},{18,2},{3,19},{19,3},{4,20},{20... | collective-permute-start | bytes 1376264 | tf_op jit(solution)/shard_map/ppermute | solution.py:56
  718.7 4.4 collective-permute-start.47
  720.5 27.9 %collective-permute-start.53 = (bf16[448,1792]{1,0:T(8,128)(2,1)S(1)}, bf16[448,1792]{1,0:T(8,128)(2,1)S(1)}, u32[]{:S(2)}, u32[]{:S(2)}) collective-permute-start(bf16[448,1792]{1,0:T(8,128)(2,1)S(1)} %broadcast_select_fusion.2), channel_id=1, source_target_pairs={{0,16},{16,0},{1,17},{17,1},{2,18},{18,2},{3,19},{19,3},{4,20},{20... | collective-permute-start | bytes 4816904 | tf_op jit(solution)/shard_map/ppermute | solution.py:56
  723.1 8.6 %collective-permute-start.48 = (f32[2,5,1792]{2,0,1:T(2,128)S(1)}, f32[2,5,1792]{2,0,1:T(2,128)S(1)}, u32[]{:S(2)}, u32[]{:S(2)}) collective-permute-start(f32[2,5,1792]{2,0,1:T(2,128)S(1)} %add.436), channel_id=1, source_target_pairs={{0,4},{4,0},{8,12},{12,8},{1,5},{5,1},{9,13},{13,9},{2,6},{6,2},{1... | collective-permute-start | bytes 215048 | tf_op jit(solution)/shard_map/ppermute | solution.py:90
  731.7 10.8 %collective-permute-start.49 = (f32[2,5,1792]{2,0,1:T(2,128)S(1)}, f32[2,5,1792]{2,0,1:T(2,128)S(1)}, u32[]{:S(2)}, u32[]{:S(2)}) collective-permute-start(f32[2,5,1792]{2,0,1:T(2,128)S(1)} %add.437), channel_id=1, source_target_pairs={{0,8},{4,12},{8,0},{12,4},{1,9},{5,13},{9,1},{13,5},{2,10},{6,14},... | collective-permute-start | bytes 215048 | tf_op jit(solution)/shard_map/ppermute | solution.py:90
  732.6 12.3 %collective-permute-start.51 = (bf16[448,448]{1,0:T(8,128)(2,1)S(1)}, bf16[448,448]{1,0:T(8,128)(2,1)S(1)}, u32[]{:S(2)}, u32[]{:S(2)}) collective-permute-start(bf16[448,448]{1,0:T(8,128)(2,1)S(1)} %slice.541), channel_id=1, source_target_pairs={{0,16},{16,0},{1,17},{17,1},{2,18},{18,2},{3,19},{19,3},{4,20},{20... | collective-permute-start | bytes 1204232 | tf_op jit(solution)/shard_map/ppermute | solution.py:56
  777.9 5.0 collective-permute-start.52
  (120 other events, 809.1 us)
Sparse Core Ops, SparseCore 0:
  16.8 59.5 all-gather.4
  78.6 116.2 all-gather.6
  196.4 77.8 all-gather.8
  275.8 116.0 all-gather.10
  408.1 111.0 reduce-scatter.4
  521.9 76.2 reduce-scatter.6
  600.7 113.3 reduce-scatter.8
  716.5 56.8 reduce-scatter.10

commit v5 on v4

v5 whole, which is shorter than its diff:
```python
import functools
import math

import jax
import jax.numpy as jnp
from jax import lax
from jax.experimental import pallas as pl
from jax.experimental.layout import Layout, with_layout_constraint
from jax.experimental.pallas import tpu as pltpu
from jax.sharding import PartitionSpec as P

WIN = 64
HD = 112
LANES = 128
WIDE = 256
SUBLANES = 8

EPS = 1e-06


def silu_slope(value):
    sigma = jax.nn.sigmoid(value)
    return sigma * (1.0 + value * (1.0 - sigma))


def rms_rows(rows, gain):
    scale = lax.rsqrt(jnp.mean(rows * rows, axis=-1, keepdims=True) + EPS)
    return (scale, rows * scale * gain)


def rms_back(rows, scale, gain, grad):
    normal = rows * scale
    weighted = grad * gain
    inner = jnp.mean(weighted * normal, axis=-1, keepdims=True)
    return (scale * (weighted - normal * inner), jnp.sum(grad * normal, axis=0))


def swap(block):
    return lax.ppermute(block, "section", [(0, 1), (1, 0)])


def spread_pair(rows):
    mine = lax.all_gather(rows.astype(jnp.bfloat16), "tensor", axis=0, tiled=True)
    return (mine, swap(mine))


def spread(rows):
    return jnp.concatenate(spread_pair(rows), axis=0)


def collect(terms):
    length = terms.shape[0] // 2
    return collect_pair(terms[:length], terms[length:].astype(jnp.bfloat16))


def collect_pair(mine, other):
    size = lax.axis_size("tensor")
    count = mine.shape[0] // size
    index = lax.axis_index("tensor")
    part = mine + swap(other).astype(jnp.float32)
    low = part.astype(jnp.bfloat16)
    total = lax.dynamic_slice_in_dim(part, index * count, count, 0)
    for offset in range(1, size):
        block = lax.dynamic_slice_in_dim(low, (index ^ offset) * count, count, 0)
        pairs = [(i, i ^ offset) for i in range(size)]
        total = total + lax.ppermute(block, "tensor", pairs).astype(jnp.float32)
    return total


def sum_all(block):
    for axis in ("section", "tensor", "dp"):
        size = lax.axis_size(axis)
        step = 1
        while step < size:
            pairs = [(i, i ^ step) for i in range(size)]
            block = block + lax.ppermute(block, axis, pairs)
            step *= 2
    return block


def dot(one, two):
    return jnp.dot(one, two, preferred_element_type=jnp.float32)


def dot_nt(one, two):
    return lax.dot_general(one, two, (((1,), (1,)), ((), ())), preferred_element_type=jnp.float32)


def dot_tn(one, two):
    return lax.dot_general(one, two, (((0,), (0,)), ((), ())), preferred_element_type=jnp.float32)


def gates(halves, units):
    main = units // LANES * LANES
    stop = main + units
    return (
        (halves[:, :main], halves[:, main : 2 * main]),
        (halves[:, 2 * main : stop], halves[:, stop : 2 * units]),
    )


def lanes(block):
    return lax.broadcasted_iota(jnp.int32, block.shape, 1)


def forward_kernel(units, tail, near_ref, far_ref, feed_ref, last_ref, mine_ref, other_ref, rows_ref, inner_ref):
    main = units // LANES * LANES
    over = units - main
    length = near_ref.shape[0]
    rows_ref[:length] = near_ref[...]
    rows_ref[length:] = far_ref[...]
    rows = rows_ref[...]
    for start in range(0, main, WIDE):
        gate = dot(rows, feed_ref[:, pl.ds(main + start, WIDE)])
        upper = dot(rows, feed_ref[:, pl.ds(2 * main + start, WIDE)])
        inner_ref[:, pl.ds(start, WIDE)] = (jax.nn.silu(gate) * upper).astype(jnp.bfloat16)
    ends = feed_ref[:, pl.ds(3 * main, WIDE)]
    both = dot(rows, ends)
    upper = pltpu.roll(both, WIDE - over, 1)
    inner = jax.nn.silu(both[:, :LANES]) * upper[:, :LANES]
    inner = jnp.where(lanes(inner) < over, inner, 0.0)
    low = pltpu.roll(jnp.concatenate([inner, jnp.zeros_like(inner)], axis=1), 2 * over, 1)
    low = jnp.where(lanes(low) < 2 * over, 0.0, low).astype(jnp.bfloat16)
    high = pltpu.roll(inner, LANES - over, 1)
    high = jnp.where(lanes(high) < LANES - tail, 0.0, high).astype(jnp.bfloat16)
    terms = dot_nt(inner_ref[...], feed_ref[:, pl.ds(0, main)]) + dot_nt(low, ends) + dot_nt(high, last_ref[...])
    mine_ref[...] = terms[:length]
    other_ref[...] = terms[length:].astype(jnp.bfloat16)


def feed_terms(units, tail, near, far, feed, attn):
    length, model = near.shape
    main = units // LANES * LANES
    width = 3 * units - tail
    end = attn.shape[1] // LANES - 1

    def whole(shape):
        return pl.BlockSpec(shape, lambda step: (0, 0), pipeline_mode=pl.Buffered(1))

    return pl.pallas_call(
        functools.partial(forward_kernel, units, tail),
        grid=(1,),
        out_shape=[
            jax.ShapeDtypeStruct((length, model), jnp.float32),
            jax.ShapeDtypeStruct((length, model), jnp.bfloat16),
        ],
        in_specs=[
            whole((length, model)),
            whole((length, model)),
            whole((model, width)),
            pl.BlockSpec((model, LANES), lambda step: (0, end)),
        ],
        out_specs=[whole((length, model))] * 2,
        scratch_shapes=[
            pltpu.VMEM((2 * length, model), jnp.bfloat16),
            pltpu.VMEM((2 * length, main), jnp.bfloat16),
        ],
        compiler_params=pltpu.CompilerParams(vmem_limit_bytes=48 * 2**20),
        cost_estimate=pl.CostEstimate(flops=2**20, bytes_accessed=2**16, transcendentals=0),
    )(near, far, feed, attn)


def feed_kernel(
    units, tail, near_ref, far_ref, near_grad_ref, far_grad_ref, feed_ref, last_ref, *refs
):
    extras, (block_ref, rest_ref, halves_ref, inner_ref, rows_ref, grads_ref) = refs[:-6], refs[-6:]
    main = units // LANES * LANES
    over = units - main
    base = 0
    for extra in extras:
        block_ref[:, pl.ds(base, extra.shape[1])] = extra[...]
        base += extra.shape[1]

    def give(column, value):
        block_ref[:, pl.ds(base + column, WIDE)] = value.astype(jnp.bfloat16)

    length = near_ref.shape[0]
    rows_ref[:length] = near_ref[...]
    rows_ref[length:] = far_ref[...]
    grads_ref[:length] = near_grad_ref[...]
    grads_ref[length:] = far_grad_ref[...]
    rows = rows_ref[...]
    branch = grads_ref[...]

    def parts(gate, upper, grad):
        sigma = jax.nn.sigmoid(gate)
        act = gate * sigma
        slope = sigma * (1.0 + gate * (1.0 - sigma))
        return (act * upper, grad * upper * slope, grad * act)

    for start in range(0, main, WIDE):
        places = tuple(start + i * main for i in range(3))
        first, second, third = (pl.ds(place, WIDE) for place in places)
        gate = dot(rows, feed_ref[:, second])
        upper = dot(rows, feed_ref[:, third])
        grad = dot(branch, feed_ref[:, first])
        inner, grad_gate, grad_upper = (part.astype(jnp.bfloat16) for part in parts(gate, upper, grad))
        inner_ref[:, first] = inner
        halves_ref[:, first] = grad_gate
        halves_ref[:, second] = grad_upper
        give(places[0], dot_tn(branch, inner))
        give(places[1], dot_tn(rows, grad_gate))
        give(places[2], dot_tn(rows, grad_upper))

    ends = feed_ref[:, pl.ds(3 * main, WIDE)]
    both = dot(rows, ends)
    upper = pltpu.roll(both, WIDE - over, 1)
    grad = pltpu.roll(dot(branch, ends), WIDE - 2 * over, 1)[:, :LANES]
    more = pltpu.roll(dot(branch, last_ref[...]), over, 1)
    grad = jnp.where(lanes(grad) < over - tail, grad, more)
    inner, grad_gate, grad_upper = (
        jnp.where(lanes(part) < over, part, 0.0)
        for part in parts(both[:, :LANES], upper[:, :LANES], grad)
    )
    inner = inner.astype(jnp.bfloat16)
    inner_ref[:, pl.ds(main, over)] = inner[:, :over]
    empty = jnp.zeros_like(grad_gate)
    wide = jnp.concatenate([grad_gate, empty], axis=1)
    wide = wide + pltpu.roll(jnp.concatenate([grad_upper, empty], axis=1), over, 1)
    wide = wide.astype(jnp.bfloat16)
    halves_ref[:, pl.ds(2 * main, WIDE)] = wide
    down = dot_tn(branch, inner)
    moved = pltpu.roll(jnp.concatenate([down, jnp.zeros_like(down)], axis=1), 2 * over, 1)
    wide = dot_tn(rows, wide)
    give(3 * main, jnp.where(lanes(wide) < 2 * over, wide, moved))
    moved = pltpu.roll(jnp.concatenate([down, jnp.zeros_like(down)], axis=1), WIDE - over, 1)
    rest_ref[...] = jnp.where(lanes(moved) < WIDE - tail, 0.0, moved).astype(jnp.bfloat16)


def feed_both(units, tail, near, far, near_grad, far_grad, feed, attn, *extras):
    count, model = 2 * near.shape[0], near.shape[1]
    main = units // LANES * LANES
    width = 3 * units - tail
    shapes = (
        (model, width + sum(extra.shape[1] for extra in extras)),
        (model, WIDE),
        (count, width - main),
        (count, units),
    )
    blocks = (near, far, near_grad, far_grad)

    def whole(shape):
        return pl.BlockSpec(shape, lambda step: (0, 0), pipeline_mode=pl.Buffered(1))

    end = attn.shape[1] // LANES - 1
    return pl.pallas_call(
        functools.partial(feed_kernel, units, tail),
        grid=(1,),
        out_shape=[jax.ShapeDtypeStruct(shape, jnp.bfloat16) for shape in shapes],
        in_specs=[whole(block.shape) for block in blocks]
        + [whole((model, width)), pl.BlockSpec((model, LANES), lambda step: (0, end))]
        + [whole(extra.shape) for extra in extras],
        out_specs=[whole(shape) for shape in shapes],
        scratch_shapes=[pltpu.VMEM((count, model), jnp.bfloat16)] * 2,
        compiler_params=pltpu.CompilerParams(vmem_limit_bytes=56 * 2**20),
        cost_estimate=pl.CostEstimate(
            flops=4 * count * model * width,
            bytes_accessed=20 * 2**20,
            transcendentals=count * units,
        ),
    )(*blocks, feed, attn, *extras)


def take(block, column, width):
    base = column // LANES * LANES
    shift = column - base
    stop = base + -(-(shift + width) // LANES) * LANES
    part = block[:, base:stop]
    if shift:
        part = pltpu.roll(part, stop - base - shift, 1)
    part = part[:, : -(-width // LANES) * LANES]
    return jnp.where(lanes(part) < width, part, 0.0)


def put(target, rows, column, width, part):
    base = column // LANES * LANES
    shift = column - base
    size = -(-(shift + width) // LANES) * LANES
    if size > part.shape[1]:
        empty = jnp.zeros((part.shape[0], size - part.shape[1]), part.dtype)
        part = jnp.concatenate([part, empty], axis=1)
    if shift:
        part = pltpu.roll(part, shift, 1)
    target[rows, pl.ds(base, size)] += part


def moved(block, distance):
    count = block.shape[0]
    if distance == 0:
        return block
    row = lax.broadcasted_iota(jnp.int32, block.shape, 0)
    rolled = pltpu.roll(block, distance % count, 0)
    inside = row >= distance if distance > 0 else row < count + distance
    return jnp.where(inside, rolled, 0.0)


def mixer_parts(both, taps, channels, first):
    length = both.shape[0]
    heads = channels // HD
    width = (both.shape[1] - 2 * channels) // (2 * heads)
    pre_values = take(both, 0, channels)
    values = sum(moved(pre_values, tap) * taps[tap : tap + 1] for tap in range(3))
    values = values.astype(jnp.bfloat16).astype(jnp.float32)
    gate = take(both, channels, channels)
    query = lax.broadcasted_iota(jnp.int32, (length, length), 0)
    key = lax.broadcasted_iota(jnp.int32, (length, length), 1)
    allowed = key <= query
    if not first:
        allowed = allowed & (query - key < WIN)
    parts = []
    for head in range(heads):
        queries = take(both, 2 * channels + head * width, width).astype(jnp.bfloat16)
        keys = take(both, 2 * channels + (heads + head) * width, width).astype(jnp.bfloat16)
        scores = dot_nt(queries, keys) / math.sqrt(width)
        if first:
            kernel = jnp.where(allowed, 1.0 + scores + 0.5 * scores * scores, 0.0)
            total = jnp.sum(kernel, axis=-1, keepdims=True)
            probs = kernel / total
            slope = jnp.where(allowed, (1.0 + scores) / total, 0.0)
        else:
            scores = jnp.where(allowed, scores, -1e30)
            kernel = jnp.exp(scores - jnp.max(scores, axis=-1, keepdims=True))
            probs = kernel / jnp.sum(kernel, axis=-1, keepdims=True)
            slope = probs
        own = take(values, head * HD, HD).astype(jnp.bfloat16)
        parts.append((queries, keys, probs, slope, own, dot(probs.astype(jnp.bfloat16), own)))
    return (pre_values, gate, parts)


def join(parts):
    empty = jnp.zeros_like(parts[0])
    total = 0.0
    for head, part in enumerate(parts):
        part = jnp.concatenate([part, empty], axis=1)
        total = total + (pltpu.roll(part, head * HD, 1) if head else part)
    return total


def mixer_kernel(
    channels, first, near_ref, far_ref, attn_ref, taps_ref, mine_ref, other_ref, both_ref, gated_ref
):
    length = near_ref.shape[0]
    stop = both_ref.shape[1]
    for index, rows in enumerate((near_ref, far_ref)):
        both = dot(rows[...], attn_ref[:, pl.ds(0, stop)])
        both_ref[pl.ds(index * length, length), :] = both
        _, gate, parts = mixer_parts(both, taps_ref[...], channels, first)
        gated = (join([part[-1] for part in parts]) * gate * jax.nn.sigmoid(gate)).astype(jnp.bfloat16)
        gated_ref[pl.ds(index * length, length), :] = gated
        terms = dot_nt(gated, attn_ref[:, pl.ds(stop, WIDE)])
        if index == 0:
            mine_ref[...] = terms
        else:
            other_ref[...] = terms.astype(jnp.bfloat16)


def mixer_back_kernel(
    channels, first, near_ref, far_ref, near_grad_ref, far_grad_ref, attn_ref, taps_ref, both_ref,
    gated_ref, rest_ref, block_ref, mine_ref, other_ref, taps_grad_ref, rows_ref, grads_ref, sums_ref, low_ref,
):
    length = near_ref.shape[0]
    stop = both_ref.shape[1]
    heads = channels // HD
    width = (stop - 2 * channels) // (2 * heads)
    taps = taps_ref[...]
    sums_ref[...] = jnp.zeros_like(sums_ref)
    taps_grad = [0.0] * 3
    rows_ref[:length] = near_ref[...]
    rows_ref[length:] = far_ref[...]
    grads_ref[:length] = near_grad_ref[...]
    grads_ref[length:] = far_grad_ref[...]
    for index in range(2):
        rows = pl.ds(index * length, length)
        pre_values, gate, parts = mixer_parts(both_ref[rows, :], taps, channels, first)
        mixed = join([part[-1] for part in parts])
        grad = dot(grads_ref[rows, :], attn_ref[:, pl.ds(stop, WIDE)])
        grad = jnp.where(lanes(grad) < channels, grad, 0.0)
        sigma = jax.nn.sigmoid(gate)
        grad_mixed = (grad * (gate * sigma)).astype(jnp.bfloat16).astype(jnp.float32)
        grad_gate = (grad * mixed * silu_slope(gate)).astype(jnp.bfloat16).astype(jnp.float32)
        put(sums_ref, rows, channels, channels, grad_gate)
        grad_values = []
        for head, (queries, keys, probs, slope, own, _) in enumerate(parts):
            part = take(grad_mixed, head * HD, HD).astype(jnp.bfloat16)
            grad_values.append(dot_tn(probs.astype(jnp.bfloat16), part))
            grad_probs = dot_nt(part, own)
            centred = grad_probs - jnp.sum(probs * grad_probs, axis=-1, keepdims=True)
            score_grad = (centred * slope).astype(jnp.bfloat16)
            for place, value in (
                (head, dot(score_grad, keys)),
                (heads + head, dot_tn(score_grad, queries)),
            ):
                value = (value / math.sqrt(width)).astype(jnp.bfloat16).astype(jnp.float32)
                put(sums_ref, rows, 2 * channels + place * width, width, value)
        grad_values = join(grad_values)
        grad_pre = sum(moved(grad_values, -tap) * taps[tap : tap + 1] for tap in range(3))
        put(sums_ref, rows, 0, channels, grad_pre.astype(jnp.bfloat16).astype(jnp.float32))
        for tap in range(3):
            taps_grad[tap] = taps_grad[tap] + jnp.sum(
                grad_values * moved(pre_values, tap), axis=0, keepdims=True
            )
    for tap in range(3):
        taps_grad_ref[pl.ds(tap, 1), :] = taps_grad[tap]
    low_ref[...] = sums_ref[...].astype(jnp.bfloat16)
    for column in range(0, stop, LANES):
        size = min(WIDE, stop - column)
        if column % WIDE:
            continue
        place = pl.ds(column, size)
        block_ref[:, place] = dot_tn(rows_ref[...], low_ref[:, place]).astype(jnp.bfloat16)
    last = dot_tn(grads_ref[...], gated_ref[...]).astype(jnp.bfloat16)
    block_ref[:, pl.ds(stop, WIDE)] = last + rest_ref[...]
    for index in range(2):
        terms = dot_nt(low_ref[pl.ds(index * length, length), :], attn_ref[:, pl.ds(0, stop)])
        if index == 0:
            mine_ref[...] = terms
        else:
            other_ref[...] = terms.astype(jnp.bfloat16)


def whole_call(kernel, inputs, shapes, scratch, flops):
    def whole(shape):
        return pl.BlockSpec(shape, lambda step: (0,) * len(shape), pipeline_mode=pl.Buffered(1))

    return pl.pallas_call(
        kernel,
        grid=(1,),
        out_shape=[jax.ShapeDtypeStruct(shape, kind) for shape, kind in shapes],
        in_specs=[whole(block.shape) for block in inputs],
        out_specs=[whole(shape) for shape, _ in shapes],
        scratch_shapes=[pltpu.VMEM(shape, kind) for shape, kind in scratch],
        compiler_params=pltpu.CompilerParams(vmem_limit_bytes=56 * 2**20),
        cost_estimate=pl.CostEstimate(flops=flops, bytes_accessed=2**16, transcendentals=0),
    )(*inputs)


def mixer_forward(channels, first, near, far, attn, taps):
    length, model = near.shape
    stop = attn.shape[1] - WIDE
    shapes = (
        ((length, model), jnp.float32),
        ((length, model), jnp.bfloat16),
        ((2 * length, stop), jnp.float32),
        ((2 * length, WIDE), jnp.bfloat16),
    )
    kernel = functools.partial(mixer_kernel, channels, first)
    return whole_call(kernel, (near, far, attn, taps), shapes, (), 2**20)


def mixer_backward(channels, first, near, far, near_grad, far_grad, attn, taps, both, gated, rest):
    length, model = near.shape
    stop = both.shape[1]
    shapes = (
        ((model, stop + WIDE), jnp.bfloat16),
        ((length, model), jnp.float32),
        ((length, model), jnp.bfloat16),
        (taps.shape, jnp.float32),
    )
    scratch = (
        ((2 * length, model), jnp.bfloat16),
        ((2 * length, model), jnp.bfloat16),
        ((2 * length, stop), jnp.float32),
        ((2 * length, stop), jnp.bfloat16),
    )
    inputs = (near, far, near_grad, far_grad, attn, taps, both, gated, rest)
    return whole_call(functools.partial(mixer_back_kernel, channels, first), inputs, shapes, scratch, 2**20)


def by_rows(block):
    return with_layout_constraint(block, Layout(major_to_minor=(0, 1)))


class Queue:
    def __init__(self):
        self.done = []

    def scatter(self, *grads):
        block = by_rows(jnp.concatenate(grads, axis=1) if len(grads) > 1 else grads[0])
        if self.done:
            block, self.done[-1] = lax.optimization_barrier((block, self.done[-1]))
        self.done.append(by_rows(lax.psum_scatter(block, "dp", scatter_dimension=0, tiled=True)))


def body(
    boundary, lengths, norm_gains, conv_taps, lin_qk, win_qk, value_gate, out_weight, gate_up, down_weight
):
    core = lax.axis_index("section")
    index = lax.axis_index("tensor")
    lower = core == 0
    rows_dev, model = boundary.shape[2:]
    channels = value_gate.shape[-1] // 2
    units = gate_up.shape[-1] // 2
    main = units // LANES * LANES
    tail = -(3 * channels + lin_qk.shape[-1]) % LANES

    def half(block, axis, which):
        size = block.shape[axis] // 2
        return lax.dynamic_slice_in_dim(block, which * size, size, axis)

    def both_layers(build):
        mine = build(core)
        other = swap(build(1 - core))
        return (jnp.where(lower, mine, other), jnp.where(lower, other, mine))

    def attn_piece(which):
        values = half(value_gate[0], 2, which)
        last = half(down_weight[0], 0, which)[units - tail :]
        return jnp.concatenate(
            [values[:, 0], values[:, 1], half(out_weight[0], 0, which).T, last.T], axis=1
        )

    def feed_piece(which):
        pair = half(gate_up[0], 2, which)
        down = half(down_weight[0], 0, which).T
        return jnp.concatenate(
            [down[:, :main], pair[:, 0, :main], pair[:, 1, :main], pair[:, 0, main:], pair[:, 1, main:], down[:, main : units - tail]],
            axis=1,
        )

    def fetch(piece):
        return lax.all_gather(piece, "dp", axis=0, tiled=True)

    def with_pair(attn, pair):
        pair = half(pair, 2, core)
        both = 2 * channels
        return jnp.concatenate([attn[:, :both], pair[:, 0], pair[:, 1], attn[:, both:]], axis=1)

    attn_parts = both_layers(attn_piece)
    feed_parts = both_layers(feed_piece)
    attn_zero = fetch(with_pair(attn_parts[0], lin_qk))
    packed = fetch(jnp.concatenate([feed_parts[0], with_pair(attn_parts[1], win_qk)], axis=1))
    split = feed_parts[0].shape[1]
    attn_one = packed[:, split:]
    feed_one = fetch(feed_parts[1])
    down_one = jnp.concatenate(
        [feed_one[:, :main], feed_one[:, main + 2 * units :], attn_one[:, attn_one.shape[1] - tail :]], axis=1
    )

    small = jnp.concatenate([norm_gains[0], conv_taps[0]], axis=0)
    small_other = swap(small)
    small_zero = jnp.where(lower, small, small_other)
    small_one = jnp.where(lower, small_other, small)
    offset = (2 * index + core) * channels

    def own_taps(block):
        own = lax.dynamic_slice_in_dim(block[2:], offset, channels, 1)
        return jnp.pad(own, ((0, -own.shape[0] % SUBLANES), (0, WIDE - channels)))

    held = boundary[0]
    keep = lax.dynamic_index_in_dim(held, core, 0, keepdims=False)
    other = swap(lax.dynamic_index_in_dim(held, 1 - core, 0, keepdims=False))
    entering = jnp.where(lower, keep, other).astype(jnp.float32)
    cotangent = jnp.where(lower, other, keep).astype(jnp.float32)
    length = lax.dynamic_index_in_dim(lengths, core, 0, keepdims=False)
    place = index * rows_dev + jnp.arange(rows_dev)
    mask = (place < length).astype(jnp.float32)[:, None]

    queue = Queue()
    gains_zero, gains_one = small_zero[:2], small_one[:2]
    taps_zero, taps_one = own_taps(small_zero), own_taps(small_one)

    def mix(rows, gain, attn, taps, first):
        scale, normed = rms_rows(rows, gain)
        near, far = spread_pair(normed)
        mine, other, both, gated = mixer_forward(channels, first, near, far, attn, taps)
        return (rows + collect_pair(mine, other), (rows, scale, near, far, both, gated))

    def mix_back(kept, grad_out, gain, attn, taps, rest, first):
        rows, scale, near, far, both, gated = kept
        block, mine, other, grad_taps = mixer_backward(
            channels, first, near, far, *spread_pair(grad_out), attn, taps, both, gated, rest
        )
        back, grad_gain = rms_back(rows, scale, gain, collect_pair(mine, other))
        return (block, grad_out + back, grad_gain, grad_taps[: conv_taps.shape[1], :channels])

    hidden, kept_zero = mix(entering, gains_zero[0], attn_zero, taps_zero, True)
    scale, normed = rms_rows(hidden, gains_zero[1])
    near, far = spread_pair(normed)
    kept_feed = (hidden, scale, near, far)
    middle = hidden + collect_pair(*feed_terms(units, tail, near, far, packed, attn_zero))
    middle = middle.astype(jnp.bfloat16).astype(jnp.float32)

    hidden, kept_one = mix(middle, gains_one[0], attn_one, taps_one, False)
    scale, normed = rms_rows(hidden, gains_one[1])
    grad_out = cotangent * mask
    block, rest, grad_halves, inner = feed_both(
        units, tail, *spread_pair(normed), *spread_pair(grad_out), feed_one, packed
    )
    queue.scatter(block)
    final = hidden + collect(dot_nt(inner, down_one))
    back, gain_two = rms_back(hidden, scale, gains_one[1], collect(dot_nt(grad_halves, feed_one[:, main:])))
    attn_grads, grad_middle, gain_one, taps_one = mix_back(
        kept_one, grad_out + back, gains_one[0], attn_one, taps_one, rest, False
    )
    gains_one = jnp.stack([gain_one, gain_two])

    grad_middle = grad_middle.astype(jnp.bfloat16).astype(jnp.float32)
    hidden, scale, near, far = kept_feed
    block, rest, grad_halves, _ = feed_both(
        units, tail, near, far, *spread_pair(grad_middle), packed, attn_zero, attn_grads
    )
    queue.scatter(block)
    terms = dot_nt(grad_halves, packed[:, main:split])
    back, gain_two = rms_back(hidden, scale, gains_zero[1], collect(terms))
    attn_grads, grad_start, gain_one, taps_zero = mix_back(
        kept_zero, grad_middle + back, gains_zero[0], attn_zero, taps_zero, rest, True
    )
    queue.scatter(attn_grads)
    gains_zero = jnp.stack([gain_one, gain_two])

    edge = attn_one.shape[1]
    grads_one = (queue.done[0], queue.done[1][:, :edge])
    grads_zero = (queue.done[1][:, edge:], queue.done[2])

    def own_small(gains, taps):
        spot = jnp.zeros((taps.shape[0], model), jnp.float32)
        return jnp.concatenate([gains, lax.dynamic_update_slice_in_dim(spot, taps, offset, 1)], axis=0)

    sums = sum_all(jnp.stack([own_small(gains_zero, taps_zero), own_small(gains_one, taps_one)]))
    sums = lax.dynamic_index_in_dim(sums, core, 0, keepdims=True)

    final = final * mask
    ends_keep = jnp.where(lower, grad_start, final)
    ends_other = swap(jnp.where(lower, final, grad_start))
    ends = jnp.where(lower, jnp.stack([ends_keep, ends_other]), jnp.stack([ends_other, ends_keep]))

    def home(zero, one):
        mine = jnp.where(lower, zero, one)
        other = swap(jnp.where(lower, one, zero))
        return (jnp.where(lower, mine, other), jnp.where(lower, other, mine))

    def halves(low, high, axis):
        return jnp.concatenate([low, high], axis=axis).astype(jnp.float32)

    def pair_home(block):
        size = block.shape[1] // 2
        other = swap(block)
        low = jnp.where(lower, block, other)
        high = jnp.where(lower, other, block)
        return jnp.stack(
            [halves(low[:, :size], high[:, :size], 1), halves(low[:, size:], high[:, size:], 1)], axis=1
        )

    def split_pair(grads, tail):
        both = 2 * channels
        stop = grads.shape[1] - tail
        rest = jnp.concatenate([grads[:, :both], grads[:, stop - channels : stop]], axis=1)
        return (rest, grads[:, both : stop - channels], grads[:, stop:])

    attn_zero, pair_zero, down_zero = split_pair(grads_zero[1], tail)
    attn_one, pair_one, down_one = split_pair(grads_one[1], tail)
    low, high = home(attn_zero, attn_one)
    vgate_grad = jnp.stack(
        [
            halves(low[:, :channels], high[:, :channels], 1),
            halves(low[:, channels : 2 * channels], high[:, channels : 2 * channels], 1),
        ],
        axis=1,
    )
    out_grad = halves(low[:, 2 * channels :].T, high[:, 2 * channels :].T, 0)
    low_tail, high_tail = home(down_zero, down_one)

    def unpack(block, last):
        wide = block[:, main:]
        (gate, upper), (gate_rest, upper_rest) = gates(wide, units)
        down = jnp.concatenate([block[:, :main], wide[:, 2 * units :], last], axis=1)
        return (
            jnp.concatenate([gate, gate_rest], axis=1),
            jnp.concatenate([upper, upper_rest], axis=1),
            down.T,
        )

    low, high = home(grads_zero[0], grads_one[0])
    low, high = unpack(low, low_tail), unpack(high, high_tail)
    gate_up_grad = jnp.stack([halves(low[0], high[0], 1), halves(low[1], high[1], 1)], axis=1)
    down_grad = halves(low[2], high[2], 0)
    return (
        ends[None],
        sums[:, :2],
        sums[:, 2:],
        pair_home(pair_zero),
        pair_home(pair_one),
        vgate_grad[None],
        out_grad[None],
        gate_up_grad[None],
        down_grad[None],
    )


def solution(mesh):
    in_specs = (
        P("section", "dp", "tensor", None),
        P("dp"),
        P("section", None, None),
        P("section", None, None),
        P("dp", None, "tensor"),
        P("dp", None, "tensor"),
        P("section", "dp", None, "tensor"),
        P("section", "tensor", "dp"),
        P("section", "dp", None, "tensor"),
        P("section", "tensor", "dp"),
    )
    out_specs = (
        P("section", "dp", "tensor", None),
        P("section", None, None),
        P("section", None, None),
        P("dp", None, "tensor"),
        P("dp", None, "tensor"),
        P("section", "dp", None, "tensor"),
        P("section", "tensor", "dp"),
        P("section", "dp", None, "tensor"),
        P("section", "tensor", "dp"),
    )
    return jax.shard_map(body, mesh=mesh, in_specs=in_specs, out_specs=out_specs, check_vma=False)
```

time: 807 us -> 781 us (0.968)
  Pallas kernels: 16.1 us -> 88.4 us
  matrix products: 77.9 us -> 11.4 us
  local copies, waits for them, and re-layouts: 118 us -> 81.9 us
  waiting for transfers between devices: 365 us -> 387 us
  other arithmetic: 55.8 us -> 40.9 us
    pallas_call x0 -> x5, Pallas kernels: none -> 52.9 us  [the longest x4 41.6 us: whole_call(): pl.pallas_call(kernel, grid=(1,), out_shape=[jax.ShapeDtypeStruct(shape,...]
    dot_general x23 -> x0, matrix products: 52.2 us -> none  [the longest x6 21.7 us: dot(): return jnp.dot(one, two, preferred_element_type=jnp.float32)]
    pallas_call x1 -> x2, Pallas kernels: 16.1 us -> 35.6 us  [feed_both(): pl.pallas_call(functools.partial(feed_kernel, units, tail), grid=(1,), ou...]
    concatenate x9 -> x1, local copies, waits for them, and re-layouts: 17.8 us -> 4.68 us  [body(): jnp.concatenate([feed_parts[0], with_pair(attn_parts[1], win_qk)], axis=1)]
    slice x26 -> x12, local copies, waits for them, and re-layouts: 19.7 us -> 7.23 us  [the longest x1 4.51 us: body(): attn_one = packed[:, split:]]
    dot_general x8 -> x3, matrix products: 23.3 us -> 11.4 us  [dot_nt(): lax.dot_general(one, two, (((1,), (1,)), ((), ())), preferred_element_typ...]
    ppermute x24, waiting for transfers between devices: 60.1 us -> 69.8 us  [collect_pair(): total = total + lax.ppermute(block, 'tensor', pairs).astype(jnp.float32)]
    reduce_scatter x4 -> x3, waiting for transfers between devices: 96.6 us -> 106 us  [scatter(): lax.psum_scatter(block, 'dp', scatter_dimension=0, tiled=True)]
  transfers between devices with their start and end apart: 63 -> 61, of which waited for: 35 -> 43; matrix products, arithmetic and copies ran while one was open for 28% -> 14% of each run, Pallas kernels for 0% -> 9%
where the time goes in v5:
time: 781 us; the launch traced here: 776 us
  waiting for transfers between devices  387 us (50%)
  blocking collectives  113 us (14%)
  Pallas kernels  88.4 us (11%)
  local copies, waits for them, and re-layouts  81.9 us (10%)
  other arithmetic  40.9 us (5%)
  starting transfers between devices  37.8 us (5%)
  between operations  15.6 us (2%)
  matrix products  11.4 us (1%)
    all_gather x3, waiting for transfers between devices, fetch(): return lax.all_gather(piece, 'dp', axis=0, tiled=True)  169 us
    all_gather x8, blocking collectives, spread_pair(): lax.all_gather(rows.astype(jnp.bfloat16), 'tensor', axis=0, tiled=True)  113 us
    reduce_scatter x3, waiting for transfers between devices, scatter(): lax.psum_scatter(block, 'dp', scatter_dimension=0, tiled=True)  106 us
    ppermute x24, waiting for transfers between devices, collect_pair(): total = total + lax.ppermute(block, 'tensor', pairs).astype(jnp.float32)  69.8 us
    pallas_call x4, Pallas kernels, whole_call(): pl.pallas_call(kernel, grid=(1,), out_shape=[jax.ShapeDtypeStruct(shape,...  41.6 us
    pallas_call x2, Pallas kernels, feed_both(): pl.pallas_call(functools.partial(feed_kernel, units, tail), grid=(1,), ou...  35.6 us
    ppermute x24, starting transfers between devices, collect_pair(): total = total + lax.ppermute(block, 'tensor', pairs).astype(jnp.float32)  26.5 us
    ppermute x26, waiting for transfers between devices, swap(): return lax.ppermute(block, 'section', [(0, 1), (1, 0)])  24.9 us
  transfers between devices with their start and end apart: 61, of which 43 were waited for; matrix products, arithmetic and copies ran while one was open for 14% of the time, Pallas kernels for 9%

profile of v5, /device:TPU:0, one launch (start us, length us, event | category | flops | bytes accessed | tf_op | source)
XLA Modules:
  0.0 775.9 jit_solution(1054426114418600529)
XLA Ops:
  20.1 6.0 constant_dynamic-slice_fusion.25
  27.9 3.6 concatenate.209
  35.0 3.0 constant_dynamic-slice_fusion.24
  39.8 2.8 broadcast_select_fusion.4
  42.6 4.7 concatenate.210
  51.1 14.9 %all_gather.33.near_ref = bf16[256,1792]{1,0:T(8,128)(2,1)S(1)} all-gather(bf16[64,1792]{1,0:T(8,128)(2,1)S(1)} %fusion.20), channel_id=1, replica_groups=mesh['section'=2,'dp'=4,'tensor'=4] {'tensor'}, dimensions={0}, use_global_device_ids=true | all-gather | bytes 1146880 | tf_op jit(solution)/shard_map/all_gather | solution.py:43
  68.6 9.4 %all-gather.4.cloned.1.call-done.attn_ref.last_ref = bf16[1792,768]{1,0:T(8,128)(2,1)} async-done(((bf16[448,768]{1,0:T(8,128)(2,1)}), bf16[1792,768]{1,0:T(8,128)(2,1)}) %all-gather.4.cloned.1.call-update) | async-done | bytes 2752528 | tf_op jit(solution)/shard_map/all_gather | solution.py:521
  78.0 6.7 shard_map.169
  84.7 2.7 collective-permute-done.4
  93.8 5.1 collective-permute-done.5
  98.9 5.1 collective-permute-done.7
  107.2 12.7 %all_gather.35.near_ref = bf16[256,1792]{1,0:T(8,128)(2,1)S(1)} all-gather(bf16[64,1792]{1,0:T(8,128)(2,1)S(1)} %multiply_convert_fusion.1), channel_id=1, replica_groups=mesh['section'=2,'dp'=4,'tensor'=4] {'tensor'}, dimensions={0}, use_global_device_ids=true | all-gather | bytes 1146880 | tf_op jit(solution)/shard_map/all_gather | solution.py:43
  122.4 141.5 %all-gather.6.cloned.1.call-done.feed_ref.last_ref = bf16[1792,2944]{1,0:T(8,128)(2,1)} async-done(((bf16[448,2944]{1,0:T(8,128)(2,1)}), bf16[1792,2944]{1,0:T(8,128)(2,1)}) %all-gather.6.cloned.1.call-update) | async-done | bytes 10551312 | tf_op jit(solution)/shard_map/all_gather | solution.py:521
  263.9 11.3 %shard_map.170 = (f32[256,1792]{1,0:T(8,128)S(1)}, bf16[256,1792]{1,0:T(8,128)(2,1)S(1)}) custom-call(bf16[256,1792]{1,0:T(8,128)(2,1)S(1)} %all_gather.35.near_ref, bf16[256,1792]{1,0:T(8,128)(2,1)S(1)} %collective-permute-done.8.far_ref, bf16[1792,2944]{1,0:T(8,128)(2,1)} %all-gather.6.cloned.1.call-done.feed_ref.last_ref, ...), custom_call_target="tpu_custom_call" | custom-call | flops 1048576 | bytes 65536 | tf_op jit(solution)/shard_map/pallas_call | solution.py:140
  281.6 5.0 collective-permute-done.11
  286.5 5.1 collective-permute-done.13
  293.4 12.8 %all_gather.37.near_ref = bf16[256,1792]{1,0:T(8,128)(2,1)S(1)} all-gather(bf16[64,1792]{1,0:T(8,128)(2,1)S(1)} %fusion.27), channel_id=1, replica_groups=mesh['section'=2,'dp'=4,'tensor'=4] {'tensor'}, dimensions={0}, use_global_device_ids=true | all-gather | bytes 1146880 | tf_op jit(solution)/shard_map/all_gather | solution.py:43
  307.1 4.5 slice.395.attn_ref
  312.6 8.6 %shard_map.171 = (f32[256,1792]{1,0:T(8,128)}, bf16[256,1792]{1,0:T(8,128)(2,1)}, f32[512,896]{1,0:T(8,128)}, bf16[512,256]{1,0:T(8,128)(2,1)}) custom-call(bf16[256,1792]{1,0:T(8,128)(2,1)} %copy-done.4, bf16[256,1792]{1,0:T(8,128)(2,1)} %copy-done.12, bf16[1792,1152]{1,0:T(8,128)(2,1)} %slice.395.attn_ref, f32[8,256]{1,0:T(8,128)} %pad.8.taps_ref), custom_call_target="tpu_custom_call" | custom-call | flops 1048576 | bytes 65536 | tf_op jit(solution)/shard_map/pallas_call | solution.py:425
  329.3 19.5 %all_gather.39.near_grad_ref = bf16[256,1792]{1,0:T(8,128)(2,1)S(1)} all-gather(bf16[64,1792]{1,0:T(8,128)(2,1)S(1)} %copy-done.27), channel_id=1, replica_groups=mesh['section'=2,'dp'=4,'tensor'=4] {'tensor'}, dimensions={0}, use_global_device_ids=true | all-gather | bytes 1146880 | tf_op jit(solution)/shard_map/all_gather | solution.py:43
  349.3 14.2 %all_gather.38.near_ref = bf16[256,1792]{1,0:T(8,128)(2,1)} all-gather(bf16[64,1792]{1,0:T(8,128)(2,1)S(1)} %multiply_convert_fusion), channel_id=1, replica_groups=mesh['section'=2,'dp'=4,'tensor'=4] {'tensor'}, dimensions={0}, use_global_device_ids=true | all-gather | bytes 1146880 | tf_op jit(solution)/shard_map/all_gather | solution.py:43
  363.6 18.2 %all-gather.8.cloned.1.call-done.feed_ref = bf16[1792,1792]{1,0:T(8,128)(2,1)} async-done(((bf16[448,1792]{1,0:T(8,128)(2,1)}), bf16[1792,1792]{1,0:T(8,128)(2,1)}) %all-gather.8.cloned.1.call-update) | async-done | bytes 6422544 | tf_op jit(solution)/shard_map/all_gather | solution.py:521
  381.8 16.3 %shard_map.172 = (bf16[1792,1792]{1,0:T(8,128)(2,1)}, bf16[1792,256]{1,0:T(8,128)(2,1)}, bf16[512,1280]{1,0:T(8,128)(2,1)}, bf16[512,608]{1,0:T(8,128)(2,1)}) custom-call(bf16[256,1792]{1,0:T(8,128)(2,1)} %all_gather.38.near_ref, bf16[256,1792]{1,0:T(8,128)(2,1)} %collective-permute-done.19.far_ref, bf16[256,1792]{1,0:T(8,128)(2,1)} %copy-done.23, ...), custom_call_target="tpu_custom_call" | custom-call | flops 6576668672 | bytes 20971520 | tf_op jit(solution)/shard_map/pallas_call | solution.py:246
  399.4 4.9 fusion.2
  410.8 5.0 collective-permute-done.22
  415.7 5.1 collective-permute-done.24
  422.8 13.0 %all_gather.41.near_grad_ref = bf16[256,1792]{1,0:T(8,128)(2,1)S(1)} all-gather(bf16[64,1792]{1,0:T(8,128)(2,1)S(1)} %get-tuple-element.101), channel_id=1, replica_groups=mesh['section'=2,'dp'=4,'tensor'=4] {'tensor'}, dimensions={0}, use_global_device_ids=true | all-gather | bytes 1146880 | tf_op jit(solution)/shard_map/all_gather | solution.py:43
  439.3 14.3 %shard_map.173 = (bf16[1792,1152]{1,0:T(8,128)(2,1)}, f32[256,1792]{1,0:T(8,128)}, bf16[256,1792]{1,0:T(8,128)(2,1)}, f32[8,256]{1,0:T(8,128)}) custom-call(bf16[256,1792]{1,0:T(8,128)(2,1)} %copy-done.4, bf16[256,1792]{1,0:T(8,128)(2,1)} %copy-done.12, bf16[256,1792]{1,0:T(8,128)(2,1)} %copy-done.10, bf16[256,1792]{1,0:T(8,128)(2,1)} %copy-done.21, ...), custom_call_target="tpu_custom_call" | custom-call | flops 1048576 | bytes 65536 | tf_op jit(solution)/shard_map/pallas_call | solution.py:425
  461.6 5.0 collective-permute-done.27
  466.6 3.9 collective-permute-done.29
  472.5 12.7 %all_gather.42.near_grad_ref = bf16[256,1792]{1,0:T(8,128)(2,1)S(1)} all-gather(bf16[64,1792]{1,0:T(8,128)(2,1)S(1)} %fusion.32), channel_id=1, replica_groups=mesh['section'=2,'dp'=4,'tensor'=4] {'tensor'}, dimensions={0}, use_global_device_ids=true | all-gather | bytes 1146880 | tf_op jit(solution)/shard_map/all_gather | solution.py:43
  488.6 19.3 %shard_map.174 = (bf16[1792,2944]{1,0:T(8,128)(2,1)}, bf16[1792,256]{1,0:T(8,128)(2,1)}, bf16[512,1280]{1,0:T(8,128)(2,1)}, bf16[512,608]{1,0:T(8,128)(2,1)}) custom-call(bf16[256,1792]{1,0:T(8,128)(2,1)} %copy-done, bf16[256,1792]{1,0:T(8,128)(2,1)} %copy-done.1, bf16[256,1792]{1,0:T(8,128)(2,1)} %copy-done.24, bf16[256,1792]{1,0:T(8,128)(2,1)} %copy-done.41, ...), custom_call_target="tpu_custom_call" | custom-call | flops 6576668672 | bytes 20971520 | tf_op jit(solution)/shard_map/pallas_call | solution.py:246
  510.7 4.9 fusion
  527.0 5.1 collective-permute-done.34
  534.0 13.1 %all_gather.43.near_grad_ref = bf16[256,1792]{1,0:T(8,128)(2,1)S(1)} all-gather(bf16[64,1792]{1,0:T(8,128)(2,1)S(1)} %get-tuple-element.93), channel_id=1, replica_groups=mesh['section'=2,'dp'=4,'tensor'=4] {'tensor'}, dimensions={0}, use_global_device_ids=true | all-gather | bytes 1146880 | tf_op jit(solution)/shard_map/all_gather | solution.py:43
  550.6 12.0 %shard_map.175 = (bf16[1792,768]{1,0:T(8,128)(2,1)}, f32[256,1792]{1,0:T(8,128)}, bf16[256,1792]{1,0:T(8,128)(2,1)}, f32[8,256]{1,0:T(8,128)}) custom-call(bf16[256,1792]{1,0:T(8,128)(2,1)} %copy-done.3, bf16[256,1792]{1,0:T(8,128)(2,1)} %copy-done.11, bf16[256,1792]{1,0:T(8,128)(2,1)} %copy-done.9, bf16[256,1792]{1,0:T(8,128)(2,1)} %copy-done.20, ...), custom_call_target="tpu_custom_call" | custom-call | flops 1048576 | bytes 65536 | tf_op jit(solution)/shard_map/pallas_call | solution.py:425
  562.7 2.7 fusion.44
  576.4 4.4 collective-permute-done.39
  586.2 4.3 collective-permute-done.43
  594.2 97.0 %reduce-scatter.6.cloned.1.call-done = bf16[448,2944]{1,0:T(8,128)(2,1)} async-done(((bf16[1792,2944]{1,0:T(8,128)(2,1)}), bf16[448,2944]{1,0:T(8,128)(2,1)}) %reduce-scatter.6.cloned.1.call-update) | async-done | bytes 2637840 | tf_op jit(solution)/shard_map/reduce_scatter | solution.py:481
  701.9 6.4 collective-permute-done.48
  710.6 7.1 collective-permute-done.49
  721.6 2.6 copy.30
  729.6 3.4 concatenate.241
  733.1 3.3 concatenate.246
  738.3 5.7 copy.33
  744.0 6.9 reduce-scatter.8.cloned.1.call-done
  766.2 2.6 copy.31
  (351 shorter events, 161.9 us)
Async XLA Ops:
  7.2 70.8 %all-gather.4.cloned.1.call-start = ((), (), s32[]{:S(2)}) async-start(), calls=%async_computation.3 | async-start | bytes 3440640 | tf_op jit(solution)/shard_map/all_gather | solution.py:521
  18.3 245.7 %all-gather.6.cloned.1.call-start = ((), (), s32[]{:S(2)}) async-start(), calls=%async_computation.4 | async-start | bytes 13189120 | tf_op jit(solution)/shard_map/all_gather | solution.py:521
  31.5 8.3 %collective-permute-start.9 = (bf16[448,1792]{1,0:T(8,128)(2,1)}, bf16[448,1792]{1,0:T(8,128)(2,1)}, u32[]{:S(2)}, u32[]{:S(2)}) collective-permute-start(bf16[448,1792]{1,0:T(8,128)(2,1)} %concatenate.209), channel_id=1, source_target_pairs={{0,16},{16,0},{1,17},{17,1},{2,18},{18,2},{3,19},{19,3},{4,20},{20... | collective-permute-start | bytes 4816904 | tf_op jit(solution)/shard_map/ppermute | solution.py:39
  47.3 334.5 %all-gather.8.cloned.1.call-start = ((), (), s32[]{:S(2)}) async-start(), calls=%async_computation.5 | async-start | bytes 8028160 | tf_op jit(solution)/shard_map/all_gather | solution.py:521
  84.7 2.7 collective-permute-start.4
  90.2 8.7 %collective-permute-start.5 = (bf16[64,1792]{1,0:T(8,128)(2,1)}, bf16[64,1792]{1,0:T(8,128)(2,1)S(1)}, u32[]{:S(2)}, u32[]{:S(2)}) collective-permute-start(bf16[64,1792]{1,0:T(8,128)(2,1)} %get-tuple-element.182), channel_id=1, source_target_pairs={{0,1},{1,0},{2,3},{3,2},{4,5},{5,4},{6,7},{7,6},{8,9},{9,8},{10,11... | collective-permute-start | bytes 688136 | tf_op jit(solution)/shard_map/ppermute | solution.py:66
  91.7 12.3 %collective-permute-start.7 = (bf16[64,1792]{1,0:T(8,128)(2,1)}, bf16[64,1792]{1,0:T(8,128)(2,1)S(1)}, u32[]{:S(2)}, u32[]{:S(2)}) collective-permute-start(bf16[64,1792]{1,0:T(8,128)(2,1)} %get-tuple-element.183), channel_id=1, source_target_pairs={{0,3},{1,2},{2,1},{3,0},{4,7},{5,6},{6,5},{7,4},{8,11},{9,10},{10,... | collective-permute-start | bytes 688136 | tf_op jit(solution)/shard_map/ppermute | solution.py:66
  93.1 12.0 %collective-permute-start.6 = (bf16[64,1792]{1,0:T(8,128)(2,1)S(1)}, bf16[64,1792]{1,0:T(8,128)(2,1)S(1)}, u32[]{:S(2)}, u32[]{:S(2)}) collective-permute-start(bf16[64,1792]{1,0:T(8,128)(2,1)S(1)} %get-tuple-element.184), channel_id=1, source_target_pairs={{0,2},{1,3},{2,0},{3,1},{4,6},{5,7},{6,4},{7,5},{8,10},{9,11},{10,... | collective-permute-start | bytes 688136 | tf_op jit(solution)/shard_map/ppermute | solution.py:66
  93.7 415.7 %reduce-scatter.4.cloned.1.call-start = ((), (), s32[]{:S(2)}) async-start(), calls=%async_computation.6 | async-start | bytes 8028160 | tf_op jit(solution)/shard_map/reduce_scatter | solution.py:481
  278.0 8.5 %collective-permute-start.11 = (bf16[64,1792]{1,0:T(8,128)(2,1)S(1)}, bf16[64,1792]{1,0:T(8,128)(2,1)S(1)}, u32[]{:S(2)}, u32[]{:S(2)}) collective-permute-start(bf16[64,1792]{1,0:T(8,128)(2,1)S(1)} %get-tuple-element.177), channel_id=1, source_target_pairs={{0,1},{1,0},{2,3},{3,2},{4,5},{5,4},{6,7},{7,6},{8,9},{9,8},{10,11... | collective-permute-start | bytes 688136 | tf_op jit(solution)/shard_map/ppermute | solution.py:66
  279.6 12.1 %collective-permute-start.13 = (bf16[64,1792]{1,0:T(8,128)(2,1)S(1)}, bf16[64,1792]{1,0:T(8,128)(2,1)S(1)}, u32[]{:S(2)}, u32[]{:S(2)}) collective-permute-start(bf16[64,1792]{1,0:T(8,128)(2,1)S(1)} %get-tuple-element.178), channel_id=1, source_target_pairs={{0,3},{1,2},{2,1},{3,0},{4,7},{5,6},{6,5},{7,4},{8,11},{9,10},{10,... | collective-permute-start | bytes 688136 | tf_op jit(solution)/shard_map/ppermute | solution.py:66
  281.0 12.0 %collective-permute-start.12 = (bf16[64,1792]{1,0:T(8,128)(2,1)S(1)}, bf16[64,1792]{1,0:T(8,128)(2,1)S(1)}, u32[]{:S(2)}, u32[]{:S(2)}) collective-permute-start(bf16[64,1792]{1,0:T(8,128)(2,1)S(1)} %get-tuple-element.179), channel_id=1, source_target_pairs={{0,2},{1,3},{2,0},{3,1},{4,6},{5,7},{6,4},{7,5},{8,10},{9,11},{10,... | collective-permute-start | bytes 688136 | tf_op jit(solution)/shard_map/ppermute | solution.py:66
  306.2 5.4 collective-permute-start.14
  325.7 23.1 %collective-permute-start.16 = (bf16[64,1792]{1,0:T(8,128)(2,1)S(1)}, bf16[64,1792]{1,0:T(8,128)(2,1)S(1)}, u32[]{:S(2)}, u32[]{:S(2)}) collective-permute-start(bf16[64,1792]{1,0:T(8,128)(2,1)S(1)} %get-tuple-element.174), channel_id=1, source_target_pairs={{0,1},{1,0},{2,3},{3,2},{4,5},{5,4},{6,7},{7,6},{8,9},{9,8},{10,11... | collective-permute-start | bytes 688136 | tf_op jit(solution)/shard_map/ppermute | solution.py:66
  325.8 23.1 %collective-permute-start.18 = (bf16[64,1792]{1,0:T(8,128)(2,1)S(1)}, bf16[64,1792]{1,0:T(8,128)(2,1)S(1)}, u32[]{:S(2)}, u32[]{:S(2)}) collective-permute-start(bf16[64,1792]{1,0:T(8,128)(2,1)S(1)} %get-tuple-element.175), channel_id=1, source_target_pairs={{0,3},{1,2},{2,1},{3,0},{4,7},{5,6},{6,5},{7,4},{8,11},{9,10},{10,... | collective-permute-start | bytes 688136 | tf_op jit(solution)/shard_map/ppermute | solution.py:66
  327.3 21.5 %collective-permute-start.17 = (bf16[64,1792]{1,0:T(8,128)(2,1)S(1)}, bf16[64,1792]{1,0:T(8,128)(2,1)S(1)}, u32[]{:S(2)}, u32[]{:S(2)}) collective-permute-start(bf16[64,1792]{1,0:T(8,128)(2,1)S(1)} %get-tuple-element.176), channel_id=1, source_target_pairs={{0,2},{1,3},{2,0},{3,1},{4,6},{5,7},{6,4},{7,5},{8,10},{9,11},{10,... | collective-permute-start | bytes 688136 | tf_op jit(solution)/shard_map/ppermute | solution.py:66
  348.8 14.8 %collective-permute-start.20 = (bf16[256,1792]{1,0:T(8,128)(2,1)S(1)}, bf16[256,1792]{1,0:T(8,128)(2,1)}, u32[]{:S(2)}, u32[]{:S(2)}) collective-permute-start(bf16[256,1792]{1,0:T(8,128)(2,1)S(1)} %all_gather.39.near_grad_ref), channel_id=1, source_target_pairs={{0,16},{16,0},{1,17},{17,1},{2,18},{18,2},{3,19},{19,3},{4,20},{20... | collective-permute-start | bytes 2752520 | tf_op jit(solution)/shard_map/ppermute | solution.py:39
  363.5 18.3 %collective-permute-start.19 = (bf16[256,1792]{1,0:T(8,128)(2,1)}, bf16[256,1792]{1,0:T(8,128)(2,1)}, u32[]{:S(2)}, u32[]{:S(2)}) collective-permute-start(bf16[256,1792]{1,0:T(8,128)(2,1)} %all_gather.38.near_ref), channel_id=1, source_target_pairs={{0,16},{16,0},{1,17},{17,1},{2,18},{18,2},{3,19},{19,3},{4,20},{20... | collective-permute-start | bytes 2752520 | tf_op jit(solution)/shard_map/ppermute | solution.py:39
  398.1 293.1 %reduce-scatter.6.cloned.1.call-start = ((), (), s32[]{:S(2)}) async-start(), calls=%async_computation.7 | async-start | bytes 13189120 | tf_op jit(solution)/shard_map/reduce_scatter | solution.py:481
  407.2 8.5 %collective-permute-start.22 = (bf16[64,1792]{1,0:T(8,128)(2,1)S(1)}, bf16[64,1792]{1,0:T(8,128)(2,1)S(1)}, u32[]{:S(2)}, u32[]{:S(2)}) collective-permute-start(bf16[64,1792]{1,0:T(8,128)(2,1)S(1)} %get-tuple-element.171), channel_id=1, source_target_pairs={{0,1},{1,0},{2,3},{3,2},{4,5},{5,4},{6,7},{7,6},{8,9},{9,8},{10,11... | collective-permute-start | bytes 688136 | tf_op jit(solution)/shard_map/ppermute | solution.py:66
  408.8 12.1 %collective-permute-start.24 = (bf16[64,1792]{1,0:T(8,128)(2,1)S(1)}, bf16[64,1792]{1,0:T(8,128)(2,1)S(1)}, u32[]{:S(2)}, u32[]{:S(2)}) collective-permute-start(bf16[64,1792]{1,0:T(8,128)(2,1)S(1)} %get-tuple-element.172), channel_id=1, source_target_pairs={{0,3},{1,2},{2,1},{3,0},{4,7},{5,6},{6,5},{7,4},{8,11},{9,10},{10,... | collective-permute-start | bytes 688136 | tf_op jit(solution)/shard_map/ppermute | solution.py:66
  410.2 12.0 %collective-permute-start.23 = (bf16[64,1792]{1,0:T(8,128)(2,1)S(1)}, bf16[64,1792]{1,0:T(8,128)(2,1)S(1)}, u32[]{:S(2)}, u32[]{:S(2)}) collective-permute-start(bf16[64,1792]{1,0:T(8,128)(2,1)S(1)} %get-tuple-element.173), channel_id=1, source_target_pairs={{0,2},{1,3},{2,0},{3,1},{4,6},{5,7},{6,4},{7,5},{8,10},{9,11},{10,... | collective-permute-start | bytes 688136 | tf_op jit(solution)/shard_map/ppermute | solution.py:66
  458.0 8.5 %collective-permute-start.27 = (bf16[64,1792]{1,0:T(8,128)(2,1)S(1)}, bf16[64,1792]{1,0:T(8,128)(2,1)S(1)}, u32[]{:S(2)}, u32[]{:S(2)}) collective-permute-start(bf16[64,1792]{1,0:T(8,128)(2,1)S(1)} %get-tuple-element.168), channel_id=1, source_target_pairs={{0,1},{1,0},{2,3},{3,2},{4,5},{5,4},{6,7},{7,6},{8,9},{9,8},{10,11... | collective-permute-start | bytes 688136 | tf_op jit(solution)/shard_map/ppermute | solution.py:66
  458.1 12.4 %collective-permute-start.29 = (bf16[64,1792]{1,0:T(8,128)(2,1)S(1)}, bf16[64,1792]{1,0:T(8,128)(2,1)S(1)}, u32[]{:S(2)}, u32[]{:S(2)}) collective-permute-start(bf16[64,1792]{1,0:T(8,128)(2,1)S(1)} %get-tuple-element.169), channel_id=1, source_target_pairs={{0,3},{1,2},{2,1},{3,0},{4,7},{5,6},{6,5},{7,4},{8,11},{9,10},{10,... | collective-permute-start | bytes 688136 | tf_op jit(solution)/shard_map/ppermute | solution.py:66
  459.7 12.2 %collective-permute-start.28 = (bf16[64,1792]{1,0:T(8,128)(2,1)S(1)}, bf16[64,1792]{1,0:T(8,128)(2,1)S(1)}, u32[]{:S(2)}, u32[]{:S(2)}) collective-permute-start(bf16[64,1792]{1,0:T(8,128)(2,1)S(1)} %get-tuple-element.170), channel_id=1, source_target_pairs={{0,2},{1,3},{2,0},{3,1},{4,6},{5,7},{6,4},{7,5},{8,10},{9,11},{10,... | collective-permute-start | bytes 688136 | tf_op jit(solution)/shard_map/ppermute | solution.py:66
  509.4 241.5 %reduce-scatter.8.cloned.1.call-start = ((), (), s32[]{:S(2)}) async-start(), calls=%async_computation.8 | async-start | bytes 3440640 | tf_op jit(solution)/shard_map/reduce_scatter | solution.py:481
  518.5 8.5 %collective-permute-start.32 = (bf16[64,1792]{1,0:T(8,128)(2,1)S(1)}, bf16[64,1792]{1,0:T(8,128)(2,1)S(1)}, u32[]{:S(2)}, u32[]{:S(2)}) collective-permute-start(bf16[64,1792]{1,0:T(8,128)(2,1)S(1)} %get-tuple-element.165), channel_id=1, source_target_pairs={{0,1},{1,0},{2,3},{3,2},{4,5},{5,4},{6,7},{7,6},{8,9},{9,8},{10,11... | collective-permute-start | bytes 688136 | tf_op jit(solution)/shard_map/ppermute | solution.py:66
  520.0 12.1 %collective-permute-start.34 = (bf16[64,1792]{1,0:T(8,128)(2,1)S(1)}, bf16[64,1792]{1,0:T(8,128)(2,1)S(1)}, u32[]{:S(2)}, u32[]{:S(2)}) collective-permute-start(bf16[64,1792]{1,0:T(8,128)(2,1)S(1)} %get-tuple-element.166), channel_id=1, source_target_pairs={{0,3},{1,2},{2,1},{3,0},{4,7},{5,6},{6,5},{7,4},{8,11},{9,10},{10,... | collective-permute-start | bytes 688136 | tf_op jit(solution)/shard_map/ppermute | solution.py:66
  521.5 12.0 %collective-permute-start.33 = (bf16[64,1792]{1,0:T(8,128)(2,1)S(1)}, bf16[64,1792]{1,0:T(8,128)(2,1)S(1)}, u32[]{:S(2)}, u32[]{:S(2)}) collective-permute-start(bf16[64,1792]{1,0:T(8,128)(2,1)S(1)} %get-tuple-element.167), channel_id=1, source_target_pairs={{0,2},{1,3},{2,0},{3,1},{4,6},{5,7},{6,4},{7,5},{8,10},{9,11},{10,... | collective-permute-start | bytes 688136 | tf_op jit(solution)/shard_map/ppermute | solution.py:66
  549.0 13.7 %collective-permute-start.40 = (bf16[256,1792]{1,0:T(8,128)(2,1)S(1)}, bf16[256,1792]{1,0:T(8,128)(2,1)}, u32[]{:S(2)}, u32[]{:S(2)}) collective-permute-start(bf16[256,1792]{1,0:T(8,128)(2,1)S(1)} %slice.511), channel_id=1, source_target_pairs={{0,16},{16,0},{1,17},{17,1},{2,18},{18,2},{3,19},{19,3},{4,20},{20... | collective-permute-start | bytes 2752520 | tf_op jit(solution)/shard_map/ppermute | solution.py:39
  562.5 2.9 collective-permute-start.36
  567.7 8.6 %collective-permute-start.37 = (bf16[64,1792]{1,0:T(8,128)(2,1)}, bf16[64,1792]{1,0:T(8,128)(2,1)S(1)}, u32[]{:S(2)}, u32[]{:S(2)}) collective-permute-start(bf16[64,1792]{1,0:T(8,128)(2,1)} %get-tuple-element.162), channel_id=1, source_target_pairs={{0,1},{1,0},{2,3},{3,2},{4,5},{5,4},{6,7},{7,6},{8,9},{9,8},{10,11... | collective-permute-start | bytes 688136 | tf_op jit(solution)/shard_map/ppermute | solution.py:66
  567.7 13.1 %collective-permute-start.39 = (bf16[64,1792]{1,0:T(8,128)(2,1)}, bf16[64,1792]{1,0:T(8,128)(2,1)S(1)}, u32[]{:S(2)}, u32[]{:S(2)}) collective-permute-start(bf16[64,1792]{1,0:T(8,128)(2,1)} %get-tuple-element.163), channel_id=1, source_target_pairs={{0,3},{1,2},{2,1},{3,0},{4,7},{5,6},{6,5},{7,4},{8,11},{9,10},{10,... | collective-permute-start | bytes 688136 | tf_op jit(solution)/shard_map/ppermute | solution.py:66
  569.2 13.7 %collective-permute-start.38 = (bf16[64,1792]{1,0:T(8,128)(2,1)}, bf16[64,1792]{1,0:T(8,128)(2,1)}, u32[]{:S(2)}, u32[]{:S(2)}) collective-permute-start(bf16[64,1792]{1,0:T(8,128)(2,1)} %get-tuple-element.164), channel_id=1, source_target_pairs={{0,2},{1,3},{2,0},{3,1},{4,6},{5,7},{6,4},{7,5},{8,10},{9,11},{10,... | collective-permute-start | bytes 688136 | tf_op jit(solution)/shard_map/ppermute | solution.py:66
  571.3 15.0 %collective-permute-start.41 = (bf16[64,1792]{1,0:T(8,128)(2,1)S(1)}, bf16[64,1792]{1,0:T(8,128)(2,1)S(1)}, u32[]{:S(2)}, u32[]{:S(2)}) collective-permute-start(bf16[64,1792]{1,0:T(8,128)(2,1)S(1)} %get-tuple-element.159), channel_id=1, source_target_pairs={{0,1},{1,0},{2,3},{3,2},{4,5},{5,4},{6,7},{7,6},{8,9},{9,8},{10,11... | collective-permute-start | bytes 688136 | tf_op jit(solution)/shard_map/ppermute | solution.py:66
  571.4 19.1 %collective-permute-start.43 = (bf16[64,1792]{1,0:T(8,128)(2,1)S(1)}, bf16[64,1792]{1,0:T(8,128)(2,1)S(1)}, u32[]{:S(2)}, u32[]{:S(2)}) collective-permute-start(bf16[64,1792]{1,0:T(8,128)(2,1)S(1)} %get-tuple-element.160), channel_id=1, source_target_pairs={{0,3},{1,2},{2,1},{3,0},{4,7},{5,6},{6,5},{7,4},{8,11},{9,10},{10,... | collective-permute-start | bytes 688136 | tf_op jit(solution)/shard_map/ppermute | solution.py:66
  576.3 15.5 %collective-permute-start.42 = (bf16[64,1792]{1,0:T(8,128)(2,1)S(1)}, bf16[64,1792]{1,0:T(8,128)(2,1)S(1)}, u32[]{:S(2)}, u32[]{:S(2)}) collective-permute-start(bf16[64,1792]{1,0:T(8,128)(2,1)S(1)} %get-tuple-element.161), channel_id=1, source_target_pairs={{0,2},{1,3},{2,0},{3,1},{4,6},{5,7},{6,4},{7,5},{8,10},{9,11},{10,... | collective-permute-start | bytes 688136 | tf_op jit(solution)/shard_map/ppermute | solution.py:66
  584.6 106.7 %collective-permute-start.45 = (f32[2,5,1792]{2,0,1:T(2,128)S(1)}, f32[2,5,1792]{2,0,1:T(2,128)S(1)}, u32[]{:S(2)}, u32[]{:S(2)}) collective-permute-start(f32[2,5,1792]{2,0,1:T(2,128)S(1)} %pad_maximum_fusion.5), channel_id=1, source_target_pairs={{0,16},{16,0},{1,17},{17,1},{2,18},{18,2},{3,19},{19,3},{4,20},{20... | collective-permute-start | bytes 215048 | tf_op jit(solution)/shard_map/ppermute | solution.py:76
  691.4 4.4 collective-permute-start.46
  694.3 24.7 %collective-permute-start.44 = (f32[64,1792]{1,0:T(8,128)S(1)}, f32[64,1792]{1,0:T(8,128)S(1)}, u32[]{:S(2)}, u32[]{:S(2)}) collective-permute-start(f32[64,1792]{1,0:T(8,128)S(1)} %broadcast_select_fusion.14), channel_id=1, source_target_pairs={{0,16},{16,0},{1,17},{17,1},{2,18},{18,2},{3,19},{19,3},{4,20},{20... | collective-permute-start | bytes 1376264 | tf_op jit(solution)/shard_map/ppermute | solution.py:39
  695.9 4.4 collective-permute-start.47
  697.6 26.6 %collective-permute-start.53 = (bf16[448,1792]{1,0:T(8,128)(2,1)S(1)}, bf16[448,1792]{1,0:T(8,128)(2,1)S(1)}, u32[]{:S(2)}, u32[]{:S(2)}) collective-permute-start(bf16[448,1792]{1,0:T(8,128)(2,1)S(1)} %broadcast_select_fusion.2), channel_id=1, source_target_pairs={{0,16},{16,0},{1,17},{17,1},{2,18},{18,2},{3,19},{19,3},{4,20},{20... | collective-permute-start | bytes 4816904 | tf_op jit(solution)/shard_map/ppermute | solution.py:39
  700.3 7.9 %collective-permute-start.48 = (f32[2,5,1792]{2,0,1:T(2,128)S(1)}, f32[2,5,1792]{2,0,1:T(2,128)S(1)}, u32[]{:S(2)}, u32[]{:S(2)}) collective-permute-start(f32[2,5,1792]{2,0,1:T(2,128)S(1)} %add.331), channel_id=1, source_target_pairs={{0,4},{4,0},{8,12},{12,8},{1,5},{5,1},{9,13},{13,9},{2,6},{6,2},{1... | collective-permute-start | bytes 215048 | tf_op jit(solution)/shard_map/ppermute | solution.py:76
  708.3 9.4 %collective-permute-start.49 = (f32[2,5,1792]{2,0,1:T(2,128)S(1)}, f32[2,5,1792]{2,0,1:T(2,128)S(1)}, u32[]{:S(2)}, u32[]{:S(2)}) collective-permute-start(f32[2,5,1792]{2,0,1:T(2,128)S(1)} %add.332), channel_id=1, source_target_pairs={{0,8},{4,12},{8,0},{12,4},{1,9},{5,13},{9,1},{13,5},{2,10},{6,14},... | collective-permute-start | bytes 215048 | tf_op jit(solution)/shard_map/ppermute | solution.py:76
  710.6 9.4 %collective-permute-start.51 = (bf16[448,448]{1,0:T(8,128)(2,1)S(1)}, bf16[448,448]{1,0:T(8,128)(2,1)S(1)}, u32[]{:S(2)}, u32[]{:S(2)}) collective-permute-start(bf16[448,448]{1,0:T(8,128)(2,1)S(1)} %slice.341), channel_id=1, source_target_pairs={{0,16},{16,0},{1,17},{17,1},{2,18},{18,2},{3,19},{19,3},{4,20},{20... | collective-permute-start | bytes 1204232 | tf_op jit(solution)/shard_map/ppermute | solution.py:39
  752.0 8.0 %collective-permute-start.50 = (bf16[448,64]{1,0:T(8,128)(2,1)S(1)}, bf16[448,64]{1,0:T(8,128)(2,1)S(1)}, u32[]{:S(2)}, u32[]{:S(2)}) collective-permute-start(bf16[448,64]{1,0:T(8,128)(2,1)S(1)} %slice.411), channel_id=1, source_target_pairs={{0,16},{16,0},{1,17},{17,1},{2,18},{18,2},{3,19},{19,3},{4,20},{20... | collective-permute-start | bytes 172040 | tf_op jit(solution)/shard_map/ppermute | solution.py:39
  753.1 3.9 collective-permute-start.54
  757.0 5.3 collective-permute-start.52
  (60 other events, 1566.9 us)
Sparse Core Ops, SparseCore 0:
  18.4 59.5 all-gather.3
  80.2 183.7 all-gather.5
  266.1 115.6 all-gather.7
  398.3 111.0 reduce-scatter.3
  511.6 179.5 reduce-scatter.5
  693.4 57.4 reduce-scatter.7

commit v6 on v5

--- a/solution.py
+++ b/solution.py
@@ -466,8 +466,74 @@
     return whole_call(functools.partial(mixer_back_kernel, channels, first), inputs, shapes, scratch, 2**20)
 
 
+def end_kernel(
+    channels, units, tail, core_ref, mine_ref, other_ref, low_ref, high_ref, kept_ref,
+    vgate_ref, out_ref, pair_ref, down_ref,
+):
+    step = pl.program_id(0)
+    lower = core_ref[0] == 0
+    mine, other = (ref[...].astype(jnp.float32) for ref in (mine_ref, other_ref))
+    low = jnp.where(lower, mine, low_ref[...].astype(jnp.float32))
+    high = jnp.where(lower, other, high_ref[...].astype(jnp.float32))
+    size = mine.shape[1]
+    wide = pair_ref.shape[1] // 2
+
+    @pl.when(step == 0)
+    def _():
+        for place in range(2):
+            parts = [take(block, place * channels, channels) for block in (low, high)]
+            empty = jnp.zeros_like(parts[0])
+            first = jnp.concatenate([parts[0], empty], axis=1)
+            second = pltpu.roll(jnp.concatenate([parts[1], empty], axis=1), channels, 1)
+            vgate_ref[:, place, :] = (first + second)[:, : 2 * channels]
+        for place, block in enumerate((low, high)):
+            turned = jnp.swapaxes(block[:, size - WIDE :], 0, 1)
+            out_ref[pl.ds(place * channels, channels), :] = turned[:channels]
+        for place, block in enumerate((jnp.where(lower, mine, other), jnp.where(lower, other, mine))):
+            turned = jnp.swapaxes(block[:, size - WIDE - LANES : size - WIDE], 0, 1)
+            for half in range(2):
+                start = LANES - (2 - half) * wide
+                pair_ref[half, pl.ds(place * wide, wide), :] = turned[start : start + wide]
+
+    for place, block in enumerate((low, high)):
+
+        @pl.when(step == place)
+        def _(place=place, block=block):
+            stop = units * (place + 1) % LANES or LANES
+            last = block[:, size - LANES :]
+            if stop < LANES:
+                last = pltpu.roll(last, stop, 1)
+            column = lanes(last)
+            inside = (column >= stop - tail) & (column < stop)
+            down_ref[...] = jnp.where(inside, last, kept_ref[...])
+
+
+def end_call(channels, tail, width, core, mine, other, low, high, down):
+    count, size = mine.shape
+    units = down.shape[1] // 2
+    first, second = (units - 1) // LANES, (2 * units - 1) // LANES
+
+    def whole(shape):
+        return pl.BlockSpec(shape, lambda step: (0,) * len(shape))
+
+    tile = pl.BlockSpec((count, LANES), lambda step: (0, first + step * (second - first)))
+    shapes = ((count, 2, 2 * channels), (2 * channels, count), (2, width, count))
+    return pl.pallas_call(
+        functools.partial(end_kernel, channels, units, tail),
+        grid=(2,),
+        out_shape=[jax.ShapeDtypeStruct(shape, jnp.float32) for shape in (*shapes, down.shape)],
+        in_specs=[pl.BlockSpec(memory_space=pltpu.SMEM)]
+        + [whole((count, size))] * 4
+        + [tile],
+        out_specs=[whole(shape) for shape in shapes] + [tile],
+        input_output_aliases={5: 3},
+        compiler_params=pltpu.CompilerParams(vmem_limit_bytes=48 * 2**20),
+        cost_estimate=pl.CostEstimate(flops=2**20, bytes_accessed=2**27, transcendentals=0),
+    )(core.reshape(1), mine, other, low, high, down)
+
+
 def by_rows(block):
-    return with_layout_constraint(block, Layout(major_to_minor=(0, 1)))
+    return with_layout_constraint(block, Layout(major_to_minor=tuple(range(block.ndim))))
 
 
 class Queue:
@@ -641,49 +707,50 @@
             [halves(low[:, :size], high[:, :size], 1), halves(low[:, size:], high[:, size:], 1)], axis=1
         )
 
-    def split_pair(grads, tail):
-        both = 2 * channels
-        stop = grads.shape[1] - tail
-        rest = jnp.concatenate([grads[:, :both], grads[:, stop - channels : stop]], axis=1)
-        return (rest, grads[:, both : stop - channels], grads[:, stop:])
-
-    attn_zero, pair_zero, down_zero = split_pair(grads_zero[1], tail)
-    attn_one, pair_one, down_one = split_pair(grads_one[1], tail)
-    low, high = home(attn_zero, attn_one)
-    vgate_grad = jnp.stack(
-        [
-            halves(low[:, :channels], high[:, :channels], 1),
-            halves(low[:, channels : 2 * channels], high[:, channels : 2 * channels], 1),
-        ],
+    last = grads_zero[1]
+    early = grads_one[1]
+    both = 2 * channels
+    gap = last.shape[1] - both - WIDE
+    own = jnp.concatenate(
+        [early[:, :both], jnp.zeros((early.shape[0], gap), early.dtype), early[:, early.shape[1] - WIDE :]],
         axis=1,
     )
-    out_grad = halves(low[:, 2 * channels :].T, high[:, 2 * channels :].T, 0)
-    low_tail, high_tail = home(down_zero, down_one)
-
-    def unpack(block, last):
+    away = swap(own)
+
+    def unpack(block):
         wide = block[:, main:]
         (gate, upper), (gate_rest, upper_rest) = gates(wide, units)
-        down = jnp.concatenate([block[:, :main], wide[:, 2 * units :], last], axis=1)
+        empty = jnp.zeros((block.shape[0], tail), block.dtype)
+        down = jnp.concatenate([block[:, :main], wide[:, 2 * units :], empty], axis=1)
         return (
             jnp.concatenate([gate, gate_rest], axis=1),
             jnp.concatenate([upper, upper_rest], axis=1),
-            down.T,
+            down,
         )
 
     low, high = home(grads_zero[0], grads_one[0])
-    low, high = unpack(low, low_tail), unpack(high, high_tail)
+    low, high = unpack(low), unpack(high)
     gate_up_grad = jnp.stack([halves(low[0], high[0], 1), halves(low[1], high[1], 1)], axis=1)
-    down_grad = halves(low[2], high[2], 0)
+    down_grad = by_rows(halves(low[2], high[2], 1))
+    win_grad = by_rows(pair_home(early[:, both : early.shape[1] - WIDE]))
+    gate_up_grad = by_rows(gate_up_grad)
+    low, high = jnp.where(lower, own, away), jnp.where(lower, away, own)
+    last, low, high, gate_up_grad, down_grad, win_grad, ends, sums = lax.optimization_barrier(
+        (last, low, high, gate_up_grad, down_grad, win_grad, ends, sums)
+    )
+    vgate_grad, out_grad, pair_grad, down_grad = end_call(
+        channels, tail, gap, core, last, swap(last), low, high, down_grad
+    )
     return (
         ends[None],
         sums[:, :2],
         sums[:, 2:],
-        pair_home(pair_zero),
-        pair_home(pair_one),
+        jnp.transpose(pair_grad, (2, 0, 1)),
+        win_grad,
         vgate_grad[None],
         out_grad[None],
         gate_up_grad[None],
-        down_grad[None],
+        down_grad.T[None],
     )
 
 

time: 781 us -> 769 us (0.985)
  waiting for transfers between devices: 387 us -> 372 us
    unnamed x101 -> x82, local copies, waits for them, and re-layouts: 24.6 us -> 13.2 us
    ppermute x24, waiting for transfers between devices: 69.8 us -> 60.2 us  [collect_pair(): total = total + lax.ppermute(block, 'tensor', pairs).astype(jnp.float32)]
    ppermute x26 -> x25, waiting for transfers between devices: 24.9 us -> 29 us  [swap(): return lax.ppermute(block, 'section', [(0, 1), (1, 0)])]
  transfers between devices with their start and end apart: 61 -> 60, of which waited for: 43 -> 39; matrix products, arithmetic and copies ran while one was open for 14% -> 15% of each run, Pallas kernels for 9% -> 9%
where the time goes in v6:
time: 769 us; the launch traced here: 764 us
  waiting for transfers between devices  372 us (48%)
  blocking collectives  113 us (15%)
  Pallas kernels  93.2 us (12%)
  local copies, waits for them, and re-layouts  80.3 us (10%)
  starting transfers between devices  40 us (5%)
  other arithmetic  36.4 us (5%)
  between operations  15.5 us (2%)
  matrix products  13.2 us (2%)
    all_gather x3, waiting for transfers between devices, fetch(): return lax.all_gather(piece, 'dp', axis=0, tiled=True)  167 us
    all_gather x8, blocking collectives, spread_pair(): lax.all_gather(rows.astype(jnp.bfloat16), 'tensor', axis=0, tiled=True)  113 us
    reduce_scatter x3, waiting for transfers between devices, scatter(): lax.psum_scatter(block, 'dp', scatter_dimension=0, tiled=True)  101 us
    ppermute x24, waiting for transfers between devices, collect_pair(): total = total + lax.ppermute(block, 'tensor', pairs).astype(jnp.float32)  60.2 us
    pallas_call x4, Pallas kernels, whole_call(): pl.pallas_call(kernel, grid=(1,), out_shape=[jax.ShapeDtypeStruct(shape,...  41.6 us
    pallas_call x2, Pallas kernels, feed_both(): pl.pallas_call(functools.partial(feed_kernel, units, tail), grid=(1,), ou...  35.6 us
    ppermute x25, waiting for transfers between devices, swap(): return lax.ppermute(block, 'section', [(0, 1), (1, 0)])  29 us
    ppermute x24, starting transfers between devices, collect_pair(): total = total + lax.ppermute(block, 'tensor', pairs).astype(jnp.float32)  28.3 us
  transfers between devices with their start and end apart: 60, of which 39 were waited for; matrix products, arithmetic and copies ran while one was open for 15% of the time, Pallas kernels for 9%

profile of v6, /device:TPU:0, one launch (start us, length us, event | category | flops | bytes accessed | tf_op | source)
XLA Modules:
  0.0 763.9 jit_solution(13210583771013705065)
XLA Ops:
  18.6 6.0 constant_dynamic-slice_fusion.25
  26.4 3.6 concatenate.105
  33.4 3.0 constant_dynamic-slice_fusion.24
  38.2 2.8 broadcast_select_fusion.4
  41.0 4.7 concatenate.106
  49.6 14.9 %all_gather.33.near_ref = bf16[256,1792]{1,0:T(8,128)(2,1)S(1)} all-gather(bf16[64,1792]{1,0:T(8,128)(2,1)S(1)} %fusion.18), channel_id=1, replica_groups=mesh['section'=2,'dp'=4,'tensor'=4] {'tensor'}, dimensions={0}, use_global_device_ids=true | all-gather | bytes 1146880 | tf_op jit(solution)/shard_map/all_gather | solution.py:43
  67.0 9.5 %all-gather.4.cloned.1.call-done.attn_ref.last_ref = bf16[1792,768]{1,0:T(8,128)(2,1)} async-done(((bf16[448,768]{1,0:T(8,128)(2,1)}), bf16[1792,768]{1,0:T(8,128)(2,1)}) %all-gather.4.cloned.1.call-update) | async-done | bytes 2752528 | tf_op jit(solution)/shard_map/all_gather | solution.py:587
  76.5 6.7 shard_map.169
  93.5 5.1 collective-permute-done.5
  98.6 5.2 collective-permute-done.7
  107.2 12.8 %all_gather.35.near_ref = bf16[256,1792]{1,0:T(8,128)(2,1)S(1)} all-gather(bf16[64,1792]{1,0:T(8,128)(2,1)S(1)} %multiply_convert_fusion.1), channel_id=1, replica_groups=mesh['section'=2,'dp'=4,'tensor'=4] {'tensor'}, dimensions={0}, use_global_device_ids=true | all-gather | bytes 1146880 | tf_op jit(solution)/shard_map/all_gather | solution.py:43
  122.5 139.9 %all-gather.6.cloned.1.call-done.feed_ref.last_ref = bf16[1792,2944]{1,0:T(8,128)(2,1)} async-done(((bf16[448,2944]{1,0:T(8,128)(2,1)}), bf16[1792,2944]{1,0:T(8,128)(2,1)}) %all-gather.6.cloned.1.call-update) | async-done | bytes 10551312 | tf_op jit(solution)/shard_map/all_gather | solution.py:587
  262.4 11.3 %shard_map.170 = (f32[256,1792]{1,0:T(8,128)S(1)}, bf16[256,1792]{1,0:T(8,128)(2,1)S(1)}) custom-call(bf16[256,1792]{1,0:T(8,128)(2,1)S(1)} %all_gather.35.near_ref, bf16[256,1792]{1,0:T(8,128)(2,1)S(1)} %collective-permute-done.8.far_ref, bf16[1792,2944]{1,0:T(8,128)(2,1)} %all-gather.6.cloned.1.call-done.feed_ref.last_ref, ...), custom_call_target="tpu_custom_call" | custom-call | flops 1048576 | bytes 65536 | tf_op jit(solution)/shard_map/pallas_call | solution.py:140
  280.0 5.0 collective-permute-done.11
  285.0 5.1 collective-permute-done.13
  291.9 12.8 %all_gather.37.near_ref = bf16[256,1792]{1,0:T(8,128)(2,1)S(1)} all-gather(bf16[64,1792]{1,0:T(8,128)(2,1)S(1)} %fusion.25), channel_id=1, replica_groups=mesh['section'=2,'dp'=4,'tensor'=4] {'tensor'}, dimensions={0}, use_global_device_ids=true | all-gather | bytes 1146880 | tf_op jit(solution)/shard_map/all_gather | solution.py:43
  305.6 4.5 slice.334.attn_ref
  311.0 8.6 %shard_map.171 = (f32[256,1792]{1,0:T(8,128)}, bf16[256,1792]{1,0:T(8,128)(2,1)}, f32[512,896]{1,0:T(8,128)}, bf16[512,256]{1,0:T(8,128)(2,1)}) custom-call(bf16[256,1792]{1,0:T(8,128)(2,1)} %copy-done.5, bf16[256,1792]{1,0:T(8,128)(2,1)} %copy-done.11, bf16[1792,1152]{1,0:T(8,128)(2,1)} %slice.334.attn_ref, f32[8,256]{1,0:T(8,128)} %pad.8.taps_ref), custom_call_target="tpu_custom_call" | custom-call | flops 1048576 | bytes 65536 | tf_op jit(solution)/shard_map/pallas_call | solution.py:425
  327.8 19.5 %all_gather.39.near_grad_ref = bf16[256,1792]{1,0:T(8,128)(2,1)S(1)} all-gather(bf16[64,1792]{1,0:T(8,128)(2,1)S(1)} %copy-done.24), channel_id=1, replica_groups=mesh['section'=2,'dp'=4,'tensor'=4] {'tensor'}, dimensions={0}, use_global_device_ids=true | all-gather | bytes 1146880 | tf_op jit(solution)/shard_map/all_gather | solution.py:43
  347.7 14.3 %all_gather.38.near_ref = bf16[256,1792]{1,0:T(8,128)(2,1)} all-gather(bf16[64,1792]{1,0:T(8,128)(2,1)S(1)} %multiply_convert_fusion), channel_id=1, replica_groups=mesh['section'=2,'dp'=4,'tensor'=4] {'tensor'}, dimensions={0}, use_global_device_ids=true | all-gather | bytes 1146880 | tf_op jit(solution)/shard_map/all_gather | solution.py:43
  362.1 18.2 %all-gather.8.cloned.1.call-done.feed_ref = bf16[1792,1792]{1,0:T(8,128)(2,1)} async-done(((bf16[448,1792]{1,0:T(8,128)(2,1)}), bf16[1792,1792]{1,0:T(8,128)(2,1)}) %all-gather.8.cloned.1.call-update) | async-done | bytes 6422544 | tf_op jit(solution)/shard_map/all_gather | solution.py:587
  380.2 16.4 %shard_map.172 = (bf16[1792,1792]{1,0:T(8,128)(2,1)}, bf16[1792,256]{1,0:T(8,128)(2,1)}, bf16[512,1280]{1,0:T(8,128)(2,1)}, bf16[512,608]{1,0:T(8,128)(2,1)}) custom-call(bf16[256,1792]{1,0:T(8,128)(2,1)} %all_gather.38.near_ref, bf16[256,1792]{1,0:T(8,128)(2,1)} %collective-permute-done.19.far_ref, bf16[256,1792]{1,0:T(8,128)(2,1)} %copy-done.20, ...), custom_call_target="tpu_custom_call" | custom-call | flops 6576668672 | bytes 20971520 | tf_op jit(solution)/shard_map/pallas_call | solution.py:246
  397.9 4.9 fusion.2
  409.3 5.0 collective-permute-done.22
  414.2 5.1 collective-permute-done.24
  421.2 13.0 %all_gather.41.near_grad_ref = bf16[256,1792]{1,0:T(8,128)(2,1)S(1)} all-gather(bf16[64,1792]{1,0:T(8,128)(2,1)S(1)} %get-tuple-element.163), channel_id=1, replica_groups=mesh['section'=2,'dp'=4,'tensor'=4] {'tensor'}, dimensions={0}, use_global_device_ids=true | all-gather | bytes 1146880 | tf_op jit(solution)/shard_map/all_gather | solution.py:43
  437.8 14.3 %shard_map.173 = (bf16[1792,1152]{1,0:T(8,128)(2,1)}, f32[256,1792]{1,0:T(8,128)}, bf16[256,1792]{1,0:T(8,128)(2,1)}, f32[8,256]{1,0:T(8,128)}) custom-call(bf16[256,1792]{1,0:T(8,128)(2,1)} %copy-done.5, bf16[256,1792]{1,0:T(8,128)(2,1)} %copy-done.11, bf16[256,1792]{1,0:T(8,128)(2,1)} %copy-done.9, bf16[256,1792]{1,0:T(8,128)(2,1)} %copy-done.18, ...), custom_call_target="tpu_custom_call" | custom-call | flops 1048576 | bytes 65536 | tf_op jit(solution)/shard_map/pallas_call | solution.py:425
  460.1 5.0 collective-permute-done.27
  465.0 3.9 collective-permute-done.29
  470.9 12.7 %all_gather.42.near_grad_ref = bf16[256,1792]{1,0:T(8,128)(2,1)S(1)} all-gather(bf16[64,1792]{1,0:T(8,128)(2,1)S(1)} %fusion.30), channel_id=1, replica_groups=mesh['section'=2,'dp'=4,'tensor'=4] {'tensor'}, dimensions={0}, use_global_device_ids=true | all-gather | bytes 1146880 | tf_op jit(solution)/shard_map/all_gather | solution.py:43
  487.0 19.3 %shard_map.174 = (bf16[1792,2944]{1,0:T(8,128)(2,1)}, bf16[1792,256]{1,0:T(8,128)(2,1)}, bf16[512,1280]{1,0:T(8,128)(2,1)}, bf16[512,608]{1,0:T(8,128)(2,1)}) custom-call(bf16[256,1792]{1,0:T(8,128)(2,1)} %copy-done, bf16[256,1792]{1,0:T(8,128)(2,1)} %copy-done.1, bf16[256,1792]{1,0:T(8,128)(2,1)} %copy-done.21, bf16[256,1792]{1,0:T(8,128)(2,1)} %copy-done.34, ...), custom_call_target="tpu_custom_call" | custom-call | flops 6576668672 | bytes 20971520 | tf_op jit(solution)/shard_map/pallas_call | solution.py:246
  509.2 4.9 fusion
  520.5 5.0 collective-permute-done.32
  525.5 5.1 collective-permute-done.34
  532.5 13.0 %all_gather.43.near_grad_ref = bf16[256,1792]{1,0:T(8,128)(2,1)S(1)} all-gather(bf16[64,1792]{1,0:T(8,128)(2,1)S(1)} %get-tuple-element.155), channel_id=1, replica_groups=mesh['section'=2,'dp'=4,'tensor'=4] {'tensor'}, dimensions={0}, use_global_device_ids=true | all-gather | bytes 1146880 | tf_op jit(solution)/shard_map/all_gather | solution.py:43
  548.9 12.0 %shard_map.175 = (bf16[1792,768]{1,0:T(8,128)(2,1)}, f32[256,1792]{1,0:T(8,128)}, bf16[256,1792]{1,0:T(8,128)(2,1)}, f32[8,256]{1,0:T(8,128)}) custom-call(bf16[256,1792]{1,0:T(8,128)(2,1)} %copy-done.4, bf16[256,1792]{1,0:T(8,128)(2,1)} %copy-done.10, bf16[256,1792]{1,0:T(8,128)(2,1)} %copy-done.8, bf16[256,1792]{1,0:T(8,128)(2,1)} %copy-done.17, ...), custom_call_target="tpu_custom_call" | custom-call | flops 1048576 | bytes 65536 | tf_op jit(solution)/shard_map/pallas_call | solution.py:425
  568.6 3.5 fusion.4
  590.2 11.3 %collective-permute-done.50 = f32[2,5,1792]{2,0,1:T(2,128)S(1)} collective-permute-done((f32[2,5,1792]{2,0,1:T(2,128)S(1)}, f32[2,5,1792]{2,0,1:T(2,128)S(1)}, u32[]{:S(2)}, u32[]{:S(2)}) %collective-permute-start.50) | collective-permute-done | bytes 71712 | tf_op jit(solution)/shard_map/ppermute | solution.py:76
  603.1 88.1 %reduce-scatter.6.cloned.1.call-done = bf16[448,2944]{1,0:T(8,128)(2,1)} async-done(((bf16[1792,2944]{1,0:T(8,128)(2,1)}), bf16[448,2944]{1,0:T(8,128)(2,1)}) %reduce-scatter.6.cloned.1.call-update) | async-done | bytes 2637840 | tf_op jit(solution)/shard_map/reduce_scatter | solution.py:547
  694.0 3.5 collective-permute-start.52
  697.8 3.4 collective-permute-done.52
  706.2 5.3 maximum_convert_fusion.1
  715.8 3.2 concatenate.118
  719.0 2.8 convert_element_type.252.kept_ref
  726.9 3.3 concatenate.117
  731.9 5.7 copy.82
  737.5 11.1 %reduce-scatter.8.cloned.1.call-done.mine_ref = bf16[448,768]{1,0:T(8,128)(2,1)} async-done(((bf16[1792,768]{1,0:T(8,128)(2,1)}), bf16[448,768]{1,0:T(8,128)(2,1)}) %reduce-scatter.8.cloned.1.call-update) | async-done | bytes 688144 | tf_op jit(solution)/shard_map/reduce_scatter | solution.py:547
  752.1 4.7 shard_map.176
  (326 shorter events, 149.9 us)
Async XLA Ops:
  7.2 69.3 %all-gather.4.cloned.1.call-start = ((), (), s32[]{:S(2)}) async-start(), calls=%async_computation.3 | async-start | bytes 3440640 | tf_op jit(solution)/shard_map/all_gather | solution.py:587
  16.7 245.7 %all-gather.6.cloned.1.call-start = ((), (), s32[]{:S(2)}) async-start(), calls=%async_computation.4 | async-start | bytes 13189120 | tf_op jit(solution)/shard_map/all_gather | solution.py:587
  29.9 8.3 %collective-permute-start.9 = (bf16[448,1792]{1,0:T(8,128)(2,1)}, bf16[448,1792]{1,0:T(8,128)(2,1)}, u32[]{:S(2)}, u32[]{:S(2)}) collective-permute-start(bf16[448,1792]{1,0:T(8,128)(2,1)} %concatenate.105), channel_id=1, source_target_pairs={{0,16},{16,0},{1,17},{17,1},{2,18},{18,2},{3,19},{19,3},{4,20},{20... | collective-permute-start | bytes 4816904 | tf_op jit(solution)/shard_map/ppermute | solution.py:39
  45.7 334.5 %all-gather.8.cloned.1.call-start = ((), (), s32[]{:S(2)}) async-start(), calls=%async_computation.5 | async-start | bytes 8028160 | tf_op jit(solution)/shard_map/all_gather | solution.py:587
  83.2 2.7 collective-permute-start.4
  89.9 8.7 %collective-permute-start.5 = (bf16[64,1792]{1,0:T(8,128)(2,1)}, bf16[64,1792]{1,0:T(8,128)(2,1)S(1)}, u32[]{:S(2)}, u32[]{:S(2)}) collective-permute-start(bf16[64,1792]{1,0:T(8,128)(2,1)} %get-tuple-element.240), channel_id=1, source_target_pairs={{0,1},{1,0},{2,3},{3,2},{4,5},{5,4},{6,7},{7,6},{8,9},{9,8},{10,11... | collective-permute-start | bytes 688136 | tf_op jit(solution)/shard_map/ppermute | solution.py:66
  91.4 12.3 %collective-permute-start.7 = (bf16[64,1792]{1,0:T(8,128)(2,1)}, bf16[64,1792]{1,0:T(8,128)(2,1)S(1)}, u32[]{:S(2)}, u32[]{:S(2)}) collective-permute-start(bf16[64,1792]{1,0:T(8,128)(2,1)} %get-tuple-element.241), channel_id=1, source_target_pairs={{0,3},{1,2},{2,1},{3,0},{4,7},{5,6},{6,5},{7,4},{8,11},{9,10},{10,... | collective-permute-start | bytes 688136 | tf_op jit(solution)/shard_map/ppermute | solution.py:66
  92.9 12.2 %collective-permute-start.6 = (bf16[64,1792]{1,0:T(8,128)(2,1)}, bf16[64,1792]{1,0:T(8,128)(2,1)S(1)}, u32[]{:S(2)}, u32[]{:S(2)}) collective-permute-start(bf16[64,1792]{1,0:T(8,128)(2,1)} %get-tuple-element.242), channel_id=1, source_target_pairs={{0,2},{1,3},{2,0},{3,1},{4,6},{5,7},{6,4},{7,5},{8,10},{9,11},{10,... | collective-permute-start | bytes 688136 | tf_op jit(solution)/shard_map/ppermute | solution.py:66
  93.4 414.5 %reduce-scatter.4.cloned.1.call-start = ((), (), s32[]{:S(2)}) async-start(), calls=%async_computation.6 | async-start | bytes 8028160 | tf_op jit(solution)/shard_map/reduce_scatter | solution.py:547
  273.7 2.5 collective-permute-start.10
  276.5 8.5 %collective-permute-start.11 = (bf16[64,1792]{1,0:T(8,128)(2,1)S(1)}, bf16[64,1792]{1,0:T(8,128)(2,1)S(1)}, u32[]{:S(2)}, u32[]{:S(2)}) collective-permute-start(bf16[64,1792]{1,0:T(8,128)(2,1)S(1)} %get-tuple-element.235), channel_id=1, source_target_pairs={{0,1},{1,0},{2,3},{3,2},{4,5},{5,4},{6,7},{7,6},{8,9},{9,8},{10,11... | collective-permute-start | bytes 688136 | tf_op jit(solution)/shard_map/ppermute | solution.py:66
  278.0 12.1 %collective-permute-start.13 = (bf16[64,1792]{1,0:T(8,128)(2,1)S(1)}, bf16[64,1792]{1,0:T(8,128)(2,1)S(1)}, u32[]{:S(2)}, u32[]{:S(2)}) collective-permute-start(bf16[64,1792]{1,0:T(8,128)(2,1)S(1)} %get-tuple-element.236), channel_id=1, source_target_pairs={{0,3},{1,2},{2,1},{3,0},{4,7},{5,6},{6,5},{7,4},{8,11},{9,10},{10,... | collective-permute-start | bytes 688136 | tf_op jit(solution)/shard_map/ppermute | solution.py:66
  279.5 12.0 %collective-permute-start.12 = (bf16[64,1792]{1,0:T(8,128)(2,1)S(1)}, bf16[64,1792]{1,0:T(8,128)(2,1)S(1)}, u32[]{:S(2)}, u32[]{:S(2)}) collective-permute-start(bf16[64,1792]{1,0:T(8,128)(2,1)S(1)} %get-tuple-element.237), channel_id=1, source_target_pairs={{0,2},{1,3},{2,0},{3,1},{4,6},{5,7},{6,4},{7,5},{8,10},{9,11},{10,... | collective-permute-start | bytes 688136 | tf_op jit(solution)/shard_map/ppermute | solution.py:66
  304.7 5.4 collective-permute-start.14
  319.7 2.7 collective-permute-start.15
  324.2 23.1 %collective-permute-start.16 = (bf16[64,1792]{1,0:T(8,128)(2,1)S(1)}, bf16[64,1792]{1,0:T(8,128)(2,1)S(1)}, u32[]{:S(2)}, u32[]{:S(2)}) collective-permute-start(bf16[64,1792]{1,0:T(8,128)(2,1)S(1)} %get-tuple-element.232), channel_id=1, source_target_pairs={{0,1},{1,0},{2,3},{3,2},{4,5},{5,4},{6,7},{7,6},{8,9},{9,8},{10,11... | collective-permute-start | bytes 688136 | tf_op jit(solution)/shard_map/ppermute | solution.py:66
  324.3 23.0 %collective-permute-start.18 = (bf16[64,1792]{1,0:T(8,128)(2,1)S(1)}, bf16[64,1792]{1,0:T(8,128)(2,1)S(1)}, u32[]{:S(2)}, u32[]{:S(2)}) collective-permute-start(bf16[64,1792]{1,0:T(8,128)(2,1)S(1)} %get-tuple-element.233), channel_id=1, source_target_pairs={{0,3},{1,2},{2,1},{3,0},{4,7},{5,6},{6,5},{7,4},{8,11},{9,10},{10,... | collective-permute-start | bytes 688136 | tf_op jit(solution)/shard_map/ppermute | solution.py:66
  325.8 21.5 %collective-permute-start.17 = (bf16[64,1792]{1,0:T(8,128)(2,1)S(1)}, bf16[64,1792]{1,0:T(8,128)(2,1)S(1)}, u32[]{:S(2)}, u32[]{:S(2)}) collective-permute-start(bf16[64,1792]{1,0:T(8,128)(2,1)S(1)} %get-tuple-element.234), channel_id=1, source_target_pairs={{0,2},{1,3},{2,0},{3,1},{4,6},{5,7},{6,4},{7,5},{8,10},{9,11},{10,... | collective-permute-start | bytes 688136 | tf_op jit(solution)/shard_map/ppermute | solution.py:66
  347.2 14.8 %collective-permute-start.20 = (bf16[256,1792]{1,0:T(8,128)(2,1)S(1)}, bf16[256,1792]{1,0:T(8,128)(2,1)}, u32[]{:S(2)}, u32[]{:S(2)}) collective-permute-start(bf16[256,1792]{1,0:T(8,128)(2,1)S(1)} %all_gather.39.near_grad_ref), channel_id=1, source_target_pairs={{0,16},{16,0},{1,17},{17,1},{2,18},{18,2},{3,19},{19,3},{4,20},{20... | collective-permute-start | bytes 2752520 | tf_op jit(solution)/shard_map/ppermute | solution.py:39
  362.0 18.3 %collective-permute-start.19 = (bf16[256,1792]{1,0:T(8,128)(2,1)}, bf16[256,1792]{1,0:T(8,128)(2,1)}, u32[]{:S(2)}, u32[]{:S(2)}) collective-permute-start(bf16[256,1792]{1,0:T(8,128)(2,1)} %all_gather.38.near_ref), channel_id=1, source_target_pairs={{0,16},{16,0},{1,17},{17,1},{2,18},{18,2},{3,19},{19,3},{4,20},{20... | collective-permute-start | bytes 2752520 | tf_op jit(solution)/shard_map/ppermute | solution.py:39
  396.6 294.6 %reduce-scatter.6.cloned.1.call-start = ((), (), s32[]{:S(2)}) async-start(), calls=%async_computation.7 | async-start | bytes 13189120 | tf_op jit(solution)/shard_map/reduce_scatter | solution.py:547
  402.9 2.5 collective-permute-start.21
  405.7 8.5 %collective-permute-start.22 = (bf16[64,1792]{1,0:T(8,128)(2,1)S(1)}, bf16[64,1792]{1,0:T(8,128)(2,1)S(1)}, u32[]{:S(2)}, u32[]{:S(2)}) collective-permute-start(bf16[64,1792]{1,0:T(8,128)(2,1)S(1)} %get-tuple-element.229), channel_id=1, source_target_pairs={{0,1},{1,0},{2,3},{3,2},{4,5},{5,4},{6,7},{7,6},{8,9},{9,8},{10,11... | collective-permute-start | bytes 688136 | tf_op jit(solution)/shard_map/ppermute | solution.py:66
  407.2 12.1 %collective-permute-start.24 = (bf16[64,1792]{1,0:T(8,128)(2,1)S(1)}, bf16[64,1792]{1,0:T(8,128)(2,1)S(1)}, u32[]{:S(2)}, u32[]{:S(2)}) collective-permute-start(bf16[64,1792]{1,0:T(8,128)(2,1)S(1)} %get-tuple-element.230), channel_id=1, source_target_pairs={{0,3},{1,2},{2,1},{3,0},{4,7},{5,6},{6,5},{7,4},{8,11},{9,10},{10,... | collective-permute-start | bytes 688136 | tf_op jit(solution)/shard_map/ppermute | solution.py:66
  408.7 12.0 %collective-permute-start.23 = (bf16[64,1792]{1,0:T(8,128)(2,1)S(1)}, bf16[64,1792]{1,0:T(8,128)(2,1)S(1)}, u32[]{:S(2)}, u32[]{:S(2)}) collective-permute-start(bf16[64,1792]{1,0:T(8,128)(2,1)S(1)} %get-tuple-element.231), channel_id=1, source_target_pairs={{0,2},{1,3},{2,0},{3,1},{4,6},{5,7},{6,4},{7,5},{8,10},{9,11},{10,... | collective-permute-start | bytes 688136 | tf_op jit(solution)/shard_map/ppermute | solution.py:66
  452.1 2.7 collective-permute-start.26
  456.5 8.5 %collective-permute-start.27 = (bf16[64,1792]{1,0:T(8,128)(2,1)S(1)}, bf16[64,1792]{1,0:T(8,128)(2,1)S(1)}, u32[]{:S(2)}, u32[]{:S(2)}) collective-permute-start(bf16[64,1792]{1,0:T(8,128)(2,1)S(1)} %get-tuple-element.226), channel_id=1, source_target_pairs={{0,1},{1,0},{2,3},{3,2},{4,5},{5,4},{6,7},{7,6},{8,9},{9,8},{10,11... | collective-permute-start | bytes 688136 | tf_op jit(solution)/shard_map/ppermute | solution.py:66
  456.6 12.4 %collective-permute-start.29 = (bf16[64,1792]{1,0:T(8,128)(2,1)S(1)}, bf16[64,1792]{1,0:T(8,128)(2,1)S(1)}, u32[]{:S(2)}, u32[]{:S(2)}) collective-permute-start(bf16[64,1792]{1,0:T(8,128)(2,1)S(1)} %get-tuple-element.227), channel_id=1, source_target_pairs={{0,3},{1,2},{2,1},{3,0},{4,7},{5,6},{6,5},{7,4},{8,11},{9,10},{10,... | collective-permute-start | bytes 688136 | tf_op jit(solution)/shard_map/ppermute | solution.py:66
  458.2 12.2 %collective-permute-start.28 = (bf16[64,1792]{1,0:T(8,128)(2,1)S(1)}, bf16[64,1792]{1,0:T(8,128)(2,1)S(1)}, u32[]{:S(2)}, u32[]{:S(2)}) collective-permute-start(bf16[64,1792]{1,0:T(8,128)(2,1)S(1)} %get-tuple-element.228), channel_id=1, source_target_pairs={{0,2},{1,3},{2,0},{3,1},{4,6},{5,7},{6,4},{7,5},{8,10},{9,11},{10,... | collective-permute-start | bytes 688136 | tf_op jit(solution)/shard_map/ppermute | solution.py:66
  507.9 240.7 %reduce-scatter.8.cloned.1.call-start = ((), (), s32[]{:S(2)}) async-start(), calls=%async_computation.8 | async-start | bytes 3440640 | tf_op jit(solution)/shard_map/reduce_scatter | solution.py:547
  517.0 8.5 %collective-permute-start.32 = (bf16[64,1792]{1,0:T(8,128)(2,1)S(1)}, bf16[64,1792]{1,0:T(8,128)(2,1)S(1)}, u32[]{:S(2)}, u32[]{:S(2)}) collective-permute-start(bf16[64,1792]{1,0:T(8,128)(2,1)S(1)} %get-tuple-element.223), channel_id=1, source_target_pairs={{0,1},{1,0},{2,3},{3,2},{4,5},{5,4},{6,7},{7,6},{8,9},{9,8},{10,11... | collective-permute-start | bytes 688136 | tf_op jit(solution)/shard_map/ppermute | solution.py:66
  518.5 12.1 %collective-permute-start.34 = (bf16[64,1792]{1,0:T(8,128)(2,1)S(1)}, bf16[64,1792]{1,0:T(8,128)(2,1)S(1)}, u32[]{:S(2)}, u32[]{:S(2)}) collective-permute-start(bf16[64,1792]{1,0:T(8,128)(2,1)S(1)} %get-tuple-element.224), channel_id=1, source_target_pairs={{0,3},{1,2},{2,1},{3,0},{4,7},{5,6},{6,5},{7,4},{8,11},{9,10},{10,... | collective-permute-start | bytes 688136 | tf_op jit(solution)/shard_map/ppermute | solution.py:66
  520.0 12.0 %collective-permute-start.33 = (bf16[64,1792]{1,0:T(8,128)(2,1)S(1)}, bf16[64,1792]{1,0:T(8,128)(2,1)S(1)}, u32[]{:S(2)}, u32[]{:S(2)}) collective-permute-start(bf16[64,1792]{1,0:T(8,128)(2,1)S(1)} %get-tuple-element.225), channel_id=1, source_target_pairs={{0,2},{1,3},{2,0},{3,1},{4,6},{5,7},{6,4},{7,5},{8,10},{9,11},{10,... | collective-permute-start | bytes 688136 | tf_op jit(solution)/shard_map/ppermute | solution.py:66
  560.9 2.8 collective-permute-start.39
  565.1 10.5 %collective-permute-start.40 = (bf16[64,1792]{1,0:T(8,128)(2,1)}, bf16[64,1792]{1,0:T(8,128)(2,1)}, u32[]{:S(2)}, u32[]{:S(2)}) collective-permute-start(bf16[64,1792]{1,0:T(8,128)(2,1)} %get-tuple-element.220), channel_id=1, source_target_pairs={{0,1},{1,0},{2,3},{3,2},{4,5},{5,4},{6,7},{7,6},{8,9},{9,8},{10,11... | collective-permute-start | bytes 688136 | tf_op jit(solution)/shard_map/ppermute | solution.py:66
  565.1 12.9 %collective-permute-start.42 = (bf16[64,1792]{1,0:T(8,128)(2,1)}, bf16[64,1792]{1,0:T(8,128)(2,1)}, u32[]{:S(2)}, u32[]{:S(2)}) collective-permute-start(bf16[64,1792]{1,0:T(8,128)(2,1)} %get-tuple-element.221), channel_id=1, source_target_pairs={{0,3},{1,2},{2,1},{3,0},{4,7},{5,6},{6,5},{7,4},{8,11},{9,10},{10,... | collective-permute-start | bytes 688136 | tf_op jit(solution)/shard_map/ppermute | solution.py:66
  566.6 12.8 %collective-permute-start.41 = (bf16[64,1792]{1,0:T(8,128)(2,1)}, bf16[64,1792]{1,0:T(8,128)(2,1)}, u32[]{:S(2)}, u32[]{:S(2)}) collective-permute-start(bf16[64,1792]{1,0:T(8,128)(2,1)} %get-tuple-element.222), channel_id=1, source_target_pairs={{0,2},{1,3},{2,0},{3,1},{4,6},{5,7},{6,4},{7,5},{8,10},{9,11},{10,... | collective-permute-start | bytes 688136 | tf_op jit(solution)/shard_map/ppermute | solution.py:66
  574.6 6.5 collective-permute-start.43
  583.2 6.2 collective-permute-start.49
  585.9 105.4 %collective-permute-start.44 = (bf16[64,1792]{1,0:T(8,128)(2,1)}, bf16[64,1792]{1,0:T(8,128)(2,1)}, u32[]{:S(2)}, u32[]{:S(2)}) collective-permute-start(bf16[64,1792]{1,0:T(8,128)(2,1)} %get-tuple-element.217), channel_id=1, source_target_pairs={{0,1},{1,0},{2,3},{3,2},{4,5},{5,4},{6,7},{7,6},{8,9},{9,8},{10,11... | collective-permute-start | bytes 688136 | tf_op jit(solution)/shard_map/ppermute | solution.py:66
  586.2 105.1 %collective-permute-start.46 = (bf16[64,1792]{1,0:T(8,128)(2,1)}, bf16[64,1792]{1,0:T(8,128)(2,1)}, u32[]{:S(2)}, u32[]{:S(2)}) collective-permute-start(bf16[64,1792]{1,0:T(8,128)(2,1)} %get-tuple-element.218), channel_id=1, source_target_pairs={{0,3},{1,2},{2,1},{3,0},{4,7},{5,6},{6,5},{7,4},{8,11},{9,10},{10,... | collective-permute-start | bytes 688136 | tf_op jit(solution)/shard_map/ppermute | solution.py:66
  587.6 103.6 %collective-permute-start.45 = (bf16[64,1792]{1,0:T(8,128)(2,1)}, bf16[64,1792]{1,0:T(8,128)(2,1)}, u32[]{:S(2)}, u32[]{:S(2)}) collective-permute-start(bf16[64,1792]{1,0:T(8,128)(2,1)} %get-tuple-element.219), channel_id=1, source_target_pairs={{0,2},{1,3},{2,0},{3,1},{4,6},{5,7},{6,4},{7,5},{8,10},{9,11},{10,... | collective-permute-start | bytes 688136 | tf_op jit(solution)/shard_map/ppermute | solution.py:66
  589.5 12.0 %collective-permute-start.50 = (f32[2,5,1792]{2,0,1:T(2,128)S(1)}, f32[2,5,1792]{2,0,1:T(2,128)S(1)}, u32[]{:S(2)}, u32[]{:S(2)}) collective-permute-start(f32[2,5,1792]{2,0,1:T(2,128)S(1)} %fusion.51), channel_id=1, source_target_pairs={{0,2},{1,3},{2,0},{3,1},{4,6},{5,7},{6,4},{7,5},{8,10},{9,11},{10,... | collective-permute-start | bytes 215048 | tf_op jit(solution)/shard_map/ppermute | solution.py:76
  601.6 91.4 %collective-permute-start.51 = (f32[2,5,1792]{2,0,1:T(2,128)S(1)}, f32[2,5,1792]{2,0,1:T(2,128)}, u32[]{:S(2)}, u32[]{:S(2)}) collective-permute-start(f32[2,5,1792]{2,0,1:T(2,128)S(1)} %add.331), channel_id=1, source_target_pairs={{0,4},{4,0},{8,12},{12,8},{1,5},{5,1},{9,13},{13,9},{2,6},{6,2},{1... | collective-permute-start | bytes 215048 | tf_op jit(solution)/shard_map/ppermute | solution.py:76
  694.0 7.1 collective-permute-start.52
  697.7 5.1 collective-permute-start.47
  702.3 9.5 %collective-permute-start.37 = (bf16[448,1792]{1,0:T(8,128)(2,1)S(1)}, bf16[448,1792]{1,0:T(8,128)(2,1)S(1)}, u32[]{:S(2)}, u32[]{:S(2)}) collective-permute-start(bf16[448,1792]{1,0:T(8,128)(2,1)S(1)} %broadcast_select_fusion.2), channel_id=1, source_target_pairs={{0,16},{16,0},{1,17},{17,1},{2,18},{18,2},{3,19},{19,3},{4,20},{20... | collective-permute-start | bytes 4816904 | tf_op jit(solution)/shard_map/ppermute | solution.py:39
  704.2 7.2 collective-permute-start.36
  (53 other events, 505.5 us)
Sparse Core Ops, SparseCore 0:
  16.8 59.5 all-gather.3
  78.6 183.7 all-gather.5
  264.5 115.6 all-gather.7
  396.7 111.0 reduce-scatter.3
  510.1 181.1 reduce-scatter.5
  693.4 55.1 reduce-scatter.7

commit v7 on v6

--- a/solution.py
+++ b/solution.py
@@ -65,6 +65,18 @@
         pairs = [(i, i ^ offset) for i in range(size)]
         total = total + lax.ppermute(block, "tensor", pairs).astype(jnp.float32)
     return total
+
+
+def ring_gather(piece):
+    size = lax.axis_size("dp")
+    index = lax.axis_index("dp")
+    count = piece.shape[0]
+    full = jnp.zeros((size * count, piece.shape[1]), piece.dtype)
+    for step in range(size):
+        if step:
+            piece = lax.ppermute(piece, "dp", [(i, (i + 1) % size) for i in range(size)])
+        full = lax.dynamic_update_slice_in_dim(full, piece, (index - step) % size * count, 0)
+    return full
 
 
 def sum_all(block):
@@ -594,9 +606,10 @@
     attn_parts = both_layers(attn_piece)
     feed_parts = both_layers(feed_piece)
     attn_zero = fetch(with_pair(attn_parts[0], lin_qk))
-    packed = fetch(jnp.concatenate([feed_parts[0], with_pair(attn_parts[1], win_qk)], axis=1))
-    split = feed_parts[0].shape[1]
-    attn_one = packed[:, split:]
+    packed = fetch(feed_parts[0])
+    split = packed.shape[1]
+    attn_zero, attn_one = lax.optimization_barrier((attn_zero, with_pair(attn_parts[1], win_qk)))
+    attn_one = ring_gather(attn_one)
     feed_one = fetch(feed_parts[1])
     down_one = jnp.concatenate(
         [feed_one[:, :main], feed_one[:, main + 2 * units :], attn_one[:, attn_one.shape[1] - tail :]], axis=1
@@ -642,6 +655,7 @@
     hidden, kept_zero = mix(entering, gains_zero[0], attn_zero, taps_zero, True)
     scale, normed = rms_rows(hidden, gains_zero[1])
     near, far = spread_pair(normed)
+    near, far, attn_one = lax.optimization_barrier((near, far, attn_one))
     kept_feed = (hidden, scale, near, far)
     middle = hidden + collect_pair(*feed_terms(units, tail, near, far, packed, attn_zero))
     middle = middle.astype(jnp.bfloat16).astype(jnp.float32)
@@ -650,7 +664,7 @@
     scale, normed = rms_rows(hidden, gains_one[1])
     grad_out = cotangent * mask
     block, rest, grad_halves, inner = feed_both(
-        units, tail, *spread_pair(normed), *spread_pair(grad_out), feed_one, packed
+        units, tail, *spread_pair(normed), *spread_pair(grad_out), feed_one, attn_one
     )
     queue.scatter(block)
     final = hidden + collect(dot_nt(inner, down_one))

time: 769 us -> 762 us (level)
  waiting for transfers between devices: 372 us -> 328 us
  starting transfers between devices: 40 us -> 79 us
    all_gather x3, waiting for transfers between devices: 167 us -> 46.1 us  [fetch(): return lax.all_gather(piece, 'dp', axis=0, tiled=True)]
    ppermute x0 -> x3, waiting for transfers between devices: none -> 82.9 us  [ring_gather(): lax.ppermute(piece, 'dp', [(i, (i + 1) % size) for i in range(size)])]
    ppermute x0 -> x3, starting transfers between devices: none -> 38.7 us  [ring_gather(): lax.ppermute(piece, 'dp', [(i, (i + 1) % size) for i in range(size)])]
  transfers between devices with their start and end apart: 60 -> 63, of which waited for: 39 -> 41; matrix products, arithmetic and copies ran while one was open for 15% -> 14% of each run, Pallas kernels for 9% -> 10%
where the time goes in v7:
time: 762 us; the launch traced here: 752 us
  waiting for transfers between devices  328 us (43%)
  blocking collectives  109 us (14%)
  Pallas kernels  93.2 us (12%)
  local copies, waits for them, and re-layouts  80.4 us (11%)
  starting transfers between devices  79 us (10%)
  other arithmetic  35.8 us (5%)
  between operations  15.9 us (2%)
  matrix products  11.4 us (1%)
    all_gather x8, blocking collectives, spread_pair(): lax.all_gather(rows.astype(jnp.bfloat16), 'tensor', axis=0, tiled=True)  109 us
    reduce_scatter x3, waiting for transfers between devices, scatter(): lax.psum_scatter(block, 'dp', scatter_dimension=0, tiled=True)  99.5 us
    ppermute x3, waiting for transfers between devices, ring_gather(): lax.ppermute(piece, 'dp', [(i, (i + 1) % size) for i in range(size)])  82.9 us
    ppermute x24, waiting for transfers between devices, collect_pair(): total = total + lax.ppermute(block, 'tensor', pairs).astype(jnp.float32)  57.9 us
    all_gather x3, waiting for transfers between devices, fetch(): return lax.all_gather(piece, 'dp', axis=0, tiled=True)  46.1 us
    pallas_call x4, Pallas kernels, whole_call(): pl.pallas_call(kernel, grid=(1,), out_shape=[jax.ShapeDtypeStruct(shape,...  41.7 us
    ppermute x3, starting transfers between devices, ring_gather(): lax.ppermute(piece, 'dp', [(i, (i + 1) % size) for i in range(size)])  38.7 us
    pallas_call x2, Pallas kernels, feed_both(): pl.pallas_call(functools.partial(feed_kernel, units, tail), grid=(1,), ou...  35.6 us
  transfers between devices with their start and end apart: 63, of which 41 were waited for; matrix products, arithmetic and copies ran while one was open for 14% of the time, Pallas kernels for 10%

profile of v7, /device:TPU:0, one launch (start us, length us, event | category | flops | bytes accessed | tf_op | source)
XLA Modules:
  0.0 752.2 jit_solution(10905513130955939982)
XLA Ops:
  18.5 5.9 constant_dynamic-slice_fusion.24
  30.6 3.3 broadcast_select_fusion.4
  38.9 14.8 %all_gather.33.near_ref = bf16[256,1792]{1,0:T(8,128)(2,1)S(1)} all-gather(bf16[64,1792]{1,0:T(8,128)(2,1)S(1)} %fusion.18), channel_id=1, replica_groups=mesh['section'=2,'dp'=4,'tensor'=4] {'tensor'}, dimensions={0}, use_global_device_ids=true | all-gather | bytes 1146880 | tf_op jit(solution)/shard_map/all_gather | solution.py:43
  53.8 3.3 constant_dynamic-slice_fusion.30
  61.5 14.8 %all-gather.4.cloned.1.call-done.attn_ref.last_ref = bf16[1792,768]{1,0:T(8,128)(2,1)} async-done(((bf16[448,768]{1,0:T(8,128)(2,1)}), bf16[1792,768]{1,0:T(8,128)(2,1)}) %all-gather.4.cloned.1.call-update) | async-done | bytes 2752528 | tf_op jit(solution)/shard_map/all_gather | solution.py:599
  78.7 6.7 shard_map.169
  85.4 30.4 %collective-permute-done.9 = bf16[448,1152]{1,0:T(8,128)(2,1)} collective-permute-done((bf16[448,1152]{1,0:T(8,128)(2,1)S(1)}, bf16[448,1152]{1,0:T(8,128)(2,1)}, u32[]{:S(2)}, u32[]{:S(2)}) %collective-permute-start.9) | collective-permute-done | bytes 1032224 | tf_op jit(solution)/shard_map/ppermute | solution.py:77
  115.8 10.2 %collective-permute-start.10 = (bf16[448,1152]{1,0:T(8,128)(2,1)}, bf16[448,1152]{1,0:T(8,128)(2,1)}, u32[]{:S(2)}, u32[]{:S(2)}) collective-permute-start(bf16[448,1152]{1,0:T(8,128)(2,1)} %collective-permute-done.9), channel_id=1, source_target_pairs={{0,4},{4,8},{8,12},{12,0},{1,5},{5,9},{9,13},{13,1},{2,6},{6,10},{... | collective-permute-start | bytes 3096584 | tf_op jit(solution)/shard_map/ppermute | solution.py:77
  135.9 3.4 collective-permute-done.7
  141.3 27.1 %collective-permute-done.10 = bf16[448,1152]{1,0:T(8,128)(2,1)} collective-permute-done((bf16[448,1152]{1,0:T(8,128)(2,1)}, bf16[448,1152]{1,0:T(8,128)(2,1)}, u32[]{:S(2)}, u32[]{:S(2)}) %collective-permute-start.10) | collective-permute-done | bytes 1032224 | tf_op jit(solution)/shard_map/ppermute | solution.py:77
  168.4 28.4 %collective-permute-start.11 = (bf16[448,1152]{1,0:T(8,128)(2,1)}, bf16[448,1152]{1,0:T(8,128)(2,1)S(1)}, u32[]{:S(2)}, u32[]{:S(2)}) collective-permute-start(bf16[448,1152]{1,0:T(8,128)(2,1)} %collective-permute-done.10), channel_id=1, source_target_pairs={{0,4},{4,8},{8,12},{12,0},{1,5},{5,9},{9,13},{13,1},{2,6},{6,10},{... | collective-permute-start | bytes 3096584 | tf_op jit(solution)/shard_map/ppermute | solution.py:77
  197.0 10.5 %all_gather.35.near_ref = bf16[256,1792]{1,0:T(8,128)(2,1)S(1)} all-gather(bf16[64,1792]{1,0:T(8,128)(2,1)S(1)} %multiply_convert_fusion.1), channel_id=1, replica_groups=mesh['section'=2,'dp'=4,'tensor'=4] {'tensor'}, dimensions={0}, use_global_device_ids=true | all-gather | bytes 1146880 | tf_op jit(solution)/shard_map/all_gather | solution.py:43
  215.4 25.4 %collective-permute-done.11 = bf16[448,1152]{1,0:T(8,128)(2,1)S(1)} collective-permute-done((bf16[448,1152]{1,0:T(8,128)(2,1)}, bf16[448,1152]{1,0:T(8,128)(2,1)S(1)}, u32[]{:S(2)}, u32[]{:S(2)}) %collective-permute-start.11) | collective-permute-done | bytes 1032224 | tf_op jit(solution)/shard_map/ppermute | solution.py:77
  241.9 8.6 %all-gather.6.cloned.1.call-done.feed_ref = bf16[1792,1792]{1,0:T(8,128)(2,1)} async-done(((bf16[448,1792]{1,0:T(8,128)(2,1)}), bf16[1792,1792]{1,0:T(8,128)(2,1)}) %all-gather.6.cloned.1.call-update) | async-done | bytes 6422544 | tf_op jit(solution)/shard_map/all_gather | solution.py:599
  250.5 11.3 %shard_map.170 = (f32[256,1792]{1,0:T(8,128)S(1)}, bf16[256,1792]{1,0:T(8,128)(2,1)S(1)}) custom-call(bf16[256,1792]{1,0:T(8,128)(2,1)S(1)} %all_gather.35.near_ref, bf16[256,1792]{1,0:T(8,128)(2,1)S(1)} %collective-permute-done.8.far_ref, bf16[1792,1792]{1,0:T(8,128)(2,1)} %all-gather.6.cloned.1.call-done.feed_ref, ...), custom_call_target="tpu_custom_call" | custom-call | flops 1048576 | bytes 65536 | tf_op jit(solution)/shard_map/pallas_call | solution.py:152
  268.2 5.0 collective-permute-done.14
  273.1 5.2 collective-permute-done.16
  280.1 12.8 %all_gather.37.near_ref = bf16[256,1792]{1,0:T(8,128)(2,1)S(1)} all-gather(bf16[64,1792]{1,0:T(8,128)(2,1)S(1)} %fusion.25), channel_id=1, replica_groups=mesh['section'=2,'dp'=4,'tensor'=4] {'tensor'}, dimensions={0}, use_global_device_ids=true | all-gather | bytes 1146880 | tf_op jit(solution)/shard_map/all_gather | solution.py:43
  296.3 8.6 %shard_map.171 = (f32[256,1792]{1,0:T(8,128)}, bf16[256,1792]{1,0:T(8,128)(2,1)}, f32[512,896]{1,0:T(8,128)}, bf16[512,256]{1,0:T(8,128)(2,1)}) custom-call(bf16[256,1792]{1,0:T(8,128)(2,1)} %copy-done.5, bf16[256,1792]{1,0:T(8,128)(2,1)} %copy-done.13, bf16[1792,1152]{1,0:T(8,128)(2,1)} %constant_dynamic-update-slice_fusion.attn_ref.last_ref, ...), custom_call_target="tpu_custom_call" | custom-call | flops 1048576 | bytes 65536 | tf_op jit(solution)/shard_map/pallas_call | solution.py:437
  313.0 19.0 %all_gather.39.near_grad_ref = bf16[256,1792]{1,0:T(8,128)(2,1)S(1)} all-gather(bf16[64,1792]{1,0:T(8,128)(2,1)S(1)} %copy-done.29), channel_id=1, replica_groups=mesh['section'=2,'dp'=4,'tensor'=4] {'tensor'}, dimensions={0}, use_global_device_ids=true | all-gather | bytes 1146880 | tf_op jit(solution)/shard_map/all_gather | solution.py:43
  332.5 13.1 %all_gather.38.near_ref = bf16[256,1792]{1,0:T(8,128)(2,1)S(1)} all-gather(bf16[64,1792]{1,0:T(8,128)(2,1)S(1)} %multiply_convert_fusion), channel_id=1, replica_groups=mesh['section'=2,'dp'=4,'tensor'=4] {'tensor'}, dimensions={0}, use_global_device_ids=true | all-gather | bytes 1146880 | tf_op jit(solution)/shard_map/all_gather | solution.py:43
  345.7 22.7 %all-gather.8.cloned.1.call-done.feed_ref = bf16[1792,1792]{1,0:T(8,128)(2,1)} async-done(((bf16[448,1792]{1,0:T(8,128)(2,1)}), bf16[1792,1792]{1,0:T(8,128)(2,1)}) %all-gather.8.cloned.1.call-update) | async-done | bytes 6422544 | tf_op jit(solution)/shard_map/all_gather | solution.py:599
  368.5 16.3 %shard_map.172 = (bf16[1792,1792]{1,0:T(8,128)(2,1)}, bf16[1792,256]{1,0:T(8,128)(2,1)}, bf16[512,1280]{1,0:T(8,128)(2,1)}, bf16[512,608]{1,0:T(8,128)(2,1)}) custom-call(bf16[256,1792]{1,0:T(8,128)(2,1)} %copy-done.25, bf16[256,1792]{1,0:T(8,128)(2,1)} %collective-permute-done.22.far_ref, bf16[256,1792]{1,0:T(8,128)(2,1)} %copy-done.24, ...), custom_call_target="tpu_custom_call" | custom-call | flops 6576668672 | bytes 20971520 | tf_op jit(solution)/shard_map/pallas_call | solution.py:258
  386.1 4.9 fusion.2
  397.5 5.0 collective-permute-done.25
  402.4 5.1 collective-permute-done.27
  409.5 13.0 %all_gather.41.near_grad_ref = bf16[256,1792]{1,0:T(8,128)(2,1)S(1)} all-gather(bf16[64,1792]{1,0:T(8,128)(2,1)S(1)} %get-tuple-element.173), channel_id=1, replica_groups=mesh['section'=2,'dp'=4,'tensor'=4] {'tensor'}, dimensions={0}, use_global_device_ids=true | all-gather | bytes 1146880 | tf_op jit(solution)/shard_map/all_gather | solution.py:43
  426.0 14.4 %shard_map.173 = (bf16[1792,1152]{1,0:T(8,128)(2,1)}, f32[256,1792]{1,0:T(8,128)}, bf16[256,1792]{1,0:T(8,128)(2,1)}, f32[8,256]{1,0:T(8,128)}) custom-call(bf16[256,1792]{1,0:T(8,128)(2,1)} %copy-done.5, bf16[256,1792]{1,0:T(8,128)(2,1)} %copy-done.13, bf16[256,1792]{1,0:T(8,128)(2,1)} %copy-done.11, bf16[256,1792]{1,0:T(8,128)(2,1)} %copy-done.22, ...), custom_call_target="tpu_custom_call" | custom-call | flops 1048576 | bytes 65536 | tf_op jit(solution)/shard_map/pallas_call | solution.py:437
  448.4 5.0 collective-permute-done.30
  453.3 3.9 collective-permute-done.32
  459.2 12.7 %all_gather.42.near_grad_ref = bf16[256,1792]{1,0:T(8,128)(2,1)S(1)} all-gather(bf16[64,1792]{1,0:T(8,128)(2,1)S(1)} %fusion.30), channel_id=1, replica_groups=mesh['section'=2,'dp'=4,'tensor'=4] {'tensor'}, dimensions={0}, use_global_device_ids=true | all-gather | bytes 1146880 | tf_op jit(solution)/shard_map/all_gather | solution.py:43
  475.3 19.3 %shard_map.174 = (bf16[1792,2944]{1,0:T(8,128)(2,1)}, bf16[1792,256]{1,0:T(8,128)(2,1)}, bf16[512,1280]{1,0:T(8,128)(2,1)}, bf16[512,608]{1,0:T(8,128)(2,1)}) custom-call(bf16[256,1792]{1,0:T(8,128)(2,1)} %copy-done, bf16[256,1792]{1,0:T(8,128)(2,1)} %copy-done.1, bf16[256,1792]{1,0:T(8,128)(2,1)} %copy-done.26, bf16[256,1792]{1,0:T(8,128)(2,1)} %copy-done.50, ...), custom_call_target="tpu_custom_call" | custom-call | flops 6576668672 | bytes 20971520 | tf_op jit(solution)/shard_map/pallas_call | solution.py:258
  497.4 4.9 fusion
  508.7 5.0 collective-permute-done.35
  513.7 5.1 collective-permute-done.37
  520.6 13.0 %all_gather.43.near_grad_ref = bf16[256,1792]{1,0:T(8,128)(2,1)S(1)} all-gather(bf16[64,1792]{1,0:T(8,128)(2,1)S(1)} %get-tuple-element.165), channel_id=1, replica_groups=mesh['section'=2,'dp'=4,'tensor'=4] {'tensor'}, dimensions={0}, use_global_device_ids=true | all-gather | bytes 1146880 | tf_op jit(solution)/shard_map/all_gather | solution.py:43
  537.1 12.0 %shard_map.175 = (bf16[1792,768]{1,0:T(8,128)(2,1)}, f32[256,1792]{1,0:T(8,128)}, bf16[256,1792]{1,0:T(8,128)(2,1)}, f32[8,256]{1,0:T(8,128)}) custom-call(bf16[256,1792]{1,0:T(8,128)(2,1)} %copy-done.4, bf16[256,1792]{1,0:T(8,128)(2,1)} %copy-done.12, bf16[256,1792]{1,0:T(8,128)(2,1)} %copy-done.10, bf16[256,1792]{1,0:T(8,128)(2,1)} %copy-done.21, ...), custom_call_target="tpu_custom_call" | custom-call | flops 1048576 | bytes 65536 | tf_op jit(solution)/shard_map/pallas_call | solution.py:437
  563.3 4.0 collective-permute-done.45
  579.6 11.3 %collective-permute-done.53 = f32[2,5,1792]{2,0,1:T(2,128)S(1)} collective-permute-done((f32[2,5,1792]{2,0,1:T(2,128)S(1)}, f32[2,5,1792]{2,0,1:T(2,128)S(1)}, u32[]{:S(2)}, u32[]{:S(2)}) %collective-permute-start.53) | collective-permute-done | bytes 71712 | tf_op jit(solution)/shard_map/ppermute | solution.py:88
  592.5 86.9 %reduce-scatter.6.cloned.1.call-done = bf16[448,2944]{1,0:T(8,128)(2,1)} async-done(((bf16[1792,2944]{1,0:T(8,128)(2,1)}), bf16[448,2944]{1,0:T(8,128)(2,1)}) %reduce-scatter.6.cloned.1.call-update) | async-done | bytes 2637840 | tf_op jit(solution)/shard_map/reduce_scatter | solution.py:559
  682.2 3.5 collective-permute-start.55
  685.9 3.3 collective-permute-done.55
  694.3 5.3 maximum_convert_fusion.1
  704.0 3.2 concatenate.118
  715.0 3.3 concatenate.117
  720.0 5.7 copy.82
  725.7 11.1 %reduce-scatter.8.cloned.1.call-done.mine_ref = bf16[448,768]{1,0:T(8,128)(2,1)} async-done(((bf16[1792,768]{1,0:T(8,128)(2,1)}), bf16[448,768]{1,0:T(8,128)(2,1)}) %reduce-scatter.8.cloned.1.call-update) | async-done | bytes 688144 | tf_op jit(solution)/shard_map/reduce_scatter | solution.py:559
  740.2 4.7 shard_map.176
  (368 shorter events, 164.2 us)
Async XLA Ops:
  7.2 69.0 %all-gather.4.cloned.1.call-start = ((), (), s32[]{:S(2)}) async-start(), calls=%async_computation.3 | async-start | bytes 3440640 | tf_op jit(solution)/shard_map/all_gather | solution.py:599
  16.5 234.0 %all-gather.6.cloned.1.call-start = ((), (), s32[]{:S(2)}) async-start(), calls=%async_computation.4 | async-start | bytes 8028160 | tf_op jit(solution)/shard_map/all_gather | solution.py:599
  26.8 3.8 collective-permute-start.12
  33.9 334.5 %all-gather.8.cloned.1.call-start = ((), (), s32[]{:S(2)}) async-start(), calls=%async_computation.5 | async-start | bytes 8028160 | tf_op jit(solution)/shard_map/all_gather | solution.py:599
  53.8 24.0 %collective-permute-start.2 = (bf16[256,1792]{1,0:T(8,128)(2,1)S(1)}, bf16[256,1792]{1,0:T(8,128)(2,1)S(1)}, u32[]{:S(2)}, u32[]{:S(2)}) collective-permute-start(bf16[256,1792]{1,0:T(8,128)(2,1)S(1)} %all_gather.33.near_ref), channel_id=1, source_target_pairs={{0,16},{16,0},{1,17},{17,1},{2,18},{18,2},{3,19},{19,3},{4,20},{20... | collective-permute-start | bytes 2752520 | tf_op jit(solution)/shard_map/ppermute | solution.py:39
  76.2 39.5 %collective-permute-start.9 = (bf16[448,1152]{1,0:T(8,128)(2,1)S(1)}, bf16[448,1152]{1,0:T(8,128)(2,1)}, u32[]{:S(2)}, u32[]{:S(2)}) collective-permute-start(bf16[448,1152]{1,0:T(8,128)(2,1)S(1)} %concatenate.104), channel_id=1, source_target_pairs={{0,4},{4,8},{8,12},{12,0},{1,5},{5,9},{9,13},{13,1},{2,6},{6,10},{... | collective-permute-start | bytes 3096584 | tf_op jit(solution)/shard_map/ppermute | solution.py:77
  85.4 40.6 %collective-permute-start.4 = (bf16[256,1792]{1,0:T(8,128)(2,1)}, bf16[256,1792]{1,0:T(8,128)(2,1)S(1)}, u32[]{:S(2)}, u32[]{:S(2)}) collective-permute-start(bf16[256,1792]{1,0:T(8,128)(2,1)} %get-tuple-element.57), channel_id=1, source_target_pairs={{0,16},{16,0},{1,17},{17,1},{2,18},{18,2},{3,19},{19,3},{4,20},{20... | collective-permute-start | bytes 2752520 | tf_op jit(solution)/shard_map/ppermute | solution.py:39
  115.8 52.7 %collective-permute-start.10 = (bf16[448,1152]{1,0:T(8,128)(2,1)}, bf16[448,1152]{1,0:T(8,128)(2,1)}, u32[]{:S(2)}, u32[]{:S(2)}) collective-permute-start(bf16[448,1152]{1,0:T(8,128)(2,1)} %collective-permute-done.9), channel_id=1, source_target_pairs={{0,4},{4,8},{8,12},{12,0},{1,5},{5,9},{9,13},{13,1},{2,6},{6,10},{... | collective-permute-start | bytes 3096584 | tf_op jit(solution)/shard_map/ppermute | solution.py:77
  129.7 6.2 collective-permute-start.5
  131.1 8.2 %collective-permute-start.7 = (bf16[64,1792]{1,0:T(8,128)(2,1)}, bf16[64,1792]{1,0:T(8,128)(2,1)S(1)}, u32[]{:S(2)}, u32[]{:S(2)}) collective-permute-start(bf16[64,1792]{1,0:T(8,128)(2,1)} %get-tuple-element.249), channel_id=1, source_target_pairs={{0,3},{1,2},{2,1},{3,0},{4,7},{5,6},{6,5},{7,4},{8,11},{9,10},{10,... | collective-permute-start | bytes 688136 | tf_op jit(solution)/shard_map/ppermute | solution.py:66
  132.6 8.5 %collective-permute-start.6 = (bf16[64,1792]{1,0:T(8,128)(2,1)S(1)}, bf16[64,1792]{1,0:T(8,128)(2,1)S(1)}, u32[]{:S(2)}, u32[]{:S(2)}) collective-permute-start(bf16[64,1792]{1,0:T(8,128)(2,1)S(1)} %get-tuple-element.250), channel_id=1, source_target_pairs={{0,2},{1,3},{2,0},{3,1},{4,6},{5,7},{6,4},{7,5},{8,10},{9,11},{10,... | collective-permute-start | bytes 688136 | tf_op jit(solution)/shard_map/ppermute | solution.py:66
  133.2 362.8 %reduce-scatter.4.cloned.1.call-start = ((), (), s32[]{:S(2)}) async-start(), calls=%async_computation.6 | async-start | bytes 8028160 | tf_op jit(solution)/shard_map/reduce_scatter | solution.py:559
  168.4 72.4 %collective-permute-start.11 = (bf16[448,1152]{1,0:T(8,128)(2,1)}, bf16[448,1152]{1,0:T(8,128)(2,1)S(1)}, u32[]{:S(2)}, u32[]{:S(2)}) collective-permute-start(bf16[448,1152]{1,0:T(8,128)(2,1)} %collective-permute-done.10), channel_id=1, source_target_pairs={{0,4},{4,8},{8,12},{12,0},{1,5},{5,9},{9,13},{13,1},{2,6},{6,10},{... | collective-permute-start | bytes 3096584 | tf_op jit(solution)/shard_map/ppermute | solution.py:77
  207.5 34.4 %collective-permute-start.8 = (bf16[256,1792]{1,0:T(8,128)(2,1)S(1)}, bf16[256,1792]{1,0:T(8,128)(2,1)S(1)}, u32[]{:S(2)}, u32[]{:S(2)}) collective-permute-start(bf16[256,1792]{1,0:T(8,128)(2,1)S(1)} %all_gather.35.near_ref), channel_id=1, source_target_pairs={{0,16},{16,0},{1,17},{17,1},{2,18},{18,2},{3,19},{19,3},{4,20},{20... | collective-permute-start | bytes 2752520 | tf_op jit(solution)/shard_map/ppermute | solution.py:39
  264.6 8.5 %collective-permute-start.14 = (bf16[64,1792]{1,0:T(8,128)(2,1)S(1)}, bf16[64,1792]{1,0:T(8,128)(2,1)S(1)}, u32[]{:S(2)}, u32[]{:S(2)}) collective-permute-start(bf16[64,1792]{1,0:T(8,128)(2,1)S(1)} %get-tuple-element.245), channel_id=1, source_target_pairs={{0,1},{1,0},{2,3},{3,2},{4,5},{5,4},{6,7},{7,6},{8,9},{9,8},{10,11... | collective-permute-start | bytes 688136 | tf_op jit(solution)/shard_map/ppermute | solution.py:66
  266.2 12.1 %collective-permute-start.16 = (bf16[64,1792]{1,0:T(8,128)(2,1)S(1)}, bf16[64,1792]{1,0:T(8,128)(2,1)S(1)}, u32[]{:S(2)}, u32[]{:S(2)}) collective-permute-start(bf16[64,1792]{1,0:T(8,128)(2,1)S(1)} %get-tuple-element.246), channel_id=1, source_target_pairs={{0,3},{1,2},{2,1},{3,0},{4,7},{5,6},{6,5},{7,4},{8,11},{9,10},{10,... | collective-permute-start | bytes 688136 | tf_op jit(solution)/shard_map/ppermute | solution.py:66
  267.7 12.0 %collective-permute-start.15 = (bf16[64,1792]{1,0:T(8,128)(2,1)S(1)}, bf16[64,1792]{1,0:T(8,128)(2,1)S(1)}, u32[]{:S(2)}, u32[]{:S(2)}) collective-permute-start(bf16[64,1792]{1,0:T(8,128)(2,1)S(1)} %get-tuple-element.247), channel_id=1, source_target_pairs={{0,2},{1,3},{2,0},{3,1},{4,6},{5,7},{6,4},{7,5},{8,10},{9,11},{10,... | collective-permute-start | bytes 688136 | tf_op jit(solution)/shard_map/ppermute | solution.py:66
  304.9 2.7 collective-permute-start.18
  309.5 22.6 %collective-permute-start.19 = (bf16[64,1792]{1,0:T(8,128)(2,1)S(1)}, bf16[64,1792]{1,0:T(8,128)(2,1)S(1)}, u32[]{:S(2)}, u32[]{:S(2)}) collective-permute-start(bf16[64,1792]{1,0:T(8,128)(2,1)S(1)} %get-tuple-element.242), channel_id=1, source_target_pairs={{0,1},{1,0},{2,3},{3,2},{4,5},{5,4},{6,7},{7,6},{8,9},{9,8},{10,11... | collective-permute-start | bytes 688136 | tf_op jit(solution)/shard_map/ppermute | solution.py:66
  309.5 22.6 %collective-permute-start.21 = (bf16[64,1792]{1,0:T(8,128)(2,1)S(1)}, bf16[64,1792]{1,0:T(8,128)(2,1)S(1)}, u32[]{:S(2)}, u32[]{:S(2)}) collective-permute-start(bf16[64,1792]{1,0:T(8,128)(2,1)S(1)} %get-tuple-element.243), channel_id=1, source_target_pairs={{0,3},{1,2},{2,1},{3,0},{4,7},{5,6},{6,5},{7,4},{8,11},{9,10},{10,... | collective-permute-start | bytes 688136 | tf_op jit(solution)/shard_map/ppermute | solution.py:66
  311.1 21.0 %collective-permute-start.20 = (bf16[64,1792]{1,0:T(8,128)(2,1)S(1)}, bf16[64,1792]{1,0:T(8,128)(2,1)S(1)}, u32[]{:S(2)}, u32[]{:S(2)}) collective-permute-start(bf16[64,1792]{1,0:T(8,128)(2,1)S(1)} %get-tuple-element.244), channel_id=1, source_target_pairs={{0,2},{1,3},{2,0},{3,1},{4,6},{5,7},{6,4},{7,5},{8,10},{9,11},{10,... | collective-permute-start | bytes 688136 | tf_op jit(solution)/shard_map/ppermute | solution.py:66
  332.0 13.7 %collective-permute-start.23 = (bf16[256,1792]{1,0:T(8,128)(2,1)S(1)}, bf16[256,1792]{1,0:T(8,128)(2,1)}, u32[]{:S(2)}, u32[]{:S(2)}) collective-permute-start(bf16[256,1792]{1,0:T(8,128)(2,1)S(1)} %all_gather.39.near_grad_ref), channel_id=1, source_target_pairs={{0,16},{16,0},{1,17},{17,1},{2,18},{18,2},{3,19},{19,3},{4,20},{20... | collective-permute-start | bytes 2752520 | tf_op jit(solution)/shard_map/ppermute | solution.py:39
  345.6 22.8 %collective-permute-start.22 = (bf16[256,1792]{1,0:T(8,128)(2,1)S(1)}, bf16[256,1792]{1,0:T(8,128)(2,1)}, u32[]{:S(2)}, u32[]{:S(2)}) collective-permute-start(bf16[256,1792]{1,0:T(8,128)(2,1)S(1)} %all_gather.38.near_ref), channel_id=1, source_target_pairs={{0,16},{16,0},{1,17},{17,1},{2,18},{18,2},{3,19},{19,3},{4,20},{20... | collective-permute-start | bytes 2752520 | tf_op jit(solution)/shard_map/ppermute | solution.py:39
  384.8 294.6 %reduce-scatter.6.cloned.1.call-start = ((), (), s32[]{:S(2)}) async-start(), calls=%async_computation.7 | async-start | bytes 13189120 | tf_op jit(solution)/shard_map/reduce_scatter | solution.py:559
  393.9 8.5 %collective-permute-start.25 = (bf16[64,1792]{1,0:T(8,128)(2,1)S(1)}, bf16[64,1792]{1,0:T(8,128)(2,1)S(1)}, u32[]{:S(2)}, u32[]{:S(2)}) collective-permute-start(bf16[64,1792]{1,0:T(8,128)(2,1)S(1)} %get-tuple-element.239), channel_id=1, source_target_pairs={{0,1},{1,0},{2,3},{3,2},{4,5},{5,4},{6,7},{7,6},{8,9},{9,8},{10,11... | collective-permute-start | bytes 688136 | tf_op jit(solution)/shard_map/ppermute | solution.py:66
  395.4 12.1 %collective-permute-start.27 = (bf16[64,1792]{1,0:T(8,128)(2,1)S(1)}, bf16[64,1792]{1,0:T(8,128)(2,1)S(1)}, u32[]{:S(2)}, u32[]{:S(2)}) collective-permute-start(bf16[64,1792]{1,0:T(8,128)(2,1)S(1)} %get-tuple-element.240), channel_id=1, source_target_pairs={{0,3},{1,2},{2,1},{3,0},{4,7},{5,6},{6,5},{7,4},{8,11},{9,10},{10,... | collective-permute-start | bytes 688136 | tf_op jit(solution)/shard_map/ppermute | solution.py:66
  396.9 12.0 %collective-permute-start.26 = (bf16[64,1792]{1,0:T(8,128)(2,1)S(1)}, bf16[64,1792]{1,0:T(8,128)(2,1)S(1)}, u32[]{:S(2)}, u32[]{:S(2)}) collective-permute-start(bf16[64,1792]{1,0:T(8,128)(2,1)S(1)} %get-tuple-element.241), channel_id=1, source_target_pairs={{0,2},{1,3},{2,0},{3,1},{4,6},{5,7},{6,4},{7,5},{8,10},{9,11},{10,... | collective-permute-start | bytes 688136 | tf_op jit(solution)/shard_map/ppermute | solution.py:66
  444.8 8.5 %collective-permute-start.30 = (bf16[64,1792]{1,0:T(8,128)(2,1)S(1)}, bf16[64,1792]{1,0:T(8,128)(2,1)S(1)}, u32[]{:S(2)}, u32[]{:S(2)}) collective-permute-start(bf16[64,1792]{1,0:T(8,128)(2,1)S(1)} %get-tuple-element.236), channel_id=1, source_target_pairs={{0,1},{1,0},{2,3},{3,2},{4,5},{5,4},{6,7},{7,6},{8,9},{9,8},{10,11... | collective-permute-start | bytes 688136 | tf_op jit(solution)/shard_map/ppermute | solution.py:66
  444.9 12.4 %collective-permute-start.32 = (bf16[64,1792]{1,0:T(8,128)(2,1)S(1)}, bf16[64,1792]{1,0:T(8,128)(2,1)S(1)}, u32[]{:S(2)}, u32[]{:S(2)}) collective-permute-start(bf16[64,1792]{1,0:T(8,128)(2,1)S(1)} %get-tuple-element.237), channel_id=1, source_target_pairs={{0,3},{1,2},{2,1},{3,0},{4,7},{5,6},{6,5},{7,4},{8,11},{9,10},{10,... | collective-permute-start | bytes 688136 | tf_op jit(solution)/shard_map/ppermute | solution.py:66
  446.4 12.3 %collective-permute-start.31 = (bf16[64,1792]{1,0:T(8,128)(2,1)S(1)}, bf16[64,1792]{1,0:T(8,128)(2,1)S(1)}, u32[]{:S(2)}, u32[]{:S(2)}) collective-permute-start(bf16[64,1792]{1,0:T(8,128)(2,1)S(1)} %get-tuple-element.238), channel_id=1, source_target_pairs={{0,2},{1,3},{2,0},{3,1},{4,6},{5,7},{6,4},{7,5},{8,10},{9,11},{10,... | collective-permute-start | bytes 688136 | tf_op jit(solution)/shard_map/ppermute | solution.py:66
  496.1 240.7 %reduce-scatter.8.cloned.1.call-start = ((), (), s32[]{:S(2)}) async-start(), calls=%async_computation.8 | async-start | bytes 3440640 | tf_op jit(solution)/shard_map/reduce_scatter | solution.py:559
  505.2 8.5 %collective-permute-start.35 = (bf16[64,1792]{1,0:T(8,128)(2,1)S(1)}, bf16[64,1792]{1,0:T(8,128)(2,1)S(1)}, u32[]{:S(2)}, u32[]{:S(2)}) collective-permute-start(bf16[64,1792]{1,0:T(8,128)(2,1)S(1)} %get-tuple-element.233), channel_id=1, source_target_pairs={{0,1},{1,0},{2,3},{3,2},{4,5},{5,4},{6,7},{7,6},{8,9},{9,8},{10,11... | collective-permute-start | bytes 688136 | tf_op jit(solution)/shard_map/ppermute | solution.py:66
  506.7 12.1 %collective-permute-start.37 = (bf16[64,1792]{1,0:T(8,128)(2,1)S(1)}, bf16[64,1792]{1,0:T(8,128)(2,1)S(1)}, u32[]{:S(2)}, u32[]{:S(2)}) collective-permute-start(bf16[64,1792]{1,0:T(8,128)(2,1)S(1)} %get-tuple-element.234), channel_id=1, source_target_pairs={{0,3},{1,2},{2,1},{3,0},{4,7},{5,6},{6,5},{7,4},{8,11},{9,10},{10,... | collective-permute-start | bytes 688136 | tf_op jit(solution)/shard_map/ppermute | solution.py:66
  508.2 12.0 %collective-permute-start.36 = (bf16[64,1792]{1,0:T(8,128)(2,1)S(1)}, bf16[64,1792]{1,0:T(8,128)(2,1)S(1)}, u32[]{:S(2)}, u32[]{:S(2)}) collective-permute-start(bf16[64,1792]{1,0:T(8,128)(2,1)S(1)} %get-tuple-element.235), channel_id=1, source_target_pairs={{0,2},{1,3},{2,0},{3,1},{4,6},{5,7},{6,4},{7,5},{8,10},{9,11},{10,... | collective-permute-start | bytes 688136 | tf_op jit(solution)/shard_map/ppermute | solution.py:66
  554.3 8.9 %collective-permute-start.43 = (bf16[64,1792]{1,0:T(8,128)(2,1)}, bf16[64,1792]{1,0:T(8,128)(2,1)}, u32[]{:S(2)}, u32[]{:S(2)}) collective-permute-start(bf16[64,1792]{1,0:T(8,128)(2,1)} %get-tuple-element.230), channel_id=1, source_target_pairs={{0,1},{1,0},{2,3},{3,2},{4,5},{5,4},{6,7},{7,6},{8,9},{9,8},{10,11... | collective-permute-start | bytes 688136 | tf_op jit(solution)/shard_map/ppermute | solution.py:66
  554.3 12.9 %collective-permute-start.45 = (bf16[64,1792]{1,0:T(8,128)(2,1)}, bf16[64,1792]{1,0:T(8,128)(2,1)}, u32[]{:S(2)}, u32[]{:S(2)}) collective-permute-start(bf16[64,1792]{1,0:T(8,128)(2,1)} %get-tuple-element.231), channel_id=1, source_target_pairs={{0,3},{1,2},{2,1},{3,0},{4,7},{5,6},{6,5},{7,4},{8,11},{9,10},{10,... | collective-permute-start | bytes 688136 | tf_op jit(solution)/shard_map/ppermute | solution.py:66
  555.8 12.8 %collective-permute-start.44 = (bf16[64,1792]{1,0:T(8,128)(2,1)}, bf16[64,1792]{1,0:T(8,128)(2,1)}, u32[]{:S(2)}, u32[]{:S(2)}) collective-permute-start(bf16[64,1792]{1,0:T(8,128)(2,1)} %get-tuple-element.232), channel_id=1, source_target_pairs={{0,2},{1,3},{2,0},{3,1},{4,6},{5,7},{6,4},{7,5},{8,10},{9,11},{10,... | collective-permute-start | bytes 688136 | tf_op jit(solution)/shard_map/ppermute | solution.py:66
  562.4 8.0 %collective-permute-start.46 = (bf16[256,1792]{1,0:T(8,128)(2,1)}, bf16[256,1792]{1,0:T(8,128)(2,1)}, u32[]{:S(2)}, u32[]{:S(2)}) collective-permute-start(bf16[256,1792]{1,0:T(8,128)(2,1)} %slice.404), channel_id=1, source_target_pairs={{0,16},{16,0},{1,17},{17,1},{2,18},{18,2},{3,19},{19,3},{4,20},{20... | collective-permute-start | bytes 2752520 | tf_op jit(solution)/shard_map/ppermute | solution.py:39
  572.5 6.3 collective-permute-start.52
  575.3 104.2 %collective-permute-start.47 = (bf16[64,1792]{1,0:T(8,128)(2,1)}, bf16[64,1792]{1,0:T(8,128)(2,1)}, u32[]{:S(2)}, u32[]{:S(2)}) collective-permute-start(bf16[64,1792]{1,0:T(8,128)(2,1)} %get-tuple-element.227), channel_id=1, source_target_pairs={{0,1},{1,0},{2,3},{3,2},{4,5},{5,4},{6,7},{7,6},{8,9},{9,8},{10,11... | collective-permute-start | bytes 688136 | tf_op jit(solution)/shard_map/ppermute | solution.py:66
  575.4 104.0 %collective-permute-start.49 = (bf16[64,1792]{1,0:T(8,128)(2,1)}, bf16[64,1792]{1,0:T(8,128)(2,1)}, u32[]{:S(2)}, u32[]{:S(2)}) collective-permute-start(bf16[64,1792]{1,0:T(8,128)(2,1)} %get-tuple-element.228), channel_id=1, source_target_pairs={{0,3},{1,2},{2,1},{3,0},{4,7},{5,6},{6,5},{7,4},{8,11},{9,10},{10,... | collective-permute-start | bytes 688136 | tf_op jit(solution)/shard_map/ppermute | solution.py:66
  576.9 102.6 %collective-permute-start.48 = (bf16[64,1792]{1,0:T(8,128)(2,1)}, bf16[64,1792]{1,0:T(8,128)(2,1)}, u32[]{:S(2)}, u32[]{:S(2)}) collective-permute-start(bf16[64,1792]{1,0:T(8,128)(2,1)} %get-tuple-element.229), channel_id=1, source_target_pairs={{0,2},{1,3},{2,0},{3,1},{4,6},{5,7},{6,4},{7,5},{8,10},{9,11},{10,... | collective-permute-start | bytes 688136 | tf_op jit(solution)/shard_map/ppermute | solution.py:66
  578.9 12.0 %collective-permute-start.53 = (f32[2,5,1792]{2,0,1:T(2,128)S(1)}, f32[2,5,1792]{2,0,1:T(2,128)S(1)}, u32[]{:S(2)}, u32[]{:S(2)}) collective-permute-start(f32[2,5,1792]{2,0,1:T(2,128)S(1)} %fusion.51), channel_id=1, source_target_pairs={{0,2},{1,3},{2,0},{3,1},{4,6},{5,7},{6,4},{7,5},{8,10},{9,11},{10,... | collective-permute-start | bytes 215048 | tf_op jit(solution)/shard_map/ppermute | solution.py:88
  591.0 90.2 %collective-permute-start.54 = (f32[2,5,1792]{2,0,1:T(2,128)S(1)}, f32[2,5,1792]{2,0,1:T(2,128)}, u32[]{:S(2)}, u32[]{:S(2)}) collective-permute-start(f32[2,5,1792]{2,0,1:T(2,128)S(1)} %add.367), channel_id=1, source_target_pairs={{0,4},{4,0},{8,12},{12,8},{1,5},{5,1},{9,13},{13,9},{2,6},{6,2},{1... | collective-permute-start | bytes 215048 | tf_op jit(solution)/shard_map/ppermute | solution.py:88
  682.2 7.1 collective-permute-start.55
  685.9 5.1 collective-permute-start.50
  690.4 9.5 %collective-permute-start.40 = (bf16[448,1792]{1,0:T(8,128)(2,1)S(1)}, bf16[448,1792]{1,0:T(8,128)(2,1)S(1)}, u32[]{:S(2)}, u32[]{:S(2)}) collective-permute-start(bf16[448,1792]{1,0:T(8,128)(2,1)S(1)} %broadcast_select_fusion.2), channel_id=1, source_target_pairs={{0,16},{16,0},{1,17},{17,1},{2,18},{18,2},{3,19},{19,3},{4,20},{20... | collective-permute-start | bytes 4816904 | tf_op jit(solution)/shard_map/ppermute | solution.py:39
  692.4 7.2 collective-permute-start.39
  (72 other events, 532.0 us)
Sparse Core Ops, SparseCore 0:
  16.6 59.5 all-gather.3
  78.4 172.0 all-gather.5
  252.7 115.7 all-gather.7
  384.9 111.0 reduce-scatter.3
  498.3 181.1 reduce-scatter.5
  681.6 55.1 reduce-scatter.7

commit v8 on v7

--- a/solution.py
+++ b/solution.py
@@ -14,6 +14,7 @@
 LANES = 128
 WIDE = 256
 SUBLANES = 8
+CHUNKS = 2
 
 EPS = 1e-06
 
@@ -67,14 +68,21 @@
     return total
 
 
-def ring_gather(piece):
+def ring_step(piece):
+    size = lax.axis_size("dp")
+    return lax.ppermute(piece, "dp", [(i, (i + 1) % size) for i in range(size)])
+
+
+def ring_gather(piece, moved=None):
     size = lax.axis_size("dp")
     index = lax.axis_index("dp")
     count = piece.shape[0]
     full = jnp.zeros((size * count, piece.shape[1]), piece.dtype)
     for step in range(size):
-        if step:
-            piece = lax.ppermute(piece, "dp", [(i, (i + 1) % size) for i in range(size)])
+        if step == 1 and moved is not None:
+            piece = moved
+        elif step:
+            piece = ring_step(piece)
         full = lax.dynamic_update_slice_in_dim(full, piece, (index - step) % size * count, 0)
     return full
 
@@ -175,24 +183,14 @@
 def feed_kernel(
     units, tail, near_ref, far_ref, near_grad_ref, far_grad_ref, feed_ref, last_ref, *refs
 ):
-    extras, (block_ref, rest_ref, halves_ref, inner_ref, rows_ref, grads_ref) = refs[:-6], refs[-6:]
+    extras, refs = refs[:-8], refs[-8:]
+    block_ref, rest_ref, halves_ref, inner_ref, rows_ref, grads_ref, wide_ref, down_ref = refs
     main = units // LANES * LANES
     over = units - main
-    base = 0
-    for extra in extras:
-        block_ref[:, pl.ds(base, extra.shape[1])] = extra[...]
-        base += extra.shape[1]
-
-    def give(column, value):
-        block_ref[:, pl.ds(base + column, WIDE)] = value.astype(jnp.bfloat16)
-
+    step = pl.program_id(0)
     length = near_ref.shape[0]
-    rows_ref[:length] = near_ref[...]
-    rows_ref[length:] = far_ref[...]
-    grads_ref[:length] = near_grad_ref[...]
-    grads_ref[length:] = far_grad_ref[...]
-    rows = rows_ref[...]
-    branch = grads_ref[...]
+    size = feed_ref.shape[0]
+    chunks = rows_ref.shape[1] // size
 
     def parts(gate, upper, grad):
         sigma = jax.nn.sigmoid(gate)
@@ -200,77 +198,111 @@
         slope = sigma * (1.0 + gate * (1.0 - sigma))
         return (act * upper, grad * upper * slope, grad * act)
 
-    for start in range(0, main, WIDE):
-        places = tuple(start + i * main for i in range(3))
-        first, second, third = (pl.ds(place, WIDE) for place in places)
-        gate = dot(rows, feed_ref[:, second])
-        upper = dot(rows, feed_ref[:, third])
-        grad = dot(branch, feed_ref[:, first])
-        inner, grad_gate, grad_upper = (part.astype(jnp.bfloat16) for part in parts(gate, upper, grad))
-        inner_ref[:, first] = inner
-        halves_ref[:, first] = grad_gate
-        halves_ref[:, second] = grad_upper
-        give(places[0], dot_tn(branch, inner))
-        give(places[1], dot_tn(rows, grad_gate))
-        give(places[2], dot_tn(rows, grad_upper))
-
-    ends = feed_ref[:, pl.ds(3 * main, WIDE)]
-    both = dot(rows, ends)
-    upper = pltpu.roll(both, WIDE - over, 1)
-    grad = pltpu.roll(dot(branch, ends), WIDE - 2 * over, 1)[:, :LANES]
-    more = pltpu.roll(dot(branch, last_ref[...]), over, 1)
-    grad = jnp.where(lanes(grad) < over - tail, grad, more)
-    inner, grad_gate, grad_upper = (
-        jnp.where(lanes(part) < over, part, 0.0)
-        for part in parts(both[:, :LANES], upper[:, :LANES], grad)
-    )
-    inner = inner.astype(jnp.bfloat16)
-    inner_ref[:, pl.ds(main, over)] = inner[:, :over]
-    empty = jnp.zeros_like(grad_gate)
-    wide = jnp.concatenate([grad_gate, empty], axis=1)
-    wide = wide + pltpu.roll(jnp.concatenate([grad_upper, empty], axis=1), over, 1)
-    wide = wide.astype(jnp.bfloat16)
-    halves_ref[:, pl.ds(2 * main, WIDE)] = wide
-    down = dot_tn(branch, inner)
-    moved = pltpu.roll(jnp.concatenate([down, jnp.zeros_like(down)], axis=1), 2 * over, 1)
-    wide = dot_tn(rows, wide)
-    give(3 * main, jnp.where(lanes(wide) < 2 * over, wide, moved))
-    moved = pltpu.roll(jnp.concatenate([down, jnp.zeros_like(down)], axis=1), WIDE - over, 1)
-    rest_ref[...] = jnp.where(lanes(moved) < WIDE - tail, 0.0, moved).astype(jnp.bfloat16)
+    @pl.when(step == 0)
+    def _():
+        rows_ref[:length] = near_ref[...]
+        rows_ref[length:] = far_ref[...]
+        grads_ref[:length] = near_grad_ref[...]
+        grads_ref[length:] = far_grad_ref[...]
+
+    for chunk in range(chunks):
+        place = pl.ds(chunk * size, size)
+
+        @pl.when(step == chunk)
+        def _(chunk=chunk, place=place):
+            rows, branch = rows_ref[:, place], grads_ref[:, place]
+            wide = dot(rows, feed_ref[:, pl.ds(main, 2 * main + WIDE)])
+            down = dot(branch, feed_ref[:, pl.ds(0, main)])
+            ends = dot(branch, feed_ref[:, pl.ds(3 * main, WIDE)])
+            if chunk:
+                wide = wide + wide_ref[...]
+                down = down + down_ref[:, pl.ds(0, main)]
+                ends = ends + down_ref[:, pl.ds(main, WIDE)]
+            if chunk < chunks - 1:
+                wide_ref[...] = wide
+                down_ref[:, pl.ds(0, main)] = down
+                down_ref[:, pl.ds(main, WIDE)] = ends
+                return
+            inner, grad_gate, grad_upper = (
+                part.astype(jnp.bfloat16) for part in parts(wide[:, :main], wide[:, main : 2 * main], down)
+            )
+            inner_ref[:, pl.ds(0, main)] = inner
+            halves_ref[:, pl.ds(0, main)] = grad_gate
+            halves_ref[:, pl.ds(main, main)] = grad_upper
+            both = wide[:, 2 * main :]
+            upper = pltpu.roll(both, WIDE - over, 1)
+            grad = pltpu.roll(ends, WIDE - 2 * over, 1)[:, :LANES]
+            more = pltpu.roll(dot(grads_ref[...], last_ref[...]), over, 1)
+            grad = jnp.where(lanes(grad) < over - tail, grad, more)
+            inner, grad_gate, grad_upper = (
+                jnp.where(lanes(part) < over, part, 0.0)
+                for part in parts(both[:, :LANES], upper[:, :LANES], grad)
+            )
+            inner_ref[:, pl.ds(main, LANES)] = inner.astype(jnp.bfloat16)
+            empty = jnp.zeros_like(grad_gate)
+            last = jnp.concatenate([grad_gate, empty], axis=1)
+            last = last + pltpu.roll(jnp.concatenate([grad_upper, empty], axis=1), over, 1)
+            halves_ref[:, pl.ds(2 * main, WIDE)] = last.astype(jnp.bfloat16)
+
+        @pl.when(step == chunks + chunk)
+        def _(place=place):
+            base = 0
+            for extra in extras:
+                block_ref[:, pl.ds(base, extra.shape[1])] = extra[...]
+                base += extra.shape[1]
+            rows, branch = rows_ref[:, place], grads_ref[:, place]
+            down = dot_tn(branch, inner_ref[:, pl.ds(0, main)])
+            block_ref[:, pl.ds(base, main)] = down.astype(jnp.bfloat16)
+            wide = dot_tn(rows, halves_ref[:, pl.ds(0, 2 * main)])
+            block_ref[:, pl.ds(base + main, 2 * main)] = wide.astype(jnp.bfloat16)
+            down = dot_tn(branch, inner_ref[:, pl.ds(main, LANES)])
+            down = jnp.concatenate([down, jnp.zeros_like(down)], axis=1)
+            wide = dot_tn(rows, halves_ref[:, pl.ds(2 * main, WIDE)])
+            wide = jnp.where(lanes(wide) < 2 * over, wide, pltpu.roll(down, 2 * over, 1))
+            block_ref[:, pl.ds(base + 3 * main, WIDE)] = wide.astype(jnp.bfloat16)
+            moved = pltpu.roll(down, WIDE - over, 1)
+            rest_ref[...] = jnp.where(lanes(moved) < WIDE - tail, 0.0, moved).astype(jnp.bfloat16)
 
 
 def feed_both(units, tail, near, far, near_grad, far_grad, feed, attn, *extras):
     count, model = 2 * near.shape[0], near.shape[1]
     main = units // LANES * LANES
     width = 3 * units - tail
-    shapes = (
-        (model, width + sum(extra.shape[1] for extra in extras)),
-        (model, WIDE),
-        (count, width - main),
-        (count, units),
-    )
-    blocks = (near, far, near_grad, far_grad)
+    size = model // CHUNKS
+    total = width + sum(extra.shape[1] for extra in extras)
+    shapes = ((model, total), (model, WIDE), (count, width - main), (count, main + LANES))
+    end = attn.shape[1] // LANES - 1
+
+    def later(columns):
+        return pl.BlockSpec((size, columns), lambda step: (jnp.maximum(step - CHUNKS, 0), 0))
 
     def whole(shape):
         return pl.BlockSpec(shape, lambda step: (0, 0), pipeline_mode=pl.Buffered(1))
 
-    end = attn.shape[1] // LANES - 1
     return pl.pallas_call(
         functools.partial(feed_kernel, units, tail),
-        grid=(1,),
+        grid=(2 * CHUNKS,),
         out_shape=[jax.ShapeDtypeStruct(shape, jnp.bfloat16) for shape in shapes],
-        in_specs=[whole(block.shape) for block in blocks]
-        + [whole((model, width)), pl.BlockSpec((model, LANES), lambda step: (0, end))]
-        + [whole(extra.shape) for extra in extras],
-        out_specs=[whole(shape) for shape in shapes],
-        scratch_shapes=[pltpu.VMEM((count, model), jnp.bfloat16)] * 2,
+        in_specs=[whole(near.shape)] * 4
+        + [
+            pl.BlockSpec((size, width), lambda step: (jnp.minimum(step, CHUNKS - 1), 0)),
+            pl.BlockSpec((model, LANES), lambda step: (0, end), pipeline_mode=pl.Buffered(1)),
+        ]
+        + [later(extra.shape[1]) for extra in extras],
+        out_specs=[later(total), later(WIDE), whole(shapes[2]), whole(shapes[3])],
+        scratch_shapes=[
+            pltpu.VMEM((count, model), jnp.bfloat16),
+            pltpu.VMEM((count, model), jnp.bfloat16),
+            pltpu.VMEM((count, width - main), jnp.float32),
+            pltpu.VMEM((count, main + WIDE), jnp.float32),
+        ],
         compiler_params=pltpu.CompilerParams(vmem_limit_bytes=56 * 2**20),
         cost_estimate=pl.CostEstimate(
             flops=4 * count * model * width,
             bytes_accessed=20 * 2**20,
             transcendentals=count * units,
         ),
-    )(*blocks, feed, attn, *extras)
+    )(near, far, near_grad, far_grad, feed, attn, *extras)
 
 
 def take(block, column, width):
@@ -580,12 +612,14 @@
         other = swap(build(1 - core))
         return (jnp.where(lower, mine, other), jnp.where(lower, other, mine))
 
-    def attn_piece(which):
-        values = half(value_gate[0], 2, which)
-        last = half(down_weight[0], 0, which)[units - tail :]
-        return jnp.concatenate(
-            [values[:, 0], values[:, 1], half(out_weight[0], 0, which).T, last.T], axis=1
-        )
+    def attn_piece(pair, which):
+        own = slice(which * channels, (which + 1) * channels)
+        wide = pair.shape[2] // 2
+        pair = pair[:, :, which * wide : (which + 1) * wide]
+        last = down_weight[0][(which + 1) * units - tail : (which + 1) * units]
+        values = value_gate[0][:, :, own]
+        parts = [values[:, 0], values[:, 1], pair[:, 0], pair[:, 1], out_weight[0][own].T, last.T]
+        return jnp.concatenate(parts, axis=1)
 
     def feed_piece(which):
         pair = half(gate_up[0], 2, which)
@@ -598,18 +632,16 @@
     def fetch(piece):
         return lax.all_gather(piece, "dp", axis=0, tiled=True)
 
-    def with_pair(attn, pair):
-        pair = half(pair, 2, core)
-        both = 2 * channels
-        return jnp.concatenate([attn[:, :both], pair[:, 0], pair[:, 1], attn[:, both:]], axis=1)
-
-    attn_parts = both_layers(attn_piece)
+    attn_zero = fetch(jnp.where(lower, attn_piece(lin_qk, 0), swap(attn_piece(lin_qk, 1))))
     feed_parts = both_layers(feed_piece)
-    attn_zero = fetch(with_pair(attn_parts[0], lin_qk))
-    packed = fetch(feed_parts[0])
-    split = packed.shape[1]
-    attn_zero, attn_one = lax.optimization_barrier((attn_zero, with_pair(attn_parts[1], win_qk)))
-    attn_one = ring_gather(attn_one)
+    split = feed_parts[0].shape[1]
+    edge = split - WIDE
+    most = fetch(feed_parts[0][:, :edge])
+    attn_one = jnp.where(lower, swap(attn_piece(win_qk, 0)), attn_piece(win_qk, 1))
+    piece = jnp.concatenate([attn_one, feed_parts[0][:, edge:]], axis=1)
+    attn_zero, moved = lax.optimization_barrier((attn_zero, ring_step(piece)))
+    ring = ring_gather(piece, moved)
+    attn_one, ends_zero = ring[:, : attn_one.shape[1]], ring[:, attn_one.shape[1] :]
     feed_one = fetch(feed_parts[1])
     down_one = jnp.concatenate(
         [feed_one[:, :main], feed_one[:, main + 2 * units :], attn_one[:, attn_one.shape[1] - tail :]], axis=1
@@ -655,19 +687,22 @@
     hidden, kept_zero = mix(entering, gains_zero[0], attn_zero, taps_zero, True)
     scale, normed = rms_rows(hidden, gains_zero[1])
     near, far = spread_pair(normed)
-    near, far, attn_one = lax.optimization_barrier((near, far, attn_one))
+    grad_out = cotangent * mask
+    near, far, attn_one, ends_zero, *grads_one = lax.optimization_barrier(
+        (near, far, attn_one, ends_zero, *spread_pair(grad_out))
+    )
+    packed = jnp.concatenate([most, ends_zero], axis=1)
     kept_feed = (hidden, scale, near, far)
     middle = hidden + collect_pair(*feed_terms(units, tail, near, far, packed, attn_zero))
     middle = middle.astype(jnp.bfloat16).astype(jnp.float32)
 
     hidden, kept_one = mix(middle, gains_one[0], attn_one, taps_one, False)
     scale, normed = rms_rows(hidden, gains_one[1])
-    grad_out = cotangent * mask
     block, rest, grad_halves, inner = feed_both(
-        units, tail, *spread_pair(normed), *spread_pair(grad_out), feed_one, attn_one
+        units, tail, *spread_pair(normed), *grads_one, feed_one, attn_one
     )
     queue.scatter(block)
-    final = hidden + collect(dot_nt(inner, down_one))
+    final = hidden + collect(dot_nt(inner[:, :units], down_one))
     back, gain_two = rms_back(hidden, scale, gains_one[1], collect(dot_nt(grad_halves, feed_one[:, main:])))
     attn_grads, grad_middle, gain_one, taps_one = mix_back(
         kept_one, grad_out + back, gains_one[0], attn_one, taps_one, rest, False
@@ -749,16 +784,17 @@
     win_grad = by_rows(pair_home(early[:, both : early.shape[1] - WIDE]))
     gate_up_grad = by_rows(gate_up_grad)
     low, high = jnp.where(lower, own, away), jnp.where(lower, away, own)
-    last, low, high, gate_up_grad, down_grad, win_grad, ends, sums = lax.optimization_barrier(
-        (last, low, high, gate_up_grad, down_grad, win_grad, ends, sums)
+    gain_sums, taps_sums = by_rows(sums[:, :2]), by_rows(sums[:, 2:])
+    last, low, high, gate_up_grad, down_grad, win_grad, ends, gain_sums, taps_sums = lax.optimization_barrier(
+        (last, low, high, gate_up_grad, down_grad, win_grad, ends, gain_sums, taps_sums)
     )
     vgate_grad, out_grad, pair_grad, down_grad = end_call(
         channels, tail, gap, core, last, swap(last), low, high, down_grad
     )
     return (
         ends[None],
-        sums[:, :2],
-        sums[:, 2:],
+        gain_sums,
+        taps_sums,
         jnp.transpose(pair_grad, (2, 0, 1)),
         win_grad,
         vgate_grad[None],

time: 762 us -> 745 us (0.978)
  waiting for transfers between devices: 328 us -> 288 us
  local copies, waits for them, and re-layouts: 80.4 us -> 104 us
    all_gather x3, waiting for transfers between devices: 46.1 us -> 1.74 us  [fetch(): return lax.all_gather(piece, 'dp', axis=0, tiled=True)]
    unnamed x114 -> x128, local copies, waits for them, and re-layouts: 14.3 us -> 21.9 us
    ppermute x25 -> x26, waiting for transfers between devices: 26.6 us -> 27.4 us  [swap(): return lax.ppermute(block, 'section', [(0, 1), (1, 0)])]
  transfers between devices with their start and end apart: 63 -> 64, of which waited for: 41 -> 40; matrix products, arithmetic and copies ran while one was open for 14% -> 18% of each run, Pallas kernels for 10% -> 10%
where the time goes in v8:
time: 745 us; the launch traced here: 736 us
  waiting for transfers between devices  288 us (39%)
  blocking collectives  110 us (15%)
  local copies, waits for them, and re-layouts  104 us (14%)
  Pallas kernels  90.8 us (12%)
  starting transfers between devices  76.6 us (10%)
  other arithmetic  39.7 us (5%)
  between operations  15.6 us (2%)
  matrix products  11.4 us (2%)
    all_gather x8, blocking collectives, spread_pair(): lax.all_gather(rows.astype(jnp.bfloat16), 'tensor', axis=0, tiled=True)  110 us
    reduce_scatter x3, waiting for transfers between devices, scatter(): lax.psum_scatter(block, 'dp', scatter_dimension=0, tiled=True)  101 us
    ppermute x3, waiting for transfers between devices, ring_step(): return lax.ppermute(piece, 'dp', [(i, (i + 1) % size) for i in range(size)])  82.3 us
    ppermute x24, waiting for transfers between devices, collect_pair(): total = total + lax.ppermute(block, 'tensor', pairs).astype(jnp.float32)  59.3 us
    pallas_call x4, Pallas kernels, whole_call(): pl.pallas_call(kernel, grid=(1,), out_shape=[jax.ShapeDtypeStruct(shape,...  41.6 us
    ppermute x3, starting transfers between devices, ring_step(): return lax.ppermute(piece, 'dp', [(i, (i + 1) % size) for i in range(size)])  34.6 us
    pallas_call x2, Pallas kernels, feed_both(): pl.pallas_call(functools.partial(feed_kernel, units, tail), grid=(2 * CHU...  33.1 us
    ppermute x24, starting transfers between devices, collect_pair(): total = total + lax.ppermute(block, 'tensor', pairs).astype(jnp.float32)  28.9 us
  transfers between devices with their start and end apart: 64, of which 40 were waited for; matrix products, arithmetic and copies ran while one was open for 18% of the time, Pallas kernels for 10%

profile of v8, /device:TPU:0, one launch (start us, length us, event | category | flops | bytes accessed | tf_op | source)
XLA Modules:
  0.0 735.7 jit_solution(12390728876588212532)
XLA Ops:
  17.7 5.9 constant_dynamic-slice_fusion.26
  24.9 3.2 concatenate.112
  43.4 3.3 concatenate.109
  64.1 12.0 %all_gather.33.near_ref = bf16[256,1792]{1,0:T(8,128)(2,1)S(1)} all-gather(bf16[64,1792]{1,0:T(8,128)(2,1)S(1)} %fusion.19), channel_id=1, replica_groups=mesh['section'=2,'dp'=4,'tensor'=4] {'tensor'}, dimensions={0}, use_global_device_ids=true | all-gather | bytes 1146880 | tf_op jit(solution)/shard_map/all_gather | solution.py:44
  77.0 30.0 %collective-permute-done.6 = bf16[448,1408]{1,0:T(8,128)(2,1)} collective-permute-done((bf16[448,1408]{1,0:T(8,128)(2,1)S(1)}, bf16[448,1408]{1,0:T(8,128)(2,1)}, u32[]{:S(2)}, u32[]{:S(2)}) %collective-permute-start.6) | collective-permute-done | bytes 1261600 | tf_op jit(solution)/shard_map/ppermute | solution.py:73
  108.0 6.7 shard_map.169
  124.1 21.0 %all_gather.36.near_grad_ref = bf16[256,1792]{1,0:T(8,128)(2,1)} all-gather(bf16[64,1792]{1,0:T(8,128)(2,1)S(1)} %copy-done.36), channel_id=1, replica_groups=mesh['section'=2,'dp'=4,'tensor'=4] {'tensor'}, dimensions={0}, use_global_device_ids=true | all-gather | bytes 1146880 | tf_op jit(solution)/shard_map/all_gather | solution.py:44
  145.3 28.9 %collective-permute-done.12 = bf16[448,1408]{1,0:T(8,128)(2,1)} collective-permute-done((bf16[448,1408]{1,0:T(8,128)(2,1)}, bf16[448,1408]{1,0:T(8,128)(2,1)}, u32[]{:S(2)}, u32[]{:S(2)}) %collective-permute-start.12) | collective-permute-done | bytes 1261600 | tf_op jit(solution)/shard_map/ppermute | solution.py:73
  174.2 31.6 %collective-permute-start.13 = (bf16[448,1408]{1,0:T(8,128)(2,1)}, bf16[448,1408]{1,0:T(8,128)(2,1)}, u32[]{:S(2)}, u32[]{:S(2)}) collective-permute-start(bf16[448,1408]{1,0:T(8,128)(2,1)} %collective-permute-done.12), channel_id=1, source_target_pairs={{0,4},{4,8},{8,12},{12,0},{1,5},{5,9},{9,13},{13,1},{2,6},{6,10},{... | collective-permute-start | bytes 3784712 | tf_op jit(solution)/shard_map/ppermute | solution.py:73
  206.0 12.5 %all_gather.35.near_ref = bf16[256,1792]{1,0:T(8,128)(2,1)S(1)} all-gather(bf16[64,1792]{1,0:T(8,128)(2,1)S(1)} %multiply_convert_fusion.1), channel_id=1, replica_groups=mesh['section'=2,'dp'=4,'tensor'=4] {'tensor'}, dimensions={0}, use_global_device_ids=true | all-gather | bytes 1146880 | tf_op jit(solution)/shard_map/all_gather | solution.py:44
  223.7 23.3 %collective-permute-done.13 = bf16[448,1408]{1,0:T(8,128)(2,1)} collective-permute-done((bf16[448,1408]{1,0:T(8,128)(2,1)}, bf16[448,1408]{1,0:T(8,128)(2,1)}, u32[]{:S(2)}, u32[]{:S(2)}) %collective-permute-start.13) | collective-permute-done | bytes 1261600 | tf_op jit(solution)/shard_map/ppermute | solution.py:73
  250.7 4.5 slice.390.attn_ref.last_ref
  255.3 3.2 constant_dynamic-update-slice_fusion.5
  261.3 11.3 %shard_map.170 = (f32[256,1792]{1,0:T(8,128)S(1)}, bf16[256,1792]{1,0:T(8,128)(2,1)S(1)}) custom-call(bf16[256,1792]{1,0:T(8,128)(2,1)S(1)} %all_gather.35.near_ref, bf16[256,1792]{1,0:T(8,128)(2,1)S(1)} %collective-permute-done.11.far_ref, bf16[1792,1792]{1,0:T(8,128)(2,1)} %copy-done.3, bf16[1792,768]{1,0:T(8,128)(2,1)} %all-gather.4.cloned.1.call-done.attn_ref.last_ref), custom_call_target="tpu_custom_call" | custom-call | flops 1048576 | bytes 65536 | tf_op jit(solution)/shard_map/pallas_call | solution.py:160
  279.0 5.0 collective-permute-done.16
  283.9 5.1 collective-permute-done.18
  290.8 12.8 %all_gather.38.near_ref = bf16[256,1792]{1,0:T(8,128)(2,1)S(1)} all-gather(bf16[64,1792]{1,0:T(8,128)(2,1)S(1)} %fusion.26), channel_id=1, replica_groups=mesh['section'=2,'dp'=4,'tensor'=4] {'tensor'}, dimensions={0}, use_global_device_ids=true | all-gather | bytes 1146880 | tf_op jit(solution)/shard_map/all_gather | solution.py:44
  307.1 8.6 %shard_map.171 = (f32[256,1792]{1,0:T(8,128)}, bf16[256,1792]{1,0:T(8,128)(2,1)}, f32[512,896]{1,0:T(8,128)}, bf16[512,256]{1,0:T(8,128)(2,1)}) custom-call(bf16[256,1792]{1,0:T(8,128)(2,1)} %copy-done.6, bf16[256,1792]{1,0:T(8,128)(2,1)} %copy-done.12, bf16[1792,1152]{1,0:T(8,128)(2,1)} %slice.390.attn_ref.last_ref, f32[8,256]{1,0:T(8,128)} %pad.8.taps_ref), custom_call_target="tpu_custom_call" | custom-call | flops 1048576 | bytes 65536 | tf_op jit(solution)/shard_map/pallas_call | solution.py:469
  323.7 5.0 collective-permute-done.21
  328.7 4.0 collective-permute-done.23
  334.5 12.5 %all_gather.39.near_ref = bf16[256,1792]{1,0:T(8,128)(2,1)S(1)} all-gather(bf16[64,1792]{1,0:T(8,128)(2,1)S(1)} %multiply_convert_fusion), channel_id=1, replica_groups=mesh['section'=2,'dp'=4,'tensor'=4] {'tensor'}, dimensions={0}, use_global_device_ids=true | all-gather | bytes 1146880 | tf_op jit(solution)/shard_map/all_gather | solution.py:44
  350.4 15.9 %shard_map.172 = (bf16[1792,1792]{1,0:T(8,128)(2,1)}, bf16[1792,256]{1,0:T(8,128)(2,1)}, bf16[512,1280]{1,0:T(8,128)(2,1)}, bf16[512,640]{1,0:T(8,128)(2,1)}) custom-call(bf16[256,1792]{1,0:T(8,128)(2,1)} %copy-done.34, bf16[256,1792]{1,0:T(8,128)(2,1)} %copy-done.53, bf16[256,1792]{1,0:T(8,128)(2,1)} %all_gather.36.near_grad_ref, ...), custom_call_target="tpu_custom_call" | custom-call | flops 6576668672 | bytes 20971520 | tf_op jit(solution)/shard_map/pallas_call | solution.py:282
  367.6 4.9 fusion.2
  379.0 5.0 collective-permute-done.26
  384.0 4.4 collective-permute-done.28
  391.2 13.2 %all_gather.41.near_grad_ref = bf16[256,1792]{1,0:T(8,128)(2,1)S(1)} all-gather(bf16[64,1792]{1,0:T(8,128)(2,1)S(1)} %get-tuple-element.181), channel_id=1, replica_groups=mesh['section'=2,'dp'=4,'tensor'=4] {'tensor'}, dimensions={0}, use_global_device_ids=true | all-gather | bytes 1146880 | tf_op jit(solution)/shard_map/all_gather | solution.py:44
  407.9 14.3 %shard_map.173 = (bf16[1792,1152]{1,0:T(8,128)(2,1)}, f32[256,1792]{1,0:T(8,128)}, bf16[256,1792]{1,0:T(8,128)(2,1)}, f32[8,256]{1,0:T(8,128)}) custom-call(bf16[256,1792]{1,0:T(8,128)(2,1)} %copy-done.6, bf16[256,1792]{1,0:T(8,128)(2,1)} %copy-done.12, bf16[256,1792]{1,0:T(8,128)(2,1)} %copy-done.10, bf16[256,1792]{1,0:T(8,128)(2,1)} %copy-done.32, ...), custom_call_target="tpu_custom_call" | custom-call | flops 1048576 | bytes 65536 | tf_op jit(solution)/shard_map/pallas_call | solution.py:469
  430.2 5.0 collective-permute-done.31
  435.2 4.3 collective-permute-done.33
  441.3 13.0 %all_gather.42.near_grad_ref = bf16[256,1792]{1,0:T(8,128)(2,1)S(1)} all-gather(bf16[64,1792]{1,0:T(8,128)(2,1)S(1)} %fusion.31), channel_id=1, replica_groups=mesh['section'=2,'dp'=4,'tensor'=4] {'tensor'}, dimensions={0}, use_global_device_ids=true | all-gather | bytes 1146880 | tf_op jit(solution)/shard_map/all_gather | solution.py:44
  457.8 17.2 %shard_map.174 = (bf16[1792,2944]{1,0:T(8,128)(2,1)}, bf16[1792,256]{1,0:T(8,128)(2,1)}, bf16[512,1280]{1,0:T(8,128)(2,1)}, bf16[512,640]{1,0:T(8,128)(2,1)}) custom-call(bf16[256,1792]{1,0:T(8,128)(2,1)} %copy-done, bf16[256,1792]{1,0:T(8,128)(2,1)} %copy-done.1, bf16[256,1792]{1,0:T(8,128)(2,1)} %copy-done.35, bf16[256,1792]{1,0:T(8,128)(2,1)} %copy-done.54, ...), custom_call_target="tpu_custom_call" | custom-call | flops 6576668672 | bytes 20971520 | tf_op jit(solution)/shard_map/pallas_call | solution.py:282
  475.0 4.0 reduce-scatter.4.cloned.1.call-done
  480.3 4.9 fusion
  491.7 5.0 collective-permute-done.36
  496.6 5.1 collective-permute-done.38
  503.6 13.0 %all_gather.43.near_grad_ref = bf16[256,1792]{1,0:T(8,128)(2,1)S(1)} all-gather(bf16[64,1792]{1,0:T(8,128)(2,1)S(1)} %get-tuple-element.173), channel_id=1, replica_groups=mesh['section'=2,'dp'=4,'tensor'=4] {'tensor'}, dimensions={0}, use_global_device_ids=true | all-gather | bytes 1146880 | tf_op jit(solution)/shard_map/all_gather | solution.py:44
  520.1 12.0 %shard_map.175 = (bf16[1792,768]{1,0:T(8,128)(2,1)}, f32[256,1792]{1,0:T(8,128)}, bf16[256,1792]{1,0:T(8,128)(2,1)}, f32[8,256]{1,0:T(8,128)}) custom-call(bf16[256,1792]{1,0:T(8,128)(2,1)} %copy-done.5, bf16[256,1792]{1,0:T(8,128)(2,1)} %copy-done.11, bf16[256,1792]{1,0:T(8,128)(2,1)} %copy-done.9, bf16[256,1792]{1,0:T(8,128)(2,1)} %copy-done.31, ...), custom_call_target="tpu_custom_call" | custom-call | flops 1048576 | bytes 65536 | tf_op jit(solution)/shard_map/pallas_call | solution.py:469
  547.4 3.3 collective-permute-done.46
  564.5 10.7 %collective-permute-done.54 = f32[2,5,1792]{2,1,0:T(8,128)S(1)} collective-permute-done((f32[2,5,1792]{2,1,0:T(8,128)S(1)}, f32[2,5,1792]{2,1,0:T(8,128)S(1)}, u32[]{:S(2)}, u32[]{:S(2)}) %collective-permute-start.54) | collective-permute-done | bytes 71712 | tf_op jit(solution)/shard_map/ppermute | solution.py:96
  576.8 86.5 %reduce-scatter.6.cloned.1.call-done = bf16[448,2944]{1,0:T(8,128)(2,1)} async-done(((bf16[1792,2944]{1,0:T(8,128)(2,1)}), bf16[448,2944]{1,0:T(8,128)(2,1)}) %reduce-scatter.6.cloned.1.call-update) | async-done | bytes 2637840 | tf_op jit(solution)/shard_map/reduce_scatter | solution.py:591
  666.1 3.5 collective-permute-start.56
  669.9 5.2 collective-permute-done.56
  680.4 5.3 maximum_convert_fusion.1
  688.9 3.4 concatenate.126
  698.9 3.7 concatenate.125
  704.2 5.7 copy.103
  709.9 10.7 %reduce-scatter.8.cloned.1.call-done.mine_ref = bf16[448,768]{1,0:T(8,128)(2,1)} async-done(((bf16[1792,768]{1,0:T(8,128)(2,1)}), bf16[448,768]{1,0:T(8,128)(2,1)}) %reduce-scatter.8.cloned.1.call-update) | async-done | bytes 688144 | tf_op jit(solution)/shard_map/reduce_scatter | solution.py:591
  724.0 4.7 shard_map.176
  (380 shorter events, 186.0 us)
Async XLA Ops:
  7.2 99.9 %all-gather.4.cloned.1.call-start = ((), (), s32[]{:S(2)}) async-start(), calls=%async_computation.3 | async-start | bytes 3440640 | tf_op jit(solution)/shard_map/all_gather | solution.py:633
  15.0 240.3 %all-gather.6.cloned.1.call-start = ((), (), s32[]{:S(2)}) async-start(), calls=%async_computation.4 | async-start | bytes 6881280 | tf_op jit(solution)/shard_map/all_gather | solution.py:633
  28.1 4.4 collective-permute-start.5
  36.6 312.2 %all-gather.8.cloned.1.call-start = ((), (), s32[]{:S(2)}) async-start(), calls=%async_computation.5 | async-start | bytes 8028160 | tf_op jit(solution)/shard_map/all_gather | solution.py:633
  38.4 13.9 %collective-permute-start.1 = (f32[5,1792]{1,0:T(8,128)}, f32[5,1792]{1,0:T(8,128)}, u32[]{:S(2)}, u32[]{:S(2)}) collective-permute-start(f32[5,1792]{1,0:T(8,128)} %pad_maximum_fusion.3), channel_id=1, source_target_pairs={{0,16},{16,0},{1,17},{17,1},{2,18},{18,2},{3,19},{19,3},{4,20},{20... | collective-permute-start | bytes 107528 | tf_op jit(solution)/shard_map/ppermute | solution.py:40
  39.3 14.5 %collective-permute-start = (bf16[64,1792]{1,0:T(8,128)(2,1)}, bf16[64,1792]{1,0:T(8,128)(2,1)}, u32[]{:S(2)}, u32[]{:S(2)}) collective-permute-start(bf16[64,1792]{1,0:T(8,128)(2,1)} %dynamic-slice_bitcast_fusion.2), channel_id=1, source_target_pairs={{0,16},{16,0},{1,17},{17,1},{2,18},{18,2},{3,19},{19,3},{4,20},{20... | collective-permute-start | bytes 688136 | tf_op jit(solution)/shard_map/ppermute | solution.py:40
  46.7 9.1 %collective-permute-start.4 = (bf16[448,1152]{1,0:T(8,128)(2,1)}, bf16[448,1152]{1,0:T(8,128)(2,1)}, u32[]{:S(2)}, u32[]{:S(2)}) collective-permute-start(bf16[448,1152]{1,0:T(8,128)(2,1)} %concatenate.109), channel_id=1, source_target_pairs={{0,16},{16,0},{1,17},{17,1},{2,18},{18,2},{3,19},{19,3},{4,20},{20... | collective-permute-start | bytes 3096584 | tf_op jit(solution)/shard_map/ppermute | solution.py:40
  61.0 46.0 %collective-permute-start.6 = (bf16[448,1408]{1,0:T(8,128)(2,1)S(1)}, bf16[448,1408]{1,0:T(8,128)(2,1)}, u32[]{:S(2)}, u32[]{:S(2)}) collective-permute-start(bf16[448,1408]{1,0:T(8,128)(2,1)S(1)} %get-tuple-element.222), channel_id=1, source_target_pairs={{0,4},{4,8},{8,12},{12,0},{1,5},{5,9},{9,13},{13,1},{2,6},{6,10},{... | collective-permute-start | bytes 3784712 | tf_op jit(solution)/shard_map/ppermute | solution.py:73
  76.1 30.9 %collective-permute-start.2 = (bf16[256,1792]{1,0:T(8,128)(2,1)S(1)}, bf16[256,1792]{1,0:T(8,128)(2,1)S(1)}, u32[]{:S(2)}, u32[]{:S(2)}) collective-permute-start(bf16[256,1792]{1,0:T(8,128)(2,1)S(1)} %all_gather.33.near_ref), channel_id=1, source_target_pairs={{0,16},{16,0},{1,17},{17,1},{2,18},{18,2},{3,19},{19,3},{4,20},{20... | collective-permute-start | bytes 2752520 | tf_op jit(solution)/shard_map/ppermute | solution.py:40
  114.7 59.6 %collective-permute-start.12 = (bf16[448,1408]{1,0:T(8,128)(2,1)}, bf16[448,1408]{1,0:T(8,128)(2,1)}, u32[]{:S(2)}, u32[]{:S(2)}) collective-permute-start(bf16[448,1408]{1,0:T(8,128)(2,1)} %collective-permute-done.6), channel_id=1, source_target_pairs={{0,4},{4,8},{8,12},{12,0},{1,5},{5,9},{9,13},{13,1},{2,6},{6,10},{... | collective-permute-start | bytes 3784712 | tf_op jit(solution)/shard_map/ppermute | solution.py:73
  119.9 25.1 %collective-permute-start.8 = (bf16[64,1792]{1,0:T(8,128)(2,1)}, bf16[64,1792]{1,0:T(8,128)(2,1)S(1)}, u32[]{:S(2)}, u32[]{:S(2)}) collective-permute-start(bf16[64,1792]{1,0:T(8,128)(2,1)} %get-tuple-element.256), channel_id=1, source_target_pairs={{0,1},{1,0},{2,3},{3,2},{4,5},{5,4},{6,7},{7,6},{8,9},{9,8},{10,11... | collective-permute-start | bytes 688136 | tf_op jit(solution)/shard_map/ppermute | solution.py:67
  122.6 22.4 %collective-permute-start.10 = (bf16[64,1792]{1,0:T(8,128)(2,1)S(1)}, bf16[64,1792]{1,0:T(8,128)(2,1)S(1)}, u32[]{:S(2)}, u32[]{:S(2)}) collective-permute-start(bf16[64,1792]{1,0:T(8,128)(2,1)S(1)} %get-tuple-element.257), channel_id=1, source_target_pairs={{0,3},{1,2},{2,1},{3,0},{4,7},{5,6},{6,5},{7,4},{8,11},{9,10},{10,... | collective-permute-start | bytes 688136 | tf_op jit(solution)/shard_map/ppermute | solution.py:67
  124.0 21.0 %collective-permute-start.9 = (bf16[64,1792]{1,0:T(8,128)(2,1)S(1)}, bf16[64,1792]{1,0:T(8,128)(2,1)S(1)}, u32[]{:S(2)}, u32[]{:S(2)}) collective-permute-start(bf16[64,1792]{1,0:T(8,128)(2,1)S(1)} %get-tuple-element.258), channel_id=1, source_target_pairs={{0,2},{1,3},{2,0},{3,1},{4,6},{5,7},{6,4},{7,5},{8,10},{9,11},{10,... | collective-permute-start | bytes 688136 | tf_op jit(solution)/shard_map/ppermute | solution.py:67
  145.0 110.2 %collective-permute-start.14 = (bf16[256,1792]{1,0:T(8,128)(2,1)}, bf16[256,1792]{1,0:T(8,128)(2,1)}, u32[]{:S(2)}, u32[]{:S(2)}) collective-permute-start(bf16[256,1792]{1,0:T(8,128)(2,1)} %all_gather.36.near_grad_ref), channel_id=1, source_target_pairs={{0,16},{16,0},{1,17},{17,1},{2,18},{18,2},{3,19},{19,3},{4,20},{20... | collective-permute-start | bytes 2752520 | tf_op jit(solution)/shard_map/ppermute | solution.py:40
  174.2 72.8 %collective-permute-start.13 = (bf16[448,1408]{1,0:T(8,128)(2,1)}, bf16[448,1408]{1,0:T(8,128)(2,1)}, u32[]{:S(2)}, u32[]{:S(2)}) collective-permute-start(bf16[448,1408]{1,0:T(8,128)(2,1)} %collective-permute-done.12), channel_id=1, source_target_pairs={{0,4},{4,8},{8,12},{12,0},{1,5},{5,9},{9,13},{13,1},{2,6},{6,10},{... | collective-permute-start | bytes 3784712 | tf_op jit(solution)/shard_map/ppermute | solution.py:73
  218.5 36.8 %collective-permute-start.11 = (bf16[256,1792]{1,0:T(8,128)(2,1)S(1)}, bf16[256,1792]{1,0:T(8,128)(2,1)S(1)}, u32[]{:S(2)}, u32[]{:S(2)}) collective-permute-start(bf16[256,1792]{1,0:T(8,128)(2,1)S(1)} %all_gather.35.near_ref), channel_id=1, source_target_pairs={{0,16},{16,0},{1,17},{17,1},{2,18},{18,2},{3,19},{19,3},{4,20},{20... | collective-permute-start | bytes 2752520 | tf_op jit(solution)/shard_map/ppermute | solution.py:40
  218.6 260.4 %reduce-scatter.4.cloned.1.call-start = ((), (), s32[]{:S(2)}) async-start(), calls=%async_computation.6 | async-start | bytes 8028160 | tf_op jit(solution)/shard_map/reduce_scatter | solution.py:591
  275.4 8.5 %collective-permute-start.16 = (bf16[64,1792]{1,0:T(8,128)(2,1)S(1)}, bf16[64,1792]{1,0:T(8,128)(2,1)S(1)}, u32[]{:S(2)}, u32[]{:S(2)}) collective-permute-start(bf16[64,1792]{1,0:T(8,128)(2,1)S(1)} %get-tuple-element.253), channel_id=1, source_target_pairs={{0,1},{1,0},{2,3},{3,2},{4,5},{5,4},{6,7},{7,6},{8,9},{9,8},{10,11... | collective-permute-start | bytes 688136 | tf_op jit(solution)/shard_map/ppermute | solution.py:67
  277.0 12.1 %collective-permute-start.18 = (bf16[64,1792]{1,0:T(8,128)(2,1)S(1)}, bf16[64,1792]{1,0:T(8,128)(2,1)S(1)}, u32[]{:S(2)}, u32[]{:S(2)}) collective-permute-start(bf16[64,1792]{1,0:T(8,128)(2,1)S(1)} %get-tuple-element.254), channel_id=1, source_target_pairs={{0,3},{1,2},{2,1},{3,0},{4,7},{5,6},{6,5},{7,4},{8,11},{9,10},{10,... | collective-permute-start | bytes 688136 | tf_op jit(solution)/shard_map/ppermute | solution.py:67
  278.4 12.0 %collective-permute-start.17 = (bf16[64,1792]{1,0:T(8,128)(2,1)S(1)}, bf16[64,1792]{1,0:T(8,128)(2,1)S(1)}, u32[]{:S(2)}, u32[]{:S(2)}) collective-permute-start(bf16[64,1792]{1,0:T(8,128)(2,1)S(1)} %get-tuple-element.255), channel_id=1, source_target_pairs={{0,2},{1,3},{2,0},{3,1},{4,6},{5,7},{6,4},{7,5},{8,10},{9,11},{10,... | collective-permute-start | bytes 688136 | tf_op jit(solution)/shard_map/ppermute | solution.py:67
  320.2 8.5 %collective-permute-start.21 = (bf16[64,1792]{1,0:T(8,128)(2,1)S(1)}, bf16[64,1792]{1,0:T(8,128)(2,1)S(1)}, u32[]{:S(2)}, u32[]{:S(2)}) collective-permute-start(bf16[64,1792]{1,0:T(8,128)(2,1)S(1)} %get-tuple-element.250), channel_id=1, source_target_pairs={{0,1},{1,0},{2,3},{3,2},{4,5},{5,4},{6,7},{7,6},{8,9},{9,8},{10,11... | collective-permute-start | bytes 688136 | tf_op jit(solution)/shard_map/ppermute | solution.py:67
  320.3 12.4 %collective-permute-start.23 = (bf16[64,1792]{1,0:T(8,128)(2,1)S(1)}, bf16[64,1792]{1,0:T(8,128)(2,1)S(1)}, u32[]{:S(2)}, u32[]{:S(2)}) collective-permute-start(bf16[64,1792]{1,0:T(8,128)(2,1)S(1)} %get-tuple-element.251), channel_id=1, source_target_pairs={{0,3},{1,2},{2,1},{3,0},{4,7},{5,6},{6,5},{7,4},{8,11},{9,10},{10,... | collective-permute-start | bytes 688136 | tf_op jit(solution)/shard_map/ppermute | solution.py:67
  321.8 12.3 %collective-permute-start.22 = (bf16[64,1792]{1,0:T(8,128)(2,1)S(1)}, bf16[64,1792]{1,0:T(8,128)(2,1)S(1)}, u32[]{:S(2)}, u32[]{:S(2)}) collective-permute-start(bf16[64,1792]{1,0:T(8,128)(2,1)S(1)} %get-tuple-element.252), channel_id=1, source_target_pairs={{0,2},{1,3},{2,0},{3,1},{4,6},{5,7},{6,4},{7,5},{8,10},{9,11},{10,... | collective-permute-start | bytes 688136 | tf_op jit(solution)/shard_map/ppermute | solution.py:67
  366.4 296.9 %reduce-scatter.6.cloned.1.call-start = ((), (), s32[]{:S(2)}) async-start(), calls=%async_computation.7 | async-start | bytes 13189120 | tf_op jit(solution)/shard_map/reduce_scatter | solution.py:591
  375.5 8.5 %collective-permute-start.26 = (bf16[64,1792]{1,0:T(8,128)(2,1)S(1)}, bf16[64,1792]{1,0:T(8,128)(2,1)S(1)}, u32[]{:S(2)}, u32[]{:S(2)}) collective-permute-start(bf16[64,1792]{1,0:T(8,128)(2,1)S(1)} %get-tuple-element.247), channel_id=1, source_target_pairs={{0,1},{1,0},{2,3},{3,2},{4,5},{5,4},{6,7},{7,6},{8,9},{9,8},{10,11... | collective-permute-start | bytes 688136 | tf_op jit(solution)/shard_map/ppermute | solution.py:67
  376.3 12.1 %collective-permute-start.28 = (bf16[64,1792]{1,0:T(8,128)(2,1)S(1)}, bf16[64,1792]{1,0:T(8,128)(2,1)S(1)}, u32[]{:S(2)}, u32[]{:S(2)}) collective-permute-start(bf16[64,1792]{1,0:T(8,128)(2,1)S(1)} %get-tuple-element.248), channel_id=1, source_target_pairs={{0,3},{1,2},{2,1},{3,0},{4,7},{5,6},{6,5},{7,4},{8,11},{9,10},{10,... | collective-permute-start | bytes 688136 | tf_op jit(solution)/shard_map/ppermute | solution.py:67
  377.7 12.0 %collective-permute-start.27 = (bf16[64,1792]{1,0:T(8,128)(2,1)S(1)}, bf16[64,1792]{1,0:T(8,128)(2,1)S(1)}, u32[]{:S(2)}, u32[]{:S(2)}) collective-permute-start(bf16[64,1792]{1,0:T(8,128)(2,1)S(1)} %get-tuple-element.249), channel_id=1, source_target_pairs={{0,2},{1,3},{2,0},{3,1},{4,6},{5,7},{6,4},{7,5},{8,10},{9,11},{10,... | collective-permute-start | bytes 688136 | tf_op jit(solution)/shard_map/ppermute | solution.py:67
  426.7 8.5 %collective-permute-start.31 = (bf16[64,1792]{1,0:T(8,128)(2,1)S(1)}, bf16[64,1792]{1,0:T(8,128)(2,1)S(1)}, u32[]{:S(2)}, u32[]{:S(2)}) collective-permute-start(bf16[64,1792]{1,0:T(8,128)(2,1)S(1)} %get-tuple-element.244), channel_id=1, source_target_pairs={{0,1},{1,0},{2,3},{3,2},{4,5},{5,4},{6,7},{7,6},{8,9},{9,8},{10,11... | collective-permute-start | bytes 688136 | tf_op jit(solution)/shard_map/ppermute | solution.py:67
  427.3 12.1 %collective-permute-start.33 = (bf16[64,1792]{1,0:T(8,128)(2,1)S(1)}, bf16[64,1792]{1,0:T(8,128)(2,1)S(1)}, u32[]{:S(2)}, u32[]{:S(2)}) collective-permute-start(bf16[64,1792]{1,0:T(8,128)(2,1)S(1)} %get-tuple-element.245), channel_id=1, source_target_pairs={{0,3},{1,2},{2,1},{3,0},{4,7},{5,6},{6,5},{7,4},{8,11},{9,10},{10,... | collective-permute-start | bytes 688136 | tf_op jit(solution)/shard_map/ppermute | solution.py:67
  428.8 12.0 %collective-permute-start.32 = (bf16[64,1792]{1,0:T(8,128)(2,1)S(1)}, bf16[64,1792]{1,0:T(8,128)(2,1)S(1)}, u32[]{:S(2)}, u32[]{:S(2)}) collective-permute-start(bf16[64,1792]{1,0:T(8,128)(2,1)S(1)} %get-tuple-element.246), channel_id=1, source_target_pairs={{0,2},{1,3},{2,0},{3,1},{4,6},{5,7},{6,4},{7,5},{8,10},{9,11},{10,... | collective-permute-start | bytes 688136 | tf_op jit(solution)/shard_map/ppermute | solution.py:67
  479.0 241.5 %reduce-scatter.8.cloned.1.call-start = ((), (), s32[]{:S(2)}) async-start(), calls=%async_computation.8 | async-start | bytes 3440640 | tf_op jit(solution)/shard_map/reduce_scatter | solution.py:591
  488.1 8.5 %collective-permute-start.36 = (bf16[64,1792]{1,0:T(8,128)(2,1)S(1)}, bf16[64,1792]{1,0:T(8,128)(2,1)S(1)}, u32[]{:S(2)}, u32[]{:S(2)}) collective-permute-start(bf16[64,1792]{1,0:T(8,128)(2,1)S(1)} %get-tuple-element.241), channel_id=1, source_target_pairs={{0,1},{1,0},{2,3},{3,2},{4,5},{5,4},{6,7},{7,6},{8,9},{9,8},{10,11... | collective-permute-start | bytes 688136 | tf_op jit(solution)/shard_map/ppermute | solution.py:67
  489.6 12.1 %collective-permute-start.38 = (bf16[64,1792]{1,0:T(8,128)(2,1)S(1)}, bf16[64,1792]{1,0:T(8,128)(2,1)S(1)}, u32[]{:S(2)}, u32[]{:S(2)}) collective-permute-start(bf16[64,1792]{1,0:T(8,128)(2,1)S(1)} %get-tuple-element.242), channel_id=1, source_target_pairs={{0,3},{1,2},{2,1},{3,0},{4,7},{5,6},{6,5},{7,4},{8,11},{9,10},{10,... | collective-permute-start | bytes 688136 | tf_op jit(solution)/shard_map/ppermute | solution.py:67
  491.1 12.0 %collective-permute-start.37 = (bf16[64,1792]{1,0:T(8,128)(2,1)S(1)}, bf16[64,1792]{1,0:T(8,128)(2,1)S(1)}, u32[]{:S(2)}, u32[]{:S(2)}) collective-permute-start(bf16[64,1792]{1,0:T(8,128)(2,1)S(1)} %get-tuple-element.243), channel_id=1, source_target_pairs={{0,2},{1,3},{2,0},{3,1},{4,6},{5,7},{6,4},{7,5},{8,10},{9,11},{10,... | collective-permute-start | bytes 688136 | tf_op jit(solution)/shard_map/ppermute | solution.py:67
  537.8 9.5 %collective-permute-start.44 = (bf16[64,1792]{1,0:T(8,128)(2,1)}, bf16[64,1792]{1,0:T(8,128)(2,1)S(1)}, u32[]{:S(2)}, u32[]{:S(2)}) collective-permute-start(bf16[64,1792]{1,0:T(8,128)(2,1)} %get-tuple-element.238), channel_id=1, source_target_pairs={{0,1},{1,0},{2,3},{3,2},{4,5},{5,4},{6,7},{7,6},{8,9},{9,8},{10,11... | collective-permute-start | bytes 688136 | tf_op jit(solution)/shard_map/ppermute | solution.py:67
  537.8 12.8 %collective-permute-start.46 = (bf16[64,1792]{1,0:T(8,128)(2,1)}, bf16[64,1792]{1,0:T(8,128)(2,1)S(1)}, u32[]{:S(2)}, u32[]{:S(2)}) collective-permute-start(bf16[64,1792]{1,0:T(8,128)(2,1)} %get-tuple-element.239), channel_id=1, source_target_pairs={{0,3},{1,2},{2,1},{3,0},{4,7},{5,6},{6,5},{7,4},{8,11},{9,10},{10,... | collective-permute-start | bytes 688136 | tf_op jit(solution)/shard_map/ppermute | solution.py:67
  539.3 12.8 %collective-permute-start.45 = (bf16[64,1792]{1,0:T(8,128)(2,1)}, bf16[64,1792]{1,0:T(8,128)(2,1)}, u32[]{:S(2)}, u32[]{:S(2)}) collective-permute-start(bf16[64,1792]{1,0:T(8,128)(2,1)} %get-tuple-element.240), channel_id=1, source_target_pairs={{0,2},{1,3},{2,0},{3,1},{4,6},{5,7},{6,4},{7,5},{8,10},{9,11},{10,... | collective-permute-start | bytes 688136 | tf_op jit(solution)/shard_map/ppermute | solution.py:67
  545.9 7.9 %collective-permute-start.47 = (bf16[256,1792]{1,0:T(8,128)(2,1)}, bf16[256,1792]{1,0:T(8,128)(2,1)}, u32[]{:S(2)}, u32[]{:S(2)}) collective-permute-start(bf16[256,1792]{1,0:T(8,128)(2,1)} %slice.475), channel_id=1, source_target_pairs={{0,16},{16,0},{1,17},{17,1},{2,18},{18,2},{3,19},{19,3},{4,20},{20... | collective-permute-start | bytes 2752520 | tf_op jit(solution)/shard_map/ppermute | solution.py:40
  556.1 6.1 collective-permute-start.53
  558.8 104.5 %collective-permute-start.48 = (bf16[64,1792]{1,0:T(8,128)(2,1)}, bf16[64,1792]{1,0:T(8,128)(2,1)}, u32[]{:S(2)}, u32[]{:S(2)}) collective-permute-start(bf16[64,1792]{1,0:T(8,128)(2,1)} %get-tuple-element.235), channel_id=1, source_target_pairs={{0,1},{1,0},{2,3},{3,2},{4,5},{5,4},{6,7},{7,6},{8,9},{9,8},{10,11... | collective-permute-start | bytes 688136 | tf_op jit(solution)/shard_map/ppermute | solution.py:67
  559.0 104.2 %collective-permute-start.50 = (bf16[64,1792]{1,0:T(8,128)(2,1)}, bf16[64,1792]{1,0:T(8,128)(2,1)}, u32[]{:S(2)}, u32[]{:S(2)}) collective-permute-start(bf16[64,1792]{1,0:T(8,128)(2,1)} %get-tuple-element.236), channel_id=1, source_target_pairs={{0,3},{1,2},{2,1},{3,0},{4,7},{5,6},{6,5},{7,4},{8,11},{9,10},{10,... | collective-permute-start | bytes 688136 | tf_op jit(solution)/shard_map/ppermute | solution.py:67
  560.3 103.0 %collective-permute-start.49 = (bf16[64,1792]{1,0:T(8,128)(2,1)}, bf16[64,1792]{1,0:T(8,128)(2,1)}, u32[]{:S(2)}, u32[]{:S(2)}) collective-permute-start(bf16[64,1792]{1,0:T(8,128)(2,1)} %get-tuple-element.237), channel_id=1, source_target_pairs={{0,2},{1,3},{2,0},{3,1},{4,6},{5,7},{6,4},{7,5},{8,10},{9,11},{10,... | collective-permute-start | bytes 688136 | tf_op jit(solution)/shard_map/ppermute | solution.py:67
  562.3 13.0 %collective-permute-start.54 = (f32[2,5,1792]{2,1,0:T(8,128)S(1)}, f32[2,5,1792]{2,1,0:T(8,128)S(1)}, u32[]{:S(2)}, u32[]{:S(2)}) collective-permute-start(f32[2,5,1792]{2,1,0:T(8,128)S(1)} %fusion.54), channel_id=1, source_target_pairs={{0,2},{1,3},{2,0},{3,1},{4,6},{5,7},{6,4},{7,5},{8,10},{9,11},{10,... | collective-permute-start | bytes 215048 | tf_op jit(solution)/shard_map/ppermute | solution.py:96
  575.2 89.7 %collective-permute-start.55 = (f32[2,5,1792]{2,1,0:T(8,128)S(1)}, f32[2,5,1792]{2,1,0:T(8,128)}, u32[]{:S(2)}, u32[]{:S(2)}) collective-permute-start(f32[2,5,1792]{2,1,0:T(8,128)S(1)} %add.350), channel_id=1, source_target_pairs={{0,4},{4,0},{8,12},{12,8},{1,5},{5,1},{9,13},{13,9},{2,6},{6,2},{1... | collective-permute-start | bytes 215048 | tf_op jit(solution)/shard_map/ppermute | solution.py:96
  666.1 9.0 %collective-permute-start.56 = (f32[2,5,1792]{2,1,0:T(8,128)S(1)}, f32[2,5,1792]{2,1,0:T(8,128)S(1)}, u32[]{:S(2)}, u32[]{:S(2)}) collective-permute-start(f32[2,5,1792]{2,1,0:T(8,128)S(1)} %add.351), channel_id=1, source_target_pairs={{0,8},{4,12},{8,0},{12,4},{1,9},{5,13},{9,1},{13,5},{2,10},{6,14},... | collective-permute-start | bytes 215048 | tf_op jit(solution)/shard_map/ppermute | solution.py:96
  669.8 7.0 collective-permute-start.51
  676.2 9.7 %collective-permute-start.41 = (bf16[448,1792]{1,0:T(8,128)(2,1)S(1)}, bf16[448,1792]{1,0:T(8,128)(2,1)S(1)}, u32[]{:S(2)}, u32[]{:S(2)}) collective-permute-start(bf16[448,1792]{1,0:T(8,128)(2,1)S(1)} %broadcast_select_fusion.2), channel_id=1, source_target_pairs={{0,16},{16,0},{1,17},{17,1},{2,18},{18,2},{3,19},{19,3},{4,20},{20... | collective-permute-start | bytes 4816904 | tf_op jit(solution)/shard_map/ppermute | solution.py:40
  678.6 7.1 collective-permute-start.40
  (76 other events, 1316.2 us)
Sparse Core Ops, SparseCore 0:
  15.1 67.5 all-gather.3
  84.8 144.0 all-gather.5
  231.1 117.6 all-gather.7
  366.5 112.4 reduce-scatter.3
  481.2 182.0 reduce-scatter.5
  665.4 55.0 reduce-scatter.7

commit v9 on v8

--- a/solution.py
+++ b/solution.py
@@ -641,11 +641,8 @@
     piece = jnp.concatenate([attn_one, feed_parts[0][:, edge:]], axis=1)
     attn_zero, moved = lax.optimization_barrier((attn_zero, ring_step(piece)))
     ring = ring_gather(piece, moved)
-    attn_one, ends_zero = ring[:, : attn_one.shape[1]], ring[:, attn_one.shape[1] :]
+    wide = attn_one.shape[1]
     feed_one = fetch(feed_parts[1])
-    down_one = jnp.concatenate(
-        [feed_one[:, :main], feed_one[:, main + 2 * units :], attn_one[:, attn_one.shape[1] - tail :]], axis=1
-    )
 
     small = jnp.concatenate([norm_gains[0], conv_taps[0]], axis=0)
     small_other = swap(small)
@@ -688,12 +685,16 @@
     scale, normed = rms_rows(hidden, gains_zero[1])
     near, far = spread_pair(normed)
     grad_out = cotangent * mask
-    near, far, attn_one, ends_zero, *grads_one = lax.optimization_barrier(
-        (near, far, attn_one, ends_zero, *spread_pair(grad_out))
-    )
-    packed = jnp.concatenate([most, ends_zero], axis=1)
+    near, far, ring, *grads_one = lax.optimization_barrier((near, far, ring, *spread_pair(grad_out)))
+    packed = jnp.concatenate([most, ring[:, wide:]], axis=1)
     kept_feed = (hidden, scale, near, far)
-    middle = hidden + collect_pair(*feed_terms(units, tail, near, far, packed, attn_zero))
+    mine, other = feed_terms(units, tail, near, far, packed, attn_zero)
+    other, ring = lax.optimization_barrier((other, ring))
+    attn_one = ring[:, :wide]
+    down_one = jnp.concatenate(
+        [feed_one[:, :main], feed_one[:, main + 2 * units :], attn_one[:, attn_one.shape[1] - tail :]], axis=1
+    )
+    middle = hidden + collect_pair(mine, other)
     middle = middle.astype(jnp.bfloat16).astype(jnp.float32)
 
     hidden, kept_one = mix(middle, gains_one[0], attn_one, taps_one, False)

time: 745 us -> 743 us (level)
  local copies, waits for them, and re-layouts: 104 us -> 94.9 us
    unnamed x128 -> x119, local copies, waits for them, and re-layouts: 21.9 us -> 12.8 us
  transfers between devices with their start and end apart: 64 -> 64, of which waited for: 40 -> 38; matrix products, arithmetic and copies ran while one was open for 18% -> 19% of each run, Pallas kernels for 10% -> 10%
where the time goes in v9:
time: 743 us; the launch traced here: 733 us
  waiting for transfers between devices  288 us (39%)
  blocking collectives  116 us (16%)
  local copies, waits for them, and re-layouts  94.9 us (13%)
  Pallas kernels  91 us (12%)
  starting transfers between devices  69.6 us (9%)
  other arithmetic  46.2 us (6%)
  between operations  16 us (2%)
  matrix products  11.9 us (2%)
    all_gather x8, blocking collectives, spread_pair(): lax.all_gather(rows.astype(jnp.bfloat16), 'tensor', axis=0, tiled=True)  116 us
    reduce_scatter x3, waiting for transfers between devices, scatter(): lax.psum_scatter(block, 'dp', scatter_dimension=0, tiled=True)  101 us
    ppermute x3, waiting for transfers between devices, ring_step(): return lax.ppermute(piece, 'dp', [(i, (i + 1) % size) for i in range(size)])  82.2 us
    ppermute x24, waiting for transfers between devices, collect_pair(): total = total + lax.ppermute(block, 'tensor', pairs).astype(jnp.float32)  60.1 us
    pallas_call x4, Pallas kernels, whole_call(): pl.pallas_call(kernel, grid=(1,), out_shape=[jax.ShapeDtypeStruct(shape,...  41.7 us
    pallas_call x2, Pallas kernels, feed_both(): pl.pallas_call(functools.partial(feed_kernel, units, tail), grid=(2 * CHU...  33.3 us
    ppermute x24, starting transfers between devices, collect_pair(): total = total + lax.ppermute(block, 'tensor', pairs).astype(jnp.float32)  28.3 us
    ppermute x3, starting transfers between devices, ring_step(): return lax.ppermute(piece, 'dp', [(i, (i + 1) % size) for i in range(size)])  28 us
  transfers between devices with their start and end apart: 64, of which 38 were waited for; matrix products, arithmetic and copies ran while one was open for 19% of the time, Pallas kernels for 10%

profile of v9, /device:TPU:0, one launch (start us, length us, event | category | flops | bytes accessed | tf_op | source)
XLA Modules:
  0.0 733.4 jit_solution(2544575779910811388)
XLA Ops:
  17.7 5.9 constant_dynamic-slice_fusion.26
  24.9 3.2 concatenate.112
  43.4 3.3 concatenate.109
  63.5 12.0 %all_gather.33.near_ref = bf16[256,1792]{1,0:T(8,128)(2,1)S(1)} all-gather(bf16[64,1792]{1,0:T(8,128)(2,1)S(1)} %fusion.20), channel_id=1, replica_groups=mesh['section'=2,'dp'=4,'tensor'=4] {'tensor'}, dimensions={0}, use_global_device_ids=true | all-gather | bytes 1146880 | tf_op jit(solution)/shard_map/all_gather | solution.py:44
  76.4 30.1 %collective-permute-done.6 = bf16[448,1408]{1,0:T(8,128)(2,1)} collective-permute-done((bf16[448,1408]{1,0:T(8,128)(2,1)S(1)}, bf16[448,1408]{1,0:T(8,128)(2,1)}, u32[]{:S(2)}, u32[]{:S(2)}) %collective-permute-start.6) | collective-permute-done | bytes 1261600 | tf_op jit(solution)/shard_map/ppermute | solution.py:73
  107.4 6.7 shard_map.169
  122.9 20.2 %all_gather.36.near_grad_ref = bf16[256,1792]{1,0:T(8,128)(2,1)S(1)} all-gather(bf16[64,1792]{1,0:T(8,128)(2,1)S(1)} %copy-done.36), channel_id=1, replica_groups=mesh['section'=2,'dp'=4,'tensor'=4] {'tensor'}, dimensions={0}, use_global_device_ids=true | all-gather | bytes 1146880 | tf_op jit(solution)/shard_map/all_gather | solution.py:44
  145.3 28.4 %collective-permute-done.12 = bf16[448,1408]{1,0:T(8,128)(2,1)} collective-permute-done((bf16[448,1408]{1,0:T(8,128)(2,1)}, bf16[448,1408]{1,0:T(8,128)(2,1)}, u32[]{:S(2)}, u32[]{:S(2)}) %collective-permute-start.12) | collective-permute-done | bytes 1261600 | tf_op jit(solution)/shard_map/ppermute | solution.py:73
  173.7 24.8 %collective-permute-start.13 = (bf16[448,1408]{1,0:T(8,128)(2,1)}, bf16[448,1408]{1,0:T(8,128)(2,1)}, u32[]{:S(2)}, u32[]{:S(2)}) collective-permute-start(bf16[448,1408]{1,0:T(8,128)(2,1)} %collective-permute-done.12), channel_id=1, source_target_pairs={{0,4},{4,8},{8,12},{12,0},{1,5},{5,9},{9,13},{13,1},{2,6},{6,10},{... | collective-permute-start | bytes 3784712 | tf_op jit(solution)/shard_map/ppermute | solution.py:73
  198.5 19.4 %all_gather.35.near_ref = bf16[256,1792]{1,0:T(8,128)(2,1)S(1)} all-gather(bf16[64,1792]{1,0:T(8,128)(2,1)S(1)} %multiply_convert_fusion.1), channel_id=1, replica_groups=mesh['section'=2,'dp'=4,'tensor'=4] {'tensor'}, dimensions={0}, use_global_device_ids=true | all-gather | bytes 1146880 | tf_op jit(solution)/shard_map/all_gather | solution.py:44
  223.3 23.7 %collective-permute-done.13 = bf16[448,1408]{1,0:T(8,128)(2,1)} collective-permute-done((bf16[448,1408]{1,0:T(8,128)(2,1)}, bf16[448,1408]{1,0:T(8,128)(2,1)}, u32[]{:S(2)}, u32[]{:S(2)}) %collective-permute-start.13) | collective-permute-done | bytes 1261600 | tf_op jit(solution)/shard_map/ppermute | solution.py:73
  251.0 5.7 pad_maximum_fusion.feed_ref
  256.7 11.3 %shard_map.170 = (f32[256,1792]{1,0:T(8,128)S(1)}, bf16[256,1792]{1,0:T(8,128)(2,1)S(1)}) custom-call(bf16[256,1792]{1,0:T(8,128)(2,1)S(1)} %all_gather.35.near_ref, bf16[256,1792]{1,0:T(8,128)(2,1)S(1)} %collective-permute-done.11.far_ref, bf16[1792,1792]{1,0:T(8,128)(2,1)} %pad_maximum_fusion.feed_ref, ...), custom_call_target="tpu_custom_call" | custom-call | flops 1048576 | bytes 65536 | tf_op jit(solution)/shard_map/pallas_call | solution.py:160
  274.3 5.0 collective-permute-done.16
  279.3 5.0 collective-permute-done.18
  286.1 12.8 %all_gather.38.near_ref = bf16[256,1792]{1,0:T(8,128)(2,1)S(1)} all-gather(bf16[64,1792]{1,0:T(8,128)(2,1)S(1)} %fusion.27), channel_id=1, replica_groups=mesh['section'=2,'dp'=4,'tensor'=4] {'tensor'}, dimensions={0}, use_global_device_ids=true | all-gather | bytes 1146880 | tf_op jit(solution)/shard_map/all_gather | solution.py:44
  299.8 4.5 slice.331.attn_ref.last_ref
  305.2 8.6 %shard_map.171 = (f32[256,1792]{1,0:T(8,128)}, bf16[256,1792]{1,0:T(8,128)(2,1)}, f32[512,896]{1,0:T(8,128)}, bf16[512,256]{1,0:T(8,128)(2,1)}) custom-call(bf16[256,1792]{1,0:T(8,128)(2,1)} %copy-done.5, bf16[256,1792]{1,0:T(8,128)(2,1)} %copy-done.11, bf16[1792,1152]{1,0:T(8,128)(2,1)} %slice.331.attn_ref.last_ref, f32[8,256]{1,0:T(8,128)} %pad.8.taps_ref), custom_call_target="tpu_custom_call" | custom-call | flops 1048576 | bytes 65536 | tf_op jit(solution)/shard_map/pallas_call | solution.py:469
  321.9 4.9 collective-permute-done.21
  326.8 4.2 collective-permute-done.23
  332.8 12.2 %all_gather.39.near_ref = bf16[256,1792]{1,0:T(8,128)(2,1)S(1)} all-gather(bf16[64,1792]{1,0:T(8,128)(2,1)S(1)} %multiply_convert_fusion), channel_id=1, replica_groups=mesh['section'=2,'dp'=4,'tensor'=4] {'tensor'}, dimensions={0}, use_global_device_ids=true | all-gather | bytes 1146880 | tf_op jit(solution)/shard_map/all_gather | solution.py:44
  345.1 3.7 all-gather.8.cloned.1.call-done.feed_ref
  348.8 15.9 %shard_map.172 = (bf16[1792,1792]{1,0:T(8,128)(2,1)}, bf16[1792,256]{1,0:T(8,128)(2,1)}, bf16[512,1280]{1,0:T(8,128)(2,1)}, bf16[512,640]{1,0:T(8,128)(2,1)}) custom-call(bf16[256,1792]{1,0:T(8,128)(2,1)} %copy-done.34, bf16[256,1792]{1,0:T(8,128)(2,1)} %collective-permute-done.24.far_ref, bf16[256,1792]{1,0:T(8,128)(2,1)} %copy-done.33, ...), custom_call_target="tpu_custom_call" | custom-call | flops 6576668672 | bytes 20971520 | tf_op jit(solution)/shard_map/pallas_call | solution.py:282
  364.8 5.3 fusion.3
  376.6 5.0 collective-permute-done.26
  381.5 5.1 collective-permute-done.28
  389.5 13.2 %all_gather.41.near_grad_ref = bf16[256,1792]{1,0:T(8,128)(2,1)S(1)} all-gather(bf16[64,1792]{1,0:T(8,128)(2,1)S(1)} %get-tuple-element.183), channel_id=1, replica_groups=mesh['section'=2,'dp'=4,'tensor'=4] {'tensor'}, dimensions={0}, use_global_device_ids=true | all-gather | bytes 1146880 | tf_op jit(solution)/shard_map/all_gather | solution.py:44
  406.2 14.4 %shard_map.173 = (bf16[1792,1152]{1,0:T(8,128)(2,1)}, f32[256,1792]{1,0:T(8,128)}, bf16[256,1792]{1,0:T(8,128)(2,1)}, f32[8,256]{1,0:T(8,128)}) custom-call(bf16[256,1792]{1,0:T(8,128)(2,1)} %copy-done.5, bf16[256,1792]{1,0:T(8,128)(2,1)} %copy-done.11, bf16[256,1792]{1,0:T(8,128)(2,1)} %copy-done.9, bf16[256,1792]{1,0:T(8,128)(2,1)} %copy-done.31, ...), custom_call_target="tpu_custom_call" | custom-call | flops 1048576 | bytes 65536 | tf_op jit(solution)/shard_map/pallas_call | solution.py:469
  428.6 5.0 collective-permute-done.31
  433.6 4.2 collective-permute-done.33
  439.7 13.0 %all_gather.42.near_grad_ref = bf16[256,1792]{1,0:T(8,128)(2,1)S(1)} all-gather(bf16[64,1792]{1,0:T(8,128)(2,1)S(1)} %fusion.32), channel_id=1, replica_groups=mesh['section'=2,'dp'=4,'tensor'=4] {'tensor'}, dimensions={0}, use_global_device_ids=true | all-gather | bytes 1146880 | tf_op jit(solution)/shard_map/all_gather | solution.py:44
  456.1 17.3 %shard_map.174 = (bf16[1792,2944]{1,0:T(8,128)(2,1)}, bf16[1792,256]{1,0:T(8,128)(2,1)}, bf16[512,1280]{1,0:T(8,128)(2,1)}, bf16[512,640]{1,0:T(8,128)(2,1)}) custom-call(bf16[256,1792]{1,0:T(8,128)(2,1)} %copy-done, bf16[256,1792]{1,0:T(8,128)(2,1)} %copy-done.1, bf16[256,1792]{1,0:T(8,128)(2,1)} %copy-done.35, bf16[256,1792]{1,0:T(8,128)(2,1)} %copy-done.52, ...), custom_call_target="tpu_custom_call" | custom-call | flops 6576668672 | bytes 20971520 | tf_op jit(solution)/shard_map/pallas_call | solution.py:282
  476.4 5.0 fusion.1
  487.9 5.0 collective-permute-done.36
  492.8 5.1 collective-permute-done.38
  499.8 13.0 %all_gather.43.near_grad_ref = bf16[256,1792]{1,0:T(8,128)(2,1)S(1)} all-gather(bf16[64,1792]{1,0:T(8,128)(2,1)S(1)} %get-tuple-element.175), channel_id=1, replica_groups=mesh['section'=2,'dp'=4,'tensor'=4] {'tensor'}, dimensions={0}, use_global_device_ids=true | all-gather | bytes 1146880 | tf_op jit(solution)/shard_map/all_gather | solution.py:44
  516.3 12.0 %shard_map.175 = (bf16[1792,768]{1,0:T(8,128)(2,1)}, f32[256,1792]{1,0:T(8,128)}, bf16[256,1792]{1,0:T(8,128)(2,1)}, f32[8,256]{1,0:T(8,128)}) custom-call(bf16[256,1792]{1,0:T(8,128)(2,1)} %copy-done.4, bf16[256,1792]{1,0:T(8,128)(2,1)} %copy-done.10, bf16[256,1792]{1,0:T(8,128)(2,1)} %copy-done.8, bf16[256,1792]{1,0:T(8,128)(2,1)} %copy-done.30, ...), custom_call_target="tpu_custom_call" | custom-call | flops 1048576 | bytes 65536 | tf_op jit(solution)/shard_map/pallas_call | solution.py:469
  543.6 3.3 collective-permute-done.46
  560.5 11.0 %collective-permute-done.54 = f32[2,5,1792]{2,1,0:T(8,128)S(1)} collective-permute-done((f32[2,5,1792]{2,1,0:T(8,128)S(1)}, f32[2,5,1792]{2,1,0:T(8,128)S(1)}, u32[]{:S(2)}, u32[]{:S(2)}) %collective-permute-start.54) | collective-permute-done | bytes 71712 | tf_op jit(solution)/shard_map/ppermute | solution.py:96
  573.0 87.5 %reduce-scatter.6.cloned.1.call-done = bf16[448,2944]{1,0:T(8,128)(2,1)} async-done(((bf16[1792,2944]{1,0:T(8,128)(2,1)}), bf16[448,2944]{1,0:T(8,128)(2,1)}) %reduce-scatter.6.cloned.1.call-update) | async-done | bytes 2637840 | tf_op jit(solution)/shard_map/reduce_scatter | solution.py:591
  663.4 3.5 collective-permute-start.56
  667.2 5.2 collective-permute-done.56
  677.7 5.3 maximum_convert_fusion.1
  686.3 3.4 concatenate.126
  696.2 3.5 concatenate.125
  701.4 5.7 copy.103
  707.0 10.8 %reduce-scatter.8.cloned.1.call-done.mine_ref = bf16[448,768]{1,0:T(8,128)(2,1)} async-done(((bf16[1792,768]{1,0:T(8,128)(2,1)}), bf16[448,768]{1,0:T(8,128)(2,1)}) %reduce-scatter.8.cloned.1.call-update) | async-done | bytes 688144 | tf_op jit(solution)/shard_map/reduce_scatter | solution.py:591
  721.3 4.7 shard_map.176
  (371 shorter events, 179.4 us)
Async XLA Ops:
  7.2 99.3 %all-gather.4.cloned.1.call-start = ((), (), s32[]{:S(2)}) async-start(), calls=%async_computation.3 | async-start | bytes 3440640 | tf_op jit(solution)/shard_map/all_gather | solution.py:633
  15.0 236.0 %all-gather.6.cloned.1.call-start = ((), (), s32[]{:S(2)}) async-start(), calls=%async_computation.4 | async-start | bytes 6881280 | tf_op jit(solution)/shard_map/all_gather | solution.py:633
  36.6 312.2 %all-gather.8.cloned.1.call-start = ((), (), s32[]{:S(2)}) async-start(), calls=%async_computation.5 | async-start | bytes 8028160 | tf_op jit(solution)/shard_map/all_gather | solution.py:633
  38.4 13.8 %collective-permute-start.1 = (f32[5,1792]{1,0:T(8,128)}, f32[5,1792]{1,0:T(8,128)}, u32[]{:S(2)}, u32[]{:S(2)}) collective-permute-start(f32[5,1792]{1,0:T(8,128)} %pad_maximum_fusion.4), channel_id=1, source_target_pairs={{0,16},{16,0},{1,17},{17,1},{2,18},{18,2},{3,19},{19,3},{4,20},{20... | collective-permute-start | bytes 107528 | tf_op jit(solution)/shard_map/ppermute | solution.py:40
  39.3 13.9 %collective-permute-start = (bf16[64,1792]{1,0:T(8,128)(2,1)}, bf16[64,1792]{1,0:T(8,128)(2,1)}, u32[]{:S(2)}, u32[]{:S(2)}) collective-permute-start(bf16[64,1792]{1,0:T(8,128)(2,1)} %dynamic-slice_bitcast_fusion.2), channel_id=1, source_target_pairs={{0,16},{16,0},{1,17},{17,1},{2,18},{18,2},{3,19},{19,3},{4,20},{20... | collective-permute-start | bytes 688136 | tf_op jit(solution)/shard_map/ppermute | solution.py:40
  46.7 8.5 %collective-permute-start.4 = (bf16[448,1152]{1,0:T(8,128)(2,1)}, bf16[448,1152]{1,0:T(8,128)(2,1)}, u32[]{:S(2)}, u32[]{:S(2)}) collective-permute-start(bf16[448,1152]{1,0:T(8,128)(2,1)} %concatenate.109), channel_id=1, source_target_pairs={{0,16},{16,0},{1,17},{17,1},{2,18},{18,2},{3,19},{19,3},{4,20},{20... | collective-permute-start | bytes 3096584 | tf_op jit(solution)/shard_map/ppermute | solution.py:40
  60.4 46.1 %collective-permute-start.6 = (bf16[448,1408]{1,0:T(8,128)(2,1)S(1)}, bf16[448,1408]{1,0:T(8,128)(2,1)}, u32[]{:S(2)}, u32[]{:S(2)}) collective-permute-start(bf16[448,1408]{1,0:T(8,128)(2,1)S(1)} %get-tuple-element.224), channel_id=1, source_target_pairs={{0,4},{4,8},{8,12},{12,0},{1,5},{5,9},{9,13},{13,1},{2,6},{6,10},{... | collective-permute-start | bytes 3784712 | tf_op jit(solution)/shard_map/ppermute | solution.py:73
  75.5 31.0 %collective-permute-start.2 = (bf16[256,1792]{1,0:T(8,128)(2,1)S(1)}, bf16[256,1792]{1,0:T(8,128)(2,1)S(1)}, u32[]{:S(2)}, u32[]{:S(2)}) collective-permute-start(bf16[256,1792]{1,0:T(8,128)(2,1)S(1)} %all_gather.33.near_ref), channel_id=1, source_target_pairs={{0,16},{16,0},{1,17},{17,1},{2,18},{18,2},{3,19},{19,3},{4,20},{20... | collective-permute-start | bytes 2752520 | tf_op jit(solution)/shard_map/ppermute | solution.py:40
  114.1 59.5 %collective-permute-start.12 = (bf16[448,1408]{1,0:T(8,128)(2,1)}, bf16[448,1408]{1,0:T(8,128)(2,1)}, u32[]{:S(2)}, u32[]{:S(2)}) collective-permute-start(bf16[448,1408]{1,0:T(8,128)(2,1)} %collective-permute-done.6), channel_id=1, source_target_pairs={{0,4},{4,8},{8,12},{12,0},{1,5},{5,9},{9,13},{13,1},{2,6},{6,10},{... | collective-permute-start | bytes 3784712 | tf_op jit(solution)/shard_map/ppermute | solution.py:73
  119.4 23.7 %collective-permute-start.8 = (bf16[64,1792]{1,0:T(8,128)(2,1)}, bf16[64,1792]{1,0:T(8,128)(2,1)S(1)}, u32[]{:S(2)}, u32[]{:S(2)}) collective-permute-start(bf16[64,1792]{1,0:T(8,128)(2,1)} %get-tuple-element.258), channel_id=1, source_target_pairs={{0,1},{1,0},{2,3},{3,2},{4,5},{5,4},{6,7},{7,6},{8,9},{9,8},{10,11... | collective-permute-start | bytes 688136 | tf_op jit(solution)/shard_map/ppermute | solution.py:67
  120.9 22.2 %collective-permute-start.10 = (bf16[64,1792]{1,0:T(8,128)(2,1)}, bf16[64,1792]{1,0:T(8,128)(2,1)}, u32[]{:S(2)}, u32[]{:S(2)}) collective-permute-start(bf16[64,1792]{1,0:T(8,128)(2,1)} %get-tuple-element.259), channel_id=1, source_target_pairs={{0,3},{1,2},{2,1},{3,0},{4,7},{5,6},{6,5},{7,4},{8,11},{9,10},{10,... | collective-permute-start | bytes 688136 | tf_op jit(solution)/shard_map/ppermute | solution.py:67
  122.4 20.7 %collective-permute-start.9 = (bf16[64,1792]{1,0:T(8,128)(2,1)}, bf16[64,1792]{1,0:T(8,128)(2,1)}, u32[]{:S(2)}, u32[]{:S(2)}) collective-permute-start(bf16[64,1792]{1,0:T(8,128)(2,1)} %get-tuple-element.260), channel_id=1, source_target_pairs={{0,2},{1,3},{2,0},{3,1},{4,6},{5,7},{6,4},{7,5},{8,10},{9,11},{10,... | collective-permute-start | bytes 688136 | tf_op jit(solution)/shard_map/ppermute | solution.py:67
  143.1 106.3 %collective-permute-start.14 = (bf16[256,1792]{1,0:T(8,128)(2,1)S(1)}, bf16[256,1792]{1,0:T(8,128)(2,1)}, u32[]{:S(2)}, u32[]{:S(2)}) collective-permute-start(bf16[256,1792]{1,0:T(8,128)(2,1)S(1)} %all_gather.36.near_grad_ref), channel_id=1, source_target_pairs={{0,16},{16,0},{1,17},{17,1},{2,18},{18,2},{3,19},{19,3},{4,20},{20... | collective-permute-start | bytes 2752520 | tf_op jit(solution)/shard_map/ppermute | solution.py:40
  173.7 73.3 %collective-permute-start.13 = (bf16[448,1408]{1,0:T(8,128)(2,1)}, bf16[448,1408]{1,0:T(8,128)(2,1)}, u32[]{:S(2)}, u32[]{:S(2)}) collective-permute-start(bf16[448,1408]{1,0:T(8,128)(2,1)} %collective-permute-done.12), channel_id=1, source_target_pairs={{0,4},{4,8},{8,12},{12,0},{1,5},{5,9},{9,13},{13,1},{2,6},{6,10},{... | collective-permute-start | bytes 3784712 | tf_op jit(solution)/shard_map/ppermute | solution.py:73
  217.9 31.5 %collective-permute-start.11 = (bf16[256,1792]{1,0:T(8,128)(2,1)S(1)}, bf16[256,1792]{1,0:T(8,128)(2,1)S(1)}, u32[]{:S(2)}, u32[]{:S(2)}) collective-permute-start(bf16[256,1792]{1,0:T(8,128)(2,1)S(1)} %all_gather.35.near_ref), channel_id=1, source_target_pairs={{0,16},{16,0},{1,17},{17,1},{2,18},{18,2},{3,19},{19,3},{4,20},{20... | collective-permute-start | bytes 2752520 | tf_op jit(solution)/shard_map/ppermute | solution.py:40
  218.0 258.3 %reduce-scatter.4.cloned.1.call-start = ((), (), s32[]{:S(2)}) async-start(), calls=%async_computation.6 | async-start | bytes 8028160 | tf_op jit(solution)/shard_map/reduce_scatter | solution.py:591
  270.8 8.5 %collective-permute-start.16 = (bf16[64,1792]{1,0:T(8,128)(2,1)S(1)}, bf16[64,1792]{1,0:T(8,128)(2,1)S(1)}, u32[]{:S(2)}, u32[]{:S(2)}) collective-permute-start(bf16[64,1792]{1,0:T(8,128)(2,1)S(1)} %get-tuple-element.255), channel_id=1, source_target_pairs={{0,1},{1,0},{2,3},{3,2},{4,5},{5,4},{6,7},{7,6},{8,9},{9,8},{10,11... | collective-permute-start | bytes 688136 | tf_op jit(solution)/shard_map/ppermute | solution.py:67
  272.2 12.1 %collective-permute-start.18 = (bf16[64,1792]{1,0:T(8,128)(2,1)S(1)}, bf16[64,1792]{1,0:T(8,128)(2,1)S(1)}, u32[]{:S(2)}, u32[]{:S(2)}) collective-permute-start(bf16[64,1792]{1,0:T(8,128)(2,1)S(1)} %get-tuple-element.256), channel_id=1, source_target_pairs={{0,3},{1,2},{2,1},{3,0},{4,7},{5,6},{6,5},{7,4},{8,11},{9,10},{10,... | collective-permute-start | bytes 688136 | tf_op jit(solution)/shard_map/ppermute | solution.py:67
  273.7 12.0 %collective-permute-start.17 = (bf16[64,1792]{1,0:T(8,128)(2,1)S(1)}, bf16[64,1792]{1,0:T(8,128)(2,1)S(1)}, u32[]{:S(2)}, u32[]{:S(2)}) collective-permute-start(bf16[64,1792]{1,0:T(8,128)(2,1)S(1)} %get-tuple-element.257), channel_id=1, source_target_pairs={{0,2},{1,3},{2,0},{3,1},{4,6},{5,7},{6,4},{7,5},{8,10},{9,11},{10,... | collective-permute-start | bytes 688136 | tf_op jit(solution)/shard_map/ppermute | solution.py:67
  298.9 5.4 collective-permute-start.19
  318.3 8.5 %collective-permute-start.21 = (bf16[64,1792]{1,0:T(8,128)(2,1)S(1)}, bf16[64,1792]{1,0:T(8,128)(2,1)S(1)}, u32[]{:S(2)}, u32[]{:S(2)}) collective-permute-start(bf16[64,1792]{1,0:T(8,128)(2,1)S(1)} %get-tuple-element.252), channel_id=1, source_target_pairs={{0,1},{1,0},{2,3},{3,2},{4,5},{5,4},{6,7},{7,6},{8,9},{9,8},{10,11... | collective-permute-start | bytes 688136 | tf_op jit(solution)/shard_map/ppermute | solution.py:67
  318.4 12.6 %collective-permute-start.23 = (bf16[64,1792]{1,0:T(8,128)(2,1)S(1)}, bf16[64,1792]{1,0:T(8,128)(2,1)S(1)}, u32[]{:S(2)}, u32[]{:S(2)}) collective-permute-start(bf16[64,1792]{1,0:T(8,128)(2,1)S(1)} %get-tuple-element.253), channel_id=1, source_target_pairs={{0,3},{1,2},{2,1},{3,0},{4,7},{5,6},{6,5},{7,4},{8,11},{9,10},{10,... | collective-permute-start | bytes 688136 | tf_op jit(solution)/shard_map/ppermute | solution.py:67
  319.9 12.5 %collective-permute-start.22 = (bf16[64,1792]{1,0:T(8,128)(2,1)S(1)}, bf16[64,1792]{1,0:T(8,128)(2,1)S(1)}, u32[]{:S(2)}, u32[]{:S(2)}) collective-permute-start(bf16[64,1792]{1,0:T(8,128)(2,1)S(1)} %get-tuple-element.254), channel_id=1, source_target_pairs={{0,2},{1,3},{2,0},{3,1},{4,6},{5,7},{6,4},{7,5},{8,10},{9,11},{10,... | collective-permute-start | bytes 688136 | tf_op jit(solution)/shard_map/ppermute | solution.py:67
  364.7 295.8 %reduce-scatter.6.cloned.1.call-start = ((), (), s32[]{:S(2)}) async-start(), calls=%async_computation.7 | async-start | bytes 13189120 | tf_op jit(solution)/shard_map/reduce_scatter | solution.py:591
  373.0 8.5 %collective-permute-start.26 = (bf16[64,1792]{1,0:T(8,128)(2,1)S(1)}, bf16[64,1792]{1,0:T(8,128)(2,1)S(1)}, u32[]{:S(2)}, u32[]{:S(2)}) collective-permute-start(bf16[64,1792]{1,0:T(8,128)(2,1)S(1)} %get-tuple-element.249), channel_id=1, source_target_pairs={{0,1},{1,0},{2,3},{3,2},{4,5},{5,4},{6,7},{7,6},{8,9},{9,8},{10,11... | collective-permute-start | bytes 688136 | tf_op jit(solution)/shard_map/ppermute | solution.py:67
  374.5 12.1 %collective-permute-start.28 = (bf16[64,1792]{1,0:T(8,128)(2,1)S(1)}, bf16[64,1792]{1,0:T(8,128)(2,1)S(1)}, u32[]{:S(2)}, u32[]{:S(2)}) collective-permute-start(bf16[64,1792]{1,0:T(8,128)(2,1)S(1)} %get-tuple-element.250), channel_id=1, source_target_pairs={{0,3},{1,2},{2,1},{3,0},{4,7},{5,6},{6,5},{7,4},{8,11},{9,10},{10,... | collective-permute-start | bytes 688136 | tf_op jit(solution)/shard_map/ppermute | solution.py:67
  376.0 12.0 %collective-permute-start.27 = (bf16[64,1792]{1,0:T(8,128)(2,1)S(1)}, bf16[64,1792]{1,0:T(8,128)(2,1)S(1)}, u32[]{:S(2)}, u32[]{:S(2)}) collective-permute-start(bf16[64,1792]{1,0:T(8,128)(2,1)S(1)} %get-tuple-element.251), channel_id=1, source_target_pairs={{0,2},{1,3},{2,0},{3,1},{4,6},{5,7},{6,4},{7,5},{8,10},{9,11},{10,... | collective-permute-start | bytes 688136 | tf_op jit(solution)/shard_map/ppermute | solution.py:67
  425.1 8.5 %collective-permute-start.31 = (bf16[64,1792]{1,0:T(8,128)(2,1)S(1)}, bf16[64,1792]{1,0:T(8,128)(2,1)S(1)}, u32[]{:S(2)}, u32[]{:S(2)}) collective-permute-start(bf16[64,1792]{1,0:T(8,128)(2,1)S(1)} %get-tuple-element.246), channel_id=1, source_target_pairs={{0,1},{1,0},{2,3},{3,2},{4,5},{5,4},{6,7},{7,6},{8,9},{9,8},{10,11... | collective-permute-start | bytes 688136 | tf_op jit(solution)/shard_map/ppermute | solution.py:67
  425.7 12.1 %collective-permute-start.33 = (bf16[64,1792]{1,0:T(8,128)(2,1)S(1)}, bf16[64,1792]{1,0:T(8,128)(2,1)S(1)}, u32[]{:S(2)}, u32[]{:S(2)}) collective-permute-start(bf16[64,1792]{1,0:T(8,128)(2,1)S(1)} %get-tuple-element.247), channel_id=1, source_target_pairs={{0,3},{1,2},{2,1},{3,0},{4,7},{5,6},{6,5},{7,4},{8,11},{9,10},{10,... | collective-permute-start | bytes 688136 | tf_op jit(solution)/shard_map/ppermute | solution.py:67
  427.2 12.0 %collective-permute-start.32 = (bf16[64,1792]{1,0:T(8,128)(2,1)S(1)}, bf16[64,1792]{1,0:T(8,128)(2,1)S(1)}, u32[]{:S(2)}, u32[]{:S(2)}) collective-permute-start(bf16[64,1792]{1,0:T(8,128)(2,1)S(1)} %get-tuple-element.248), channel_id=1, source_target_pairs={{0,2},{1,3},{2,0},{3,1},{4,6},{5,7},{6,4},{7,5},{8,10},{9,11},{10,... | collective-permute-start | bytes 688136 | tf_op jit(solution)/shard_map/ppermute | solution.py:67
  476.3 241.6 %reduce-scatter.8.cloned.1.call-start = ((), (), s32[]{:S(2)}) async-start(), calls=%async_computation.8 | async-start | bytes 3440640 | tf_op jit(solution)/shard_map/reduce_scatter | solution.py:591
  484.3 8.5 %collective-permute-start.36 = (bf16[64,1792]{1,0:T(8,128)(2,1)S(1)}, bf16[64,1792]{1,0:T(8,128)(2,1)S(1)}, u32[]{:S(2)}, u32[]{:S(2)}) collective-permute-start(bf16[64,1792]{1,0:T(8,128)(2,1)S(1)} %get-tuple-element.243), channel_id=1, source_target_pairs={{0,1},{1,0},{2,3},{3,2},{4,5},{5,4},{6,7},{7,6},{8,9},{9,8},{10,11... | collective-permute-start | bytes 688136 | tf_op jit(solution)/shard_map/ppermute | solution.py:67
  485.8 12.1 %collective-permute-start.38 = (bf16[64,1792]{1,0:T(8,128)(2,1)S(1)}, bf16[64,1792]{1,0:T(8,128)(2,1)S(1)}, u32[]{:S(2)}, u32[]{:S(2)}) collective-permute-start(bf16[64,1792]{1,0:T(8,128)(2,1)S(1)} %get-tuple-element.244), channel_id=1, source_target_pairs={{0,3},{1,2},{2,1},{3,0},{4,7},{5,6},{6,5},{7,4},{8,11},{9,10},{10,... | collective-permute-start | bytes 688136 | tf_op jit(solution)/shard_map/ppermute | solution.py:67
  487.3 12.0 %collective-permute-start.37 = (bf16[64,1792]{1,0:T(8,128)(2,1)S(1)}, bf16[64,1792]{1,0:T(8,128)(2,1)S(1)}, u32[]{:S(2)}, u32[]{:S(2)}) collective-permute-start(bf16[64,1792]{1,0:T(8,128)(2,1)S(1)} %get-tuple-element.245), channel_id=1, source_target_pairs={{0,2},{1,3},{2,0},{3,1},{4,6},{5,7},{6,4},{7,5},{8,10},{9,11},{10,... | collective-permute-start | bytes 688136 | tf_op jit(solution)/shard_map/ppermute | solution.py:67
  534.0 9.5 %collective-permute-start.44 = (bf16[64,1792]{1,0:T(8,128)(2,1)}, bf16[64,1792]{1,0:T(8,128)(2,1)S(1)}, u32[]{:S(2)}, u32[]{:S(2)}) collective-permute-start(bf16[64,1792]{1,0:T(8,128)(2,1)} %get-tuple-element.240), channel_id=1, source_target_pairs={{0,1},{1,0},{2,3},{3,2},{4,5},{5,4},{6,7},{7,6},{8,9},{9,8},{10,11... | collective-permute-start | bytes 688136 | tf_op jit(solution)/shard_map/ppermute | solution.py:67
  534.1 12.8 %collective-permute-start.46 = (bf16[64,1792]{1,0:T(8,128)(2,1)}, bf16[64,1792]{1,0:T(8,128)(2,1)S(1)}, u32[]{:S(2)}, u32[]{:S(2)}) collective-permute-start(bf16[64,1792]{1,0:T(8,128)(2,1)} %get-tuple-element.241), channel_id=1, source_target_pairs={{0,3},{1,2},{2,1},{3,0},{4,7},{5,6},{6,5},{7,4},{8,11},{9,10},{10,... | collective-permute-start | bytes 688136 | tf_op jit(solution)/shard_map/ppermute | solution.py:67
  535.6 12.8 %collective-permute-start.45 = (bf16[64,1792]{1,0:T(8,128)(2,1)}, bf16[64,1792]{1,0:T(8,128)(2,1)}, u32[]{:S(2)}, u32[]{:S(2)}) collective-permute-start(bf16[64,1792]{1,0:T(8,128)(2,1)} %get-tuple-element.242), channel_id=1, source_target_pairs={{0,2},{1,3},{2,0},{3,1},{4,6},{5,7},{6,4},{7,5},{8,10},{9,11},{10,... | collective-permute-start | bytes 688136 | tf_op jit(solution)/shard_map/ppermute | solution.py:67
  542.1 8.0 %collective-permute-start.47 = (bf16[256,1792]{1,0:T(8,128)(2,1)}, bf16[256,1792]{1,0:T(8,128)(2,1)}, u32[]{:S(2)}, u32[]{:S(2)}) collective-permute-start(bf16[256,1792]{1,0:T(8,128)(2,1)} %slice.479), channel_id=1, source_target_pairs={{0,16},{16,0},{1,17},{17,1},{2,18},{18,2},{3,19},{19,3},{4,20},{20... | collective-permute-start | bytes 2752520 | tf_op jit(solution)/shard_map/ppermute | solution.py:40
  552.1 6.2 collective-permute-start.53
  554.7 105.9 %collective-permute-start.48 = (bf16[64,1792]{1,0:T(8,128)(2,1)}, bf16[64,1792]{1,0:T(8,128)(2,1)}, u32[]{:S(2)}, u32[]{:S(2)}) collective-permute-start(bf16[64,1792]{1,0:T(8,128)(2,1)} %get-tuple-element.237), channel_id=1, source_target_pairs={{0,1},{1,0},{2,3},{3,2},{4,5},{5,4},{6,7},{7,6},{8,9},{9,8},{10,11... | collective-permute-start | bytes 688136 | tf_op jit(solution)/shard_map/ppermute | solution.py:67
  555.0 105.6 %collective-permute-start.50 = (bf16[64,1792]{1,0:T(8,128)(2,1)}, bf16[64,1792]{1,0:T(8,128)(2,1)}, u32[]{:S(2)}, u32[]{:S(2)}) collective-permute-start(bf16[64,1792]{1,0:T(8,128)(2,1)} %get-tuple-element.238), channel_id=1, source_target_pairs={{0,3},{1,2},{2,1},{3,0},{4,7},{5,6},{6,5},{7,4},{8,11},{9,10},{10,... | collective-permute-start | bytes 688136 | tf_op jit(solution)/shard_map/ppermute | solution.py:67
  556.5 104.2 %collective-permute-start.49 = (bf16[64,1792]{1,0:T(8,128)(2,1)}, bf16[64,1792]{1,0:T(8,128)(2,1)}, u32[]{:S(2)}, u32[]{:S(2)}) collective-permute-start(bf16[64,1792]{1,0:T(8,128)(2,1)} %get-tuple-element.239), channel_id=1, source_target_pairs={{0,2},{1,3},{2,0},{3,1},{4,6},{5,7},{6,4},{7,5},{8,10},{9,11},{10,... | collective-permute-start | bytes 688136 | tf_op jit(solution)/shard_map/ppermute | solution.py:67
  558.3 13.2 %collective-permute-start.54 = (f32[2,5,1792]{2,1,0:T(8,128)S(1)}, f32[2,5,1792]{2,1,0:T(8,128)S(1)}, u32[]{:S(2)}, u32[]{:S(2)}) collective-permute-start(f32[2,5,1792]{2,1,0:T(8,128)S(1)} %fusion.56), channel_id=1, source_target_pairs={{0,2},{1,3},{2,0},{3,1},{4,6},{5,7},{6,4},{7,5},{8,10},{9,11},{10,... | collective-permute-start | bytes 215048 | tf_op jit(solution)/shard_map/ppermute | solution.py:96
  571.5 90.8 %collective-permute-start.55 = (f32[2,5,1792]{2,1,0:T(8,128)S(1)}, f32[2,5,1792]{2,1,0:T(8,128)}, u32[]{:S(2)}, u32[]{:S(2)}) collective-permute-start(f32[2,5,1792]{2,1,0:T(8,128)S(1)} %add.350), channel_id=1, source_target_pairs={{0,4},{4,0},{8,12},{12,8},{1,5},{5,1},{9,13},{13,9},{2,6},{6,2},{1... | collective-permute-start | bytes 215048 | tf_op jit(solution)/shard_map/ppermute | solution.py:96
  663.4 9.0 %collective-permute-start.56 = (f32[2,5,1792]{2,1,0:T(8,128)S(1)}, f32[2,5,1792]{2,1,0:T(8,128)S(1)}, u32[]{:S(2)}, u32[]{:S(2)}) collective-permute-start(f32[2,5,1792]{2,1,0:T(8,128)S(1)} %add.351), channel_id=1, source_target_pairs={{0,8},{4,12},{8,0},{12,4},{1,9},{5,13},{9,1},{13,5},{2,10},{6,14},... | collective-permute-start | bytes 215048 | tf_op jit(solution)/shard_map/ppermute | solution.py:96
  667.1 7.0 collective-permute-start.51
  673.5 9.7 %collective-permute-start.41 = (bf16[448,1792]{1,0:T(8,128)(2,1)S(1)}, bf16[448,1792]{1,0:T(8,128)(2,1)S(1)}, u32[]{:S(2)}, u32[]{:S(2)}) collective-permute-start(bf16[448,1792]{1,0:T(8,128)(2,1)S(1)} %broadcast_select_fusion.2), channel_id=1, source_target_pairs={{0,16},{16,0},{1,17},{17,1},{2,18},{18,2},{3,19},{19,3},{4,20},{20... | collective-permute-start | bytes 4816904 | tf_op jit(solution)/shard_map/ppermute | solution.py:40
  675.9 7.1 collective-permute-start.40
  (72 other events, 1374.1 us)
Sparse Core Ops, SparseCore 0:
  15.1 68.1 all-gather.3
  85.4 144.7 all-gather.5
  232.3 116.3 all-gather.7
  364.9 111.3 reduce-scatter.3
  478.5 182.0 reduce-scatter.5
  662.8 55.0 reduce-scatter.7

commit v10 on v9

--- a/solution.py
+++ b/solution.py
@@ -264,14 +264,14 @@
             rest_ref[...] = jnp.where(lanes(moved) < WIDE - tail, 0.0, moved).astype(jnp.bfloat16)
 
 
-def feed_both(units, tail, near, far, near_grad, far_grad, feed, attn, *extras):
+def feed_both(units, tail, near, far, near_grad, far_grad, feed, attn, stop, *extras):
     count, model = 2 * near.shape[0], near.shape[1]
     main = units // LANES * LANES
     width = 3 * units - tail
     size = model // CHUNKS
     total = width + sum(extra.shape[1] for extra in extras)
     shapes = ((model, total), (model, WIDE), (count, width - main), (count, main + LANES))
-    end = attn.shape[1] // LANES - 1
+    end = stop // LANES - 1
 
     def later(columns):
         return pl.BlockSpec((size, columns), lambda step: (jnp.maximum(step - CHUNKS, 0), 0))
@@ -462,7 +462,9 @@
             other_ref[...] = terms.astype(jnp.bfloat16)
 
 
-def whole_call(kernel, inputs, shapes, scratch, flops):
+def whole_call(kernel, inputs, shapes, scratch, flops, columns=()):
+    columns = dict(columns)
+
     def whole(shape):
         return pl.BlockSpec(shape, lambda step: (0,) * len(shape), pipeline_mode=pl.Buffered(1))
 
@@ -470,7 +472,9 @@
         kernel,
         grid=(1,),
         out_shape=[jax.ShapeDtypeStruct(shape, kind) for shape, kind in shapes],
-        in_specs=[whole(block.shape) for block in inputs],
+        in_specs=[
+            whole((*block.shape[:-1], columns.get(place, block.shape[-1]))) for place, block in enumerate(inputs)
+        ],
         out_specs=[whole(shape) for shape, _ in shapes],
         scratch_shapes=[pltpu.VMEM(shape, kind) for shape, kind in scratch],
         compiler_params=pltpu.CompilerParams(vmem_limit_bytes=56 * 2**20),
@@ -478,9 +482,9 @@
     )(*inputs)
 
 
-def mixer_forward(channels, first, near, far, attn, taps):
+def mixer_forward(channels, first, near, far, attn, width, taps):
     length, model = near.shape
-    stop = attn.shape[1] - WIDE
+    stop = width - WIDE
     shapes = (
         ((length, model), jnp.float32),
         ((length, model), jnp.bfloat16),
@@ -488,7 +492,7 @@
         ((2 * length, WIDE), jnp.bfloat16),
     )
     kernel = functools.partial(mixer_kernel, channels, first)
-    return whole_call(kernel, (near, far, attn, taps), shapes, (), 2**20)
+    return whole_call(kernel, (near, far, attn, taps), shapes, (), 2**20, ((2, width),))
 
 
 def mixer_backward(channels, first, near, far, near_grad, far_grad, attn, taps, both, gated, rest):
@@ -507,7 +511,8 @@
         ((2 * length, stop), jnp.bfloat16),
     )
     inputs = (near, far, near_grad, far_grad, attn, taps, both, gated, rest)
-    return whole_call(functools.partial(mixer_back_kernel, channels, first), inputs, shapes, scratch, 2**20)
+    kernel = functools.partial(mixer_back_kernel, channels, first)
+    return whole_call(kernel, inputs, shapes, scratch, 2**20, ((4, stop + WIDE),))
 
 
 def end_kernel(
@@ -667,10 +672,10 @@
     gains_zero, gains_one = small_zero[:2], small_one[:2]
     taps_zero, taps_one = own_taps(small_zero), own_taps(small_one)
 
-    def mix(rows, gain, attn, taps, first):
+    def mix(rows, gain, attn, size, taps, first):
         scale, normed = rms_rows(rows, gain)
         near, far = spread_pair(normed)
-        mine, other, both, gated = mixer_forward(channels, first, near, far, attn, taps)
+        mine, other, both, gated = mixer_forward(channels, first, near, far, attn, size, taps)
         return (rows + collect_pair(mine, other), (rows, scale, near, far, both, gated))
 
     def mix_back(kept, grad_out, gain, attn, taps, rest, first):
@@ -681,7 +686,7 @@
         back, grad_gain = rms_back(rows, scale, gain, collect_pair(mine, other))
         return (block, grad_out + back, grad_gain, grad_taps[: conv_taps.shape[1], :channels])
 
-    hidden, kept_zero = mix(entering, gains_zero[0], attn_zero, taps_zero, True)
+    hidden, kept_zero = mix(entering, gains_zero[0], attn_zero, attn_zero.shape[1], taps_zero, True)
     scale, normed = rms_rows(hidden, gains_zero[1])
     near, far = spread_pair(normed)
     grad_out = cotangent * mask
@@ -690,30 +695,29 @@
     kept_feed = (hidden, scale, near, far)
     mine, other = feed_terms(units, tail, near, far, packed, attn_zero)
     other, ring = lax.optimization_barrier((other, ring))
-    attn_one = ring[:, :wide]
     down_one = jnp.concatenate(
-        [feed_one[:, :main], feed_one[:, main + 2 * units :], attn_one[:, attn_one.shape[1] - tail :]], axis=1
+        [feed_one[:, :main], feed_one[:, main + 2 * units :], ring[:, wide - tail : wide]], axis=1
     )
     middle = hidden + collect_pair(mine, other)
     middle = middle.astype(jnp.bfloat16).astype(jnp.float32)
 
-    hidden, kept_one = mix(middle, gains_one[0], attn_one, taps_one, False)
+    hidden, kept_one = mix(middle, gains_one[0], ring, wide, taps_one, False)
     scale, normed = rms_rows(hidden, gains_one[1])
     block, rest, grad_halves, inner = feed_both(
-        units, tail, *spread_pair(normed), *grads_one, feed_one, attn_one
+        units, tail, *spread_pair(normed), *grads_one, feed_one, ring, wide
     )
     queue.scatter(block)
     final = hidden + collect(dot_nt(inner[:, :units], down_one))
     back, gain_two = rms_back(hidden, scale, gains_one[1], collect(dot_nt(grad_halves, feed_one[:, main:])))
     attn_grads, grad_middle, gain_one, taps_one = mix_back(
-        kept_one, grad_out + back, gains_one[0], attn_one, taps_one, rest, False
+        kept_one, grad_out + back, gains_one[0], ring, taps_one, rest, False
     )
     gains_one = jnp.stack([gain_one, gain_two])
 
     grad_middle = grad_middle.astype(jnp.bfloat16).astype(jnp.float32)
     hidden, scale, near, far = kept_feed
     block, rest, grad_halves, _ = feed_both(
-        units, tail, near, far, *spread_pair(grad_middle), packed, attn_zero, attn_grads
+        units, tail, near, far, *spread_pair(grad_middle), packed, attn_zero, attn_zero.shape[1], attn_grads
     )
     queue.scatter(block)
     terms = dot_nt(grad_halves, packed[:, main:split])
@@ -724,7 +728,7 @@
     queue.scatter(attn_grads)
     gains_zero = jnp.stack([gain_one, gain_two])
 
-    edge = attn_one.shape[1]
+    edge = wide
     grads_one = (queue.done[0], queue.done[1][:, :edge])
     grads_zero = (queue.done[1][:, edge:], queue.done[2])
 

time: 743 us -> 743 us (level)
  transfers between devices with their start and end apart: 64 -> 64, of which waited for: 38 -> 39; matrix products, arithmetic and copies ran while one was open for 19% -> 18% of each run, Pallas kernels for 10% -> 10%
where the time goes in v10:
time: 743 us; the launch traced here: 733 us
  waiting for transfers between devices  292 us (39%)
  blocking collectives  116 us (16%)
  Pallas kernels  91 us (12%)
  local copies, waits for them, and re-layouts  90.4 us (12%)
  starting transfers between devices  69.3 us (9%)
  other arithmetic  46.2 us (6%)
  between operations  16 us (2%)
  matrix products  11.9 us (2%)
    all_gather x8, blocking collectives, spread_pair(): lax.all_gather(rows.astype(jnp.bfloat16), 'tensor', axis=0, tiled=True)  116 us
    reduce_scatter x3, waiting for transfers between devices, scatter(): lax.psum_scatter(block, 'dp', scatter_dimension=0, tiled=True)  101 us
    ppermute x3, waiting for transfers between devices, ring_step(): return lax.ppermute(piece, 'dp', [(i, (i + 1) % size) for i in range(size)])  82.1 us
    ppermute x24, waiting for transfers between devices, collect_pair(): total = total + lax.ppermute(block, 'tensor', pairs).astype(jnp.float32)  59.9 us
    pallas_call x4, Pallas kernels, whole_call(): pl.pallas_call(kernel, grid=(1,), out_shape=[jax.ShapeDtypeStruct(shape,...  41.6 us
    pallas_call x2, Pallas kernels, feed_both(): pl.pallas_call(functools.partial(feed_kernel, units, tail), grid=(2 * CHU...  33.4 us
    ppermute x24, starting transfers between devices, collect_pair(): total = total + lax.ppermute(block, 'tensor', pairs).astype(jnp.float32)  28.2 us
    ppermute x3, starting transfers between devices, ring_step(): return lax.ppermute(piece, 'dp', [(i, (i + 1) % size) for i in range(size)])  28 us
  transfers between devices with their start and end apart: 64, of which 39 were waited for; matrix products, arithmetic and copies ran while one was open for 18% of the time, Pallas kernels for 10%

profile of v10, /device:TPU:0, one launch (start us, length us, event | category | flops | bytes accessed | tf_op | source)
XLA Modules:
  0.0 733.0 jit_solution(8059280880087099096)
XLA Ops:
  17.7 5.9 constant_dynamic-slice_fusion.26
  24.9 3.2 concatenate.112
  43.4 3.3 concatenate.109
  60.4 3.0 collective-permute-start.6
  63.5 12.0 %all_gather.33.near_ref = bf16[256,1792]{1,0:T(8,128)(2,1)S(1)} all-gather(bf16[64,1792]{1,0:T(8,128)(2,1)S(1)} %fusion.20), channel_id=1, replica_groups=mesh['section'=2,'dp'=4,'tensor'=4] {'tensor'}, dimensions={0}, use_global_device_ids=true | all-gather | bytes 1146880 | tf_op jit(solution)/shard_map/all_gather | solution.py:44
  76.4 30.1 %collective-permute-done.6 = bf16[448,1408]{1,0:T(8,128)(2,1)} collective-permute-done((bf16[448,1408]{1,0:T(8,128)(2,1)S(1)}, bf16[448,1408]{1,0:T(8,128)(2,1)}, u32[]{:S(2)}, u32[]{:S(2)}) %collective-permute-start.6) | collective-permute-done | bytes 1261600 | tf_op jit(solution)/shard_map/ppermute | solution.py:73
  107.5 6.7 shard_map.169
  123.0 20.2 %all_gather.36.near_grad_ref = bf16[256,1792]{1,0:T(8,128)(2,1)S(1)} all-gather(bf16[64,1792]{1,0:T(8,128)(2,1)S(1)} %copy-done.36), channel_id=1, replica_groups=mesh['section'=2,'dp'=4,'tensor'=4] {'tensor'}, dimensions={0}, use_global_device_ids=true | all-gather | bytes 1146880 | tf_op jit(solution)/shard_map/all_gather | solution.py:44
  145.4 28.4 %collective-permute-done.12 = bf16[448,1408]{1,0:T(8,128)(2,1)} collective-permute-done((bf16[448,1408]{1,0:T(8,128)(2,1)}, bf16[448,1408]{1,0:T(8,128)(2,1)}, u32[]{:S(2)}, u32[]{:S(2)}) %collective-permute-start.12) | collective-permute-done | bytes 1261600 | tf_op jit(solution)/shard_map/ppermute | solution.py:73
  173.7 24.6 %collective-permute-start.13 = (bf16[448,1408]{1,0:T(8,128)(2,1)}, bf16[448,1408]{1,0:T(8,128)(2,1)}, u32[]{:S(2)}, u32[]{:S(2)}) collective-permute-start(bf16[448,1408]{1,0:T(8,128)(2,1)} %collective-permute-done.12), channel_id=1, source_target_pairs={{0,4},{4,8},{8,12},{12,0},{1,5},{5,9},{9,13},{13,1},{2,6},{6,10},{... | collective-permute-start | bytes 3784712 | tf_op jit(solution)/shard_map/ppermute | solution.py:73
  198.5 19.5 %all_gather.35.near_ref = bf16[256,1792]{1,0:T(8,128)(2,1)S(1)} all-gather(bf16[64,1792]{1,0:T(8,128)(2,1)S(1)} %multiply_convert_fusion.1), channel_id=1, replica_groups=mesh['section'=2,'dp'=4,'tensor'=4] {'tensor'}, dimensions={0}, use_global_device_ids=true | all-gather | bytes 1146880 | tf_op jit(solution)/shard_map/all_gather | solution.py:44
  223.3 23.7 %collective-permute-done.13 = bf16[448,1408]{1,0:T(8,128)(2,1)} collective-permute-done((bf16[448,1408]{1,0:T(8,128)(2,1)}, bf16[448,1408]{1,0:T(8,128)(2,1)}, u32[]{:S(2)}, u32[]{:S(2)}) %collective-permute-start.13) | collective-permute-done | bytes 1261600 | tf_op jit(solution)/shard_map/ppermute | solution.py:73
  251.1 5.7 pad_maximum_fusion.feed_ref
  256.7 11.3 %shard_map.170 = (f32[256,1792]{1,0:T(8,128)S(1)}, bf16[256,1792]{1,0:T(8,128)(2,1)S(1)}) custom-call(bf16[256,1792]{1,0:T(8,128)(2,1)S(1)} %all_gather.35.near_ref, bf16[256,1792]{1,0:T(8,128)(2,1)S(1)} %collective-permute-done.11.far_ref, bf16[1792,1792]{1,0:T(8,128)(2,1)} %pad_maximum_fusion.feed_ref, ...), custom_call_target="tpu_custom_call" | custom-call | flops 1048576 | bytes 65536 | tf_op jit(solution)/shard_map/pallas_call | solution.py:160
  274.4 5.0 collective-permute-done.16
  279.4 5.0 collective-permute-done.18
  286.1 12.8 %all_gather.38.near_ref = bf16[256,1792]{1,0:T(8,128)(2,1)S(1)} all-gather(bf16[64,1792]{1,0:T(8,128)(2,1)S(1)} %fusion.27), channel_id=1, replica_groups=mesh['section'=2,'dp'=4,'tensor'=4] {'tensor'}, dimensions={0}, use_global_device_ids=true | all-gather | bytes 1146880 | tf_op jit(solution)/shard_map/all_gather | solution.py:44
  302.4 8.6 %shard_map.171 = (f32[256,1792]{1,0:T(8,128)}, bf16[256,1792]{1,0:T(8,128)(2,1)}, f32[512,896]{1,0:T(8,128)}, bf16[512,256]{1,0:T(8,128)(2,1)}) custom-call(bf16[256,1792]{1,0:T(8,128)(2,1)} %copy-done.5, bf16[256,1792]{1,0:T(8,128)(2,1)} %copy-done.11, bf16[1792,1408]{1,0:T(8,128)(2,1)} %constant_dynamic-update-slice_fusion.attn_ref.last_ref, ...), custom_call_target="tpu_custom_call" | custom-call | flops 1048576 | bytes 65536 | tf_op jit(solution)/shard_map/pallas_call | solution.py:471
  319.0 5.0 collective-permute-done.21
  324.0 4.0 collective-permute-done.23
  329.8 12.5 %all_gather.39.near_ref = bf16[256,1792]{1,0:T(8,128)(2,1)S(1)} all-gather(bf16[64,1792]{1,0:T(8,128)(2,1)S(1)} %multiply_convert_fusion), channel_id=1, replica_groups=mesh['section'=2,'dp'=4,'tensor'=4] {'tensor'}, dimensions={0}, use_global_device_ids=true | all-gather | bytes 1146880 | tf_op jit(solution)/shard_map/all_gather | solution.py:44
  342.3 6.4 all-gather.8.cloned.1.call-done.feed_ref
  348.8 15.9 %shard_map.172 = (bf16[1792,1792]{1,0:T(8,128)(2,1)}, bf16[1792,256]{1,0:T(8,128)(2,1)}, bf16[512,1280]{1,0:T(8,128)(2,1)}, bf16[512,640]{1,0:T(8,128)(2,1)}) custom-call(bf16[256,1792]{1,0:T(8,128)(2,1)} %copy-done.34, bf16[256,1792]{1,0:T(8,128)(2,1)} %collective-permute-done.24.far_ref, bf16[256,1792]{1,0:T(8,128)(2,1)} %copy-done.33, ...), custom_call_target="tpu_custom_call" | custom-call | flops 6576668672 | bytes 20971520 | tf_op jit(solution)/shard_map/pallas_call | solution.py:282
  364.7 5.3 fusion.3
  376.5 5.0 collective-permute-done.26
  381.5 5.1 collective-permute-done.28
  389.5 13.2 %all_gather.41.near_grad_ref = bf16[256,1792]{1,0:T(8,128)(2,1)S(1)} all-gather(bf16[64,1792]{1,0:T(8,128)(2,1)S(1)} %get-tuple-element.183), channel_id=1, replica_groups=mesh['section'=2,'dp'=4,'tensor'=4] {'tensor'}, dimensions={0}, use_global_device_ids=true | all-gather | bytes 1146880 | tf_op jit(solution)/shard_map/all_gather | solution.py:44
  406.2 14.3 %shard_map.173 = (bf16[1792,1152]{1,0:T(8,128)(2,1)}, f32[256,1792]{1,0:T(8,128)}, bf16[256,1792]{1,0:T(8,128)(2,1)}, f32[8,256]{1,0:T(8,128)}) custom-call(bf16[256,1792]{1,0:T(8,128)(2,1)} %copy-done.5, bf16[256,1792]{1,0:T(8,128)(2,1)} %copy-done.11, bf16[256,1792]{1,0:T(8,128)(2,1)} %copy-done.9, bf16[256,1792]{1,0:T(8,128)(2,1)} %copy-done.31, ...), custom_call_target="tpu_custom_call" | custom-call | flops 1048576 | bytes 65536 | tf_op jit(solution)/shard_map/pallas_call | solution.py:471
  428.5 5.0 collective-permute-done.31
  433.5 4.2 collective-permute-done.33
  439.5 13.0 %all_gather.42.near_grad_ref = bf16[256,1792]{1,0:T(8,128)(2,1)S(1)} all-gather(bf16[64,1792]{1,0:T(8,128)(2,1)S(1)} %fusion.32), channel_id=1, replica_groups=mesh['section'=2,'dp'=4,'tensor'=4] {'tensor'}, dimensions={0}, use_global_device_ids=true | all-gather | bytes 1146880 | tf_op jit(solution)/shard_map/all_gather | solution.py:44
  456.0 17.5 %shard_map.174 = (bf16[1792,2944]{1,0:T(8,128)(2,1)}, bf16[1792,256]{1,0:T(8,128)(2,1)}, bf16[512,1280]{1,0:T(8,128)(2,1)}, bf16[512,640]{1,0:T(8,128)(2,1)}) custom-call(bf16[256,1792]{1,0:T(8,128)(2,1)} %copy-done, bf16[256,1792]{1,0:T(8,128)(2,1)} %copy-done.1, bf16[256,1792]{1,0:T(8,128)(2,1)} %copy-done.35, bf16[256,1792]{1,0:T(8,128)(2,1)} %copy-done.52, ...), custom_call_target="tpu_custom_call" | custom-call | flops 6576668672 | bytes 20971520 | tf_op jit(solution)/shard_map/pallas_call | solution.py:282
  476.0 5.0 fusion.1
  487.5 5.0 collective-permute-done.36
  492.5 5.1 collective-permute-done.38
  499.4 13.0 %all_gather.43.near_grad_ref = bf16[256,1792]{1,0:T(8,128)(2,1)S(1)} all-gather(bf16[64,1792]{1,0:T(8,128)(2,1)S(1)} %get-tuple-element.175), channel_id=1, replica_groups=mesh['section'=2,'dp'=4,'tensor'=4] {'tensor'}, dimensions={0}, use_global_device_ids=true | all-gather | bytes 1146880 | tf_op jit(solution)/shard_map/all_gather | solution.py:44
  515.9 11.9 %shard_map.175 = (bf16[1792,768]{1,0:T(8,128)(2,1)}, f32[256,1792]{1,0:T(8,128)}, bf16[256,1792]{1,0:T(8,128)(2,1)}, f32[8,256]{1,0:T(8,128)}) custom-call(bf16[256,1792]{1,0:T(8,128)(2,1)} %copy-done.4, bf16[256,1792]{1,0:T(8,128)(2,1)} %copy-done.10, bf16[256,1792]{1,0:T(8,128)(2,1)} %copy-done.8, bf16[256,1792]{1,0:T(8,128)(2,1)} %copy-done.30, ...), custom_call_target="tpu_custom_call" | custom-call | flops 1048576 | bytes 65536 | tf_op jit(solution)/shard_map/pallas_call | solution.py:471
  543.2 3.3 collective-permute-done.46
  560.1 11.0 %collective-permute-done.54 = f32[2,5,1792]{2,1,0:T(8,128)S(1)} collective-permute-done((f32[2,5,1792]{2,1,0:T(8,128)S(1)}, f32[2,5,1792]{2,1,0:T(8,128)S(1)}, u32[]{:S(2)}, u32[]{:S(2)}) %collective-permute-start.54) | collective-permute-done | bytes 71712 | tf_op jit(solution)/shard_map/ppermute | solution.py:96
  572.6 87.6 %reduce-scatter.6.cloned.1.call-done = bf16[448,2944]{1,0:T(8,128)(2,1)} async-done(((bf16[1792,2944]{1,0:T(8,128)(2,1)}), bf16[448,2944]{1,0:T(8,128)(2,1)}) %reduce-scatter.6.cloned.1.call-update) | async-done | bytes 2637840 | tf_op jit(solution)/shard_map/reduce_scatter | solution.py:596
  663.0 3.5 collective-permute-start.56
  666.8 5.2 collective-permute-done.56
  677.3 5.3 maximum_convert_fusion.1
  685.9 3.4 concatenate.126
  695.8 3.5 concatenate.125
  701.0 5.7 copy.103
  706.6 10.8 %reduce-scatter.8.cloned.1.call-done.mine_ref = bf16[448,768]{1,0:T(8,128)(2,1)} async-done(((bf16[1792,768]{1,0:T(8,128)(2,1)}), bf16[448,768]{1,0:T(8,128)(2,1)}) %reduce-scatter.8.cloned.1.call-update) | async-done | bytes 688144 | tf_op jit(solution)/shard_map/reduce_scatter | solution.py:596
  720.9 4.7 shard_map.176
  (370 shorter events, 177.7 us)
Async XLA Ops:
  7.2 99.3 %all-gather.4.cloned.1.call-start = ((), (), s32[]{:S(2)}) async-start(), calls=%async_computation.3 | async-start | bytes 3440640 | tf_op jit(solution)/shard_map/all_gather | solution.py:638
  15.0 236.0 %all-gather.6.cloned.1.call-start = ((), (), s32[]{:S(2)}) async-start(), calls=%async_computation.4 | async-start | bytes 6881280 | tf_op jit(solution)/shard_map/all_gather | solution.py:638
  36.6 312.2 %all-gather.8.cloned.1.call-start = ((), (), s32[]{:S(2)}) async-start(), calls=%async_computation.5 | async-start | bytes 8028160 | tf_op jit(solution)/shard_map/all_gather | solution.py:638
  38.4 13.8 %collective-permute-start.1 = (f32[5,1792]{1,0:T(8,128)}, f32[5,1792]{1,0:T(8,128)}, u32[]{:S(2)}, u32[]{:S(2)}) collective-permute-start(f32[5,1792]{1,0:T(8,128)} %pad_maximum_fusion.4), channel_id=1, source_target_pairs={{0,16},{16,0},{1,17},{17,1},{2,18},{18,2},{3,19},{19,3},{4,20},{20... | collective-permute-start | bytes 107528 | tf_op jit(solution)/shard_map/ppermute | solution.py:40
  39.3 13.9 %collective-permute-start = (bf16[64,1792]{1,0:T(8,128)(2,1)}, bf16[64,1792]{1,0:T(8,128)(2,1)}, u32[]{:S(2)}, u32[]{:S(2)}) collective-permute-start(bf16[64,1792]{1,0:T(8,128)(2,1)} %dynamic-slice_bitcast_fusion.2), channel_id=1, source_target_pairs={{0,16},{16,0},{1,17},{17,1},{2,18},{18,2},{3,19},{19,3},{4,20},{20... | collective-permute-start | bytes 688136 | tf_op jit(solution)/shard_map/ppermute | solution.py:40
  46.7 8.5 %collective-permute-start.4 = (bf16[448,1152]{1,0:T(8,128)(2,1)}, bf16[448,1152]{1,0:T(8,128)(2,1)}, u32[]{:S(2)}, u32[]{:S(2)}) collective-permute-start(bf16[448,1152]{1,0:T(8,128)(2,1)} %concatenate.109), channel_id=1, source_target_pairs={{0,16},{16,0},{1,17},{17,1},{2,18},{18,2},{3,19},{19,3},{4,20},{20... | collective-permute-start | bytes 3096584 | tf_op jit(solution)/shard_map/ppermute | solution.py:40
  60.4 46.1 %collective-permute-start.6 = (bf16[448,1408]{1,0:T(8,128)(2,1)S(1)}, bf16[448,1408]{1,0:T(8,128)(2,1)}, u32[]{:S(2)}, u32[]{:S(2)}) collective-permute-start(bf16[448,1408]{1,0:T(8,128)(2,1)S(1)} %get-tuple-element.224), channel_id=1, source_target_pairs={{0,4},{4,8},{8,12},{12,0},{1,5},{5,9},{9,13},{13,1},{2,6},{6,10},{... | collective-permute-start | bytes 3784712 | tf_op jit(solution)/shard_map/ppermute | solution.py:73
  75.5 31.0 %collective-permute-start.2 = (bf16[256,1792]{1,0:T(8,128)(2,1)S(1)}, bf16[256,1792]{1,0:T(8,128)(2,1)S(1)}, u32[]{:S(2)}, u32[]{:S(2)}) collective-permute-start(bf16[256,1792]{1,0:T(8,128)(2,1)S(1)} %all_gather.33.near_ref), channel_id=1, source_target_pairs={{0,16},{16,0},{1,17},{17,1},{2,18},{18,2},{3,19},{19,3},{4,20},{20... | collective-permute-start | bytes 2752520 | tf_op jit(solution)/shard_map/ppermute | solution.py:40
  114.2 59.5 %collective-permute-start.12 = (bf16[448,1408]{1,0:T(8,128)(2,1)}, bf16[448,1408]{1,0:T(8,128)(2,1)}, u32[]{:S(2)}, u32[]{:S(2)}) collective-permute-start(bf16[448,1408]{1,0:T(8,128)(2,1)} %collective-permute-done.6), channel_id=1, source_target_pairs={{0,4},{4,8},{8,12},{12,0},{1,5},{5,9},{9,13},{13,1},{2,6},{6,10},{... | collective-permute-start | bytes 3784712 | tf_op jit(solution)/shard_map/ppermute | solution.py:73
  119.5 23.7 %collective-permute-start.8 = (bf16[64,1792]{1,0:T(8,128)(2,1)}, bf16[64,1792]{1,0:T(8,128)(2,1)S(1)}, u32[]{:S(2)}, u32[]{:S(2)}) collective-permute-start(bf16[64,1792]{1,0:T(8,128)(2,1)} %get-tuple-element.258), channel_id=1, source_target_pairs={{0,1},{1,0},{2,3},{3,2},{4,5},{5,4},{6,7},{7,6},{8,9},{9,8},{10,11... | collective-permute-start | bytes 688136 | tf_op jit(solution)/shard_map/ppermute | solution.py:67
  121.0 22.2 %collective-permute-start.10 = (bf16[64,1792]{1,0:T(8,128)(2,1)}, bf16[64,1792]{1,0:T(8,128)(2,1)}, u32[]{:S(2)}, u32[]{:S(2)}) collective-permute-start(bf16[64,1792]{1,0:T(8,128)(2,1)} %get-tuple-element.259), channel_id=1, source_target_pairs={{0,3},{1,2},{2,1},{3,0},{4,7},{5,6},{6,5},{7,4},{8,11},{9,10},{10,... | collective-permute-start | bytes 688136 | tf_op jit(solution)/shard_map/ppermute | solution.py:67
  122.5 20.7 %collective-permute-start.9 = (bf16[64,1792]{1,0:T(8,128)(2,1)}, bf16[64,1792]{1,0:T(8,128)(2,1)}, u32[]{:S(2)}, u32[]{:S(2)}) collective-permute-start(bf16[64,1792]{1,0:T(8,128)(2,1)} %get-tuple-element.260), channel_id=1, source_target_pairs={{0,2},{1,3},{2,0},{3,1},{4,6},{5,7},{6,4},{7,5},{8,10},{9,11},{10,... | collective-permute-start | bytes 688136 | tf_op jit(solution)/shard_map/ppermute | solution.py:67
  143.2 106.3 %collective-permute-start.14 = (bf16[256,1792]{1,0:T(8,128)(2,1)S(1)}, bf16[256,1792]{1,0:T(8,128)(2,1)}, u32[]{:S(2)}, u32[]{:S(2)}) collective-permute-start(bf16[256,1792]{1,0:T(8,128)(2,1)S(1)} %all_gather.36.near_grad_ref), channel_id=1, source_target_pairs={{0,16},{16,0},{1,17},{17,1},{2,18},{18,2},{3,19},{19,3},{4,20},{20... | collective-permute-start | bytes 2752520 | tf_op jit(solution)/shard_map/ppermute | solution.py:40
  173.7 73.3 %collective-permute-start.13 = (bf16[448,1408]{1,0:T(8,128)(2,1)}, bf16[448,1408]{1,0:T(8,128)(2,1)}, u32[]{:S(2)}, u32[]{:S(2)}) collective-permute-start(bf16[448,1408]{1,0:T(8,128)(2,1)} %collective-permute-done.12), channel_id=1, source_target_pairs={{0,4},{4,8},{8,12},{12,0},{1,5},{5,9},{9,13},{13,1},{2,6},{6,10},{... | collective-permute-start | bytes 3784712 | tf_op jit(solution)/shard_map/ppermute | solution.py:73
  218.0 31.5 %collective-permute-start.11 = (bf16[256,1792]{1,0:T(8,128)(2,1)S(1)}, bf16[256,1792]{1,0:T(8,128)(2,1)S(1)}, u32[]{:S(2)}, u32[]{:S(2)}) collective-permute-start(bf16[256,1792]{1,0:T(8,128)(2,1)S(1)} %all_gather.35.near_ref), channel_id=1, source_target_pairs={{0,16},{16,0},{1,17},{17,1},{2,18},{18,2},{3,19},{19,3},{4,20},{20... | collective-permute-start | bytes 2752520 | tf_op jit(solution)/shard_map/ppermute | solution.py:40
  218.1 257.8 %reduce-scatter.4.cloned.1.call-start = ((), (), s32[]{:S(2)}) async-start(), calls=%async_computation.6 | async-start | bytes 8028160 | tf_op jit(solution)/shard_map/reduce_scatter | solution.py:596
  270.9 8.5 %collective-permute-start.16 = (bf16[64,1792]{1,0:T(8,128)(2,1)S(1)}, bf16[64,1792]{1,0:T(8,128)(2,1)S(1)}, u32[]{:S(2)}, u32[]{:S(2)}) collective-permute-start(bf16[64,1792]{1,0:T(8,128)(2,1)S(1)} %get-tuple-element.255), channel_id=1, source_target_pairs={{0,1},{1,0},{2,3},{3,2},{4,5},{5,4},{6,7},{7,6},{8,9},{9,8},{10,11... | collective-permute-start | bytes 688136 | tf_op jit(solution)/shard_map/ppermute | solution.py:67
  272.3 12.1 %collective-permute-start.18 = (bf16[64,1792]{1,0:T(8,128)(2,1)S(1)}, bf16[64,1792]{1,0:T(8,128)(2,1)S(1)}, u32[]{:S(2)}, u32[]{:S(2)}) collective-permute-start(bf16[64,1792]{1,0:T(8,128)(2,1)S(1)} %get-tuple-element.256), channel_id=1, source_target_pairs={{0,3},{1,2},{2,1},{3,0},{4,7},{5,6},{6,5},{7,4},{8,11},{9,10},{10,... | collective-permute-start | bytes 688136 | tf_op jit(solution)/shard_map/ppermute | solution.py:67
  273.7 12.0 %collective-permute-start.17 = (bf16[64,1792]{1,0:T(8,128)(2,1)S(1)}, bf16[64,1792]{1,0:T(8,128)(2,1)S(1)}, u32[]{:S(2)}, u32[]{:S(2)}) collective-permute-start(bf16[64,1792]{1,0:T(8,128)(2,1)S(1)} %get-tuple-element.257), channel_id=1, source_target_pairs={{0,2},{1,3},{2,0},{3,1},{4,6},{5,7},{6,4},{7,5},{8,10},{9,11},{10,... | collective-permute-start | bytes 688136 | tf_op jit(solution)/shard_map/ppermute | solution.py:67
  315.5 8.5 %collective-permute-start.21 = (bf16[64,1792]{1,0:T(8,128)(2,1)S(1)}, bf16[64,1792]{1,0:T(8,128)(2,1)S(1)}, u32[]{:S(2)}, u32[]{:S(2)}) collective-permute-start(bf16[64,1792]{1,0:T(8,128)(2,1)S(1)} %get-tuple-element.252), channel_id=1, source_target_pairs={{0,1},{1,0},{2,3},{3,2},{4,5},{5,4},{6,7},{7,6},{8,9},{9,8},{10,11... | collective-permute-start | bytes 688136 | tf_op jit(solution)/shard_map/ppermute | solution.py:67
  315.6 12.4 %collective-permute-start.23 = (bf16[64,1792]{1,0:T(8,128)(2,1)S(1)}, bf16[64,1792]{1,0:T(8,128)(2,1)S(1)}, u32[]{:S(2)}, u32[]{:S(2)}) collective-permute-start(bf16[64,1792]{1,0:T(8,128)(2,1)S(1)} %get-tuple-element.253), channel_id=1, source_target_pairs={{0,3},{1,2},{2,1},{3,0},{4,7},{5,6},{6,5},{7,4},{8,11},{9,10},{10,... | collective-permute-start | bytes 688136 | tf_op jit(solution)/shard_map/ppermute | solution.py:67
  317.1 12.3 %collective-permute-start.22 = (bf16[64,1792]{1,0:T(8,128)(2,1)S(1)}, bf16[64,1792]{1,0:T(8,128)(2,1)S(1)}, u32[]{:S(2)}, u32[]{:S(2)}) collective-permute-start(bf16[64,1792]{1,0:T(8,128)(2,1)S(1)} %get-tuple-element.254), channel_id=1, source_target_pairs={{0,2},{1,3},{2,0},{3,1},{4,6},{5,7},{6,4},{7,5},{8,10},{9,11},{10,... | collective-permute-start | bytes 688136 | tf_op jit(solution)/shard_map/ppermute | solution.py:67
  342.3 6.5 collective-permute-start.24
  364.7 295.5 %reduce-scatter.6.cloned.1.call-start = ((), (), s32[]{:S(2)}) async-start(), calls=%async_computation.7 | async-start | bytes 13189120 | tf_op jit(solution)/shard_map/reduce_scatter | solution.py:596
  373.0 8.5 %collective-permute-start.26 = (bf16[64,1792]{1,0:T(8,128)(2,1)S(1)}, bf16[64,1792]{1,0:T(8,128)(2,1)S(1)}, u32[]{:S(2)}, u32[]{:S(2)}) collective-permute-start(bf16[64,1792]{1,0:T(8,128)(2,1)S(1)} %get-tuple-element.249), channel_id=1, source_target_pairs={{0,1},{1,0},{2,3},{3,2},{4,5},{5,4},{6,7},{7,6},{8,9},{9,8},{10,11... | collective-permute-start | bytes 688136 | tf_op jit(solution)/shard_map/ppermute | solution.py:67
  374.5 12.1 %collective-permute-start.28 = (bf16[64,1792]{1,0:T(8,128)(2,1)S(1)}, bf16[64,1792]{1,0:T(8,128)(2,1)S(1)}, u32[]{:S(2)}, u32[]{:S(2)}) collective-permute-start(bf16[64,1792]{1,0:T(8,128)(2,1)S(1)} %get-tuple-element.250), channel_id=1, source_target_pairs={{0,3},{1,2},{2,1},{3,0},{4,7},{5,6},{6,5},{7,4},{8,11},{9,10},{10,... | collective-permute-start | bytes 688136 | tf_op jit(solution)/shard_map/ppermute | solution.py:67
  376.0 12.0 %collective-permute-start.27 = (bf16[64,1792]{1,0:T(8,128)(2,1)S(1)}, bf16[64,1792]{1,0:T(8,128)(2,1)S(1)}, u32[]{:S(2)}, u32[]{:S(2)}) collective-permute-start(bf16[64,1792]{1,0:T(8,128)(2,1)S(1)} %get-tuple-element.251), channel_id=1, source_target_pairs={{0,2},{1,3},{2,0},{3,1},{4,6},{5,7},{6,4},{7,5},{8,10},{9,11},{10,... | collective-permute-start | bytes 688136 | tf_op jit(solution)/shard_map/ppermute | solution.py:67
  424.9 8.5 %collective-permute-start.31 = (bf16[64,1792]{1,0:T(8,128)(2,1)S(1)}, bf16[64,1792]{1,0:T(8,128)(2,1)S(1)}, u32[]{:S(2)}, u32[]{:S(2)}) collective-permute-start(bf16[64,1792]{1,0:T(8,128)(2,1)S(1)} %get-tuple-element.246), channel_id=1, source_target_pairs={{0,1},{1,0},{2,3},{3,2},{4,5},{5,4},{6,7},{7,6},{8,9},{9,8},{10,11... | collective-permute-start | bytes 688136 | tf_op jit(solution)/shard_map/ppermute | solution.py:67
  425.6 12.1 %collective-permute-start.33 = (bf16[64,1792]{1,0:T(8,128)(2,1)S(1)}, bf16[64,1792]{1,0:T(8,128)(2,1)S(1)}, u32[]{:S(2)}, u32[]{:S(2)}) collective-permute-start(bf16[64,1792]{1,0:T(8,128)(2,1)S(1)} %get-tuple-element.247), channel_id=1, source_target_pairs={{0,3},{1,2},{2,1},{3,0},{4,7},{5,6},{6,5},{7,4},{8,11},{9,10},{10,... | collective-permute-start | bytes 688136 | tf_op jit(solution)/shard_map/ppermute | solution.py:67
  427.0 12.0 %collective-permute-start.32 = (bf16[64,1792]{1,0:T(8,128)(2,1)S(1)}, bf16[64,1792]{1,0:T(8,128)(2,1)S(1)}, u32[]{:S(2)}, u32[]{:S(2)}) collective-permute-start(bf16[64,1792]{1,0:T(8,128)(2,1)S(1)} %get-tuple-element.248), channel_id=1, source_target_pairs={{0,2},{1,3},{2,0},{3,1},{4,6},{5,7},{6,4},{7,5},{8,10},{9,11},{10,... | collective-permute-start | bytes 688136 | tf_op jit(solution)/shard_map/ppermute | solution.py:67
  475.9 241.5 %reduce-scatter.8.cloned.1.call-start = ((), (), s32[]{:S(2)}) async-start(), calls=%async_computation.8 | async-start | bytes 3440640 | tf_op jit(solution)/shard_map/reduce_scatter | solution.py:596
  483.9 8.5 %collective-permute-start.36 = (bf16[64,1792]{1,0:T(8,128)(2,1)S(1)}, bf16[64,1792]{1,0:T(8,128)(2,1)S(1)}, u32[]{:S(2)}, u32[]{:S(2)}) collective-permute-start(bf16[64,1792]{1,0:T(8,128)(2,1)S(1)} %get-tuple-element.243), channel_id=1, source_target_pairs={{0,1},{1,0},{2,3},{3,2},{4,5},{5,4},{6,7},{7,6},{8,9},{9,8},{10,11... | collective-permute-start | bytes 688136 | tf_op jit(solution)/shard_map/ppermute | solution.py:67
  485.5 12.1 %collective-permute-start.38 = (bf16[64,1792]{1,0:T(8,128)(2,1)S(1)}, bf16[64,1792]{1,0:T(8,128)(2,1)S(1)}, u32[]{:S(2)}, u32[]{:S(2)}) collective-permute-start(bf16[64,1792]{1,0:T(8,128)(2,1)S(1)} %get-tuple-element.244), channel_id=1, source_target_pairs={{0,3},{1,2},{2,1},{3,0},{4,7},{5,6},{6,5},{7,4},{8,11},{9,10},{10,... | collective-permute-start | bytes 688136 | tf_op jit(solution)/shard_map/ppermute | solution.py:67
  486.9 12.0 %collective-permute-start.37 = (bf16[64,1792]{1,0:T(8,128)(2,1)S(1)}, bf16[64,1792]{1,0:T(8,128)(2,1)S(1)}, u32[]{:S(2)}, u32[]{:S(2)}) collective-permute-start(bf16[64,1792]{1,0:T(8,128)(2,1)S(1)} %get-tuple-element.245), channel_id=1, source_target_pairs={{0,2},{1,3},{2,0},{3,1},{4,6},{5,7},{6,4},{7,5},{8,10},{9,11},{10,... | collective-permute-start | bytes 688136 | tf_op jit(solution)/shard_map/ppermute | solution.py:67
  533.6 9.5 %collective-permute-start.44 = (bf16[64,1792]{1,0:T(8,128)(2,1)}, bf16[64,1792]{1,0:T(8,128)(2,1)S(1)}, u32[]{:S(2)}, u32[]{:S(2)}) collective-permute-start(bf16[64,1792]{1,0:T(8,128)(2,1)} %get-tuple-element.240), channel_id=1, source_target_pairs={{0,1},{1,0},{2,3},{3,2},{4,5},{5,4},{6,7},{7,6},{8,9},{9,8},{10,11... | collective-permute-start | bytes 688136 | tf_op jit(solution)/shard_map/ppermute | solution.py:67
  533.7 12.8 %collective-permute-start.46 = (bf16[64,1792]{1,0:T(8,128)(2,1)}, bf16[64,1792]{1,0:T(8,128)(2,1)S(1)}, u32[]{:S(2)}, u32[]{:S(2)}) collective-permute-start(bf16[64,1792]{1,0:T(8,128)(2,1)} %get-tuple-element.241), channel_id=1, source_target_pairs={{0,3},{1,2},{2,1},{3,0},{4,7},{5,6},{6,5},{7,4},{8,11},{9,10},{10,... | collective-permute-start | bytes 688136 | tf_op jit(solution)/shard_map/ppermute | solution.py:67
  535.1 12.8 %collective-permute-start.45 = (bf16[64,1792]{1,0:T(8,128)(2,1)}, bf16[64,1792]{1,0:T(8,128)(2,1)}, u32[]{:S(2)}, u32[]{:S(2)}) collective-permute-start(bf16[64,1792]{1,0:T(8,128)(2,1)} %get-tuple-element.242), channel_id=1, source_target_pairs={{0,2},{1,3},{2,0},{3,1},{4,6},{5,7},{6,4},{7,5},{8,10},{9,11},{10,... | collective-permute-start | bytes 688136 | tf_op jit(solution)/shard_map/ppermute | solution.py:67
  541.7 8.0 %collective-permute-start.47 = (bf16[256,1792]{1,0:T(8,128)(2,1)}, bf16[256,1792]{1,0:T(8,128)(2,1)}, u32[]{:S(2)}, u32[]{:S(2)}) collective-permute-start(bf16[256,1792]{1,0:T(8,128)(2,1)} %slice.474), channel_id=1, source_target_pairs={{0,16},{16,0},{1,17},{17,1},{2,18},{18,2},{3,19},{19,3},{4,20},{20... | collective-permute-start | bytes 2752520 | tf_op jit(solution)/shard_map/ppermute | solution.py:40
  551.7 6.2 collective-permute-start.53
  554.3 105.9 %collective-permute-start.48 = (bf16[64,1792]{1,0:T(8,128)(2,1)}, bf16[64,1792]{1,0:T(8,128)(2,1)}, u32[]{:S(2)}, u32[]{:S(2)}) collective-permute-start(bf16[64,1792]{1,0:T(8,128)(2,1)} %get-tuple-element.237), channel_id=1, source_target_pairs={{0,1},{1,0},{2,3},{3,2},{4,5},{5,4},{6,7},{7,6},{8,9},{9,8},{10,11... | collective-permute-start | bytes 688136 | tf_op jit(solution)/shard_map/ppermute | solution.py:67
  554.6 105.6 %collective-permute-start.50 = (bf16[64,1792]{1,0:T(8,128)(2,1)}, bf16[64,1792]{1,0:T(8,128)(2,1)}, u32[]{:S(2)}, u32[]{:S(2)}) collective-permute-start(bf16[64,1792]{1,0:T(8,128)(2,1)} %get-tuple-element.238), channel_id=1, source_target_pairs={{0,3},{1,2},{2,1},{3,0},{4,7},{5,6},{6,5},{7,4},{8,11},{9,10},{10,... | collective-permute-start | bytes 688136 | tf_op jit(solution)/shard_map/ppermute | solution.py:67
  556.1 104.2 %collective-permute-start.49 = (bf16[64,1792]{1,0:T(8,128)(2,1)}, bf16[64,1792]{1,0:T(8,128)(2,1)}, u32[]{:S(2)}, u32[]{:S(2)}) collective-permute-start(bf16[64,1792]{1,0:T(8,128)(2,1)} %get-tuple-element.239), channel_id=1, source_target_pairs={{0,2},{1,3},{2,0},{3,1},{4,6},{5,7},{6,4},{7,5},{8,10},{9,11},{10,... | collective-permute-start | bytes 688136 | tf_op jit(solution)/shard_map/ppermute | solution.py:67
  557.9 13.2 %collective-permute-start.54 = (f32[2,5,1792]{2,1,0:T(8,128)S(1)}, f32[2,5,1792]{2,1,0:T(8,128)S(1)}, u32[]{:S(2)}, u32[]{:S(2)}) collective-permute-start(f32[2,5,1792]{2,1,0:T(8,128)S(1)} %fusion.56), channel_id=1, source_target_pairs={{0,2},{1,3},{2,0},{3,1},{4,6},{5,7},{6,4},{7,5},{8,10},{9,11},{10,... | collective-permute-start | bytes 215048 | tf_op jit(solution)/shard_map/ppermute | solution.py:96
  571.1 90.9 %collective-permute-start.55 = (f32[2,5,1792]{2,1,0:T(8,128)S(1)}, f32[2,5,1792]{2,1,0:T(8,128)}, u32[]{:S(2)}, u32[]{:S(2)}) collective-permute-start(f32[2,5,1792]{2,1,0:T(8,128)S(1)} %add.350), channel_id=1, source_target_pairs={{0,4},{4,0},{8,12},{12,8},{1,5},{5,1},{9,13},{13,9},{2,6},{6,2},{1... | collective-permute-start | bytes 215048 | tf_op jit(solution)/shard_map/ppermute | solution.py:96
  663.0 9.0 %collective-permute-start.56 = (f32[2,5,1792]{2,1,0:T(8,128)S(1)}, f32[2,5,1792]{2,1,0:T(8,128)S(1)}, u32[]{:S(2)}, u32[]{:S(2)}) collective-permute-start(f32[2,5,1792]{2,1,0:T(8,128)S(1)} %add.351), channel_id=1, source_target_pairs={{0,8},{4,12},{8,0},{12,4},{1,9},{5,13},{9,1},{13,5},{2,10},{6,14},... | collective-permute-start | bytes 215048 | tf_op jit(solution)/shard_map/ppermute | solution.py:96
  666.7 7.0 collective-permute-start.51
  673.2 9.7 %collective-permute-start.41 = (bf16[448,1792]{1,0:T(8,128)(2,1)S(1)}, bf16[448,1792]{1,0:T(8,128)(2,1)S(1)}, u32[]{:S(2)}, u32[]{:S(2)}) collective-permute-start(bf16[448,1792]{1,0:T(8,128)(2,1)S(1)} %broadcast_select_fusion.2), channel_id=1, source_target_pairs={{0,16},{16,0},{1,17},{17,1},{2,18},{18,2},{3,19},{19,3},{4,20},{20... | collective-permute-start | bytes 4816904 | tf_op jit(solution)/shard_map/ppermute | solution.py:40
  675.5 7.1 collective-permute-start.40
  (72 other events, 1372.0 us)
Sparse Core Ops, SparseCore 0:
  15.1 68.0 all-gather.3
  85.3 144.4 all-gather.5
  232.0 116.7 all-gather.7
  364.8 111.0 reduce-scatter.3
  478.1 182.0 reduce-scatter.5
  662.4 55.0 reduce-scatter.7
